TPU v7x, 256 devices: a whole 4x4x8 slice. The times are simulated.
256 devices in a mesh: dp: 32 (over z_hi, y, core), hd: 8 (over x, z_lo).
Axes of the slice: x: 4, y: 4, z: 8 (z_hi: 4, z_lo: 2; z = z_hi * 2 + z_lo), core: 2. Of those that a mesh axis runs over, the one named last changes fastest.
Arguments:
- query_nope: bfloat16 [2048, 16384], P('dp', 'hd'), may hold values from -6 to 6
- query_rope: bfloat16 [2048, 8192], P('dp', 'hd')
- latent: bfloat16 [2048, 512], P('dp'), may hold values from -6 to 6
- key_rope: bfloat16 [2048, 64], P('dp'), may hold values from -6 to 6
- key_up: bfloat16 [512, 16384], P(None, 'hd'), may hold values from -0.25 to 0.25
- value_up: bfloat16 [512, 16384], P(None, 'hd'), may hold values from -0.25 to 0.25
- output_weight: bfloat16 [16384, 7168], P('hd', 'dp'), may hold values from -0.046875 to 0.046875
- residual: bfloat16 [2048, 7168], P('dp', 'hd'), may hold values from -6 to 6
- norm_gain: float32 [7168], P('hd'), may hold values from 0.1 to 1.9
- gate_weight: bfloat16 [7168, 18432], P('hd', 'dp'), may hold values from -0.0625 to 0.0625
- up_weight: bfloat16 [7168, 18432], P('hd', 'dp'), may hold values from -0.0625 to 0.0625
- down_weight: bfloat16 [18432, 7168], P('dp', 'hd'), may hold values from -0.046875 to 0.046875
- rank_tokens: int32 [32], replicated, may hold values from 1 to 64, 1024 in all
- request_ids: int32 [32, 64], P('dp'), may hold values from 0 to 3, never falling along the last dimension, each value on 1 to 32 neighbouring positions
Outputs:
- layer_out: bfloat16 [2048, 7168], P('dp', 'hd')
Inputs may be any that keep to these rules, and one draw needn't show every extreme that they name: `rank_tokens`: the counts sum to 1024. `request_ids`: along each rank's slots the number never falls; one request covers at most 32 slots.
All inputs are finite; a program needn't handle non-finite values.
Results may differ from a plain program's by a relative error of at most 0.0085.
Values may be sent and summed in bfloat16 or wider, within the bound.
No kernel may reach another device: no remote copies, remote signals or barrier semaphores. Data moves between devices by JAX's collectives and lax.ppermute only.
A program may use at most 128 MiB of HBM per device.

v0:
```python
import jax
import jax.numpy as jnp
from jax import lax
from jax.sharding import PartitionSpec as P

D = 7168
NOPE = 128
ROPE = 64
VH = 128


def attend(query_nope, query_rope, latent, key_rope, key_up, value_up, request_row):
    slots = latent.shape[0]
    heads = key_up.shape[1] // NOPE
    key_nope = jnp.dot(latent, key_up, preferred_element_type=jnp.float32).astype(jnp.bfloat16)
    values = jnp.dot(latent, value_up, preferred_element_type=jnp.float32).astype(jnp.bfloat16)
    query_heads = query_nope.reshape(slots, heads, NOPE)
    rotary_heads = query_rope.reshape(slots, heads, ROPE)
    scores = jnp.einsum(
        "shd,thd->hst",
        query_heads,
        key_nope.reshape(slots, heads, NOPE),
        preferred_element_type=jnp.float32,
    )
    scores = scores + jnp.einsum(
        "shd,td->hst", rotary_heads, key_rope, preferred_element_type=jnp.float32
    )
    scores = scores * (NOPE + ROPE) ** (-0.5)
    position = jnp.arange(slots, dtype=jnp.int32)
    allowed = (request_row[:, None] == request_row[None, :]) & (
        position[None, :] <= position[:, None]
    )
    scores = jnp.where(allowed[None, :, :], scores, jnp.float32(-1e30))
    top = jnp.max(scores, axis=-1, keepdims=True)
    raised = jnp.exp(scores - top)
    weights = (raised / jnp.sum(raised, axis=-1, keepdims=True)).astype(jnp.bfloat16)
    attended = jnp.einsum(
        "hst,thd->shd",
        weights,
        values.reshape(slots, heads, VH),
        preferred_element_type=jnp.float32,
    )
    return attended.astype(jnp.bfloat16).reshape(slots, heads * VH)


def feed_forward(partial_gate, down_weight):
    width = down_weight.shape[0]
    totals = lax.psum(partial_gate, "hd")
    hidden = (jax.nn.silu(totals[:, :width]) * totals[:, width:]).astype(jnp.bfloat16)
    return jnp.dot(hidden, down_weight, preferred_element_type=jnp.float32)


def on_device(
    query_nope,
    query_rope,
    latent,
    key_rope,
    key_up,
    value_up,
    output_weight,
    residual,
    norm_gain,
    gate_weight,
    up_weight,
    down_weight,
    rank_tokens,
    request_ids,
):
    slots = latent.shape[0]
    ranks = lax.axis_size("dp")
    attended = attend(query_nope, query_rope, latent, key_rope, key_up, value_up, request_ids[0])
    partial_proj = jnp.dot(
        lax.all_gather(attended, "dp", axis=0, tiled=True),
        output_weight,
        preferred_element_type=jnp.float32,
    )
    by_token = lax.all_to_all(partial_proj, "dp", split_axis=0, concat_axis=1, tiled=True)
    projected = lax.psum_scatter(by_token, "hd", scatter_dimension=1, tiled=True)
    mixed = (residual.astype(jnp.float32) + projected).astype(jnp.bfloat16)
    widened = mixed.astype(jnp.float32)
    square_sum = lax.psum(jnp.sum(widened * widened, axis=1), "hd")
    normed = (widened * lax.rsqrt(square_sum[:, None] / D + 1e-06) * norm_gain).astype(jnp.bfloat16)
    piece = lax.all_gather(normed, "dp", axis=0, tiled=True)
    gate_part = jnp.dot(piece, gate_weight, preferred_element_type=jnp.float32)
    up_part = jnp.dot(piece, up_weight, preferred_element_type=jnp.float32)
    partial_gate = jnp.concatenate((gate_part, up_part), axis=1)
    down_rows = feed_forward(partial_gate, down_weight)
    mlp = lax.psum_scatter(down_rows, "dp", scatter_dimension=0, tiled=True)
    index = lax.axis_index("dp")
    count = jnp.sum(jnp.where(jnp.arange(ranks, dtype=jnp.int32) == index, rank_tokens, 0))
    live = jnp.arange(slots, dtype=jnp.int32) < count
    result = (widened + mlp).astype(jnp.bfloat16)
    return jnp.where(live[:, None], result, jnp.zeros_like(result))


def solution(mesh):
    in_specs = (
        P("dp", "hd"),
        P("dp", "hd"),
        P("dp", None),
        P("dp", None),
        P(None, "hd"),
        P(None, "hd"),
        P("hd", "dp"),
        P("dp", "hd"),
        P("hd"),
        P("hd", "dp"),
        P("hd", "dp"),
        P("dp", "hd"),
        P(),
        P("dp", None),
    )
    out_specs = P("dp", "hd")
    return jax.shard_map(
        on_device, mesh=mesh, in_specs=in_specs, out_specs=out_specs, check_vma=False
    )
```

profile of v0, /device:TPU:1, one launch (start us, length us, event | category | flops | bytes accessed | tf_op | source)
XLA Modules:
  0.0 819.0 jit_solution(870191014144648425)
XLA Ops:
  6.5 0.0 copy-start
  6.5 0.0 copy-start.3
  6.5 0.0 all-gather.3.cloned.1.call-start
  6.5 1.3 reshape.75
  7.8 0.0 copy-start.2
  7.8 0.9 fusion.25
  8.7 0.0 copy-done
  8.7 1.3 fusion.11
  10.1 0.0 copy-start.7
  10.1 1.3 convolution_bitcast_fusion.1
  11.4 1.1 fusion.8
  12.5 0.1 fusion.30
  12.6 0.0 copy-done.3
  12.6 0.0 copy-done.2
  12.6 0.5 fusion.10
  13.1 0.3 fusion.9
  13.5 0.8 copy.50
  14.2 0.0 all-gather.3.cloned.1.call-update
  14.2 0.0 reduce-scatter.3.cloned.1.call-start
  14.3 80.4 %all-gather.3.cloned.1.call-done = bf16[2048,2048]{1,0:T(8,128)(2,1)} async-done(((bf16[64,2048]{1,0:T(8,128)(2,1)}), bf16[2048,2048]{1,0:T(8,128)(2,1)}) %all-gather.3.cloned.1.call-update) | async-done | bytes 8388624 | tf_op jit(solution)/shard_map/all_gather | solution.py:73
  94.7 0.0 copy-done.7
  94.7 5.9 fusion.31
  100.6 60.4 %all_to_all.19 = f32[32,64,224]{2,1,0:T(8,128)S(1)} all-to-all(f32[32,64,224]{2,1,0:T(8,128)S(1)} %bitcast.53), channel_id=1, replica_groups=mesh['dp'=32,'hd'=8] {'dp'}, dimensions={0} | all-to-all | bytes 3670016 | tf_op jit(solution)/shard_map/all_to_all | solution.py:77
  161.0 0.0 copy-start.4
  161.0 0.0 copy-start.5
  161.0 1.2 copy.28
  162.2 2.7 all_to_all.17
  164.9 0.0 reduce-scatter.3.cloned.1.call-update
  164.9 0.0 all-gather.5.cloned.1.call-start
  165.0 46.9 %reduce-scatter.3.cloned.1.call-done = f32[64,896]{1,0:T(8,128)} async-done(((f32[64,7168]{1,0:T(8,128)}), f32[64,896]{1,0:T(8,128)}) %reduce-scatter.3.cloned.1.call-update) | async-done | bytes 229392 | tf_op jit(solution)/shard_map/reduce_scatter | solution.py:78
  211.9 0.0 copy-done.4
  211.9 1.1 fusion.20
  213.0 13.6 %psum.14 = f32[64]{0:T(128)S(1)} all-reduce(f32[64]{0:T(128)S(1)} %get-tuple-element.5), channel_id=1, replica_groups=mesh['dp'=32,'hd'=8] {'hd'}, use_global_device_ids=true, to_apply=%region_5.6 | all-reduce | flops 64 | bytes 512 | tf_op jit(solution)/shard_map/psum | solution.py:81
  226.5 0.0 copy-done.5
  226.5 0.7 fusion.22
  227.3 0.0 all-gather.5.cloned.1.call-update
  227.3 0.2 all-reduce.2.cloned.1.call-start
  227.5 61.8 %all-gather.5.cloned.1.call-done = bf16[2048,896]{1,0:T(8,128)(2,1)} async-done(((bf16[64,896]{1,0:T(8,128)(2,1)}), bf16[2048,896]{1,0:T(8,128)(2,1)}) %all-gather.5.cloned.1.call-update) | async-done | bytes 3670032 | tf_op jit(solution)/shard_map/all_gather | solution.py:83
  289.3 0.0 copy-start.6
  289.3 5.1 fusion.32
  294.4 0.0 copy-done.6
  294.4 3.9 fusion.33
  298.3 4.9 pad_maximum_fusion
  303.2 0.0 all-reduce.2.cloned.1.call-update
  303.2 0.0 reduce-scatter.5.cloned.1.call-start
  303.2 381.2 %all-reduce.2.cloned.1.call-done = f32[2048,1152]{0,1:T(8,128)} async-done(((f32[2048,1152]{0,1:T(8,128)}), f32[2048,1152]{0,1:T(8,128)}) %all-reduce.2.cloned.1.call-update) | async-done | bytes 9437200 | tf_op jit(solution)/shard_map/psum | solution.py:48
  684.4 0.0 copy-start.1
  684.4 10.6 %fusion.2 = f32[2048,896]{1,0:T(8,128)} fusion(bf16[576,896]{1,0:T(8,128)(2,1)} %param.25, f32[2048,1152]{0,1:T(8,128)} %all-reduce.2.cloned.1.call-done), kind=kOutput, calls=%fused_computation.4 | convolution fusion | flops 2121007104 | bytes 17809408 | tf_op jit(solution)/shard_map/dot_general | solution.py:50
  695.1 0.0 copy-start.8
  695.1 0.0 reduce-scatter.5.cloned.1.call-update
  695.1 0.6 copy-done.8
  695.7 0.6 fusion.27
  696.4 0.6 iota_compare_fusion.1
  697.0 113.8 %reduce-scatter.5.cloned.1.call-done = f32[64,896]{1,0:T(8,128)} async-done(((f32[2048,896]{1,0:T(8,128)}), f32[64,896]{1,0:T(8,128)}) %reduce-scatter.5.cloned.1.call-update) | async-done | bytes 229392 | tf_op jit(solution)/shard_map/reduce_scatter | solution.py:88
  810.8 1.7 fusion.24
  812.5 0.0 copy-done.1
  (1 shorter events, 0.0 us)
Async XLA Ops:
  6.5 2.2 copy-start
  6.5 6.1 copy-start.3
  6.5 88.2 %all-gather.3.cloned.1.call-start = ((), (), s32[]{:S(2)}) async-start(), calls=%async_computation.3 | async-start | bytes 8650752 | tf_op jit(solution)/shard_map/all_gather | solution.py:73
  7.8 4.8 copy-start.2
  10.1 84.7 %copy-start.7 = (bf16[2048,224]{0,1:T(8,128)(2,1)S(1)}, bf16[2048,224]{0,1:T(8,128)(2,1)}, u32[]{:S(2)}) copy-start(bf16[2048,224]{0,1:T(8,128)(2,1)} %param.20) | copy-start | bytes 2752516
  14.2 197.6 %reduce-scatter.3.cloned.1.call-start = ((), (), s32[]{:S(2)}) async-start(), calls=%async_computation.4 | async-start | bytes 2064384 | tf_op jit(solution)/shard_map/reduce_scatter | solution.py:78
  161.0 50.9 %copy-start.4 = (bf16[64,896]{1,0:T(8,128)(2,1)S(1)}, bf16[64,896]{1,0:T(8,128)(2,1)}, u32[]{:S(2)}) copy-start(bf16[64,896]{1,0:T(8,128)(2,1)} %param.21) | copy-start | bytes 344068
  161.0 65.5 %copy-start.5 = (f32[896]{0:T(1024)S(1)}, f32[896]{0:T(1024)}, u32[]{:S(2)}) copy-start(f32[896]{0:T(1024)} %param.22) | copy-start | bytes 10756
  164.9 124.4 %all-gather.5.cloned.1.call-start = ((), (), s32[]{:S(2)}) async-start(), calls=%async_computation.5 | async-start | bytes 3784704 | tf_op jit(solution)/shard_map/all_gather | solution.py:83
  227.3 457.2 %all-reduce.2.cloned.1.call-start = ((), (), s32[]{:S(2)}) async-start(), calls=%async_computation.6 | async-start | bytes 18874368 | tf_op jit(solution)/shard_map/psum | solution.py:48
  289.3 5.1 copy-start.6
  303.2 507.6 %reduce-scatter.5.cloned.1.call-start = ((), (), s32[]{:S(2)}) async-start(), calls=%async_computation.7 | async-start | bytes 7569408 | tf_op jit(solution)/shard_map/reduce_scatter | solution.py:88
  684.4 128.1 %copy-start.1 = (bf16[512,2048]{1,0:T(8,128)(2,1)S(1)}, bf16[512,2048]{1,0:T(8,128)(2,1)}, u32[]{:S(2)}) copy-start(bf16[512,2048]{1,0:T(8,128)(2,1)} %param.18) | copy-start | bytes 6291460
  695.1 0.7 copy-start.8
Sparse Core Ops, SparseCore 0:
  14.4 80.3 all-gather.2
  165.1 46.7 reduce-scatter.2
  227.4 61.8 all-gather.4
  303.3 381.0 all-reduce.1
  695.2 115.5 reduce-scatter.4
where the time goes:
time: 819 us
  waiting for transfers between devices  684 us (84%)
  blocking collectives  74 us (9%)
  matrix products  30 us (4%)
  between operations  13.3 us (2%)
  other arithmetic  10.7 us (1%)
    psum x1, waiting for transfers between devices, feed_forward(): totals = lax.psum(partial_gate, 'hd')  381 us
    reduce_scatter x1, waiting for transfers between devices, on_device(): mlp = lax.psum_scatter(down_rows, 'dp', scatter_dimension=0, tiled=True)  114 us
    all_gather x1, waiting for transfers between devices, on_device(): lax.all_gather(attended, 'dp', axis=0, tiled=True)  80.4 us
    all_gather x1, waiting for transfers between devices, on_device(): piece = lax.all_gather(normed, 'dp', axis=0, tiled=True)  61.8 us
    all_to_all x1, blocking collectives, on_device(): lax.all_to_all(partial_proj, 'dp', split_axis=0, concat_axis=1, tiled=True)  60.4 us
    reduce_scatter x1, waiting for transfers between devices, on_device(): lax.psum_scatter(by_token, 'hd', scatter_dimension=1, tiled=True)  46.9 us
  transfers between devices with their start and end apart: 5, of which 5 were waited for; matrix products, arithmetic and copies ran while one was open for 0% of the time, Pallas kernels for 0%

commit v1 on v0

v1 whole, which is shorter than its diff:
```python
import jax
import jax.numpy as jnp
from jax import lax
from jax.experimental import pallas as pl
from jax.experimental.pallas import tpu as pltpu
from jax.sharding import Mesh, PartitionSpec as P

BF = jnp.bfloat16
F32 = jnp.float32
NOPE = 128
ROPE = 64
VH = 128
WIN = 32
LIVE = 1024
BLK = 128
DP = ("zh", "y", "c")
HD = ("x", "zl")


def dot(a, b):
    return jnp.dot(a, b, preferred_element_type=F32)


def shifted(x, axis, shift):
    n = lax.axis_size(axis)
    return lax.ppermute(x, axis, [(i, (i + shift) % n) for i in range(n)])


def iota(shape, dim):
    return lax.broadcasted_iota(jnp.int32, shape, dim)


def score_kernel(place_ref, counts_ref, qn_ref, qr_ref, lat_ref, kr_ref, ku_ref, req_ref, out_ref):
    slots = lat_ref.shape[0]
    heads = ku_ref.shape[1] // NOPE
    place = place_ref[0]
    before = lax.fori_loop(
        0,
        counts_ref.shape[0],
        lambda i, a: a + jnp.where(i < place, counts_ref[i], 0),
        jnp.int32(0),
    )
    keys = dot(lat_ref[...], ku_ref[...]).astype(BF)
    key_rope = kr_ref[...]
    s_at, t_at = iota((slots, slots), 0), iota((slots, slots), 1)
    across = jnp.broadcast_to(req_ref[...], (slots, slots))
    down = jnp.sum(jnp.where(s_at == t_at, across, 0), axis=1, keepdims=True)
    allowed = (across == down) & (t_at <= s_at)
    t_row, lane = iota((slots, BLK), 0), iota((slots, BLK), 1)
    lands = ((before + t_row) & (WIN - 1)) == (lane & (WIN - 1))
    nt = (((1,), (1,)), ((), ()))
    per = BLK // WIN
    for group in range(heads // per):
        total = jnp.zeros((slots, BLK), F32)
        for i in range(per):
            h = group * per + i
            s = lax.dot_general(
                qn_ref[:, h * NOPE : (h + 1) * NOPE],
                keys[:, h * NOPE : (h + 1) * NOPE],
                nt,
                preferred_element_type=F32,
            )
            s = s + lax.dot_general(
                qr_ref[:, h * ROPE : (h + 1) * ROPE], key_rope, nt, preferred_element_type=F32
            )
            s = jnp.where(allowed, s * (NOPE + ROPE) ** (-0.5), jnp.float32(-1e30))
            raised = jnp.exp(s - jnp.max(s, axis=-1, keepdims=True))
            w = (raised / jnp.sum(raised, axis=-1, keepdims=True)).astype(BF)
            fold = jnp.where(lands & ((lane >> 5) == i), 1.0, 0.0).astype(BF)
            total = total + dot(w, fold)
        out_ref[:, group * BLK : (group + 1) * BLK] = total.astype(BF)


def score_weights(place, counts, qn, qr, lat, kr, ku, req):
    heads = ku.shape[1] // NOPE
    smem = pl.BlockSpec(memory_space=pltpu.SMEM)
    vmem = pl.BlockSpec(memory_space=pltpu.VMEM)
    return pl.pallas_call(
        score_kernel,
        out_shape=jax.ShapeDtypeStruct((lat.shape[0], heads * WIN), BF),
        in_specs=[smem, smem] + [vmem] * 6,
        out_specs=vmem,
        compiler_params=pltpu.CompilerParams(vmem_limit_bytes=32 * 1024 * 1024),
        name="score_weights",
    )(place, counts, qn, qr, lat, kr, ku, req)


def mix_kernel(wp_ref, prev_ref, cur_ref, wo_ref, out_ref, att_ref):
    heads = cur_ref.shape[1] // VH
    r_at, l_at = iota((BLK, BLK), 0), iota((BLK, BLK), 1)
    in_prev = (BLK + r_at - l_at) < WIN
    gap = r_at - l_at
    in_cur = (gap >= 0) & (gap < WIN)
    per = BLK // WIN
    for group in range(heads // per):
        packed = wp_ref[:, group * BLK : (group + 1) * BLK].astype(F32)
        for i in range(per):
            h = group * per + i
            one = jnp.where((l_at >> 5) == i, packed, 0.0)
            one = one + pltpu.roll(one, WIN, 1)
            one = one + pltpu.roll(one, 2 * WIN, 1)
            band = jnp.concatenate(
                [jnp.where(in_prev, one, 0.0), jnp.where(in_cur, one, 0.0)], axis=1
            ).astype(BF)
            cols = slice(h * VH, (h + 1) * VH)
            both = jnp.concatenate([prev_ref[:, cols], cur_ref[:, cols]], axis=0)
            att_ref[:, cols] = dot(band, both).astype(BF)
    part = dot(att_ref[...], wo_ref[...]).astype(BF)
    order = ((r_at & 15) * 8 + (r_at >> 4)) == l_at
    part = dot(jnp.where(order, 1.0, 0.0).astype(BF), part).astype(BF)
    out_ref[...] = part.reshape(out_ref.shape)


def mix_project(wp, values, wo):
    rows, width = values.shape
    n = wo.shape[1]
    return pl.pallas_call(
        mix_kernel,
        grid=(rows // BLK,),
        out_shape=jax.ShapeDtypeStruct((8, rows // 8, n), BF),
        in_specs=[
            pl.BlockSpec((BLK, wp.shape[1]), lambda b: (b, 0)),
            pl.BlockSpec((BLK, width), lambda b: (jnp.maximum(b - 1, 0), 0)),
            pl.BlockSpec((BLK, width), lambda b: (b, 0)),
            pl.BlockSpec((width, n), lambda b: (0, 0)),
        ],
        out_specs=pl.BlockSpec((8, BLK // 8, n), lambda b: (0, b, 0)),
        scratch_shapes=[pltpu.VMEM((BLK, width), BF)],
        compiler_params=pltpu.CompilerParams(vmem_limit_bytes=32 * 1024 * 1024),
        name="mix_project",
    )(wp, values, values, wo)


def gate_up_kernel(x_ref, gain_ref, gate_ref, up_ref, out_ref):
    pieces, rows, k = x_ref.shape
    ff = gate_ref.shape[1]
    gate = jnp.zeros((rows, ff), F32)
    up = jnp.zeros((rows, ff), F32)
    squares = jnp.zeros((rows, 1), F32)
    for jj in range(pieces):
        j = (jj & 1) * 2 + (jj >> 1)
        x = x_ref[jj].astype(F32)
        squares = squares + jnp.sum(x * x, axis=1, keepdims=True)
        xg = (x * gain_ref[j]).astype(BF)
        gate = gate + dot(xg, gate_ref[j * k : (j + 1) * k, :])
        up = up + dot(xg, up_ref[j * k : (j + 1) * k, :])
    lane = iota((rows, BLK), 1)
    high = squares.astype(BF).astype(F32)
    extra = jnp.where(lane == 0, high, jnp.where(lane == 1, squares - high, 0.0))
    shape = out_ref.shape
    both = jnp.concatenate([gate, up, extra], axis=1).astype(BF)
    out_ref[...] = both.reshape(shape)


def gate_up(x4, gain, gate_weight, up_weight):
    pieces, tokens, k = x4.shape
    ff = gate_weight.shape[1]
    rows = 256
    chunk = tokens // 8
    per = rows // chunk
    return pl.pallas_call(
        gate_up_kernel,
        grid=(tokens // rows,),
        out_shape=jax.ShapeDtypeStruct((8, chunk, 2 * ff + BLK), BF),
        in_specs=[
            pl.BlockSpec((pieces, rows, k), lambda b: (0, b, 0)),
            pl.BlockSpec((pieces, 1, k), lambda b: (0, 0, 0)),
            pl.BlockSpec((pieces * k, ff), lambda b: (0, 0)),
            pl.BlockSpec((pieces * k, ff), lambda b: (0, 0)),
        ],
        out_specs=pl.BlockSpec((per, chunk, 2 * ff + BLK), lambda b: (b, 0, 0)),
        compiler_params=pltpu.CompilerParams(vmem_limit_bytes=32 * 1024 * 1024),
        name="gate_up",
    )(x4, gain.reshape(pieces, 1, k), gate_weight, up_weight)


def gather_relative(x):
    x = jnp.concatenate([x] + [shifted(x, "zh", s) for s in (1, 2, 3)], axis=0)
    x = jnp.concatenate([x] + [shifted(x, "y", s) for s in (1, 2, 3)], axis=0)
    return jnp.concatenate([x, shifted(x, "c", 1)], axis=0)


def place_blocks(x, axis, spot):
    n = lax.axis_size(axis)
    me = lax.axis_index(axis)
    out = jnp.zeros((n,) + x.shape, x.dtype)
    for s in range(n):
        piece = x if s == 0 else shifted(x, axis, s)
        at = spot((me - s + n) % n)
        out = lax.dynamic_update_slice(out, piece[None], (at,) + (0,) * x.ndim)
    return out


def pick(x, index):
    return lax.dynamic_index_in_dim(x, index, 0, keepdims=False)


def on_device(
    query_nope,
    query_rope,
    latent,
    key_rope,
    key_up,
    value_up,
    output_weight,
    residual,
    norm_gain,
    gate_weight,
    up_weight,
    down_weight,
    rank_tokens,
    request_ids,
):
    slots = latent.shape[0]
    ranks = rank_tokens.shape[0]
    zh, y, c = (lax.axis_index(a) for a in DP)
    x_at, zl = (lax.axis_index(a) for a in HD)
    rank = (zh * 4 + y) * 2 + c
    chunk = LIVE // 8
    width = residual.shape[1]
    quarter = width // 4
    model = 8 * width

    every = jnp.arange(ranks, dtype=jnp.int32)

    def starts(which):
        return jnp.sum(jnp.where(every < which[..., None], rank_tokens, 0), axis=-1)

    def lengths(which):
        return jnp.sum(jnp.where(every == which[..., None], rank_tokens, 0), axis=-1)

    own_start, own_length = starts(rank), lengths(rank)
    slot = jnp.arange(slots, dtype=jnp.int32)

    latents = gather_relative(latent)
    weights = score_weights(
        rank.reshape(1), rank_tokens, query_nope, query_rope, latent, key_rope, key_up, request_ids
    )
    weights = gather_relative(weights)

    back = jnp.arange(ranks, dtype=jnp.int32)
    source = (
        ((zh - (back & 3)) & 3) * 8 + ((y - ((back >> 2) & 3)) & 3) * 2 + (c ^ (back >> 4))
    )
    goes = jnp.where(
        slot[None, :] < lengths(source)[:, None], starts(source)[:, None] + slot[None, :], -1
    ).reshape(1, ranks * slots)
    compact = (goes == jnp.arange(LIVE, dtype=jnp.int32)[:, None]).astype(BF)
    latents = dot(compact, latents).astype(BF)
    values = dot(latents, value_up).astype(BF)
    weights = dot(compact, weights).astype(BF)

    eight = jnp.arange(8, dtype=jnp.int32)
    spread = ((eight[:, None] - own_start) & 7) + 8 * eight[None, :]
    roll = (spread.reshape(slots, 1) == slot[None, :]).astype(BF)
    rows = dot(roll, residual).astype(BF).reshape(2, 4, 8, 2, 2, quarter)
    rows = rows.transpose(1, 0, 3, 4, 2, 5).reshape(ranks, 8, quarter)
    rows = lax.all_to_all(rows, DP, split_axis=0, concat_axis=0, tiled=True)
    mine = (y >> 1) * 4 + zh
    place = ((mine - starts(every)[:, None]) & 7) + 8 * eight[None, :]
    goes = jnp.where(
        place < rank_tokens[:, None], (starts(every)[:, None] + place) >> 3, -1
    ).reshape(1, ranks * 8)
    gather = (goes == jnp.arange(chunk, dtype=jnp.int32)[:, None]).astype(BF)
    rows = dot(gather, rows.reshape(ranks * 8, quarter))

    part = mix_project(weights, values, output_weight)
    part = lax.all_to_all(part, HD, split_axis=0, concat_axis=0, tiled=True)
    projected = jnp.sum(part.astype(F32), axis=0).astype(BF)
    sends = []
    for a in range(4):
        for b in range(4):
            for e in range(2):
                for f in range(4):
                    for g in range(2):
                        m = f * 2 + g
                        to = ((m & 3) * 4 + (m >> 2) * 2 + (b & 1)) * 2 + e
                        h = a * 2 + (b >> 1)
                        sends.append((((a * 4 + b) * 2 + e) * 8 + m, to * 8 + h))
    projected = lax.ppermute(projected, DP + HD, sends)
    mixed = (rows + projected.astype(F32)).astype(BF)

    full = place_blocks(mixed, "zh", lambda i: i)
    full = place_blocks(full, "y", lambda i: (i & 1) * 2 + (i >> 1))
    full = place_blocks(full, "c", lambda i: i)
    full = full.reshape(4, LIVE, quarter)

    part = gate_up(full, norm_gain, gate_weight, up_weight)
    part = lax.all_to_all(part, HD, split_axis=0, concat_axis=0, tiled=True)
    total = jnp.sum(part.astype(F32), axis=0)
    ff = down_weight.shape[0]
    scale = lax.rsqrt((total[:, 2 * ff : 2 * ff + 1] + total[:, 2 * ff + 1 : 2 * ff + 2]) / model + 1e-06)
    hidden = (jax.nn.silu(total[:, :ff] * scale) * (total[:, ff : 2 * ff] * scale)).astype(BF)
    hidden = jnp.broadcast_to(hidden[None], (8,) + hidden.shape)
    hidden = lax.all_to_all(hidden, HD, split_axis=0, concat_axis=0, tiled=True)

    down = dot(hidden.reshape(LIVE, ff), down_weight).reshape(4, 2, chunk, width)
    down = jnp.swapaxes(down, 0, 1)
    down = pick(down, c) + shifted(pick(down, 1 - c).astype(BF), "c", 1).astype(F32)
    total = pick(down, y)
    for s in (1, 2, 3):
        total = total + shifted(pick(down, (y + s) & 3).astype(BF), "y", s).astype(F32)
    m = y * 2 + c
    first = starts(every)
    place = ((m - first[:, None]) & 7) + 8 * eight[None, :]
    comes = jnp.where(place < rank_tokens[:, None], (first[:, None] + place) >> 3, -1)
    expand = (comes.reshape(4, slots, 1) == jnp.arange(chunk, dtype=jnp.int32)).astype(BF)
    planes = dot(expand.reshape(4 * slots, chunk), total.astype(BF)).reshape(4, slots, width)
    own = full.reshape(4, 8, chunk, quarter)
    own = lax.dynamic_index_in_dim(own, m, 1, keepdims=False)
    own = jnp.concatenate([own[0], own[2], own[1], own[3]], axis=1)
    result = dot(pick(expand, zh), own) + pick(planes, zh)
    for s in (1, 2, 3):
        result = result + shifted(pick(planes, (zh + s) & 3).astype(BF), "zh", s).astype(F32)
    result = lax.all_to_all(
        result.astype(BF).reshape(8, 8, width), ("y", "c"), split_axis=0, concat_axis=0, tiled=True
    )
    at = ((own_start + slot) & 7) * 8 + (slot >> 3)
    at = jnp.where(slot < own_length, at, -1)
    back = (at[:, None] == slot[None, :]).astype(BF)
    return dot(back, result.reshape(slots, width)).astype(BF)


def solution(mesh):
    mesh = Mesh(mesh.devices.reshape(4, 4, 2, 4, 2), DP + HD)
    in_specs = (
        P(DP, HD),
        P(DP, HD),
        P(DP, None),
        P(DP, None),
        P(None, HD),
        P(None, HD),
        P(HD, DP),
        P(DP, HD),
        P(HD),
        P(HD, DP),
        P(HD, DP),
        P(DP, HD),
        P(),
        P(DP, None),
    )
    return jax.shard_map(
        on_device, mesh=mesh, in_specs=in_specs, out_specs=P(DP, HD), check_vma=False
    )
```

time: 819 us -> 311 us (0.38)
  waiting for transfers between devices: 684 us -> 81.8 us
  starting transfers between devices: 0.35 us -> 87 us
  local copies, waits for them, and re-layouts: 6.59 us -> 55.1 us
  blocking collectives: 74 us -> 37.3 us
  Pallas kernels: 0 us -> 19.5 us
  between operations: 13.3 us -> 0.55 us
  matrix products: 30 us -> 19 us
    psum x1 -> x0, waiting for transfers between devices: 381 us -> none  [feed_forward(): totals = lax.psum(partial_gate, 'hd')]
    reduce_scatter x2 -> x0, waiting for transfers between devices: 161 us -> none  [the longest x1 114 us: on_device(): mlp = lax.psum_scatter(down_rows, 'dp', scatter_dimension=0, tiled=True)]
    all_gather x2 -> x0, waiting for transfers between devices: 142 us -> none  [the longest x1 80.4 us: on_device(): lax.all_gather(attended, 'dp', axis=0, tiled=True)]
    ppermute x0 -> x29, starting transfers between devices: none -> 67.5 us  [the longest x28 66.9 us: shifted(): return lax.ppermute(x, axis, [(i, (i + shift) % n) for i in range(n)])]
    ppermute x0 -> x29, waiting for transfers between devices: none -> 45.9 us  [the longest x28 45.9 us: shifted(): return lax.ppermute(x, axis, [(i, (i + shift) % n) for i in range(n)])]
    all_to_all x0 -> x4, waiting for transfers between devices: none -> 35.9 us  [the longest x1 15.7 us: on_device(): hidden = lax.all_to_all(hidden, HD, split_axis=0, concat_axis=0, tiled=True)]
    unnamed x18 -> x53, local copies, waits for them, and re-layouts: 0.66 us -> 28 us
    all_to_all x1, blocking collectives: 60.4 us -> 37.3 us  [on_device(): part = lax.all_to_all(part, HD, split_axis=0, concat_axis=0, tiled=True)]
  transfers between devices with their start and end apart: 5 -> 33, of which waited for: 5 -> 17; matrix products, arithmetic and copies ran while one was open for 0% -> 12% of each run, Pallas kernels for 0% -> 1%
where the time goes in v1:
time: 311 us; the launch traced here: 306 us
  starting transfers between devices  87 us (28%)
  waiting for transfers between devices  81.8 us (26%)
  local copies, waits for them, and re-layouts  55.1 us (18%)
  blocking collectives  37.3 us (12%)
  Pallas kernels  19.5 us (6%)
  matrix products  19 us (6%)
  other arithmetic  6.15 us (2%)
    ppermute x28, starting transfers between devices, shifted(): return lax.ppermute(x, axis, [(i, (i + shift) % n) for i in range(n)])  66.9 us
    ppermute x28, waiting for transfers between devices, shifted(): return lax.ppermute(x, axis, [(i, (i + shift) % n) for i in range(n)])  45.9 us
    all_to_all x1, blocking collectives, on_device(): part = lax.all_to_all(part, HD, split_axis=0, concat_axis=0, tiled=True)  37.3 us
    unnamed x53, local copies, waits for them, and re-layouts  28 us
    dot_general x8, matrix products, dot(): return jnp.dot(a, b, preferred_element_type=F32)  19 us
    all_to_all x1, waiting for transfers between devices, on_device(): hidden = lax.all_to_all(hidden, HD, split_axis=0, concat_axis=0, tiled=True)  15.7 us
    pallas_call x1, Pallas kernels, mix_project(): pl.pallas_call(mix_kernel, grid=(rows // BLK,), out_shape=jax.ShapeDtypeS...  10.2 us
    all_to_all x1, waiting for transfers between devices, on_device(): rows = lax.all_to_all(rows, DP, split_axis=0, concat_axis=0, tiled=True)  10 us
  transfers between devices with their start and end apart: 33, of which 17 were waited for; matrix products, arithmetic and copies ran while one was open for 12% of the time, Pallas kernels for 1%

profile of v1, /device:TPU:1, one launch (start us, length us, event | category | flops | bytes accessed | tf_op | source)
XLA Modules:
  0.0 306.4 jit_solution(7317224390438731329)
XLA Ops:
  0.0 3.8 %collective-permute-start.7 = (bf16[64,512]{1,0:T(8,128)(2,1)}, bf16[64,512]{1,0:T(8,128)(2,1)S(1)}, u32[]{:S(2)}, u32[]{:S(2)}) collective-permute-start(bf16[64,512]{1,0:T(8,128)(2,1)} %lat_ref.1), channel_id=1, source_target_pairs={{0,64},{64,128},{128,192},{192,0},{1,65},{65,129},{129,193},{193,1... | collective-permute-start | bytes 196616 | tf_op jit(solution)/shard_map/ppermute | solution.py:26
  3.8 5.1 %collective-permute-start.8 = (bf16[64,512]{1,0:T(8,128)(2,1)}, bf16[64,512]{1,0:T(8,128)(2,1)S(1)}, u32[]{:S(2)}, u32[]{:S(2)}) collective-permute-start(bf16[64,512]{1,0:T(8,128)(2,1)} %lat_ref.1), channel_id=1, source_target_pairs={{0,128},{64,192},{128,0},{192,64},{1,129},{65,193},{129,1},{193,65... | collective-permute-start | bytes 196616 | tf_op jit(solution)/shard_map/ppermute | solution.py:26
  8.9 1.6 copy-done.3
  15.3 3.9 %score_weights.1 = bf16[64,512]{1,0:T(8,128)(2,1)S(1)} custom-call(s32[1]{0:T(128)} %bitcast.4.place_ref, s32[32]{0:T(128)S(1)} %copy-done.10, bf16[64,2048]{1,0:T(8,128)(2,1)S(1)} %copy-done.7, bf16[64,1024]{1,0:T(8,128)(2,1)S(1)} %copy-done.8, bf16[64,512]{1,0:T(8,128)(2,1)S(1)} %copy-done.6, bf16[64,64]{1,0:T(8,128)(2,1)S(1)} %copy-done.9, ...), custom_call_target="tpu_custom_call" | custom-call | tf_op jit(solution)/shard_map/score_weights/pallas_call | solution.py:78
  19.3 4.4 %collective-permute-start.1 = (bf16[64,512]{1,0:T(8,128)(2,1)S(1)}, bf16[64,512]{1,0:T(8,128)(2,1)S(1)}, u32[]{:S(2)}, u32[]{:S(2)}) collective-permute-start(bf16[64,512]{1,0:T(8,128)(2,1)S(1)} %score_weights.1), channel_id=1, source_target_pairs={{0,128},{64,192},{128,0},{192,64},{1,129},{65,193},{129,1},{193,65... | collective-permute-start | bytes 196616 | tf_op jit(solution)/shard_map/ppermute | solution.py:26
  25.1 1.1 collective-permute-start.9
  26.2 1.2 collective-permute-done.1
  27.5 4.8 %collective-permute-done.2 = bf16[64,512]{1,0:T(8,128)(2,1)S(1)} collective-permute-done((bf16[64,512]{1,0:T(8,128)(2,1)S(1)}, bf16[64,512]{1,0:T(8,128)(2,1)S(1)}, u32[]{:S(2)}, u32[]{:S(2)}) %collective-permute-start.2) | collective-permute-done | bytes 65568 | tf_op jit(solution)/shard_map/ppermute | solution.py:26
  32.2 1.4 collective-permute-start.3
  33.6 2.6 collective-permute-start.4
  42.4 4.5 %collective-permute-done.4 = bf16[256,512]{1,0:T(8,128)(2,1)S(1)} collective-permute-done((bf16[256,512]{1,0:T(8,128)(2,1)S(1)}, bf16[256,512]{1,0:T(8,128)(2,1)S(1)}, u32[]{:S(2)}, u32[]{:S(2)}) %collective-permute-start.4) | collective-permute-done | bytes 262176 | tf_op jit(solution)/shard_map/ppermute | solution.py:26
  48.5 4.0 %collective-permute-start.6 = (bf16[1024,512]{1,0:T(8,128)(2,1)}, bf16[1024,512]{1,0:T(8,128)(2,1)}, u32[]{:S(2)}, u32[]{:S(2)}) collective-permute-start(bf16[1024,512]{1,0:T(8,128)(2,1)} %get-tuple-element.26), channel_id=1, source_target_pairs={{0,8},{8,0},{1,9},{9,1},{2,10},{10,2},{3,11},{11,3},{4,12},{12,4},... | collective-permute-start | bytes 3145736 | tf_op jit(solution)/shard_map/ppermute | solution.py:26
  54.1 7.9 %collective-permute-done.11 = bf16[256,512]{1,0:T(8,128)(2,1)S(1)} collective-permute-done((bf16[256,512]{1,0:T(8,128)(2,1)S(1)}, bf16[256,512]{1,0:T(8,128)(2,1)S(1)}, u32[]{:S(2)}, u32[]{:S(2)}) %collective-permute-start.11) | collective-permute-done | bytes 262176 | tf_op jit(solution)/shard_map/ppermute | solution.py:26
  62.8 1.7 collective-permute-done.12
  66.7 1.5 copy.51.wo_ref
  68.2 2.3 constant_dynamic-update-slice_fusion.7
  70.5 4.9 %fusion.4.wp_ref = bf16[1024,512]{1,0:T(8,128)(2,1)} fusion(bf16[2048,512]{1,0:T(8,128)(2,1)} %constant_dynamic-update-slice_fusion.7, s32[2048]{0:T(1024)S(1)} %select_n.179), kind=kOutput, calls=%fused_computation.9 | convolution fusion | flops 2150105088 | bytes 3153920 | tf_op jit(solution)/shard_map/dot_general | solution.py:21
  75.4 2.3 constant_dynamic-update-slice_fusion.26
  77.6 8.1 %convolution_convert_fusion.prev_ref.cur_ref = bf16[1024,2048]{1,0:T(8,128)(2,1)} fusion(bf16[512,2048]{1,0:T(8,128)(2,1)S(1)} %copy-done, bf16[2048,512]{1,0:T(8,128)(2,1)} %constant_dynamic-update-slice_fusion.26, s32[2048]{0:T(1024)S(1)} %select_n.179), kind=kOutput, calls=%fused_computation.6 | convolution fusion | flops 4299685888 | bytes 8396800 | tf_op jit(solution)/shard_map/dot_general | solution.py:21
  85.8 2.2 copy-done.1
  88.0 1.2 copy-done.5
  89.2 10.2 %mix_project.1 = bf16[8,128,224]{2,1,0:T(8,128)(2,1)S(1)} custom-call(bf16[1024,512]{1,0:T(8,128)(2,1)S(1)} %copy-done.5, bf16[1024,2048]{1,0:T(8,128)(2,1)S(1)} %copy-done.1, bf16[1024,2048]{1,0:T(8,128)(2,1)S(1)} %copy-done.1, bf16[2048,224]{1,0:T(8,128)(2,1)S(1)} %copy.51.wo_ref), custom_call_target="tpu_custom_call" | custom-call | tf_op jit(solution)/shard_map/mix_project/pallas_call | solution.py:117
  100.2 2.0 copy.52
  102.2 4.0 %all-to-all-start.1 = ((bf16[8,128,224]{1,2,0:T(8,128)(2,1)}), bf16[8,128,224]{1,2,0:T(8,128)(2,1)S(1)}, u32[]{:S(2)}, u32[]{:S(2)}) async-start(bf16[8,128,224]{1,2,0:T(8,128)(2,1)} %copy.52), calls=%async_computation.1 | async-start | bytes 917504 | tf_op jit(solution)/shard_map/all_to_all | solution.py:268
  108.8 6.3 %all-to-all-done.1 = bf16[8,128,224]{1,2,0:T(8,128)(2,1)S(1)} async-done(((bf16[8,128,224]{1,2,0:T(8,128)(2,1)}), bf16[8,128,224]{1,2,0:T(8,128)(2,1)S(1)}, u32[]{:S(2)}, u32[]{:S(2)}) %all-to-all-start.1) | async-done | bytes 458784 | tf_op jit(solution)/shard_map/all_to_all | solution.py:268
  115.1 6.8 %all-to-all-start = ((bf16[32,8,224]{2,1,0:T(8,128)(2,1)}), bf16[32,8,224]{2,1,0:T(8,128)(2,1)S(1)}, u32[]{:S(2)}, u32[]{:S(2)}) async-start(bf16[32,8,224]{2,1,0:T(8,128)(2,1)} %bitcast.2), calls=%async_computation | async-start | bytes 262144 | tf_op jit(solution)/shard_map/all_to_all | solution.py:258
  122.8 10.0 %all-to-all-done = bf16[32,8,224]{2,1,0:T(8,128)(2,1)S(1)} async-done(((bf16[32,8,224]{2,1,0:T(8,128)(2,1)}), bf16[32,8,224]{2,1,0:T(8,128)(2,1)S(1)}, u32[]{:S(2)}, u32[]{:S(2)}) %all-to-all-start) | async-done | bytes 114720 | tf_op jit(solution)/shard_map/all_to_all | solution.py:258
  133.2 2.5 collective-permute-start.15
  135.7 1.9 collective-permute-start.16
  137.6 3.4 %collective-permute-start.17 = (bf16[128,224]{0,1:T(8,128)(2,1)S(1)}, bf16[128,224]{0,1:T(8,128)(2,1)S(1)}, u32[]{:S(2)}, u32[]{:S(2)}) collective-permute-start(bf16[128,224]{0,1:T(8,128)(2,1)S(1)} %get-tuple-element.53), channel_id=1, source_target_pairs={{0,192},{64,0},{128,64},{192,128},{1,193},{65,1},{129,65},{193,129... | collective-permute-start | bytes 172040 | tf_op jit(solution)/shard_map/ppermute | solution.py:26
  141.0 3.0 collective-permute-done.16
  144.2 14.5 %collective-permute-start.19 = (bf16[4,128,224]{1,2,0:T(8,128)(2,1)S(1)}, bf16[4,128,224]{1,2,0:T(8,128)(2,1)S(1)}, u32[]{:S(2)}, u32[]{:S(2)}) collective-permute-start(bf16[4,128,224]{1,2,0:T(8,128)(2,1)S(1)} %bitcast_dynamic-update-slice_fusion.4), channel_id=1, source_target_pairs={{0,32},{16,48},{32,0},{48,16},{1,33},{17,49},{33,1},{49,17},{2,34}... | collective-permute-start | bytes 688136 | tf_op jit(solution)/shard_map/ppermute | solution.py:26
  158.7 1.2 collective-permute-start.20
  163.1 2.8 collective-permute-done.20
  166.5 4.1 %collective-permute-start.21 = (bf16[4,4,128,224]{2,3,1,0:T(8,128)(2,1)}, bf16[4,4,128,224]{2,3,1,0:T(8,128)(2,1)}, u32[]{:S(2)}, u32[]{:S(2)}) collective-permute-start(bf16[4,4,128,224]{2,3,1,0:T(8,128)(2,1)} %bitcast_dynamic-update-slice_fusion), channel_id=1, source_target_pairs={{0,8},{8,0},{1,9},{9,1},{2,10},{10,2},{3,11},{11,3},{4,12},{12,4},... | collective-permute-start | bytes 2752520 | tf_op jit(solution)/shard_map/ppermute | solution.py:26
  170.6 2.0 copy.57.gate_ref
  172.7 2.4 copy.58.up_ref
  175.1 2.2 copy.55
  177.4 1.6 broadcast_in_dim.120
  180.0 2.2 copy.56
  182.3 2.4 constant_dynamic-update-slice_fusion.34
  184.7 5.4 %gate_up.1 = bf16[8,128,1280]{2,1,0:T(8,128)(2,1)S(1)} custom-call(bf16[4,1024,224]{2,1,0:T(8,128)(2,1)} %bitcast.20.x_ref, f32[4,1,224]{2,1,0:T(1,128)S(1)} %reshape.250.gain_ref, bf16[896,576]{1,0:T(8,128)(2,1)S(1)} %copy.57.gate_ref, bf16[896,576]{1,0:T(8,128)(2,1)S(1)} %copy-done.2), custom_call_target="tpu_custom_call" | custom-call | tf_op jit(solution)/shard_map/gate_up/pallas_call | solution.py:161
  190.0 37.3 %all_to_all.25 = bf16[8,128,1280]{2,1,0:T(8,128)(2,1)S(1)} all-to-all(bf16[8,128,1280]{2,1,0:T(8,128)(2,1)S(1)} %gate_up.1), channel_id=1, replica_groups=mesh['zh'=4,'y'=4,'c'=2,'x'=4,'zl'=2] {'x','zl'}, dimensions={0} | all-to-all | bytes 5242880 | tf_op jit(solution)/shard_map/all_to_all | solution.py:289
  228.3 1.2 broadcast_in_dim.136
  229.4 3.6 %all-to-all-start.3 = ((bf16[8,128,576]{1,2,0:T(8,128)(2,1)}), bf16[8,128,576]{1,2,0:T(8,128)(2,1)S(1)}, u32[]{:S(2)}, u32[]{:S(2)}) async-start(bf16[8,128,576]{1,2,0:T(8,128)(2,1)} %broadcast_in_dim.136), calls=%async_computation.3 | async-start | bytes 2359296 | tf_op jit(solution)/shard_map/all_to_all | solution.py:295
  233.0 15.7 %all-to-all-done.3 = bf16[8,128,576]{1,2,0:T(8,128)(2,1)S(1)} async-done(((bf16[8,128,576]{1,2,0:T(8,128)(2,1)}), bf16[8,128,576]{1,2,0:T(8,128)(2,1)S(1)}, u32[]{:S(2)}, u32[]{:S(2)}) %all-to-all-start.3) | async-done | bytes 1179680 | tf_op jit(solution)/shard_map/all_to_all | solution.py:295
  248.7 3.0 fusion.6
  251.7 1.9 copy-done.13
  254.6 2.3 collective-permute-start.22
  257.6 1.7 collective-permute-done.22
  259.3 1.7 bitcast_add_fusion
  261.0 1.2 copy-done.14
  262.4 3.3 %collective-permute-start.24 = (bf16[128,896]{1,0:T(8,128)(2,1)S(1)}, bf16[128,896]{1,0:T(8,128)(2,1)S(1)}, u32[]{:S(2)}, u32[]{:S(2)}) collective-permute-start(bf16[128,896]{1,0:T(8,128)(2,1)S(1)} %get-tuple-element.16), channel_id=1, source_target_pairs={{0,32},{16,48},{32,0},{48,16},{1,33},{17,49},{33,1},{49,17},{2,34}... | collective-permute-start | bytes 688136 | tf_op jit(solution)/shard_map/ppermute | solution.py:26
  266.8 3.6 %collective-permute-done.23 = bf16[128,896]{1,0:T(8,128)(2,1)S(1)} collective-permute-done((bf16[128,896]{1,0:T(8,128)(2,1)S(1)}, bf16[128,896]{1,0:T(8,128)(2,1)S(1)}, u32[]{:S(2)}, u32[]{:S(2)}) %collective-permute-start.23) | collective-permute-done | bytes 229408 | tf_op jit(solution)/shard_map/ppermute | solution.py:26
  270.4 5.6 %collective-permute-done.24 = bf16[128,896]{1,0:T(8,128)(2,1)S(1)} collective-permute-done((bf16[128,896]{1,0:T(8,128)(2,1)S(1)}, bf16[128,896]{1,0:T(8,128)(2,1)S(1)}, u32[]{:S(2)}, u32[]{:S(2)}) %collective-permute-start.24) | collective-permute-done | bytes 229408 | tf_op jit(solution)/shard_map/ppermute | solution.py:26
  276.0 1.4 fusion.18
  277.4 1.7 collective-permute-start.26
  279.1 2.5 collective-permute-start.27
  281.6 3.5 %collective-permute-start.28 = (bf16[64,896]{1,0:T(8,128)(2,1)S(1)}, bf16[64,896]{1,0:T(8,128)(2,1)S(1)}, u32[]{:S(2)}, u32[]{:S(2)}) collective-permute-start(bf16[64,896]{1,0:T(8,128)(2,1)S(1)} %get-tuple-element.18), channel_id=1, source_target_pairs={{0,192},{64,0},{128,64},{192,128},{1,193},{65,1},{129,65},{193,129... | collective-permute-start | bytes 344072 | tf_op jit(solution)/shard_map/ppermute | solution.py:26
  285.4 3.7 %collective-permute-done.27 = bf16[64,896]{1,0:T(8,128)(2,1)S(1)} collective-permute-done((bf16[64,896]{1,0:T(8,128)(2,1)S(1)}, bf16[64,896]{1,0:T(8,128)(2,1)S(1)}, u32[]{:S(2)}, u32[]{:S(2)}) %collective-permute-start.27) | collective-permute-done | bytes 114720 | tf_op jit(solution)/shard_map/ppermute | solution.py:26
  289.1 5.3 %collective-permute-done.28 = bf16[64,896]{1,0:T(8,128)(2,1)S(1)} collective-permute-done((bf16[64,896]{1,0:T(8,128)(2,1)S(1)}, bf16[64,896]{1,0:T(8,128)(2,1)S(1)}, u32[]{:S(2)}, u32[]{:S(2)}) %collective-permute-start.28) | collective-permute-done | bytes 114720 | tf_op jit(solution)/shard_map/ppermute | solution.py:26
  295.1 5.1 %all-to-all-start.4 = ((bf16[8,8,896]{2,1,0:T(8,128)(2,1)}), bf16[8,8,896]{2,1,0:T(8,128)(2,1)S(1)}, u32[]{:S(2)}, u32[]{:S(2)}) async-start(bf16[8,8,896]{2,1,0:T(8,128)(2,1)} %fusion.32), calls=%async_computation.4 | async-start | bytes 229376 | tf_op jit(solution)/shard_map/all_to_all | solution.py:315
  300.2 1.2 compare_select_fusion.1
  301.4 3.9 %all-to-all-done.4 = bf16[8,8,896]{2,1,0:T(8,128)(2,1)S(1)} async-done(((bf16[8,8,896]{2,1,0:T(8,128)(2,1)}), bf16[8,8,896]{2,1,0:T(8,128)(2,1)S(1)}, u32[]{:S(2)}, u32[]{:S(2)}) %all-to-all-start.4) | async-done | bytes 114720 | tf_op jit(solution)/shard_map/all_to_all | solution.py:315
  (129 shorter events, 34.1 us)
Async XLA Ops:
  0.0 77.6 %copy-start = (bf16[512,2048]{1,0:T(8,128)(2,1)S(1)}, bf16[512,2048]{1,0:T(8,128)(2,1)}, u32[]{:S(2)}) copy-start(bf16[512,2048]{1,0:T(8,128)(2,1)} %param.19) | copy-start | bytes 6291460
  0.0 36.2 %collective-permute-start.7 = (bf16[64,512]{1,0:T(8,128)(2,1)}, bf16[64,512]{1,0:T(8,128)(2,1)S(1)}, u32[]{:S(2)}, u32[]{:S(2)}) collective-permute-start(bf16[64,512]{1,0:T(8,128)(2,1)} %lat_ref.1), channel_id=1, source_target_pairs={{0,64},{64,128},{128,192},{192,0},{1,65},{65,129},{129,193},{193,1... | collective-permute-start | bytes 196616 | tf_op jit(solution)/shard_map/ppermute | solution.py:26
  3.8 34.2 %collective-permute-start.8 = (bf16[64,512]{1,0:T(8,128)(2,1)}, bf16[64,512]{1,0:T(8,128)(2,1)S(1)}, u32[]{:S(2)}, u32[]{:S(2)}) collective-permute-start(bf16[64,512]{1,0:T(8,128)(2,1)} %lat_ref.1), channel_id=1, source_target_pairs={{0,128},{64,192},{128,0},{192,64},{1,129},{65,193},{129,1},{193,65... | collective-permute-start | bytes 196616 | tf_op jit(solution)/shard_map/ppermute | solution.py:26
  8.9 1.6 copy-start.3
  10.5 0.8 copy-start.6
  11.4 0.9 copy-start.7
  12.3 0.9 copy-start.8
  13.2 0.7 copy-start.9
  13.9 0.7 copy-start.10
  14.6 0.7 copy-start.12
  19.2 5.9 %collective-permute-start = (bf16[64,512]{1,0:T(8,128)(2,1)S(1)}, bf16[64,512]{1,0:T(8,128)(2,1)S(1)}, u32[]{:S(2)}, u32[]{:S(2)}) collective-permute-start(bf16[64,512]{1,0:T(8,128)(2,1)S(1)} %score_weights.1), channel_id=1, source_target_pairs={{0,64},{64,128},{128,192},{192,0},{1,65},{65,129},{129,193},{193,1... | collective-permute-start | bytes 196616 | tf_op jit(solution)/shard_map/ppermute | solution.py:26
  19.3 8.2 %collective-permute-start.1 = (bf16[64,512]{1,0:T(8,128)(2,1)S(1)}, bf16[64,512]{1,0:T(8,128)(2,1)S(1)}, u32[]{:S(2)}, u32[]{:S(2)}) collective-permute-start(bf16[64,512]{1,0:T(8,128)(2,1)S(1)} %score_weights.1), channel_id=1, source_target_pairs={{0,128},{64,192},{128,0},{192,64},{1,129},{65,193},{129,1},{193,65... | collective-permute-start | bytes 196616 | tf_op jit(solution)/shard_map/ppermute | solution.py:26
  23.6 8.6 %collective-permute-start.2 = (bf16[64,512]{1,0:T(8,128)(2,1)S(1)}, bf16[64,512]{1,0:T(8,128)(2,1)S(1)}, u32[]{:S(2)}, u32[]{:S(2)}) collective-permute-start(bf16[64,512]{1,0:T(8,128)(2,1)S(1)} %score_weights.1), channel_id=1, source_target_pairs={{0,192},{64,0},{128,64},{192,128},{1,193},{65,1},{129,65},{193,129... | collective-permute-start | bytes 196616 | tf_op jit(solution)/shard_map/ppermute | solution.py:26
  25.1 13.6 %collective-permute-start.9 = (bf16[64,512]{1,0:T(8,128)(2,1)S(1)}, bf16[64,512]{1,0:T(8,128)(2,1)S(1)}, u32[]{:S(2)}, u32[]{:S(2)}) collective-permute-start(bf16[64,512]{1,0:T(8,128)(2,1)S(1)} %copy-done.6), channel_id=1, source_target_pairs={{0,192},{64,0},{128,64},{192,128},{1,193},{65,1},{129,65},{193,129... | collective-permute-start | bytes 196616 | tf_op jit(solution)/shard_map/ppermute | solution.py:26
  32.2 9.4 %collective-permute-start.3 = (bf16[256,512]{1,0:T(8,128)(2,1)S(1)}, bf16[256,512]{1,0:T(8,128)(2,1)S(1)}, u32[]{:S(2)}, u32[]{:S(2)}) collective-permute-start(bf16[256,512]{1,0:T(8,128)(2,1)S(1)} %pad_maximum_fusion), channel_id=1, source_target_pairs={{0,16},{16,32},{32,48},{48,0},{1,17},{17,33},{33,49},{49,1},{2,18}... | collective-permute-start | bytes 786440 | tf_op jit(solution)/shard_map/ppermute | solution.py:26
  33.6 13.3 %collective-permute-start.4 = (bf16[256,512]{1,0:T(8,128)(2,1)S(1)}, bf16[256,512]{1,0:T(8,128)(2,1)S(1)}, u32[]{:S(2)}, u32[]{:S(2)}) collective-permute-start(bf16[256,512]{1,0:T(8,128)(2,1)S(1)} %pad_maximum_fusion), channel_id=1, source_target_pairs={{0,32},{16,48},{32,0},{48,16},{1,33},{17,49},{33,1},{49,17},{2,34}... | collective-permute-start | bytes 786440 | tf_op jit(solution)/shard_map/ppermute | solution.py:26
  36.2 11.5 %collective-permute-start.5 = (bf16[256,512]{1,0:T(8,128)(2,1)S(1)}, bf16[256,512]{1,0:T(8,128)(2,1)S(1)}, u32[]{:S(2)}, u32[]{:S(2)}) collective-permute-start(bf16[256,512]{1,0:T(8,128)(2,1)S(1)} %pad_maximum_fusion), channel_id=1, source_target_pairs={{0,48},{16,0},{32,16},{48,32},{1,49},{17,1},{33,17},{49,33},{2,50}... | collective-permute-start | bytes 786440 | tf_op jit(solution)/shard_map/ppermute | solution.py:26
  39.3 13.9 %collective-permute-start.10 = (bf16[256,512]{1,0:T(8,128)(2,1)S(1)}, bf16[256,512]{1,0:T(8,128)(2,1)S(1)}, u32[]{:S(2)}, u32[]{:S(2)}) collective-permute-start(bf16[256,512]{1,0:T(8,128)(2,1)S(1)} %get-tuple-element.34), channel_id=1, source_target_pairs={{0,16},{16,32},{32,48},{48,0},{1,17},{17,33},{33,49},{49,1},{2,18}... | collective-permute-start | bytes 786440 | tf_op jit(solution)/shard_map/ppermute | solution.py:26
  48.5 18.1 %copy-start.18 = (bf16[2048,512]{1,0:T(8,128)(2,1)}, bf16[2048,512]{1,0:T(8,128)(2,1)S(1)}, u32[]{:S(2)}) copy-start(bf16[2048,512]{1,0:T(8,128)(2,1)S(1)} %get-tuple-element.27) | copy-start | bytes 6291460
  48.5 19.7 %collective-permute-start.6 = (bf16[1024,512]{1,0:T(8,128)(2,1)}, bf16[1024,512]{1,0:T(8,128)(2,1)}, u32[]{:S(2)}, u32[]{:S(2)}) collective-permute-start(bf16[1024,512]{1,0:T(8,128)(2,1)} %get-tuple-element.26), channel_id=1, source_target_pairs={{0,8},{8,0},{1,9},{9,1},{2,10},{10,2},{3,11},{11,3},{4,12},{12,4},... | collective-permute-start | bytes 3145736 | tf_op jit(solution)/shard_map/ppermute | solution.py:26
  52.5 9.4 %collective-permute-start.11 = (bf16[256,512]{1,0:T(8,128)(2,1)S(1)}, bf16[256,512]{1,0:T(8,128)(2,1)S(1)}, u32[]{:S(2)}, u32[]{:S(2)}) collective-permute-start(bf16[256,512]{1,0:T(8,128)(2,1)S(1)} %get-tuple-element.34), channel_id=1, source_target_pairs={{0,32},{16,48},{32,0},{48,16},{1,33},{17,49},{33,1},{49,17},{2,34}... | collective-permute-start | bytes 786440 | tf_op jit(solution)/shard_map/ppermute | solution.py:26
  52.8 11.6 %collective-permute-start.12 = (bf16[256,512]{1,0:T(8,128)(2,1)S(1)}, bf16[256,512]{1,0:T(8,128)(2,1)S(1)}, u32[]{:S(2)}, u32[]{:S(2)}) collective-permute-start(bf16[256,512]{1,0:T(8,128)(2,1)S(1)} %get-tuple-element.34), channel_id=1, source_target_pairs={{0,48},{16,0},{32,16},{48,32},{1,49},{17,1},{33,17},{49,33},{2,50}... | collective-permute-start | bytes 786440 | tf_op jit(solution)/shard_map/ppermute | solution.py:26
  65.3 10.1 %collective-permute-start.13 = (bf16[1024,512]{1,0:T(8,128)(2,1)}, bf16[1024,512]{1,0:T(8,128)(2,1)}, u32[]{:S(2)}, u32[]{:S(2)}) collective-permute-start(bf16[1024,512]{1,0:T(8,128)(2,1)} %get-tuple-element.20), channel_id=1, source_target_pairs={{0,8},{8,0},{1,9},{9,1},{2,10},{10,2},{3,11},{11,3},{4,12},{12,4},... | collective-permute-start | bytes 3145736 | tf_op jit(solution)/shard_map/ppermute | solution.py:26
  85.8 2.2 copy-start.1
  87.9 1.2 copy-start.5
  89.2 17.0 %copy-start.11 = (s32[32]{0:T(128)S(1)}, s32[32]{0:T(128)}, u32[]{:S(2)}) copy-start(s32[32]{0:T(128)} %counts_ref.1) | copy-start | bytes 388
  89.2 18.6 %copy-start.16 = (bf16[64,896]{1,0:T(8,128)(2,1)S(1)}, bf16[64,896]{1,0:T(8,128)(2,1)}, u32[]{:S(2)}) copy-start(bf16[64,896]{1,0:T(8,128)(2,1)} %param.21) | copy-start | bytes 344068
  99.3 0.8 copy-start.4
  102.2 12.9 %all-to-all-start.1 = ((bf16[8,128,224]{1,2,0:T(8,128)(2,1)}), bf16[8,128,224]{1,2,0:T(8,128)(2,1)S(1)}, u32[]{:S(2)}, u32[]{:S(2)}) async-start(bf16[8,128,224]{1,2,0:T(8,128)(2,1)} %copy.52), calls=%async_computation.1 | async-start | bytes 917504 | tf_op jit(solution)/shard_map/all_to_all | solution.py:268
  115.1 17.7 %all-to-all-start = ((bf16[32,8,224]{2,1,0:T(8,128)(2,1)}), bf16[32,8,224]{2,1,0:T(8,128)(2,1)S(1)}, u32[]{:S(2)}, u32[]{:S(2)}) async-start(bf16[32,8,224]{2,1,0:T(8,128)(2,1)} %bitcast.2), calls=%async_computation | async-start | bytes 262144 | tf_op jit(solution)/shard_map/all_to_all | solution.py:258
  122.0 10.9 %collective-permute-start.14 = (bf16[128,224]{0,1:T(8,128)(2,1)S(1)}, bf16[128,224]{0,1:T(8,128)(2,1)S(1)}, u32[]{:S(2)}, u32[]{:S(2)}) collective-permute-start(bf16[128,224]{0,1:T(8,128)(2,1)S(1)} %reduce_sum.82), channel_id=1, source_target_pairs={{0,0},{1,64},{2,128},{3,192},{4,32},{5,96},{6,160},{7,224},{8,8},{... | collective-permute-start | bytes 172040 | tf_op jit(solution)/shard_map/ppermute | solution.py:280
  133.2 7.8 %collective-permute-start.15 = (bf16[128,224]{0,1:T(8,128)(2,1)S(1)}, bf16[128,224]{0,1:T(8,128)(2,1)S(1)}, u32[]{:S(2)}, u32[]{:S(2)}) collective-permute-start(bf16[128,224]{0,1:T(8,128)(2,1)S(1)} %get-tuple-element.53), channel_id=1, source_target_pairs={{0,64},{64,128},{128,192},{192,0},{1,65},{65,129},{129,193},{193,1... | collective-permute-start | bytes 172040 | tf_op jit(solution)/shard_map/ppermute | solution.py:26
  135.7 8.3 %collective-permute-start.16 = (bf16[128,224]{0,1:T(8,128)(2,1)S(1)}, bf16[128,224]{0,1:T(8,128)(2,1)S(1)}, u32[]{:S(2)}, u32[]{:S(2)}) collective-permute-start(bf16[128,224]{0,1:T(8,128)(2,1)S(1)} %get-tuple-element.53), channel_id=1, source_target_pairs={{0,128},{64,192},{128,0},{192,64},{1,129},{65,193},{129,1},{193,65... | collective-permute-start | bytes 172040 | tf_op jit(solution)/shard_map/ppermute | solution.py:26
  137.6 6.4 %collective-permute-start.17 = (bf16[128,224]{0,1:T(8,128)(2,1)S(1)}, bf16[128,224]{0,1:T(8,128)(2,1)S(1)}, u32[]{:S(2)}, u32[]{:S(2)}) collective-permute-start(bf16[128,224]{0,1:T(8,128)(2,1)S(1)} %get-tuple-element.53), channel_id=1, source_target_pairs={{0,192},{64,0},{128,64},{192,128},{1,193},{65,1},{129,65},{193,129... | collective-permute-start | bytes 172040 | tf_op jit(solution)/shard_map/ppermute | solution.py:26
  144.1 17.6 %collective-permute-start.18 = (bf16[4,128,224]{1,2,0:T(8,128)(2,1)S(1)}, bf16[4,128,224]{1,2,0:T(8,128)(2,1)S(1)}, u32[]{:S(2)}, u32[]{:S(2)}) collective-permute-start(bf16[4,128,224]{1,2,0:T(8,128)(2,1)S(1)} %bitcast_dynamic-update-slice_fusion.4), channel_id=1, source_target_pairs={{0,16},{16,32},{32,48},{48,0},{1,17},{17,33},{33,49},{49,1},{2,18}... | collective-permute-start | bytes 688136 | tf_op jit(solution)/shard_map/ppermute | solution.py:26
  144.2 18.2 %collective-permute-start.19 = (bf16[4,128,224]{1,2,0:T(8,128)(2,1)S(1)}, bf16[4,128,224]{1,2,0:T(8,128)(2,1)S(1)}, u32[]{:S(2)}, u32[]{:S(2)}) collective-permute-start(bf16[4,128,224]{1,2,0:T(8,128)(2,1)S(1)} %bitcast_dynamic-update-slice_fusion.4), channel_id=1, source_target_pairs={{0,32},{16,48},{32,0},{48,16},{1,33},{17,49},{33,1},{49,17},{2,34}... | collective-permute-start | bytes 688136 | tf_op jit(solution)/shard_map/ppermute | solution.py:26
  158.7 7.1 %collective-permute-start.20 = (bf16[4,128,224]{1,2,0:T(8,128)(2,1)S(1)}, bf16[4,128,224]{1,2,0:T(8,128)(2,1)S(1)}, u32[]{:S(2)}, u32[]{:S(2)}) collective-permute-start(bf16[4,128,224]{1,2,0:T(8,128)(2,1)S(1)} %bitcast_dynamic-update-slice_fusion.4), channel_id=1, source_target_pairs={{0,48},{16,0},{32,16},{48,32},{1,49},{17,1},{33,17},{49,33},{2,50}... | collective-permute-start | bytes 688136 | tf_op jit(solution)/shard_map/ppermute | solution.py:26
  166.5 13.5 %collective-permute-start.21 = (bf16[4,4,128,224]{2,3,1,0:T(8,128)(2,1)}, bf16[4,4,128,224]{2,3,1,0:T(8,128)(2,1)}, u32[]{:S(2)}, u32[]{:S(2)}) collective-permute-start(bf16[4,4,128,224]{2,3,1,0:T(8,128)(2,1)} %bitcast_dynamic-update-slice_fusion), channel_id=1, source_target_pairs={{0,8},{8,0},{1,9},{9,1},{2,10},{10,2},{3,11},{11,3},{4,12},{12,4},... | collective-permute-start | bytes 2752520 | tf_op jit(solution)/shard_map/ppermute | solution.py:26
  170.6 4.4 %copy-start.17 = (f32[896]{0:T(1024)S(1)}, f32[896]{0:T(1024)}, u32[]{:S(2)}) copy-start(f32[896]{0:T(1024)} %param.22) | copy-start | bytes 10756
  177.4 1.6 copy-start.15
  182.3 2.4 copy-start.2
  229.4 19.2 %all-to-all-start.3 = ((bf16[8,128,576]{1,2,0:T(8,128)(2,1)}), bf16[8,128,576]{1,2,0:T(8,128)(2,1)S(1)}, u32[]{:S(2)}, u32[]{:S(2)}) async-start(bf16[8,128,576]{1,2,0:T(8,128)(2,1)} %broadcast_in_dim.136), calls=%async_computation.3 | async-start | bytes 2359296 | tf_op jit(solution)/shard_map/all_to_all | solution.py:295
  251.7 1.9 copy-start.13
  254.6 4.6 %collective-permute-start.22 = (bf16[4,128,896]{2,1,0:T(8,128)(2,1)}, bf16[4,128,896]{2,1,0:T(8,128)(2,1)S(1)}, u32[]{:S(2)}, u32[]{:S(2)}) collective-permute-start(bf16[4,128,896]{2,1,0:T(8,128)(2,1)} %fusion.8), channel_id=1, source_target_pairs={{0,8},{8,0},{1,9},{9,1},{2,10},{10,2},{3,11},{11,3},{4,12},{12,4},... | collective-permute-start | bytes 2752520 | tf_op jit(solution)/shard_map/ppermute | solution.py:26
  261.0 1.3 copy-start.14
  262.3 8.1 %collective-permute-start.23 = (bf16[128,896]{1,0:T(8,128)(2,1)S(1)}, bf16[128,896]{1,0:T(8,128)(2,1)S(1)}, u32[]{:S(2)}, u32[]{:S(2)}) collective-permute-start(bf16[128,896]{1,0:T(8,128)(2,1)S(1)} %get-tuple-element.14), channel_id=1, source_target_pairs={{0,16},{16,32},{32,48},{48,0},{1,17},{17,33},{33,49},{49,1},{2,18}... | collective-permute-start | bytes 688136 | tf_op jit(solution)/shard_map/ppermute | solution.py:26
  262.4 13.6 %collective-permute-start.24 = (bf16[128,896]{1,0:T(8,128)(2,1)S(1)}, bf16[128,896]{1,0:T(8,128)(2,1)S(1)}, u32[]{:S(2)}, u32[]{:S(2)}) collective-permute-start(bf16[128,896]{1,0:T(8,128)(2,1)S(1)} %get-tuple-element.16), channel_id=1, source_target_pairs={{0,32},{16,48},{32,0},{48,16},{1,33},{17,49},{33,1},{49,17},{2,34}... | collective-permute-start | bytes 688136 | tf_op jit(solution)/shard_map/ppermute | solution.py:26
  265.7 10.3 %collective-permute-start.25 = (bf16[128,896]{1,0:T(8,128)(2,1)S(1)}, bf16[128,896]{1,0:T(8,128)(2,1)S(1)}, u32[]{:S(2)}, u32[]{:S(2)}) collective-permute-start(bf16[128,896]{1,0:T(8,128)(2,1)S(1)} %get-tuple-element.15), channel_id=1, source_target_pairs={{0,48},{16,0},{32,16},{48,32},{1,49},{17,1},{33,17},{49,33},{2,50}... | collective-permute-start | bytes 688136 | tf_op jit(solution)/shard_map/ppermute | solution.py:26
  277.4 8.0 %collective-permute-start.26 = (bf16[64,896]{1,0:T(8,128)(2,1)S(1)}, bf16[64,896]{1,0:T(8,128)(2,1)S(1)}, u32[]{:S(2)}, u32[]{:S(2)}) collective-permute-start(bf16[64,896]{1,0:T(8,128)(2,1)S(1)} %get-tuple-element.17), channel_id=1, source_target_pairs={{0,64},{64,128},{128,192},{192,0},{1,65},{65,129},{129,193},{193,1... | collective-permute-start | bytes 344072 | tf_op jit(solution)/shard_map/ppermute | solution.py:26
  279.1 10.0 %collective-permute-start.27 = (bf16[64,896]{1,0:T(8,128)(2,1)S(1)}, bf16[64,896]{1,0:T(8,128)(2,1)S(1)}, u32[]{:S(2)}, u32[]{:S(2)}) collective-permute-start(bf16[64,896]{1,0:T(8,128)(2,1)S(1)} %get-tuple-element.19), channel_id=1, source_target_pairs={{0,128},{64,192},{128,0},{192,64},{1,129},{65,193},{129,1},{193,65... | collective-permute-start | bytes 344072 | tf_op jit(solution)/shard_map/ppermute | solution.py:26
  281.6 12.8 %collective-permute-start.28 = (bf16[64,896]{1,0:T(8,128)(2,1)S(1)}, bf16[64,896]{1,0:T(8,128)(2,1)S(1)}, u32[]{:S(2)}, u32[]{:S(2)}) collective-permute-start(bf16[64,896]{1,0:T(8,128)(2,1)S(1)} %get-tuple-element.18), channel_id=1, source_target_pairs={{0,192},{64,0},{128,64},{192,128},{1,193},{65,1},{129,65},{193,129... | collective-permute-start | bytes 344072 | tf_op jit(solution)/shard_map/ppermute | solution.py:26
  295.1 10.2 %all-to-all-start.4 = ((bf16[8,8,896]{2,1,0:T(8,128)(2,1)}), bf16[8,8,896]{2,1,0:T(8,128)(2,1)S(1)}, u32[]{:S(2)}, u32[]{:S(2)}) async-start(bf16[8,8,896]{2,1,0:T(8,128)(2,1)} %fusion.32), calls=%async_computation.4 | async-start | bytes 229376 | tf_op jit(solution)/shard_map/all_to_all | solution.py:315

commit v2 on v1

v2 whole, which is shorter than its diff:
```python
import jax
import jax.numpy as jnp
from jax import lax
from jax.experimental import pallas as pl
from jax.experimental.pallas import tpu as pltpu
from jax.sharding import Mesh, PartitionSpec as P

BF = jnp.bfloat16
F32 = jnp.float32
NOPE = 128
ROPE = 64
VH = 128
WIN = 32
LIVE = 1024
BLK = 128
DP = ("zh", "y", "c")
HD = ("x", "zl")


def dot(a, b):
    return jnp.dot(a, b, preferred_element_type=F32)


def shifted(x, axis, shift):
    n = lax.axis_size(axis)
    return lax.ppermute(x, axis, [(i, (i + shift) % n) for i in range(n)])


def iota(shape, dim):
    return lax.broadcasted_iota(jnp.int32, shape, dim)


def nt(a, b):
    return lax.dot_general(a, b, (((1,), (1,)), ((), ())), preferred_element_type=F32)


def whole(shape):
    return pl.BlockSpec(shape, lambda *_: (0,) * len(shape))


def score_kernel(counts_ref, qn_ref, qr_ref, lat_ref, kr_ref, ku_ref, req_ref, out_ref):
    slots = lat_ref.shape[0]
    heads = ku_ref.shape[1] // NOPE
    place = (lax.axis_index("zh") * 4 + lax.axis_index("y")) * 2 + lax.axis_index("c")
    before = lax.fori_loop(
        0,
        counts_ref.shape[0],
        lambda i, a: a + jnp.where(i < place, counts_ref[i], 0),
        jnp.int32(0),
    )
    keys = dot(lat_ref[...], ku_ref[...]).astype(BF)
    key_rope = kr_ref[...]
    s_at, t_at = iota((slots, slots), 0), iota((slots, slots), 1)
    across = jnp.broadcast_to(req_ref[...], (slots, slots))
    down = jnp.sum(jnp.where(s_at == t_at, across, 0), axis=1, keepdims=True)
    allowed = (across == down) & (t_at <= s_at)
    t_row, lane = iota((slots, BLK), 0), iota((slots, BLK), 1)
    lands = ((before + t_row) & (WIN - 1)) == (lane & (WIN - 1))
    per = BLK // WIN
    for group in range(heads // per):
        total = jnp.zeros((slots, BLK), F32)
        for i in range(per):
            h = group * per + i
            s = nt(qn_ref[:, h * NOPE : (h + 1) * NOPE], keys[:, h * NOPE : (h + 1) * NOPE])
            s = s + nt(qr_ref[:, h * ROPE : (h + 1) * ROPE], key_rope)
            s = jnp.where(allowed, s * (NOPE + ROPE) ** (-0.5), jnp.float32(-1e30))
            raised = jnp.exp(s - jnp.max(s, axis=-1, keepdims=True))
            w = (raised / jnp.sum(raised, axis=-1, keepdims=True)).astype(BF)
            fold = jnp.where(lands & ((lane >> 5) == i), 1.0, 0.0).astype(BF)
            total = total + dot(w, fold)
        out_ref[:, group * BLK : (group + 1) * BLK] = total.astype(BF)


def score_weights(counts, *arrays):
    slots, heads = arrays[2].shape[0], arrays[4].shape[1] // NOPE
    shape = (slots, heads * WIN)
    return pl.pallas_call(
        score_kernel,
        grid=(1,),
        out_shape=jax.ShapeDtypeStruct(shape, BF),
        in_specs=[pl.BlockSpec(memory_space=pltpu.SMEM)] + [whole(a.shape) for a in arrays],
        out_specs=whole(shape),
        name="score_weights",
    )(counts, *arrays)


def live_rows(goes_ref, own_ref, other_ref):
    row = iota((BLK, own_ref.shape[0]), 0) + pl.program_id(0) * BLK
    out = dot(jnp.where(goes_ref[0] == row, 1.0, 0.0).astype(BF), own_ref[...])
    out = out + dot(jnp.where(goes_ref[1] == row, 1.0, 0.0).astype(BF), other_ref[...])
    return out.astype(BF)


def values_kernel(goes_ref, own_ref, other_ref, up_ref, out_ref):
    out_ref[...] = dot(live_rows(goes_ref, own_ref, other_ref), up_ref[...]).astype(BF)


def live_values(goes, own, other, up):
    width = up.shape[1]
    return pl.pallas_call(
        values_kernel,
        grid=(LIVE // BLK,),
        out_shape=jax.ShapeDtypeStruct((LIVE, width), BF),
        in_specs=[whole(a.shape) for a in (goes, own, other, up)],
        out_specs=pl.BlockSpec((BLK, width), lambda b: (b, 0)),
        name="live_values",
    )(goes, own, other, up)


def mix_kernel(goes_ref, own_ref, other_ref, prev_ref, cur_ref, wo_ref, out_ref, att_ref, all_ref):
    b = pl.program_id(0)
    heads = cur_ref.shape[1] // VH
    r_at, l_at = iota((BLK, BLK), 0), iota((BLK, BLK), 1)
    gap = r_at - l_at
    near = (gap >= 0) & (gap < WIN)
    per = BLK // WIN
    masks = [jnp.where(near & ((l_at >> 5) == q), 1.0, 0.0).astype(BF) for q in range(per)]
    r_at2, l_at2 = iota((WIN, BLK), 0), iota((WIN, BLK), 1)
    before = jnp.where((BLK + r_at2 - l_at2) < WIN, 1.0, 0.0).astype(BF)
    blank = jnp.zeros((BLK - WIN, BLK), BF)
    packed = live_rows(goes_ref, own_ref, other_ref)
    for group in range(heads // per):
        one = packed[:, group * BLK : (group + 1) * BLK].astype(F32)
        turned = [one.astype(BF)]
        for q in range(1, per):
            turned.append(pltpu.roll(one, q * WIN, 1).astype(BF))
        for i in range(per):
            cols = slice((group * per + i) * VH, (group * per + i + 1) * VH)
            band = turned[(-i) % per] * masks[0]
            for q in range(1, per):
                band = band + turned[(q - i) % per] * masks[q]
            old = jnp.concatenate([turned[(per - 1 - i) % per][:WIN] * before, blank], axis=0)
            band = jnp.concatenate([old, band], axis=1)
            both = jnp.concatenate([prev_ref[:, cols], cur_ref[:, cols]], axis=0)
            att_ref[:, cols] = dot(band, both).astype(BF)
    part = nt(att_ref[...], wo_ref[...]).astype(BF)
    order = ((r_at & 15) * 8 + (r_at >> 4)) == l_at
    part = dot(jnp.where(order, 1.0, 0.0).astype(BF), part)
    rows = pl.ds(pl.multiple_of(b * 16, 16), 16)
    for m in range(8):
        all_ref[m, rows, :] = part[m * 16 : (m + 1) * 16]

    @pl.when(b == pl.num_programs(0) - 1)
    def _():
        for m in range(8):
            out_ref[m] = all_ref[m].T.astype(BF)


def mix_project(goes, own, other, values, wo):
    width = values.shape[1]
    n = wo.shape[0]
    shape = (8, n, LIVE // 8)
    return pl.pallas_call(
        mix_kernel,
        grid=(LIVE // BLK,),
        out_shape=jax.ShapeDtypeStruct(shape, BF),
        in_specs=[
            whole(goes.shape),
            whole(own.shape),
            whole(other.shape),
            pl.BlockSpec((BLK, width), lambda b: (jnp.maximum(b - 1, 0), 0)),
            pl.BlockSpec((BLK, width), lambda b: (b, 0)),
            whole(wo.shape),
        ],
        out_specs=whole(shape),
        scratch_shapes=[pltpu.VMEM((BLK, width), BF), pltpu.VMEM((8, LIVE // 8, n), F32)],
        name="mix_project",
    )(goes, own, other, values, values, wo)


def gate_up_kernel(own_ref, other_ref, gain_ref, gate_ref, up_ref, out_ref, x_ref):
    core = lax.axis_index("c")
    _, lows, blocks, k, chunk = own_ref.shape
    ff = gate_ref.shape[0]
    squares = jnp.zeros((1, blocks * chunk), F32)
    for ref, flip in ((own_ref, core), (other_ref, 1 - core)):
        for low in range(lows):
            rows = pl.ds(pl.multiple_of((low * 2 + flip) * k, 32), k)
            x = jnp.concatenate([ref[0, low, i] for i in range(blocks)], axis=1).astype(F32)
            squares = squares + jnp.sum(x * x, axis=0, keepdims=True)
            x_ref[rows, :] = (x * gain_ref[rows, :]).astype(BF)
    x = x_ref[...]
    gate = dot(gate_ref[...], x).astype(BF)
    up = dot(up_ref[...], x).astype(BF)
    row = iota((16, blocks * chunk), 0)
    high = squares.astype(BF).astype(F32)
    extra = jnp.where(row == 0, high, jnp.where(row == 1, squares - high, 0.0)).astype(BF)
    for i in range(blocks):
        cols = slice(i * chunk, (i + 1) * chunk)
        out_ref[i, :ff, :] = gate[:, cols]
        out_ref[i, ff : 2 * ff, :] = up[:, cols]
        out_ref[i, 2 * ff :, :] = extra[:, cols]


def gate_up(own, other, gain, gate_weight, up_weight):
    highs, lows, planes, k, chunk = own.shape
    ff, width = gate_weight.shape
    blocks = 2
    spec = pl.BlockSpec(
        (1, lows, blocks, k, chunk),
        lambda b: (b // (planes // blocks), 0, b % (planes // blocks), 0, 0),
    )
    return pl.pallas_call(
        gate_up_kernel,
        grid=(highs * planes // blocks,),
        out_shape=jax.ShapeDtypeStruct((highs * planes, 2 * ff + 16, chunk), BF),
        in_specs=[spec, spec, whole((width, 1)), whole((ff, width)), whole((ff, width))],
        out_specs=pl.BlockSpec((blocks, 2 * ff + 16, chunk), lambda b: (b, 0, 0)),
        scratch_shapes=[pltpu.VMEM((width, blocks * chunk), BF)],
        name="gate_up",
    )(own, other, gain, gate_weight, up_weight)


def exchange(x, axes):
    return lax.all_to_all(x, axes, split_axis=0, concat_axis=0, tiled=True)


def gather(x, axes):
    n = lax.axis_size(axes)
    return exchange(jnp.broadcast_to(x[None], (n,) + x.shape), axes)


def pick(x, index):
    return lax.dynamic_index_in_dim(x, index, 0, keepdims=False)


def on_device(
    query_nope,
    query_rope,
    latent,
    key_rope,
    key_up,
    value_up,
    output_weight,
    residual,
    norm_gain,
    gate_weight,
    up_weight,
    down_weight,
    rank_tokens,
    request_ids,
):
    slots = latent.shape[0]
    ranks = rank_tokens.shape[0]
    zh, y, c = (lax.axis_index(a) for a in DP)
    x_at, zl = (lax.axis_index(a) for a in HD)
    rank = (zh * 4 + y) * 2 + c
    chunk = LIVE // 8
    width = residual.shape[1]
    quarter = width // 4
    model = 8 * width

    every = jnp.arange(ranks, dtype=jnp.int32)

    def starts(which):
        return jnp.sum(jnp.where(every < which[..., None], rank_tokens, 0), axis=-1)

    def lengths(which):
        return jnp.sum(jnp.where(every == which[..., None], rank_tokens, 0), axis=-1)

    own_start, own_length = starts(rank), lengths(rank)
    slot = jnp.arange(slots, dtype=jnp.int32)

    share = slots // 4
    latents = lax.dynamic_slice_in_dim(latent, x_at * share, share, 0)
    latents = gather(gather(latents, ("zh", "y")), "x").reshape(-1, latent.shape[1])
    latents_other = shifted(latents, "c", 1)

    weights = score_weights(
        rank_tokens, query_nope, query_rope, latent, key_rope, key_up, request_ids
    )
    weights = gather(gather(weights, "zh"), "y").reshape(-1, weights.shape[1])
    weights_other = shifted(weights, "c", 1)

    first, count = starts(every).reshape(4, 4, 2), rank_tokens.reshape(4, 4, 2)
    to = jnp.where(slot < count[..., None], first[..., None] + slot, -1)
    to = jnp.where(c == 0, jnp.stack([to[:, :, 0], to[:, :, 1]]), jnp.stack([to[:, :, 1], to[:, :, 0]]))
    goes = to.transpose(0, 2, 1, 3).reshape(2, 1, -1)
    goes_latent = to.reshape(2, 4, 4, 4, share).transpose(0, 3, 1, 2, 4).reshape(2, 1, -1)
    values = live_values(goes_latent, latents, latents_other, value_up)

    eight = jnp.arange(8, dtype=jnp.int32)
    spread = ((eight[:, None] - own_start) & 7) + 8 * eight[None, :]
    roll = (spread.reshape(slots, 1) == slot[None, :]).astype(BF)
    rows = dot(roll, residual).astype(BF).reshape(2, 4, 8, 2, 2, quarter)
    rows = rows.transpose(1, 0, 3, 4, 2, 5).reshape(ranks, 8, quarter)
    rows = exchange(rows, DP)
    mine = (y >> 1) * 4 + zh
    place = ((mine - starts(every)[:, None]) & 7) + 8 * eight[None, :]
    come = jnp.where(place < rank_tokens[:, None], (starts(every)[:, None] + place) >> 3, -1)
    come = (come.reshape(ranks * 8, 1) == jnp.arange(chunk, dtype=jnp.int32)).astype(BF)
    rows = lax.dot_general(
        rows.reshape(ranks * 8, quarter), come, (((0,), (0,)), ((), ())), preferred_element_type=F32
    )

    weights_other, rows = lax.optimization_barrier((weights_other, rows))
    part = mix_project(goes, weights, weights_other, values, output_weight.T)
    projected = jnp.sum(exchange(part, HD).astype(F32), axis=0).astype(BF)
    sends = []
    for a in range(4):
        for b in range(4):
            for e in range(2):
                for f in range(4):
                    for g in range(2):
                        m = f * 2 + g
                        to = ((m & 3) * 4 + (m >> 2) * 2 + (b & 1)) * 2 + e
                        h = a * 2 + (b >> 1)
                        sends.append((((a * 4 + b) * 2 + e) * 8 + m, to * 8 + h))
    projected = lax.ppermute(projected, DP + HD, sends)
    mixed = (rows + projected.astype(F32)).astype(BF)

    full = gather(gather(mixed, "zh"), "y").reshape(2, 2, 4, quarter, chunk)
    full_other = shifted(full, "c", 1)
    ff = down_weight.shape[0]
    part = gate_up(full, full_other, norm_gain[:, None], gate_weight.T, up_weight.T)
    total = jnp.sum(exchange(part, HD).astype(F32), axis=0)
    scale = lax.rsqrt((total[2 * ff : 2 * ff + 1] + total[2 * ff + 1 : 2 * ff + 2]) / model + 1e-06)
    hidden = (jax.nn.silu(total[:ff] * scale) * (total[ff : 2 * ff] * scale)).astype(BF)
    hidden = gather(hidden, HD).reshape(4, 2, ff, chunk)

    def down(core):
        piece = lax.dynamic_index_in_dim(hidden, core, 1, keepdims=False)
        return lax.dot_general(
            piece, down_weight, (((1,), (0,)), ((), ())), preferred_element_type=F32
        )

    sent = shifted(down(1 - c).astype(BF), "c", 1)
    total = (down(c) + sent.astype(F32)).astype(BF)
    total = jnp.sum(exchange(total, "y").astype(F32), axis=0)
    m = y * 2 + c
    first = starts(every)
    place = ((m - first[:, None]) & 7) + 8 * eight[None, :]
    comes = jnp.where(place < rank_tokens[:, None], (first[:, None] + place) >> 3, -1)
    expand = (comes.reshape(4, slots, 1) == jnp.arange(chunk, dtype=jnp.int32)).astype(BF)
    planes = dot(expand.reshape(4 * slots, chunk), total.astype(BF)).astype(BF)
    pair = [pick(a.reshape(2, 2, 4, quarter, chunk), m >> 2) for a in (full, full_other)]
    pair = [lax.dynamic_index_in_dim(a, m & 3, 1, keepdims=False) for a in pair]
    low = jnp.where(c == 0, pair[0], pair[1])
    high = jnp.where(c == 0, pair[1], pair[0])
    own = jnp.stack([low, high], axis=1).reshape(width, chunk)
    result = nt(pick(expand, zh), own)
    result = result + jnp.sum(exchange(planes.reshape(4, slots, width), "zh").astype(F32), axis=0)
    result = exchange(result.astype(BF).reshape(8, 8, width), ("y", "c"))
    at = ((own_start + slot) & 7) * 8 + (slot >> 3)
    at = jnp.where(slot < own_length, at, -1)
    back = (at[:, None] == slot[None, :]).astype(BF)
    return dot(back, result.reshape(slots, width)).astype(BF)


def solution(mesh):
    mesh = Mesh(mesh.devices.reshape(4, 4, 2, 4, 2), DP + HD)
    in_specs = (
        P(DP, HD),
        P(DP, HD),
        P(DP, None),
        P(DP, None),
        P(None, HD),
        P(None, HD),
        P(HD, DP),
        P(DP, HD),
        P(HD),
        P(HD, DP),
        P(HD, DP),
        P(DP, HD),
        P(),
        P(DP, None),
    )
    return jax.shard_map(
        on_device, mesh=mesh, in_specs=in_specs, out_specs=P(DP, HD), check_vma=False
    )
```

time: 311 us -> 292 us (0.939); the launches traced: 306 us -> 291 us
  blocking collectives: 37.3 us -> 96.1 us
  local copies, waits for them, and re-layouts: 55.1 us -> 12 us
  starting transfers between devices: 87 us -> 59.3 us
  Pallas kernels: 19.5 us -> 37.2 us
  matrix products: 19 us -> 7.21 us
  waiting for transfers between devices: 81.8 us -> 72.6 us
    all_to_all x1 -> x5, blocking collectives: 37.3 us -> 96.1 us  [exchange(): return lax.all_to_all(x, axes, split_axis=0, concat_axis=0, tiled=True)]
    ppermute x28 -> x4, starting transfers between devices: 66.9 us -> 14.2 us  [shifted(): return lax.ppermute(x, axis, [(i, (i + shift) % n) for i in range(n)])]
    ppermute x28 -> x4, waiting for transfers between devices: 45.9 us -> 3.44 us  [shifted(): return lax.ppermute(x, axis, [(i, (i + shift) % n) for i in range(n)])]
    all_to_all x4 -> x8, waiting for transfers between devices: 35.9 us -> 69.2 us  [exchange(): return lax.all_to_all(x, axes, split_axis=0, concat_axis=0, tiled=True)]
    unnamed x53 -> x16, local copies, waits for them, and re-layouts: 28 us -> 0.98 us
    all_to_all x4 -> x8, starting transfers between devices: 19.5 us -> 44.5 us  [exchange(): return lax.all_to_all(x, axes, split_axis=0, concat_axis=0, tiled=True)]
    pallas_call x3 -> x4, Pallas kernels: 19.5 us -> 37.2 us  [the longest x1 14.4 us: mix_project(): pl.pallas_call(mix_kernel, grid=(LIVE // BLK,), out_shape=jax.ShapeDtypeS...]
    dot_general x8 -> x3, matrix products: 19 us -> 2.19 us  [dot(): return jnp.dot(a, b, preferred_element_type=F32)]
  transfers between devices with their start and end apart: 33 -> 13, of which waited for: 17 -> 10; matrix products, arithmetic and copies ran while one was open for 12% -> 4% of each run, Pallas kernels for 1% -> 0%
where the time goes in v2:
time: 292 us; the launch traced here: 291 us
  blocking collectives  96.1 us (33%)
  waiting for transfers between devices  72.6 us (25%)
  starting transfers between devices  59.3 us (20%)
  Pallas kernels  37.2 us (13%)
  local copies, waits for them, and re-layouts  12 us (4%)
  matrix products  7.21 us (2%)
  other arithmetic  5.74 us (2%)
    all_to_all x5, blocking collectives, exchange(): return lax.all_to_all(x, axes, split_axis=0, concat_axis=0, tiled=True)  96.1 us
    all_to_all x8, waiting for transfers between devices, exchange(): return lax.all_to_all(x, axes, split_axis=0, concat_axis=0, tiled=True)  69.2 us
    all_to_all x8, starting transfers between devices, exchange(): return lax.all_to_all(x, axes, split_axis=0, concat_axis=0, tiled=True)  44.5 us
    pallas_call x1, Pallas kernels, mix_project(): pl.pallas_call(mix_kernel, grid=(LIVE // BLK,), out_shape=jax.ShapeDtypeS...  14.4 us
    ppermute x4, starting transfers between devices, shifted(): return lax.ppermute(x, axis, [(i, (i + shift) % n) for i in range(n)])  14.2 us
    pallas_call x1, Pallas kernels, live_values(): pl.pallas_call(values_kernel, grid=(LIVE // BLK,), out_shape=jax.ShapeDty...  9.87 us
    pallas_call x1, Pallas kernels, gate_up(): pl.pallas_call(gate_up_kernel, grid=(highs * planes // blocks,), out_shap...  7.02 us
    pallas_call x1, Pallas kernels, score_weights(): pl.pallas_call(score_kernel, grid=(1,), out_shape=jax.ShapeDtypeStruct(sh...  5.9 us
  transfers between devices with their start and end apart: 13, of which 10 were waited for; matrix products, arithmetic and copies ran while one was open for 4% of the time, Pallas kernels for 0%

profile of v2, /device:TPU:1, one launch (start us, length us, event | category | flops | bytes accessed | tf_op | source)
XLA Modules:
  0.0 290.7 jit_solution(6204679480675780638)
XLA Ops:
  0.0 5.9 %score_weights.1 = bf16[64,512]{1,0:T(8,128)(2,1)} custom-call(s32[32]{0:T(128)} %counts_ref.1, bf16[64,2048]{1,0:T(8,128)(2,1)} %qn_ref.1, bf16[64,1024]{1,0:T(8,128)(2,1)} %qr_ref.1, bf16[64,512]{1,0:T(8,128)(2,1)} %lat_ref.1, bf16[64,64]{1,0:T(8,128)(2,1)} %kr_ref.1, bf16[512,2048]{1,0:T(8,128)(2,1)} %ku_ref.1, s32[1,64]{1,0:T(1,128)} %req_ref.1), custom_call_target="tpu_custom_call" | custom-call | tf_op jit(solution)/shard_map/score_weights/pallas_call | solution.py:77
  5.9 1.6 broadcast_in_dim.56
  7.5 9.0 %all-to-all-start = ((bf16[4,64,512]{2,1,0:T(8,128)(2,1)}), bf16[4,64,512]{2,1,0:T(8,128)(2,1)S(1)}, u32[]{:S(2)}, u32[]{:S(2)}) async-start(bf16[4,64,512]{2,1,0:T(8,128)(2,1)} %broadcast_in_dim.56), calls=%async_computation | async-start | bytes 524288 | tf_op jit(solution)/shard_map/all_to_all | solution.py:215
  16.5 0.7 constant_dynamic-slice_fusion
  17.2 7.5 %all-to-all-done = bf16[4,64,512]{2,1,0:T(8,128)(2,1)S(1)} async-done(((bf16[4,64,512]{2,1,0:T(8,128)(2,1)}), bf16[4,64,512]{2,1,0:T(8,128)(2,1)S(1)}, u32[]{:S(2)}, u32[]{:S(2)}) %all-to-all-start) | async-done | bytes 262176 | tf_op jit(solution)/shard_map/all_to_all | solution.py:215
  24.7 16.9 %all_to_all.65 = bf16[16,16,512]{2,1,0:T(8,128)(2,1)S(1)} all-to-all(bf16[16,16,512]{2,1,0:T(8,128)(2,1)S(1)} %broadcast_in_dim.60), channel_id=1, replica_groups=mesh['zh'=4,'y'=4,'c'=2,'x'=4,'zl'=2] {'zh','y'}, dimensions={0} | all-to-all | bytes 524288 | tf_op jit(solution)/shard_map/all_to_all | solution.py:215
  41.6 1.1 broadcast_in_dim.57
  42.7 3.5 %all-to-all-start.1 = ((bf16[4,4,64,512]{3,2,1,0:T(8,128)(2,1)}), bf16[4,4,64,512]{3,2,1,0:T(8,128)(2,1)S(1)}, u32[]{:S(2)}, u32[]{:S(2)}) async-start(bf16[4,4,64,512]{3,2,1,0:T(8,128)(2,1)} %broadcast_in_dim.57), calls=%async_computation.1 | async-start | bytes 2097152 | tf_op jit(solution)/shard_map/all_to_all | solution.py:215
  46.3 0.1 select_reduce_fusion
  46.4 0.1 add.231
  46.5 0.1 copy.54
  46.6 0.1 copy.53
  46.7 10.4 %all-to-all-done.1 = bf16[4,4,64,512]{3,2,1,0:T(8,128)(2,1)S(1)} async-done(((bf16[4,4,64,512]{3,2,1,0:T(8,128)(2,1)}), bf16[4,4,64,512]{3,2,1,0:T(8,128)(2,1)S(1)}, u32[]{:S(2)}, u32[]{:S(2)}) %all-to-all-start.1) | async-done | bytes 1048608 | tf_op jit(solution)/shard_map/all_to_all | solution.py:215
  57.2 1.2 broadcast_in_dim.61
  58.4 4.1 %all-to-all-start.4 = ((bf16[4,16,16,512]{3,2,1,0:T(8,128)(2,1)}), bf16[4,16,16,512]{3,2,1,0:T(8,128)(2,1)S(1)}, u32[]{:S(2)}, u32[]{:S(2)}) async-start(bf16[4,16,16,512]{3,2,1,0:T(8,128)(2,1)} %broadcast_in_dim.61), calls=%async_computation.4 | async-start | bytes 2097152 | tf_op jit(solution)/shard_map/all_to_all | solution.py:215
  62.5 0.7 fusion.31
  63.2 0.7 subtract_and_fusion.2
  64.1 0.2 convolution_convert_fusion.3
  64.3 0.2 reshape.245
  64.5 0.7 copy.52
  65.3 5.4 %collective-permute-start = (bf16[1024,512]{1,0:T(8,128)(2,1)S(1)}, bf16[1024,512]{1,0:T(8,128)(2,1)}, u32[]{:S(2)}, u32[]{:S(2)}) collective-permute-start(bf16[1024,512]{1,0:T(8,128)(2,1)S(1)} %bitcast.75), channel_id=1, source_target_pairs={{0,8},{8,0},{1,9},{9,1},{2,10},{10,2},{3,11},{11,3},{4,12},{12,4},... | collective-permute-start | bytes 3145736 | tf_op jit(solution)/shard_map/ppermute | solution.py:26
  70.7 1.6 all-to-all-done.4
  72.2 10.9 %all-to-all-start.2 = ((bf16[32,8,224]{2,1,0:T(8,128)(2,1)}), bf16[32,8,224]{2,1,0:T(8,128)(2,1)S(1)}, u32[]{:S(2)}, u32[]{:S(2)}) async-start(bf16[32,8,224]{2,1,0:T(8,128)(2,1)} %bitcast.3), calls=%async_computation.2 | async-start | bytes 262144 | tf_op jit(solution)/shard_map/all_to_all | solution.py:215
  83.1 0.3 collective-permute-start.1
  83.8 0.7 reshape.249.goes_ref
  84.6 0.7 reshape.248.goes_ref
  85.3 8.5 %all-to-all-done.2 = bf16[32,8,224]{2,1,0:T(8,128)(2,1)S(1)} async-done(((bf16[32,8,224]{2,1,0:T(8,128)(2,1)}), bf16[32,8,224]{2,1,0:T(8,128)(2,1)S(1)}, u32[]{:S(2)}, u32[]{:S(2)}) %all-to-all-start.2) | async-done | bytes 114720 | tf_op jit(solution)/shard_map/all_to_all | solution.py:215
  93.7 0.3 fusion.13
  94.0 9.9 %live_values.1.prev_ref.cur_ref = bf16[1024,2048]{1,0:T(8,128)(2,1)} custom-call(s32[2,1,1024]{2,1,0:T(1,128)} %reshape.249.goes_ref, bf16[1024,512]{1,0:T(8,128)(2,1)} %bitcast.78, bf16[1024,512]{1,0:T(8,128)(2,1)} %collective-permute-done.1.other_ref, bf16[512,2048]{1,0:T(8,128)(2,1)} %up_ref.1), custom_call_target="tpu_custom_call" | custom-call | tf_op jit(solution)/shard_map/live_values/pallas_call | solution.py:100
  103.9 14.4 %mix_project.1 = bf16[8,224,128]{2,1,0:T(8,128)(2,1)} custom-call(s32[2,1,1024]{2,1,0:T(1,128)} %reshape.248.goes_ref, bf16[1024,512]{1,0:T(8,128)(2,1)} %bitcast.76, bf16[1024,512]{1,0:T(8,128)(2,1)} %collective-permute-done.other_ref, bf16[1024,2048]{1,0:T(8,128)(2,1)} %live_values.1.prev_ref.cur_ref, bf16[1024,2048]{1,0:T(8,128)(2,1)} %live_values.1.prev_ref.cur_ref, ...), custom_call_target="tpu_custom_call" | custom-call | tf_op jit(solution)/shard_map/mix_project/pallas_call | solution.py:153
  118.4 12.7 %all_to_all.66 = bf16[8,224,128]{2,1,0:T(8,128)(2,1)S(1)} all-to-all(bf16[8,224,128]{2,1,0:T(8,128)(2,1)} %mix_project.1), channel_id=1, replica_groups=mesh['zh'=4,'y'=4,'c'=2,'x'=4,'zl'=2] {'x','zl'}, dimensions={0} | all-to-all | bytes 917504 | tf_op jit(solution)/shard_map/all_to_all | solution.py:215
  131.1 0.7 collective-permute-start.2
  131.9 19.1 %all_to_all.67 = bf16[4,224,128]{2,1,0:T(8,128)(2,1)S(1)} all-to-all(bf16[4,224,128]{2,1,0:T(8,128)(2,1)S(1)} %broadcast_in_dim.62), channel_id=1, replica_groups=mesh['zh'=4,'y'=4,'c'=2,'x'=4,'zl'=2] {'zh'}, dimensions={0} | all-to-all | bytes 458752 | tf_op jit(solution)/shard_map/all_to_all | solution.py:215
  151.0 0.1 broadcast_in_dim.63
  151.1 14.1 %all_to_all.68 = bf16[4,4,224,128]{3,2,1,0:T(8,128)(2,1)S(1)} all-to-all(bf16[4,4,224,128]{3,2,1,0:T(8,128)(2,1)S(1)} %broadcast_in_dim.63), channel_id=1, replica_groups=mesh['zh'=4,'y'=4,'c'=2,'x'=4,'zl'=2] {'y'}, dimensions={0} | all-to-all | bytes 1835008 | tf_op jit(solution)/shard_map/all_to_all | solution.py:215
  165.2 5.7 %collective-permute-start.3 = (bf16[2,2,4,224,128]{4,3,2,1,0:T(8,128)(2,1)S(1)}, bf16[2,2,4,224,128]{4,3,2,1,0:T(8,128)(2,1)S(1)}, u32[]{:S(2)}, u32[]{:S(2)}) collective-permute-start(bf16[2,2,4,224,128]{4,3,2,1,0:T(8,128)(2,1)S(1)} %bitcast.71), channel_id=1, source_target_pairs={{0,8},{8,0},{1,9},{9,1},{2,10},{10,2},{3,11},{11,3},{4,12},{12,4},... | collective-permute-start | bytes 2752520 | tf_op jit(solution)/shard_map/ppermute | solution.py:26
  170.9 1.0 broadcast_in_dim.124.gain_ref
  171.8 1.1 collective-permute-done.3.other_ref
  173.0 1.0 copy-done.4
  173.9 7.0 %gate_up.1 = bf16[8,1168,128]{2,1,0:T(8,128)(2,1)} custom-call(bf16[2,2,4,224,128]{4,3,2,1,0:T(8,128)(2,1)} %bitcast.72, bf16[2,2,4,224,128]{4,3,2,1,0:T(8,128)(2,1)} %copy-done.4, f32[896,1]{1,0:T(8,128)} %broadcast_in_dim.124.gain_ref, bf16[576,896]{1,0:T(8,128)(2,1)} %bitcast.79, bf16[576,896]{1,0:T(8,128)(2,1)} %bitcast.80), custom_call_target="tpu_custom_call" | custom-call | tf_op jit(solution)/shard_map/gate_up/pallas_call | solution.py:203
  180.9 33.4 %all_to_all.69 = bf16[8,1168,128]{2,1,0:T(8,128)(2,1)S(1)} all-to-all(bf16[8,1168,128]{2,1,0:T(8,128)(2,1)} %gate_up.1), channel_id=1, replica_groups=mesh['zh'=4,'y'=4,'c'=2,'x'=4,'zl'=2] {'x','zl'}, dimensions={0} | all-to-all | bytes 4784128 | tf_op jit(solution)/shard_map/all_to_all | solution.py:215
  214.3 0.3 convert_reduce_fusion
  214.7 0.1 fusion.12
  214.8 1.2 broadcast_in_dim.67
  215.9 3.6 %all-to-all-start.9 = ((bf16[8,576,128]{2,1,0:T(8,128)(2,1)}), bf16[8,576,128]{2,1,0:T(8,128)(2,1)S(1)}, u32[]{:S(2)}, u32[]{:S(2)}) async-start(bf16[8,576,128]{2,1,0:T(8,128)(2,1)} %broadcast_in_dim.67), calls=%async_computation.9 | async-start | bytes 2359296 | tf_op jit(solution)/shard_map/all_to_all | solution.py:215
  219.5 15.2 %all-to-all-done.9 = bf16[8,576,128]{2,1,0:T(8,128)(2,1)S(1)} async-done(((bf16[8,576,128]{2,1,0:T(8,128)(2,1)}), bf16[8,576,128]{2,1,0:T(8,128)(2,1)S(1)}, u32[]{:S(2)}, u32[]{:S(2)}) %all-to-all-start.9) | async-done | bytes 1179680 | tf_op jit(solution)/shard_map/all_to_all | solution.py:215
  234.7 1.9 convolution_convert_fusion
  236.6 2.8 collective-permute-start.4
  239.4 2.3 collective-permute-done.4
  241.8 1.9 add_convert_fusion
  243.7 3.5 %all-to-all-start.10 = ((bf16[4,128,896]{2,1,0:T(8,128)(2,1)}), bf16[4,128,896]{2,1,0:T(8,128)(2,1)S(1)}, u32[]{:S(2)}, u32[]{:S(2)}) async-start(bf16[4,128,896]{2,1,0:T(8,128)(2,1)} %add_convert_fusion), calls=%async_computation.10 | async-start | bytes 1835008 | tf_op jit(solution)/shard_map/all_to_all | solution.py:215
  247.9 0.1 lt.146
  248.0 12.6 %all-to-all-done.10 = bf16[4,128,896]{2,1,0:T(8,128)(2,1)S(1)} async-done(((bf16[4,128,896]{2,1,0:T(8,128)(2,1)}), bf16[4,128,896]{2,1,0:T(8,128)(2,1)S(1)}, u32[]{:S(2)}, u32[]{:S(2)}) %all-to-all-start.10) | async-done | bytes 917536 | tf_op jit(solution)/shard_map/all_to_all | solution.py:215
  260.6 0.1 reduce_sum.89
  260.8 1.1 convolution_convert_fusion.1
  261.8 3.5 %all-to-all-start.11 = ((bf16[4,64,896]{2,1,0:T(8,128)(2,1)}), bf16[4,64,896]{2,1,0:T(8,128)(2,1)S(1)}, u32[]{:S(2)}, u32[]{:S(2)}) async-start(bf16[4,64,896]{2,1,0:T(8,128)(2,1)} %bitcast.25), calls=%async_computation.11 | async-start | bytes 917504 | tf_op jit(solution)/shard_map/all_to_all | solution.py:215
  265.6 1.0 fusion.16
  266.6 1.0 fusion.15
  267.6 9.6 %all-to-all-done.11 = bf16[4,64,896]{2,1,0:T(8,128)(2,1)S(1)} async-done(((bf16[4,64,896]{2,1,0:T(8,128)(2,1)}), bf16[4,64,896]{2,1,0:T(8,128)(2,1)S(1)}, u32[]{:S(2)}, u32[]{:S(2)}) %all-to-all-start.11) | async-done | bytes 458784 | tf_op jit(solution)/shard_map/all_to_all | solution.py:215
  277.3 0.9 fusion.1
  278.2 6.4 %all-to-all-start.12 = ((bf16[8,8,896]{2,1,0:T(8,128)(2,1)}), bf16[8,8,896]{2,1,0:T(8,128)(2,1)S(1)}, u32[]{:S(2)}, u32[]{:S(2)}) async-start(bf16[8,8,896]{2,1,0:T(8,128)(2,1)} %fusion.1), calls=%async_computation.12 | async-start | bytes 229376 | tf_op jit(solution)/shard_map/all_to_all | solution.py:215
  284.7 1.3 compare_select_fusion.2
  286.0 3.8 %all-to-all-done.12 = bf16[8,8,896]{2,1,0:T(8,128)(2,1)S(1)} async-done(((bf16[8,8,896]{2,1,0:T(8,128)(2,1)}), bf16[8,8,896]{2,1,0:T(8,128)(2,1)S(1)}, u32[]{:S(2)}, u32[]{:S(2)}) %all-to-all-start.12) | async-done | bytes 114720 | tf_op jit(solution)/shard_map/all_to_all | solution.py:215
  289.8 0.9 convolution_convert_fusion.2
  (60 shorter events, 2.0 us)
Async XLA Ops:
  0.0 234.7 %copy-start = (bf16[576,896]{1,0:T(8,128)(2,1)S(1)}, bf16[576,896]{1,0:T(8,128)(2,1)}, u32[]{:S(2)}) copy-start(bf16[576,896]{1,0:T(8,128)(2,1)} %param.25) | copy-start | bytes 3096580
  7.5 17.2 %all-to-all-start = ((bf16[4,64,512]{2,1,0:T(8,128)(2,1)}), bf16[4,64,512]{2,1,0:T(8,128)(2,1)S(1)}, u32[]{:S(2)}, u32[]{:S(2)}) async-start(bf16[4,64,512]{2,1,0:T(8,128)(2,1)} %broadcast_in_dim.56), calls=%async_computation | async-start | bytes 524288 | tf_op jit(solution)/shard_map/all_to_all | solution.py:215
  41.6 4.6 %copy-start.6 = (s32[32]{0:T(128)S(1)}, s32[32]{0:T(128)}, u32[]{:S(2)}) copy-start(s32[32]{0:T(128)} %counts_ref.1) | copy-start | bytes 388
  42.7 14.5 %all-to-all-start.1 = ((bf16[4,4,64,512]{3,2,1,0:T(8,128)(2,1)}), bf16[4,4,64,512]{3,2,1,0:T(8,128)(2,1)S(1)}, u32[]{:S(2)}, u32[]{:S(2)}) async-start(bf16[4,4,64,512]{3,2,1,0:T(8,128)(2,1)} %broadcast_in_dim.57), calls=%async_computation.1 | async-start | bytes 2097152 | tf_op jit(solution)/shard_map/all_to_all | solution.py:215
  46.2 17.9 %copy-start.5 = (bf16[64,896]{1,0:T(8,128)(2,1)S(1)}, bf16[64,896]{1,0:T(8,128)(2,1)}, u32[]{:S(2)}) copy-start(bf16[64,896]{1,0:T(8,128)(2,1)} %param.21) | copy-start | bytes 344068
  57.2 8.1 %copy-start.2 = (bf16[4,4,64,512]{3,2,1,0:T(8,128)(2,1)}, bf16[4,4,64,512]{3,2,1,0:T(8,128)(2,1)S(1)}, u32[]{:S(2)}) copy-start(bf16[4,4,64,512]{3,2,1,0:T(8,128)(2,1)S(1)} %all-to-all-done.1) | copy-start | bytes 3145732
  58.4 13.9 %all-to-all-start.4 = ((bf16[4,16,16,512]{3,2,1,0:T(8,128)(2,1)}), bf16[4,16,16,512]{3,2,1,0:T(8,128)(2,1)S(1)}, u32[]{:S(2)}, u32[]{:S(2)}) async-start(bf16[4,16,16,512]{3,2,1,0:T(8,128)(2,1)} %broadcast_in_dim.61), calls=%async_computation.4 | async-start | bytes 2097152 | tf_op jit(solution)/shard_map/all_to_all | solution.py:215
  65.3 28.7 %collective-permute-start = (bf16[1024,512]{1,0:T(8,128)(2,1)S(1)}, bf16[1024,512]{1,0:T(8,128)(2,1)}, u32[]{:S(2)}, u32[]{:S(2)}) collective-permute-start(bf16[1024,512]{1,0:T(8,128)(2,1)S(1)} %bitcast.75), channel_id=1, source_target_pairs={{0,8},{8,0},{1,9},{9,1},{2,10},{10,2},{3,11},{11,3},{4,12},{12,4},... | collective-permute-start | bytes 3145736 | tf_op jit(solution)/shard_map/ppermute | solution.py:26
  72.2 21.8 %copy-start.3 = (bf16[4,16,16,512]{3,2,1,0:T(8,128)(2,1)}, bf16[4,16,16,512]{3,2,1,0:T(8,128)(2,1)S(1)}, u32[]{:S(2)}) copy-start(bf16[4,16,16,512]{3,2,1,0:T(8,128)(2,1)S(1)} %all-to-all-done.4) | copy-start | bytes 3145732
  72.2 21.5 %all-to-all-start.2 = ((bf16[32,8,224]{2,1,0:T(8,128)(2,1)}), bf16[32,8,224]{2,1,0:T(8,128)(2,1)S(1)}, u32[]{:S(2)}, u32[]{:S(2)}) async-start(bf16[32,8,224]{2,1,0:T(8,128)(2,1)} %bitcast.3), calls=%async_computation.2 | async-start | bytes 262144 | tf_op jit(solution)/shard_map/all_to_all | solution.py:215
  83.1 10.9 %collective-permute-start.1 = (bf16[1024,512]{1,0:T(8,128)(2,1)S(1)}, bf16[1024,512]{1,0:T(8,128)(2,1)}, u32[]{:S(2)}, u32[]{:S(2)}) collective-permute-start(bf16[1024,512]{1,0:T(8,128)(2,1)S(1)} %bitcast.77), channel_id=1, source_target_pairs={{0,8},{8,0},{1,9},{9,1},{2,10},{10,2},{3,11},{11,3},{4,12},{12,4},... | collective-permute-start | bytes 3145736 | tf_op jit(solution)/shard_map/ppermute | solution.py:26
  131.1 0.7 collective-permute-start.2
  131.9 39.0 %copy-start.7 = (f32[896]{0:T(1024)S(1)}, f32[896]{0:T(1024)}, u32[]{:S(2)}) copy-start(f32[896]{0:T(1024)} %param.22) | copy-start | bytes 10756
  165.2 7.8 %copy-start.1 = (bf16[4,4,224,128]{3,2,1,0:T(8,128)(2,1)}, bf16[4,4,224,128]{3,2,1,0:T(8,128)(2,1)S(1)}, u32[]{:S(2)}) copy-start(bf16[4,4,224,128]{3,2,1,0:T(8,128)(2,1)S(1)} %all_to_all.68) | copy-start | bytes 2752516
  165.2 7.8 %collective-permute-start.3 = (bf16[2,2,4,224,128]{4,3,2,1,0:T(8,128)(2,1)S(1)}, bf16[2,2,4,224,128]{4,3,2,1,0:T(8,128)(2,1)S(1)}, u32[]{:S(2)}, u32[]{:S(2)}) collective-permute-start(bf16[2,2,4,224,128]{4,3,2,1,0:T(8,128)(2,1)S(1)} %bitcast.71), channel_id=1, source_target_pairs={{0,8},{8,0},{1,9},{9,1},{2,10},{10,2},{3,11},{11,3},{4,12},{12,4},... | collective-permute-start | bytes 2752520 | tf_op jit(solution)/shard_map/ppermute | solution.py:26
  173.0 1.0 copy-start.4
  215.9 18.8 %all-to-all-start.9 = ((bf16[8,576,128]{2,1,0:T(8,128)(2,1)}), bf16[8,576,128]{2,1,0:T(8,128)(2,1)S(1)}, u32[]{:S(2)}, u32[]{:S(2)}) async-start(bf16[8,576,128]{2,1,0:T(8,128)(2,1)} %broadcast_in_dim.67), calls=%async_computation.9 | async-start | bytes 2359296 | tf_op jit(solution)/shard_map/all_to_all | solution.py:215
  236.6 5.1 %collective-permute-start.4 = (bf16[4,128,896]{2,1,0:T(8,128)(2,1)}, bf16[4,128,896]{2,1,0:T(8,128)(2,1)S(1)}, u32[]{:S(2)}, u32[]{:S(2)}) collective-permute-start(bf16[4,128,896]{2,1,0:T(8,128)(2,1)} %convolution_convert_fusion), channel_id=1, source_target_pairs={{0,8},{8,0},{1,9},{9,1},{2,10},{10,2},{3,11},{11,3},{4,12},{12,4},... | collective-permute-start | bytes 2752520 | tf_op jit(solution)/shard_map/ppermute | solution.py:26
  243.7 16.9 %all-to-all-start.10 = ((bf16[4,128,896]{2,1,0:T(8,128)(2,1)}), bf16[4,128,896]{2,1,0:T(8,128)(2,1)S(1)}, u32[]{:S(2)}, u32[]{:S(2)}) async-start(bf16[4,128,896]{2,1,0:T(8,128)(2,1)} %add_convert_fusion), calls=%async_computation.10 | async-start | bytes 1835008 | tf_op jit(solution)/shard_map/all_to_all | solution.py:215
  261.8 15.4 %all-to-all-start.11 = ((bf16[4,64,896]{2,1,0:T(8,128)(2,1)}), bf16[4,64,896]{2,1,0:T(8,128)(2,1)S(1)}, u32[]{:S(2)}, u32[]{:S(2)}) async-start(bf16[4,64,896]{2,1,0:T(8,128)(2,1)} %bitcast.25), calls=%async_computation.11 | async-start | bytes 917504 | tf_op jit(solution)/shard_map/all_to_all | solution.py:215
  278.2 11.6 %all-to-all-start.12 = ((bf16[8,8,896]{2,1,0:T(8,128)(2,1)}), bf16[8,8,896]{2,1,0:T(8,128)(2,1)S(1)}, u32[]{:S(2)}, u32[]{:S(2)}) async-start(bf16[8,8,896]{2,1,0:T(8,128)(2,1)} %fusion.1), calls=%async_computation.12 | async-start | bytes 229376 | tf_op jit(solution)/shard_map/all_to_all | solution.py:215

commit v3 on v2

--- a/solution.py
+++ b/solution.py
@@ -13,6 +13,7 @@
 WIN = 32
 LIVE = 1024
 BLK = 128
+STEP = 256
 DP = ("zh", "y", "c")
 HD = ("x", "zl")
 
@@ -35,10 +36,14 @@
 
 
 def whole(shape):
-    return pl.BlockSpec(shape, lambda *_: (0,) * len(shape))
-
-
-def score_kernel(counts_ref, qn_ref, qr_ref, lat_ref, kr_ref, ku_ref, req_ref, out_ref):
+    return pl.BlockSpec(shape, lambda *_: (0,) * len(shape), pipeline_mode=pl.Buffered(1))
+
+
+def cost(us):
+    return pl.CostEstimate(flops=us * 10**9, bytes_accessed=us * 3 * 10**6, transcendentals=0)
+
+
+def score_kernel(counts_ref, qn_ref, qr_ref, lat_ref, kr_ref, ku_ref, req_ref, out_ref, s_ref):
     slots = lat_ref.shape[0]
     heads = ku_ref.shape[1] // NOPE
     place = (lax.axis_index("zh") * 4 + lax.axis_index("y")) * 2 + lax.axis_index("c")
@@ -57,18 +62,21 @@
     t_row, lane = iota((slots, BLK), 0), iota((slots, BLK), 1)
     lands = ((before + t_row) & (WIN - 1)) == (lane & (WIN - 1))
     per = BLK // WIN
+    for h in range(heads):
+        rows = slice(h * slots, (h + 1) * slots)
+        s = nt(qn_ref[:, h * NOPE : (h + 1) * NOPE], keys[:, h * NOPE : (h + 1) * NOPE])
+        s = s + nt(qr_ref[:, h * ROPE : (h + 1) * ROPE], key_rope)
+        s_ref[rows, :] = jnp.where(allowed, s * (NOPE + ROPE) ** (-0.5), jnp.float32(-1e30))
+    s = s_ref[...]
+    raised = jnp.exp(s - jnp.max(s, axis=-1, keepdims=True))
+    w = (raised / jnp.sum(raised, axis=-1, keepdims=True)).astype(BF)
+    folded = dot(w, jnp.where(lands, 1.0, 0.0).astype(BF))
     for group in range(heads // per):
-        total = jnp.zeros((slots, BLK), F32)
-        for i in range(per):
+        out = folded[group * per * slots : (group * per + 1) * slots]
+        for i in range(1, per):
             h = group * per + i
-            s = nt(qn_ref[:, h * NOPE : (h + 1) * NOPE], keys[:, h * NOPE : (h + 1) * NOPE])
-            s = s + nt(qr_ref[:, h * ROPE : (h + 1) * ROPE], key_rope)
-            s = jnp.where(allowed, s * (NOPE + ROPE) ** (-0.5), jnp.float32(-1e30))
-            raised = jnp.exp(s - jnp.max(s, axis=-1, keepdims=True))
-            w = (raised / jnp.sum(raised, axis=-1, keepdims=True)).astype(BF)
-            fold = jnp.where(lands & ((lane >> 5) == i), 1.0, 0.0).astype(BF)
-            total = total + dot(w, fold)
-        out_ref[:, group * BLK : (group + 1) * BLK] = total.astype(BF)
+            out = jnp.where((lane >> 5) == i, folded[h * slots : (h + 1) * slots], out)
+        out_ref[:, group * BLK : (group + 1) * BLK] = out.astype(BF)
 
 
 def score_weights(counts, *arrays):
@@ -80,12 +88,14 @@
         out_shape=jax.ShapeDtypeStruct(shape, BF),
         in_specs=[pl.BlockSpec(memory_space=pltpu.SMEM)] + [whole(a.shape) for a in arrays],
         out_specs=whole(shape),
+        scratch_shapes=[pltpu.VMEM((slots * heads, slots), F32)],
+        cost_estimate=cost(4),
         name="score_weights",
     )(counts, *arrays)
 
 
 def live_rows(goes_ref, own_ref, other_ref):
-    row = iota((BLK, own_ref.shape[0]), 0) + pl.program_id(0) * BLK
+    row = iota((STEP, own_ref.shape[0]), 0) + pl.program_id(0) * STEP
     out = dot(jnp.where(goes_ref[0] == row, 1.0, 0.0).astype(BF), own_ref[...])
     out = out + dot(jnp.where(goes_ref[1] == row, 1.0, 0.0).astype(BF), other_ref[...])
     return out.astype(BF)
@@ -99,10 +109,11 @@
     width = up.shape[1]
     return pl.pallas_call(
         values_kernel,
-        grid=(LIVE // BLK,),
+        grid=(LIVE // STEP,),
         out_shape=jax.ShapeDtypeStruct((LIVE, width), BF),
         in_specs=[whole(a.shape) for a in (goes, own, other, up)],
-        out_specs=pl.BlockSpec((BLK, width), lambda b: (b, 0)),
+        out_specs=pl.BlockSpec((STEP, width), lambda b: (b, 0)),
+        cost_estimate=cost(6),
         name="live_values",
     )(goes, own, other, up)
 
@@ -115,9 +126,9 @@
     near = (gap >= 0) & (gap < WIN)
     per = BLK // WIN
     masks = [jnp.where(near & ((l_at >> 5) == q), 1.0, 0.0).astype(BF) for q in range(per)]
-    r_at2, l_at2 = iota((WIN, BLK), 0), iota((WIN, BLK), 1)
-    before = jnp.where((BLK + r_at2 - l_at2) < WIN, 1.0, 0.0).astype(BF)
-    blank = jnp.zeros((BLK - WIN, BLK), BF)
+    r_at, l_at = iota((WIN, BLK), 0), iota((WIN, BLK), 1)
+    before = jnp.where((BLK + r_at - l_at) < WIN, 1.0, 0.0).astype(BF)
+    blank = jnp.zeros((BLK, BLK), BF)
     packed = live_rows(goes_ref, own_ref, other_ref)
     for group in range(heads // per):
         one = packed[:, group * BLK : (group + 1) * BLK].astype(F32)
@@ -126,19 +137,33 @@
             turned.append(pltpu.roll(one, q * WIN, 1).astype(BF))
         for i in range(per):
             cols = slice((group * per + i) * VH, (group * per + i + 1) * VH)
-            band = turned[(-i) % per] * masks[0]
-            for q in range(1, per):
-                band = band + turned[(q - i) % per] * masks[q]
-            old = jnp.concatenate([turned[(per - 1 - i) % per][:WIN] * before, blank], axis=0)
-            band = jnp.concatenate([old, band], axis=1)
-            both = jnp.concatenate([prev_ref[:, cols], cur_ref[:, cols]], axis=0)
-            att_ref[:, cols] = dot(band, both).astype(BF)
+            bands = []
+            for rows in (slice(0, BLK), slice(BLK, STEP)):
+                band = turned[(-i) % per][rows] * masks[0]
+                for q in range(1, per):
+                    band = band + turned[(q - i) % per][rows] * masks[q]
+                bands.append(band)
+            last = turned[(per - 1 - i) % per]
+            corner = jnp.concatenate([last[BLK : BLK + WIN] * before, blank[WIN:]], axis=0)
+            band = jnp.concatenate(
+                [
+                    jnp.concatenate([bands[0], blank], axis=1),
+                    jnp.concatenate([corner, bands[1]], axis=1),
+                ],
+                axis=0,
+            )
+            att = dot(band, cur_ref[:, cols])
+            old = dot(last[:WIN] * before, prev_ref[:, cols])
+            att_ref[:WIN, cols] = (att[:WIN] + old).astype(BF)
+            att_ref[WIN:, cols] = att[WIN:].astype(BF)
     part = nt(att_ref[...], wo_ref[...]).astype(BF)
-    order = ((r_at & 15) * 8 + (r_at >> 4)) == l_at
+    share = STEP // 8
+    r_at, l_at = iota((STEP, STEP), 0), iota((STEP, STEP), 1)
+    order = ((r_at & (share - 1)) * 8 + (r_at >> 5)) == l_at
     part = dot(jnp.where(order, 1.0, 0.0).astype(BF), part)
-    rows = pl.ds(pl.multiple_of(b * 16, 16), 16)
+    rows = pl.ds(pl.multiple_of(b * share, share), share)
     for m in range(8):
-        all_ref[m, rows, :] = part[m * 16 : (m + 1) * 16]
+        all_ref[m, rows, :] = part[m * share : (m + 1) * share]
 
     @pl.when(b == pl.num_programs(0) - 1)
     def _():
@@ -152,18 +177,19 @@
     shape = (8, n, LIVE // 8)
     return pl.pallas_call(
         mix_kernel,
-        grid=(LIVE // BLK,),
+        grid=(LIVE // STEP,),
         out_shape=jax.ShapeDtypeStruct(shape, BF),
         in_specs=[
             whole(goes.shape),
             whole(own.shape),
             whole(other.shape),
-            pl.BlockSpec((BLK, width), lambda b: (jnp.maximum(b - 1, 0), 0)),
-            pl.BlockSpec((BLK, width), lambda b: (b, 0)),
+            pl.BlockSpec((BLK, width), lambda b: (jnp.maximum(b * (STEP // BLK) - 1, 0), 0)),
+            pl.BlockSpec((STEP, width), lambda b: (b, 0)),
             whole(wo.shape),
         ],
         out_specs=whole(shape),
-        scratch_shapes=[pltpu.VMEM((BLK, width), BF), pltpu.VMEM((8, LIVE // 8, n), F32)],
+        scratch_shapes=[pltpu.VMEM((STEP, width), BF), pltpu.VMEM((8, LIVE // 8, n), F32)],
+        cost_estimate=cost(9),
         name="mix_project",
     )(goes, own, other, values, values, wo)
 
@@ -207,6 +233,7 @@
         in_specs=[spec, spec, whole((width, 1)), whole((ff, width)), whole((ff, width))],
         out_specs=pl.BlockSpec((blocks, 2 * ff + 16, chunk), lambda b: (b, 0, 0)),
         scratch_shapes=[pltpu.VMEM((width, blocks * chunk), BF)],
+        cost_estimate=cost(6),
         name="gate_up",
     )(own, other, gain, gate_weight, up_weight)
 
@@ -262,9 +289,17 @@
     slot = jnp.arange(slots, dtype=jnp.int32)
 
     share = slots // 4
+    half = width // 2
+    eight = jnp.arange(8, dtype=jnp.int32)
+    spread = ((eight[:, None] - own_start) & 7) + 8 * eight[None, :]
+    roll = (spread.reshape(slots, 1) == slot[None, :]).astype(BF)
+    rows = dot(roll, residual).astype(BF).reshape(2, 4, 8, width)
+    pad = ((0, 0),) * 3 + ((0, latent.shape[1] - half),)
+    rows = jnp.stack([jnp.pad(rows[..., :half], pad), jnp.pad(rows[..., half:], pad)], axis=1)
+    rows = rows.transpose(2, 0, 1, 3, 4).reshape(16, 8, latent.shape[1])
     latents = lax.dynamic_slice_in_dim(latent, x_at * share, share, 0)
-    latents = gather(gather(latents, ("zh", "y")), "x").reshape(-1, latent.shape[1])
-    latents_other = shifted(latents, "c", 1)
+    latents = jnp.broadcast_to(latents[None], (16,) + latents.shape)
+    got = exchange(jnp.concatenate([latents, rows], axis=1), ("zh", "y"))
 
     weights = score_weights(
         rank_tokens, query_nope, query_rope, latent, key_rope, key_up, request_ids
@@ -272,26 +307,36 @@
     weights = gather(gather(weights, "zh"), "y").reshape(-1, weights.shape[1])
     weights_other = shifted(weights, "c", 1)
 
-    first, count = starts(every).reshape(4, 4, 2), rank_tokens.reshape(4, 4, 2)
-    to = jnp.where(slot < count[..., None], first[..., None] + slot, -1)
-    to = jnp.where(c == 0, jnp.stack([to[:, :, 0], to[:, :, 1]]), jnp.stack([to[:, :, 1], to[:, :, 0]]))
-    goes = to.transpose(0, 2, 1, 3).reshape(2, 1, -1)
-    goes_latent = to.reshape(2, 4, 4, 4, share).transpose(0, 3, 1, 2, 4).reshape(2, 1, -1)
+    latents = got[:, :share].reshape(-1, latent.shape[1])
+    latents = jnp.concatenate([latents] + [shifted(latents, "x", s) for s in (1, 2, 3)], axis=0)
+    latents_other = shifted(latents, "c", 1)
+
+    def by_core(a):
+        a = a.reshape(4, 4, 2)
+        return jnp.where(c == 0, jnp.stack([a[..., 0], a[..., 1]]), jnp.stack([a[..., 1], a[..., 0]]))
+
+    first, count = by_core(starts(every)), by_core(rank_tokens)
+    goes = jnp.swapaxes(first, 1, 2)[..., None] + slot
+    goes = jnp.where(slot < jnp.swapaxes(count, 1, 2)[..., None], goes, -1).reshape(2, 1, -1)
+    block = (x_at - jnp.arange(4, dtype=jnp.int32)) & 3
+    own_slot = (block[:, None] * share + jnp.arange(share, dtype=jnp.int32)).reshape(1, 4, 1, 1, share)
+    goes_latent = first[:, None, :, :, None] + own_slot
+    goes_latent = jnp.where(own_slot < count[:, None, :, :, None], goes_latent, -1).reshape(2, 1, -1)
     values = live_values(goes_latent, latents, latents_other, value_up)
 
-    eight = jnp.arange(8, dtype=jnp.int32)
-    spread = ((eight[:, None] - own_start) & 7) + 8 * eight[None, :]
-    roll = (spread.reshape(slots, 1) == slot[None, :]).astype(BF)
-    rows = dot(roll, residual).astype(BF).reshape(2, 4, 8, 2, 2, quarter)
-    rows = rows.transpose(1, 0, 3, 4, 2, 5).reshape(ranks, 8, quarter)
-    rows = exchange(rows, DP)
     mine = (y >> 1) * 4 + zh
-    place = ((mine - starts(every)[:, None]) & 7) + 8 * eight[None, :]
-    come = jnp.where(place < rank_tokens[:, None], (starts(every)[:, None] + place) >> 3, -1)
-    come = (come.reshape(ranks * 8, 1) == jnp.arange(chunk, dtype=jnp.int32)).astype(BF)
-    rows = lax.dot_general(
-        rows.reshape(ranks * 8, quarter), come, (((0,), (0,)), ((), ())), preferred_element_type=F32
-    )
+    place = ((mine - first[..., None]) & 7) + 8 * eight
+    come = jnp.where(place < count[..., None], (first[..., None] + place) >> 3, -1)
+    come = (come.reshape(2, -1, 1) == jnp.arange(chunk, dtype=jnp.int32)).astype(BF)
+    rows = got[:, share:].reshape(-1, latent.shape[1])
+    left, right = rows[:, :quarter], rows[:, quarter:half]
+    kept = jnp.where(c == 0, left, right)
+    rows = shifted(jnp.where(c == 0, right, left), "c", 1)
+
+    def tn(a, b):
+        return lax.dot_general(a, b, (((0,), (0,)), ((), ())), preferred_element_type=F32)
+
+    rows = tn(kept, come[0]) + tn(rows, come[1])
 
     weights_other, rows = lax.optimization_barrier((weights_other, rows))
     part = mix_project(goes, weights, weights_other, values, output_weight.T)
@@ -328,23 +373,23 @@
     total = (down(c) + sent.astype(F32)).astype(BF)
     total = jnp.sum(exchange(total, "y").astype(F32), axis=0)
     m = y * 2 + c
-    first = starts(every)
-    place = ((m - first[:, None]) & 7) + 8 * eight[None, :]
-    comes = jnp.where(place < rank_tokens[:, None], (first[:, None] + place) >> 3, -1)
-    expand = (comes.reshape(4, slots, 1) == jnp.arange(chunk, dtype=jnp.int32)).astype(BF)
-    planes = dot(expand.reshape(4 * slots, chunk), total.astype(BF)).astype(BF)
+    begin = starts(every)
+    place = ((m - begin[:, None]) & 7) + 8 * eight[None, :]
+    comes = jnp.where(place < rank_tokens[:, None], (begin[:, None] + place) >> 3, -1)
+    expand = (comes.reshape(ranks * 8, 1) == jnp.arange(chunk, dtype=jnp.int32)).astype(BF)
     pair = [pick(a.reshape(2, 2, 4, quarter, chunk), m >> 2) for a in (full, full_other)]
     pair = [lax.dynamic_index_in_dim(a, m & 3, 1, keepdims=False) for a in pair]
     low = jnp.where(c == 0, pair[0], pair[1])
     high = jnp.where(c == 0, pair[1], pair[0])
     own = jnp.stack([low, high], axis=1).reshape(width, chunk)
-    result = nt(pick(expand, zh), own)
-    result = result + jnp.sum(exchange(planes.reshape(4, slots, width), "zh").astype(F32), axis=0)
-    result = exchange(result.astype(BF).reshape(8, 8, width), ("y", "c"))
+    here = (jnp.arange(ranks * 8, dtype=jnp.int32) >> 6) == zh
+    own = nt(jnp.where(here[:, None], expand, jnp.zeros_like(expand)), own)
+    result = (dot(expand, total.astype(BF)) + own).astype(BF).reshape(ranks, 8, width)
+    result = jnp.sum(exchange(result, DP).reshape(4, slots, width).astype(F32), axis=0).astype(BF)
     at = ((own_start + slot) & 7) * 8 + (slot >> 3)
     at = jnp.where(slot < own_length, at, -1)
     back = (at[:, None] == slot[None, :]).astype(BF)
-    return dot(back, result.reshape(slots, width)).astype(BF)
+    return dot(back, result).astype(BF)
 
 
 def solution(mesh):

time: 292 us -> 263 us (0.901)
  waiting for transfers between devices: 72.6 us -> 55.7 us
  blocking collectives: 96.1 us -> 84.9 us
  other arithmetic: 5.74 us -> 11.3 us
  starting transfers between devices: 59.3 us -> 53.9 us
  Pallas kernels: 37.2 us -> 33 us
    all_to_all x8 -> x6, waiting for transfers between devices: 69.2 us -> 52.4 us  [exchange(): return lax.all_to_all(x, axes, split_axis=0, concat_axis=0, tiled=True)]
    all_to_all x8 -> x6, starting transfers between devices: 44.5 us -> 32 us  [exchange(): return lax.all_to_all(x, axes, split_axis=0, concat_axis=0, tiled=True)]
    all_to_all x5 -> x4, blocking collectives: 96.1 us -> 84.9 us  [exchange(): return lax.all_to_all(x, axes, split_axis=0, concat_axis=0, tiled=True)]
    ppermute x4 -> x8, starting transfers between devices: 14.2 us -> 21.2 us  [shifted(): return lax.ppermute(x, axis, [(i, (i + shift) % n) for i in range(n)])]
  transfers between devices with their start and end apart: 13 -> 15, of which waited for: 10 -> 7; matrix products, arithmetic and copies ran while one was open for 4% -> 6% of each run, Pallas kernels for 0% -> 5%
where the time goes in v3:
time: 263 us; the launch traced here: 262 us
  blocking collectives  84.9 us (32%)
  waiting for transfers between devices  55.7 us (21%)
  starting transfers between devices  53.9 us (20%)
  Pallas kernels  33 us (13%)
  local copies, waits for them, and re-layouts  13.2 us (5%)
  other arithmetic  11.3 us (4%)
  matrix products  9.35 us (4%)
    all_to_all x4, blocking collectives, exchange(): return lax.all_to_all(x, axes, split_axis=0, concat_axis=0, tiled=True)  84.9 us
    all_to_all x6, waiting for transfers between devices, exchange(): return lax.all_to_all(x, axes, split_axis=0, concat_axis=0, tiled=True)  52.4 us
    all_to_all x6, starting transfers between devices, exchange(): return lax.all_to_all(x, axes, split_axis=0, concat_axis=0, tiled=True)  32 us
    ppermute x8, starting transfers between devices, shifted(): return lax.ppermute(x, axis, [(i, (i + shift) % n) for i in range(n)])  21.2 us
    pallas_call x1, Pallas kernels, mix_project(): pl.pallas_call(mix_kernel, grid=(LIVE // STEP,), out_shape=jax.ShapeDtype...  13.6 us
    pallas_call x1, Pallas kernels, live_values(): pl.pallas_call(values_kernel, grid=(LIVE // STEP,), out_shape=jax.ShapeDt...  8.65 us
    pallas_call x1, Pallas kernels, gate_up(): pl.pallas_call(gate_up_kernel, grid=(highs * planes // blocks,), out_shap...  7.02 us
  transfers between devices with their start and end apart: 15, of which 7 were waited for; matrix products, arithmetic and copies ran while one was open for 6% of the time, Pallas kernels for 5%

profile of v3, /device:TPU:1, one launch (start us, length us, event | category | flops | bytes accessed | tf_op | source)
XLA Modules:
  0.0 262.0 jit_solution(3977630227059153785)
XLA Ops:
  0.0 1.4 fusion.35
  1.4 0.6 subtract_and_fusion.1
  2.2 1.1 convolution_convert_fusion.2
  3.5 0.7 fusion.19
  4.2 0.7 constant_dynamic-slice_fusion
  4.9 0.8 pad_maximum_fusion.1
  5.7 11.7 %all-to-all-start.2 = ((bf16[16,24,512]{2,1,0:T(8,128)(2,1)}), bf16[16,24,512]{2,1,0:T(8,128)(2,1)S(1)}, u32[]{:S(2)}, u32[]{:S(2)}) async-start(bf16[16,24,512]{2,1,0:T(8,128)(2,1)} %pad_maximum_fusion.1), calls=%async_computation.2 | async-start | bytes 786432 | tf_op jit(solution)/shard_map/all_to_all | solution.py:242
  17.8 0.3 slice_reduce_fusion.3
  18.0 0.2 slice_reduce_fusion.1
  19.0 3.7 %score_weights.1 = bf16[64,512]{1,0:T(8,128)(2,1)} custom-call(s32[32]{0:T(128)} %counts_ref.1, bf16[64,2048]{1,0:T(8,128)(2,1)} %qn_ref.1, bf16[64,1024]{1,0:T(8,128)(2,1)} %qr_ref.1, bf16[64,512]{1,0:T(8,128)(2,1)} %lat_ref.1, bf16[64,64]{1,0:T(8,128)(2,1)} %kr_ref.1, bf16[512,2048]{1,0:T(8,128)(2,1)} %ku_ref.1, s32[1,64]{1,0:T(1,128)} %req_ref.1), custom_call_target="tpu_custom_call" | custom-call | flops 4000000000 | bytes 12000000 | tf_op jit(solution)/shard_map/score_weights/pallas_call | solution.py:85
  22.7 6.9 %all-to-all-done.2 = bf16[16,24,512]{2,1,0:T(8,128)(2,1)S(1)} async-done(((bf16[16,24,512]{2,1,0:T(8,128)(2,1)}), bf16[16,24,512]{2,1,0:T(8,128)(2,1)S(1)}, u32[]{:S(2)}, u32[]{:S(2)}) %all-to-all-start.2) | async-done | bytes 393248 | tf_op jit(solution)/shard_map/all_to_all | solution.py:242
  29.6 1.6 broadcast_in_dim.57
  31.1 4.9 %all-to-all-start = ((bf16[4,64,512]{2,1,0:T(8,128)(2,1)}), bf16[4,64,512]{2,1,0:T(8,128)(2,1)S(1)}, u32[]{:S(2)}, u32[]{:S(2)}) async-start(bf16[4,64,512]{2,1,0:T(8,128)(2,1)} %broadcast_in_dim.57), calls=%async_computation | async-start | bytes 524288 | tf_op jit(solution)/shard_map/all_to_all | solution.py:242
  36.2 1.3 collective-permute-start.2
  37.4 2.5 collective-permute-start.3
  39.9 1.2 collective-permute-start.4
  41.8 0.7 add.260
  42.6 0.7 lt.157
  43.3 0.7 lt.154
  44.0 1.1 broadcast_in_dim.58
  45.1 3.5 %all-to-all-start.1 = ((bf16[4,4,64,512]{3,2,1,0:T(8,128)(2,1)}), bf16[4,4,64,512]{3,2,1,0:T(8,128)(2,1)S(1)}, u32[]{:S(2)}, u32[]{:S(2)}) async-start(bf16[4,4,64,512]{3,2,1,0:T(8,128)(2,1)} %broadcast_in_dim.58), calls=%async_computation.1 | async-start | bytes 2097152 | tf_op jit(solution)/shard_map/all_to_all | solution.py:242
  48.6 0.6 compare_select_fusion.goes_ref
  49.3 0.7 copy-done.6
  50.0 0.7 copy-done.7
  50.7 1.3 pad_maximum_fusion.own_ref
  52.0 3.6 %collective-permute-start.5 = (bf16[1024,512]{1,0:T(8,128)(2,1)S(1)}, bf16[1024,512]{1,0:T(8,128)(2,1)}, u32[]{:S(2)}, u32[]{:S(2)}) collective-permute-start(bf16[1024,512]{1,0:T(8,128)(2,1)S(1)} %pad_maximum_fusion.own_ref), channel_id=1, source_target_pairs={{0,8},{8,0},{1,9},{9,1},{2,10},{10,2},{3,11},{11,3},{4,12},{12,4},... | collective-permute-start | bytes 3145736 | tf_op jit(solution)/shard_map/ppermute | solution.py:27
  55.6 0.6 compare_select_fusion.1.goes_ref
  56.2 0.7 slice_bitcast_fusion
  56.9 3.0 %all-to-all-done.1 = bf16[4,4,64,512]{3,2,1,0:T(8,128)(2,1)S(1)} async-done(((bf16[4,4,64,512]{3,2,1,0:T(8,128)(2,1)}), bf16[4,4,64,512]{3,2,1,0:T(8,128)(2,1)S(1)}, u32[]{:S(2)}, u32[]{:S(2)}) %all-to-all-start.1) | async-done | bytes 1048608 | tf_op jit(solution)/shard_map/all_to_all | solution.py:242
  59.9 4.7 %collective-permute-start = (bf16[1024,512]{1,0:T(8,128)(2,1)S(1)}, bf16[1024,512]{1,0:T(8,128)(2,1)}, u32[]{:S(2)}, u32[]{:S(2)}) collective-permute-start(bf16[1024,512]{1,0:T(8,128)(2,1)S(1)} %bitcast.78), channel_id=1, source_target_pairs={{0,8},{8,0},{1,9},{9,1},{2,10},{10,2},{3,11},{11,3},{4,12},{12,4},... | collective-permute-start | bytes 3145736 | tf_op jit(solution)/shard_map/ppermute | solution.py:27
  64.6 1.0 broadcast_select_fusion
  65.6 0.2 collective-permute-start.1
  65.9 1.2 fusion.20
  67.1 0.8 convolution_add_fusion.1
  68.0 8.6 %live_values.1.prev_ref.cur_ref = bf16[1024,2048]{1,0:T(8,128)(2,1)} custom-call(s32[2,1,1024]{2,1,0:T(1,128)} %compare_select_fusion.goes_ref, bf16[1024,512]{1,0:T(8,128)(2,1)} %copy-done.3, bf16[1024,512]{1,0:T(8,128)(2,1)} %collective-permute-done.5.other_ref, bf16[512,2048]{1,0:T(8,128)(2,1)} %up_ref.1), custom_call_target="tpu_custom_call" | custom-call | flops 6000000000 | bytes 18000000 | tf_op jit(solution)/shard_map/live_values/pallas_call | solution.py:110
  76.6 13.6 %mix_project.1 = bf16[8,224,128]{2,1,0:T(8,128)(2,1)} custom-call(s32[2,1,1024]{2,1,0:T(1,128)} %compare_select_fusion.1.goes_ref, bf16[1024,512]{1,0:T(8,128)(2,1)} %bitcast.79, bf16[1024,512]{1,0:T(8,128)(2,1)} %collective-permute-done.other_ref, bf16[1024,2048]{1,0:T(8,128)(2,1)} %live_values.1.prev_ref.cur_ref, ...), custom_call_target="tpu_custom_call" | custom-call | flops 8999999488 | bytes 27000000 | tf_op jit(solution)/shard_map/mix_project/pallas_call | solution.py:178
  90.3 13.4 %all_to_all.50 = bf16[8,224,128]{2,1,0:T(8,128)(2,1)S(1)} all-to-all(bf16[8,224,128]{2,1,0:T(8,128)(2,1)} %mix_project.1), channel_id=1, replica_groups=mesh['zh'=4,'y'=4,'c'=2,'x'=4,'zl'=2] {'x','zl'}, dimensions={0} | all-to-all | bytes 917504 | tf_op jit(solution)/shard_map/all_to_all | solution.py:242
  103.7 0.7 collective-permute-start.6
  104.5 22.5 %all_to_all.51 = bf16[4,224,128]{2,1,0:T(8,128)(2,1)S(1)} all-to-all(bf16[4,224,128]{2,1,0:T(8,128)(2,1)S(1)} %broadcast_in_dim.62), channel_id=1, replica_groups=mesh['zh'=4,'y'=4,'c'=2,'x'=4,'zl'=2] {'zh'}, dimensions={0} | all-to-all | bytes 458752 | tf_op jit(solution)/shard_map/all_to_all | solution.py:242
  127.1 15.5 %all_to_all.52 = bf16[4,4,224,128]{3,2,1,0:T(8,128)(2,1)S(1)} all-to-all(bf16[4,4,224,128]{3,2,1,0:T(8,128)(2,1)S(1)} %broadcast_in_dim.63), channel_id=1, replica_groups=mesh['zh'=4,'y'=4,'c'=2,'x'=4,'zl'=2] {'y'}, dimensions={0} | all-to-all | bytes 1835008 | tf_op jit(solution)/shard_map/all_to_all | solution.py:242
  142.6 5.3 %collective-permute-start.7 = (bf16[2,2,4,224,128]{4,3,2,1,0:T(8,128)(2,1)S(1)}, bf16[2,2,4,224,128]{4,3,2,1,0:T(8,128)(2,1)S(1)}, u32[]{:S(2)}, u32[]{:S(2)}) collective-permute-start(bf16[2,2,4,224,128]{4,3,2,1,0:T(8,128)(2,1)S(1)} %bitcast.74), channel_id=1, source_target_pairs={{0,8},{8,0},{1,9},{9,1},{2,10},{10,2},{3,11},{11,3},{4,12},{12,4},... | collective-permute-start | bytes 2752520 | tf_op jit(solution)/shard_map/ppermute | solution.py:27
  147.9 1.0 broadcast_in_dim.69.gain_ref
  148.9 1.1 collective-permute-done.7.other_ref
  150.0 0.9 copy-done.8
  150.9 7.0 %gate_up.1 = bf16[8,1168,128]{2,1,0:T(8,128)(2,1)} custom-call(bf16[2,2,4,224,128]{4,3,2,1,0:T(8,128)(2,1)} %bitcast.75, bf16[2,2,4,224,128]{4,3,2,1,0:T(8,128)(2,1)} %copy-done.8, f32[896,1]{1,0:T(8,128)} %broadcast_in_dim.69.gain_ref, bf16[576,896]{1,0:T(8,128)(2,1)} %bitcast.94, bf16[576,896]{1,0:T(8,128)(2,1)} %bitcast.95), custom_call_target="tpu_custom_call" | custom-call | flops 6000000000 | bytes 18000000 | tf_op jit(solution)/shard_map/gate_up/pallas_call | solution.py:229
  158.0 33.5 %all_to_all.53 = bf16[8,1168,128]{2,1,0:T(8,128)(2,1)S(1)} all-to-all(bf16[8,1168,128]{2,1,0:T(8,128)(2,1)} %gate_up.1), channel_id=1, replica_groups=mesh['zh'=4,'y'=4,'c'=2,'x'=4,'zl'=2] {'x','zl'}, dimensions={0} | all-to-all | bytes 4784128 | tf_op jit(solution)/shard_map/all_to_all | solution.py:242
  191.4 0.3 convert_reduce_fusion
  191.9 1.2 broadcast_in_dim.66
  193.1 3.7 %all-to-all-start.7 = ((bf16[8,576,128]{2,1,0:T(8,128)(2,1)}), bf16[8,576,128]{2,1,0:T(8,128)(2,1)S(1)}, u32[]{:S(2)}, u32[]{:S(2)}) async-start(bf16[8,576,128]{2,1,0:T(8,128)(2,1)} %broadcast_in_dim.66), calls=%async_computation.7 | async-start | bytes 2359296 | tf_op jit(solution)/shard_map/all_to_all | solution.py:242
  196.8 15.5 %all-to-all-done.7 = bf16[8,576,128]{2,1,0:T(8,128)(2,1)S(1)} async-done(((bf16[8,576,128]{2,1,0:T(8,128)(2,1)}), bf16[8,576,128]{2,1,0:T(8,128)(2,1)S(1)}, u32[]{:S(2)}, u32[]{:S(2)}) %all-to-all-start.7) | async-done | bytes 1179680 | tf_op jit(solution)/shard_map/all_to_all | solution.py:242
  212.3 1.9 convolution_convert_fusion
  214.2 2.5 collective-permute-start.8
  216.9 2.1 collective-permute-done.8
  219.0 1.9 add_convert_fusion
  220.9 3.5 %all-to-all-start.8 = ((bf16[4,128,896]{2,1,0:T(8,128)(2,1)}), bf16[4,128,896]{2,1,0:T(8,128)(2,1)S(1)}, u32[]{:S(2)}, u32[]{:S(2)}) async-start(bf16[4,128,896]{2,1,0:T(8,128)(2,1)} %add_convert_fusion), calls=%async_computation.8 | async-start | bytes 1835008 | tf_op jit(solution)/shard_map/all_to_all | solution.py:242
  224.5 1.0 fusion.15
  225.4 1.0 fusion.14
  226.5 0.3 fusion.17
  226.8 11.0 %all-to-all-done.8 = bf16[4,128,896]{2,1,0:T(8,128)(2,1)S(1)} async-done(((bf16[4,128,896]{2,1,0:T(8,128)(2,1)}), bf16[4,128,896]{2,1,0:T(8,128)(2,1)S(1)}, u32[]{:S(2)}, u32[]{:S(2)}) %all-to-all-start.8) | async-done | bytes 917536 | tf_op jit(solution)/shard_map/all_to_all | solution.py:242
  238.0 1.1 fusion.1
  239.1 4.7 %all-to-all-start.9 = ((bf16[32,8,896]{2,1,0:T(8,128)(2,1)}), bf16[32,8,896]{2,1,0:T(8,128)(2,1)S(1)}, u32[]{:S(2)}, u32[]{:S(2)}) async-start(bf16[32,8,896]{2,1,0:T(8,128)(2,1)} %fusion.1), calls=%async_computation.9 | async-start | bytes 917504 | tf_op jit(solution)/shard_map/all_to_all | solution.py:242
  243.9 1.2 compare_select_fusion.4
  245.0 16.0 %all-to-all-done.9 = bf16[32,8,896]{2,1,0:T(8,128)(2,1)S(1)} async-done(((bf16[32,8,896]{2,1,0:T(8,128)(2,1)}), bf16[32,8,896]{2,1,0:T(8,128)(2,1)S(1)}, u32[]{:S(2)}, u32[]{:S(2)}) %all-to-all-start.9) | async-done | bytes 458784 | tf_op jit(solution)/shard_map/all_to_all | solution.py:242
  261.1 0.9 convolution_convert_fusion.1
  (92 shorter events, 3.1 us)
Async XLA Ops:
  0.0 212.3 %copy-start = (bf16[576,896]{1,0:T(8,128)(2,1)S(1)}, bf16[576,896]{1,0:T(8,128)(2,1)}, u32[]{:S(2)}) copy-start(bf16[576,896]{1,0:T(8,128)(2,1)} %param.25) | copy-start | bytes 3096580
  0.0 17.4 %copy-start.14 = (s32[32]{0:T(128)S(1)}, s32[32]{0:T(128)}, u32[]{:S(2)}) copy-start(s32[32]{0:T(128)} %counts_ref.1) | copy-start | bytes 388
  2.0 20.6 %copy-start.12 = (s32[8]{0:T(128)}, s32[8]{0:T(128)S(1)}, u32[]{:S(2)}) copy-start(s32[8]{0:T(128)S(1)} %get-tuple-element.19) | copy-start | bytes 100
  5.7 23.9 %all-to-all-start.2 = ((bf16[16,24,512]{2,1,0:T(8,128)(2,1)}), bf16[16,24,512]{2,1,0:T(8,128)(2,1)S(1)}, u32[]{:S(2)}, u32[]{:S(2)}) async-start(bf16[16,24,512]{2,1,0:T(8,128)(2,1)} %pad_maximum_fusion.1), calls=%async_computation.2 | async-start | bytes 786432 | tf_op jit(solution)/shard_map/all_to_all | solution.py:242
  17.6 1.1 copy-start.17
  31.1 12.9 %all-to-all-start = ((bf16[4,64,512]{2,1,0:T(8,128)(2,1)}), bf16[4,64,512]{2,1,0:T(8,128)(2,1)S(1)}, u32[]{:S(2)}, u32[]{:S(2)}) async-start(bf16[4,64,512]{2,1,0:T(8,128)(2,1)} %broadcast_in_dim.57), calls=%async_computation | async-start | bytes 524288 | tf_op jit(solution)/shard_map/all_to_all | solution.py:242
  36.1 13.1 %copy-start.4 = (bf16[16,16,512]{2,1,0:T(8,128)(2,1)}, bf16[16,16,512]{2,1,0:T(8,128)(2,1)S(1)}, u32[]{:S(2)}) copy-start(bf16[16,16,512]{2,1,0:T(8,128)(2,1)S(1)} %slice.80) | copy-start | bytes 786436
  36.2 13.1 %collective-permute-start.2 = (bf16[256,512]{1,0:T(8,128)(2,1)S(1)}, bf16[256,512]{1,0:T(8,128)(2,1)S(1)}, u32[]{:S(2)}, u32[]{:S(2)}) collective-permute-start(bf16[256,512]{1,0:T(8,128)(2,1)S(1)} %bitcast.80), channel_id=1, source_target_pairs={{0,2},{2,4},{4,6},{6,0},{1,3},{3,5},{5,7},{7,1},{8,10},{10,12},{12... | collective-permute-start | bytes 786440 | tf_op jit(solution)/shard_map/ppermute | solution.py:27
  37.4 11.8 %collective-permute-start.3 = (bf16[256,512]{1,0:T(8,128)(2,1)S(1)}, bf16[256,512]{1,0:T(8,128)(2,1)S(1)}, u32[]{:S(2)}, u32[]{:S(2)}) collective-permute-start(bf16[256,512]{1,0:T(8,128)(2,1)S(1)} %bitcast.81), channel_id=1, source_target_pairs={{0,4},{2,6},{4,0},{6,2},{1,5},{3,7},{5,1},{7,3},{8,12},{10,14},{12... | collective-permute-start | bytes 786440 | tf_op jit(solution)/shard_map/ppermute | solution.py:27
  39.9 10.8 %collective-permute-start.4 = (bf16[256,512]{1,0:T(8,128)(2,1)S(1)}, bf16[256,512]{1,0:T(8,128)(2,1)}, u32[]{:S(2)}, u32[]{:S(2)}) collective-permute-start(bf16[256,512]{1,0:T(8,128)(2,1)S(1)} %bitcast.82), channel_id=1, source_target_pairs={{0,6},{2,0},{4,2},{6,4},{1,7},{3,1},{5,3},{7,5},{8,14},{10,8},{12,... | collective-permute-start | bytes 786440 | tf_op jit(solution)/shard_map/ppermute | solution.py:27
  45.1 14.8 %all-to-all-start.1 = ((bf16[4,4,64,512]{3,2,1,0:T(8,128)(2,1)}), bf16[4,4,64,512]{3,2,1,0:T(8,128)(2,1)S(1)}, u32[]{:S(2)}, u32[]{:S(2)}) async-start(bf16[4,4,64,512]{3,2,1,0:T(8,128)(2,1)} %broadcast_in_dim.58), calls=%async_computation.1 | async-start | bytes 2097152 | tf_op jit(solution)/shard_map/all_to_all | solution.py:242
  48.6 7.0 %copy-start.9 = (s32[2,1,1024]{2,1,0:T(1,128)S(1)}, s32[2,1,1024]{2,1,0:T(1,128)}, u32[]{:S(2)}) copy-start(s32[2,1,1024]{2,1,0:T(1,128)} %add.260) | copy-start | bytes 24580
  48.6 7.0 %copy-start.10 = (s32[2,1,1024]{2,1,0:T(1,128)S(1)}, s32[2,1,1024]{2,1,0:T(1,128)}, u32[]{:S(2)}) copy-start(s32[2,1,1024]{2,1,0:T(1,128)} %lt.157) | copy-start | bytes 24580
  48.6 7.0 %copy-start.11 = (s32[1024]{0:T(1024)S(1)}, s32[1024]{0:T(1024)}, u32[]{:S(2)}) copy-start(s32[1024]{0:T(1024)} %lt.154) | copy-start | bytes 12292
  49.3 0.7 copy-start.6
  50.0 0.7 copy-start.7
  52.0 16.0 %copy-start.3 = (bf16[1024,512]{1,0:T(8,128)(2,1)}, bf16[1024,512]{1,0:T(8,128)(2,1)S(1)}, u32[]{:S(2)}) copy-start(bf16[1024,512]{1,0:T(8,128)(2,1)S(1)} %pad_maximum_fusion.own_ref) | copy-start | bytes 3145732
  52.0 16.0 %collective-permute-start.5 = (bf16[1024,512]{1,0:T(8,128)(2,1)S(1)}, bf16[1024,512]{1,0:T(8,128)(2,1)}, u32[]{:S(2)}, u32[]{:S(2)}) collective-permute-start(bf16[1024,512]{1,0:T(8,128)(2,1)S(1)} %pad_maximum_fusion.own_ref), channel_id=1, source_target_pairs={{0,8},{8,0},{1,9},{9,1},{2,10},{10,2},{3,11},{11,3},{4,12},{12,4},... | collective-permute-start | bytes 3145736 | tf_op jit(solution)/shard_map/ppermute | solution.py:27
  59.9 16.7 %copy-start.2 = (bf16[4,4,64,512]{3,2,1,0:T(8,128)(2,1)}, bf16[4,4,64,512]{3,2,1,0:T(8,128)(2,1)S(1)}, u32[]{:S(2)}) copy-start(bf16[4,4,64,512]{3,2,1,0:T(8,128)(2,1)S(1)} %all-to-all-done.1) | copy-start | bytes 3145732
  59.9 16.7 %collective-permute-start = (bf16[1024,512]{1,0:T(8,128)(2,1)S(1)}, bf16[1024,512]{1,0:T(8,128)(2,1)}, u32[]{:S(2)}, u32[]{:S(2)}) collective-permute-start(bf16[1024,512]{1,0:T(8,128)(2,1)S(1)} %bitcast.78), channel_id=1, source_target_pairs={{0,8},{8,0},{1,9},{9,1},{2,10},{10,2},{3,11},{11,3},{4,12},{12,4},... | collective-permute-start | bytes 3145736 | tf_op jit(solution)/shard_map/ppermute | solution.py:27
  65.6 1.5 collective-permute-start.1
  76.6 27.8 %copy-start.5 = (f32[224,128]{1,0:T(8,128)S(1)}, f32[224,128]{1,0:T(8,128)}, u32[]{:S(2)}) copy-start(f32[224,128]{1,0:T(8,128)} %convolution_add_fusion.1) | copy-start | bytes 344068
  103.7 44.2 %copy-start.16 = (f32[896]{0:T(1024)S(1)}, f32[896]{0:T(1024)}, u32[]{:S(2)}) copy-start(f32[896]{0:T(1024)} %param.22) | copy-start | bytes 10756
  103.7 0.7 collective-permute-start.6
  142.6 7.4 %copy-start.1 = (bf16[4,4,224,128]{3,2,1,0:T(8,128)(2,1)}, bf16[4,4,224,128]{3,2,1,0:T(8,128)(2,1)S(1)}, u32[]{:S(2)}) copy-start(bf16[4,4,224,128]{3,2,1,0:T(8,128)(2,1)S(1)} %all_to_all.52) | copy-start | bytes 2752516
  142.6 7.4 %collective-permute-start.7 = (bf16[2,2,4,224,128]{4,3,2,1,0:T(8,128)(2,1)S(1)}, bf16[2,2,4,224,128]{4,3,2,1,0:T(8,128)(2,1)S(1)}, u32[]{:S(2)}, u32[]{:S(2)}) collective-permute-start(bf16[2,2,4,224,128]{4,3,2,1,0:T(8,128)(2,1)S(1)} %bitcast.74), channel_id=1, source_target_pairs={{0,8},{8,0},{1,9},{9,1},{2,10},{10,2},{3,11},{11,3},{4,12},{12,4},... | collective-permute-start | bytes 2752520 | tf_op jit(solution)/shard_map/ppermute | solution.py:27
  150.0 0.9 copy-start.8
  193.1 23.6 %copy-start.18 = (s32[32]{0:T(128)S(1)}, s32[32]{0:T(128)}, u32[]{:S(2)}) copy-start(s32[32]{0:T(128)} %copy-done.17) | copy-start | bytes 388
  193.1 23.6 %copy-start.13 = (s32[8]{0:T(128)S(1)}, s32[8]{0:T(128)}, u32[]{:S(2)}) copy-start(s32[8]{0:T(128)} %copy-done.12) | copy-start | bytes 100
  193.1 23.6 %copy-start.15 = (s32[32]{0:T(128)S(1)}, s32[32]{0:T(128)}, u32[]{:S(2)}) copy-start(s32[32]{0:T(128)} %counts_ref.1) | copy-start | bytes 388
  193.1 19.2 %all-to-all-start.7 = ((bf16[8,576,128]{2,1,0:T(8,128)(2,1)}), bf16[8,576,128]{2,1,0:T(8,128)(2,1)S(1)}, u32[]{:S(2)}, u32[]{:S(2)}) async-start(bf16[8,576,128]{2,1,0:T(8,128)(2,1)} %broadcast_in_dim.66), calls=%async_computation.7 | async-start | bytes 2359296 | tf_op jit(solution)/shard_map/all_to_all | solution.py:242
  214.2 4.8 %collective-permute-start.8 = (bf16[4,128,896]{2,1,0:T(8,128)(2,1)}, bf16[4,128,896]{2,1,0:T(8,128)(2,1)S(1)}, u32[]{:S(2)}, u32[]{:S(2)}) collective-permute-start(bf16[4,128,896]{2,1,0:T(8,128)(2,1)} %convolution_convert_fusion), channel_id=1, source_target_pairs={{0,8},{8,0},{1,9},{9,1},{2,10},{10,2},{3,11},{11,3},{4,12},{12,4},... | collective-permute-start | bytes 2752520 | tf_op jit(solution)/shard_map/ppermute | solution.py:27
  220.9 16.9 %all-to-all-start.8 = ((bf16[4,128,896]{2,1,0:T(8,128)(2,1)}), bf16[4,128,896]{2,1,0:T(8,128)(2,1)S(1)}, u32[]{:S(2)}, u32[]{:S(2)}) async-start(bf16[4,128,896]{2,1,0:T(8,128)(2,1)} %add_convert_fusion), calls=%async_computation.8 | async-start | bytes 1835008 | tf_op jit(solution)/shard_map/all_to_all | solution.py:242
  239.1 22.0 %all-to-all-start.9 = ((bf16[32,8,896]{2,1,0:T(8,128)(2,1)}), bf16[32,8,896]{2,1,0:T(8,128)(2,1)S(1)}, u32[]{:S(2)}, u32[]{:S(2)}) async-start(bf16[32,8,896]{2,1,0:T(8,128)(2,1)} %fusion.1), calls=%async_computation.9 | async-start | bytes 917504 | tf_op jit(solution)/shard_map/all_to_all | solution.py:242

commit v4 on v3

--- a/solution.py
+++ b/solution.py
@@ -43,16 +43,93 @@
     return pl.CostEstimate(flops=us * 10**9, bytes_accessed=us * 3 * 10**6, transcendentals=0)
 
 
-def score_kernel(counts_ref, qn_ref, qr_ref, lat_ref, kr_ref, ku_ref, req_ref, out_ref, s_ref):
-    slots = lat_ref.shape[0]
-    heads = ku_ref.shape[1] // NOPE
-    place = (lax.axis_index("zh") * 4 + lax.axis_index("y")) * 2 + lax.axis_index("c")
-    before = lax.fori_loop(
+def rank_here():
+    return (lax.axis_index("zh") * 4 + lax.axis_index("y")) * 2 + lax.axis_index("c")
+
+
+def live_before(counts_ref):
+    place = rank_here()
+    return lax.fori_loop(
         0,
         counts_ref.shape[0],
         lambda i, a: a + jnp.where(i < place, counts_ref[i], 0),
         jnp.int32(0),
     )
+
+
+def pack_kernel(counts_ref, lat_ref, res_ref, *refs):
+    outs, rows_ref = refs[:4], refs[4]
+    slots, width = res_ref.shape
+    half, lanes = width // 2, lat_ref.shape[1]
+    zh = lax.axis_index("zh")
+    start = live_before(counts_ref)
+    i_at, slot = iota((slots, slots), 0), iota((slots, slots), 1)
+    roll = ((((i_at >> 3) - start) & 7) + 8 * (i_at & 7)) == slot
+    rows_ref[...] = dot(jnp.where(roll, 1.0, 0.0).astype(BF), res_ref[...])
+    fill = jnp.zeros((16, lanes - half), F32)
+    for s in range(4):
+        outs[s][:slots, :] = lat_ref[...]
+        for high in range(2):
+            m = ((zh + s) & 3) * 2 + high
+            piece = rows_ref[pl.ds(pl.multiple_of(m * 8, 8), 8), :]
+            piece = jnp.concatenate([piece[:, :half], piece[:, half:]], axis=0)
+            piece = jnp.concatenate([piece, fill], axis=1)
+            outs[s][slots + 16 * high : slots + 16 * (high + 1), :] = piece.astype(BF)
+
+
+def pack(counts, latent, residual):
+    slots, lanes = latent.shape
+    shape = (slots + 32, lanes)
+    return pl.pallas_call(
+        pack_kernel,
+        grid=(1,),
+        out_shape=[jax.ShapeDtypeStruct(shape, BF)] * 4,
+        in_specs=[
+            pl.BlockSpec(memory_space=pltpu.SMEM),
+            whole(latent.shape),
+            whole(residual.shape),
+        ],
+        out_specs=[whole(shape)] * 4,
+        scratch_shapes=[pltpu.VMEM(residual.shape, F32)],
+        cost_estimate=cost(2),
+        name="pack",
+    )(counts, latent, residual)
+
+
+def repack_kernel(*refs):
+    ins, outs, rows_ref = refs[:4], refs[4:8], refs[8]
+    slots = ins[0].shape[0] - 32
+    y = lax.axis_index("y")
+    for t in range(4):
+        rows_ref[t] = ins[t][slots:, :].astype(F32)
+    for s in range(4):
+        at = pl.ds(pl.multiple_of(((y + s) & 3) * 8, 8), 8)
+        for t in range(4):
+            outs[s][t * slots : (t + 1) * slots, :] = ins[t][:slots, :]
+        for t in (0, 2):
+            pair = jnp.concatenate([rows_ref[t, at, :], rows_ref[t + 1, at, :]], axis=0)
+            outs[s][4 * slots + 8 * t : 4 * slots + 8 * t + 16, :] = pair.astype(BF)
+
+
+def repack(*pieces):
+    rows, lanes = pieces[0].shape
+    shape = (4 * (rows - 32) + 32, lanes)
+    return pl.pallas_call(
+        repack_kernel,
+        grid=(1,),
+        out_shape=[jax.ShapeDtypeStruct(shape, BF)] * 4,
+        in_specs=[whole(pieces[0].shape)] * 4,
+        out_specs=[whole(shape)] * 4,
+        scratch_shapes=[pltpu.VMEM((4, 32, lanes), F32)],
+        cost_estimate=cost(2),
+        name="repack",
+    )(*pieces)
+
+
+def score_kernel(counts_ref, qn_ref, qr_ref, lat_ref, kr_ref, ku_ref, req_ref, out_ref, s_ref):
+    slots = lat_ref.shape[0]
+    heads = ku_ref.shape[1] // NOPE
+    before = live_before(counts_ref)
     keys = dot(lat_ref[...], ku_ref[...]).astype(BF)
     key_rope = kr_ref[...]
     s_at, t_at = iota((slots, slots), 0), iota((slots, slots), 1)
@@ -194,17 +271,18 @@
     )(goes, own, other, values, values, wo)
 
 
-def gate_up_kernel(own_ref, other_ref, gain_ref, gate_ref, up_ref, out_ref, x_ref):
+def gate_up_kernel(own_ref, other_ref, gain_ref, gate_ref, up_ref, out_ref, x_ref, gain_at):
     core = lax.axis_index("c")
     _, lows, blocks, k, chunk = own_ref.shape
     ff = gate_ref.shape[0]
     squares = jnp.zeros((1, blocks * chunk), F32)
+    gain_at[...] = jnp.broadcast_to(gain_ref[...], (8, gain_ref.shape[1])).T
     for ref, flip in ((own_ref, core), (other_ref, 1 - core)):
         for low in range(lows):
             rows = pl.ds(pl.multiple_of((low * 2 + flip) * k, 32), k)
             x = jnp.concatenate([ref[0, low, i] for i in range(blocks)], axis=1).astype(F32)
             squares = squares + jnp.sum(x * x, axis=0, keepdims=True)
-            x_ref[rows, :] = (x * gain_ref[rows, :]).astype(BF)
+            x_ref[rows, :] = (x * gain_at[rows, :1]).astype(BF)
     x = x_ref[...]
     gate = dot(gate_ref[...], x).astype(BF)
     up = dot(up_ref[...], x).astype(BF)
@@ -230,9 +308,9 @@
         gate_up_kernel,
         grid=(highs * planes // blocks,),
         out_shape=jax.ShapeDtypeStruct((highs * planes, 2 * ff + 16, chunk), BF),
-        in_specs=[spec, spec, whole((width, 1)), whole((ff, width)), whole((ff, width))],
+        in_specs=[spec, spec, whole((1, width)), whole((ff, width)), whole((ff, width))],
         out_specs=pl.BlockSpec((blocks, 2 * ff + 16, chunk), lambda b: (b, 0, 0)),
-        scratch_shapes=[pltpu.VMEM((width, blocks * chunk), BF)],
+        scratch_shapes=[pltpu.VMEM((width, blocks * chunk), BF), pltpu.VMEM((width, 8), F32)],
         cost_estimate=cost(6),
         name="gate_up",
     )(own, other, gain, gate_weight, up_weight)
@@ -270,7 +348,6 @@
     slots = latent.shape[0]
     ranks = rank_tokens.shape[0]
     zh, y, c = (lax.axis_index(a) for a in DP)
-    x_at, zl = (lax.axis_index(a) for a in HD)
     rank = (zh * 4 + y) * 2 + c
     chunk = LIVE // 8
     width = residual.shape[1]
@@ -288,76 +365,72 @@
     own_start, own_length = starts(rank), lengths(rank)
     slot = jnp.arange(slots, dtype=jnp.int32)
 
-    share = slots // 4
-    half = width // 2
-    eight = jnp.arange(8, dtype=jnp.int32)
-    spread = ((eight[:, None] - own_start) & 7) + 8 * eight[None, :]
-    roll = (spread.reshape(slots, 1) == slot[None, :]).astype(BF)
-    rows = dot(roll, residual).astype(BF).reshape(2, 4, 8, width)
-    pad = ((0, 0),) * 3 + ((0, latent.shape[1] - half),)
-    rows = jnp.stack([jnp.pad(rows[..., :half], pad), jnp.pad(rows[..., half:], pad)], axis=1)
-    rows = rows.transpose(2, 0, 1, 3, 4).reshape(16, 8, latent.shape[1])
-    latents = lax.dynamic_slice_in_dim(latent, x_at * share, share, 0)
-    latents = jnp.broadcast_to(latents[None], (16,) + latents.shape)
-    got = exchange(jnp.concatenate([latents, rows], axis=1), ("zh", "y"))
+    pieces = pack(rank_tokens, latent, residual)
+    pieces = [pieces[0]] + [shifted(pieces[s], "zh", s) for s in (1, 2, 3)]
 
     weights = score_weights(
         rank_tokens, query_nope, query_rope, latent, key_rope, key_up, request_ids
     )
-    weights = gather(gather(weights, "zh"), "y").reshape(-1, weights.shape[1])
-    weights_other = shifted(weights, "c", 1)
-
-    latents = got[:, :share].reshape(-1, latent.shape[1])
-    latents = jnp.concatenate([latents] + [shifted(latents, "x", s) for s in (1, 2, 3)], axis=0)
-    latents_other = shifted(latents, "c", 1)
-
-    def by_core(a):
-        a = a.reshape(4, 4, 2)
-        return jnp.where(c == 0, jnp.stack([a[..., 0], a[..., 1]]), jnp.stack([a[..., 1], a[..., 0]]))
-
-    first, count = by_core(starts(every)), by_core(rank_tokens)
-    goes = jnp.swapaxes(first, 1, 2)[..., None] + slot
-    goes = jnp.where(slot < jnp.swapaxes(count, 1, 2)[..., None], goes, -1).reshape(2, 1, -1)
-    block = (x_at - jnp.arange(4, dtype=jnp.int32)) & 3
-    own_slot = (block[:, None] * share + jnp.arange(share, dtype=jnp.int32)).reshape(1, 4, 1, 1, share)
-    goes_latent = first[:, None, :, :, None] + own_slot
-    goes_latent = jnp.where(own_slot < count[:, None, :, :, None], goes_latent, -1).reshape(2, 1, -1)
-    values = live_values(goes_latent, latents, latents_other, value_up)
-
-    mine = (y >> 1) * 4 + zh
-    place = ((mine - first[..., None]) & 7) + 8 * eight
-    come = jnp.where(place < count[..., None], (first[..., None] + place) >> 3, -1)
+    weights = gather(weights, "zh")
+    pieces = repack(*pieces)
+    pieces = [pieces[0]] + [shifted(pieces[s], "y", s) for s in (1, 2, 3)]
+    got = jnp.concatenate(pieces, axis=0)
+    got_other = shifted(got, "c", 1)
+    weights = gather(weights, "y").reshape(-1, weights.shape[2])
+
+    four = jnp.arange(4, dtype=jnp.int32)
+    eight = jnp.arange(8, dtype=jnp.int32)
+    core = jnp.stack([c, 1 - c])[:, None, None]
+    ahead = (four[None, None, :] * 4 + four[None, :, None]) * 2 + core
+    goes = jnp.where(slot < lengths(ahead)[..., None], starts(ahead)[..., None] + slot, -1)
+    goes = goes.reshape(2, 1, -1)
+    back = (((zh - four) & 3)[None, None, :] * 4 + ((y - four) & 3)[None, :, None]) * 2 + core
+    back_start, back_count = starts(back)[..., None], lengths(back)[..., None]
+    goes_back = jnp.where(slot < back_count, back_start + slot, -1).reshape(2, 4, -1)
+    goes_back = jnp.pad(goes_back, ((0, 0), (0, 0), (0, 32)), constant_values=-1).reshape(2, 1, -1)
+    values = live_values(goes_back, got, got_other, value_up)
+
+    swap = []
+    for a in range(4):
+        for b in range(8):
+            for e in range(4):
+                for f in range(2):
+                    to = (e * 8 + (f * 4 + (b & 3))) * 8 + a * 2 + (b >> 2)
+                    swap.append(((a * 8 + b) * 8 + e * 2 + f, to))
+    place = (((zh * 2 + (y >> 1)) - back_start) & 7) + 8 * eight
+    come = jnp.where(place < back_count, (back_start + place) >> 3, -1)
     come = (come.reshape(2, -1, 1) == jnp.arange(chunk, dtype=jnp.int32)).astype(BF)
-    rows = got[:, share:].reshape(-1, latent.shape[1])
-    left, right = rows[:, :quarter], rows[:, quarter:half]
-    kept = jnp.where(c == 0, left, right)
-    rows = shifted(jnp.where(c == 0, right, left), "c", 1)
 
     def tn(a, b):
         return lax.dot_general(a, b, (((0,), (0,)), ((), ())), preferred_element_type=F32)
 
-    rows = tn(kept, come[0]) + tn(rows, come[1])
-
-    weights_other, rows = lax.optimization_barrier((weights_other, rows))
+    rows = [a.reshape(4, -1, a.shape[1])[:, 4 * slots :].reshape(-1, a.shape[1]) for a in (got, got_other)]
+    rows = tn(rows[0], come[0]) + tn(rows[1], come[1])
+    rows = jnp.where(c == 0, rows[:quarter], rows[quarter : 2 * quarter]).astype(BF)
+    rows = lax.ppermute(rows, DP + HD, swap)
+
+    weights, values, rows = lax.optimization_barrier((weights, values, rows))
+    weights_other = shifted(weights, "c", 1)
     part = mix_project(goes, weights, weights_other, values, output_weight.T)
-    projected = jnp.sum(exchange(part, HD).astype(F32), axis=0).astype(BF)
-    sends = []
-    for a in range(4):
-        for b in range(4):
-            for e in range(2):
-                for f in range(4):
-                    for g in range(2):
-                        m = f * 2 + g
-                        to = ((m & 3) * 4 + (m >> 2) * 2 + (b & 1)) * 2 + e
-                        h = a * 2 + (b >> 1)
-                        sends.append((((a * 4 + b) * 2 + e) * 8 + m, to * 8 + h))
-    projected = lax.ppermute(projected, DP + HD, sends)
-    mixed = (rows + projected.astype(F32)).astype(BF)
-
-    full = gather(gather(mixed, "zh"), "y").reshape(2, 2, 4, quarter, chunk)
+    projected = jnp.sum(exchange(part, HD).astype(F32), axis=0)
+    mixed = (rows.astype(F32) + projected).astype(BF)
+
+    full = []
+    for k in range(4):
+        sends = []
+        for a in range(4):
+            for b in range(8):
+                for e in range(4):
+                    for f in range(2):
+                        to = (((e + k) & 3) * 8 + (f * 4 + (b & 3))) * 8 + a * 2 + (b >> 2)
+                        sends.append(((a * 8 + b) * 8 + e * 2 + f, to))
+        full.append(lax.ppermute(mixed, DP + HD, sends))
+    full = jnp.stack(full)
+
+    full = gather(full, "y").reshape(2, 2, 4, quarter, chunk)
     full_other = shifted(full, "c", 1)
     ff = down_weight.shape[0]
-    part = gate_up(full, full_other, norm_gain[:, None], gate_weight.T, up_weight.T)
+    part = gate_up(full, full_other, norm_gain[None, :], gate_weight.T, up_weight.T)
     total = jnp.sum(exchange(part, HD).astype(F32), axis=0)
     scale = lax.rsqrt((total[2 * ff : 2 * ff + 1] + total[2 * ff + 1 : 2 * ff + 2]) / model + 1e-06)
     hidden = (jax.nn.silu(total[:ff] * scale) * (total[ff : 2 * ff] * scale)).astype(BF)
@@ -372,24 +445,27 @@
     sent = shifted(down(1 - c).astype(BF), "c", 1)
     total = (down(c) + sent.astype(F32)).astype(BF)
     total = jnp.sum(exchange(total, "y").astype(F32), axis=0)
-    m = y * 2 + c
+    spot = y * 2 + c
     begin = starts(every)
+    m = ((zh - (spot & 3)) & 3) * 2 + (spot >> 2)
     place = ((m - begin[:, None]) & 7) + 8 * eight[None, :]
     comes = jnp.where(place < rank_tokens[:, None], (begin[:, None] + place) >> 3, -1)
     expand = (comes.reshape(ranks * 8, 1) == jnp.arange(chunk, dtype=jnp.int32)).astype(BF)
-    pair = [pick(a.reshape(2, 2, 4, quarter, chunk), m >> 2) for a in (full, full_other)]
-    pair = [lax.dynamic_index_in_dim(a, m & 3, 1, keepdims=False) for a in pair]
+    pair = [pick(a.reshape(2, 2, 4, quarter, chunk), spot >> 2) for a in (full, full_other)]
+    pair = [lax.dynamic_index_in_dim(a, spot & 3, 1, keepdims=False) for a in pair]
     low = jnp.where(c == 0, pair[0], pair[1])
     high = jnp.where(c == 0, pair[1], pair[0])
     own = jnp.stack([low, high], axis=1).reshape(width, chunk)
     here = (jnp.arange(ranks * 8, dtype=jnp.int32) >> 6) == zh
     own = nt(jnp.where(here[:, None], expand, jnp.zeros_like(expand)), own)
     result = (dot(expand, total.astype(BF)) + own).astype(BF).reshape(ranks, 8, width)
-    result = jnp.sum(exchange(result, DP).reshape(4, slots, width).astype(F32), axis=0).astype(BF)
-    at = ((own_start + slot) & 7) * 8 + (slot >> 3)
-    at = jnp.where(slot < own_length, at, -1)
-    back = (at[:, None] == slot[None, :]).astype(BF)
-    return dot(back, result).astype(BF)
+    result = exchange(result, DP).reshape(ranks * 8, width)
+    source = jnp.arange(ranks, dtype=jnp.int32)
+    chunk_of = (((source >> 3) - (source & 3)) & 3) * 2 + ((source >> 2) & 1)
+    fits = chunk_of[None, :, None] == ((own_start + slot) & 7)[:, None, None]
+    fits = fits & (eight[None, None, :] == (slot >> 3)[:, None, None])
+    fits = fits & (slot < own_length)[:, None, None]
+    return dot(fits.astype(BF).reshape(slots, ranks * 8), result).astype(BF)
 
 
 def solution(mesh):

time: 263 us -> 257 us (0.977)
  blocking collectives: 84.9 us -> 71.2 us
  waiting for transfers between devices: 55.7 us -> 62 us
  starting transfers between devices: 53.9 us -> 59.5 us
  Pallas kernels: 33 us -> 38.5 us
  other arithmetic: 11.3 us -> 6.63 us
  matrix products: 9.35 us -> 6.59 us
    all_to_all x4 -> x3, blocking collectives: 84.9 us -> 71.2 us  [exchange(): return lax.all_to_all(x, axes, split_axis=0, concat_axis=0, tiled=True)]
    ppermute x1 -> x5, starting transfers between devices: 0.66 us -> 12.5 us  [the longest x4 11.8 us: on_device(): full.append(lax.ppermute(mixed, DP + HD, sends))]
    ppermute x8 -> x10, waiting for transfers between devices: 3.26 us -> 15.1 us  [shifted(): return lax.ppermute(x, axis, [(i, (i + shift) % n) for i in range(n)])]
    all_to_all x6 -> x5, starting transfers between devices: 32 us -> 20.8 us  [exchange(): return lax.all_to_all(x, axes, split_axis=0, concat_axis=0, tiled=True)]
    all_to_all x6 -> x5, waiting for transfers between devices: 52.4 us -> 45.1 us  [exchange(): return lax.all_to_all(x, axes, split_axis=0, concat_axis=0, tiled=True)]
    ppermute x8 -> x10, starting transfers between devices: 21.2 us -> 26.3 us  [shifted(): return lax.ppermute(x, axis, [(i, (i + shift) % n) for i in range(n)])]
    pallas_call x0 -> x2, Pallas kernels: none -> 4.35 us  [the longest x1 2.22 us: pack(): pl.pallas_call(pack_kernel, grid=(1,), out_shape=[jax.ShapeDtypeStruct(sh...]
    select_n x5 -> x3, other arithmetic: 3.41 us -> 0.63 us  [the longest x1 0.62 us: on_device(): jnp.where(slot < lengths(ahead)[..., None], starts(ahead)[..., None] + sl...]
  transfers between devices with their start and end apart: 15 -> 20, of which waited for: 7 -> 11; matrix products, arithmetic and copies ran while one was open for 6% -> 6% of each run, Pallas kernels for 5% -> 6%
where the time goes in v4:
time: 257 us; the launch traced here: 256 us
  blocking collectives  71.2 us (28%)
  waiting for transfers between devices  62 us (24%)
  starting transfers between devices  59.5 us (23%)
  Pallas kernels  38.5 us (15%)
  local copies, waits for them, and re-layouts  11.4 us (4%)
  other arithmetic  6.63 us (3%)
  matrix products  6.59 us (3%)
    all_to_all x3, blocking collectives, exchange(): return lax.all_to_all(x, axes, split_axis=0, concat_axis=0, tiled=True)  71.2 us
    all_to_all x5, waiting for transfers between devices, exchange(): return lax.all_to_all(x, axes, split_axis=0, concat_axis=0, tiled=True)  45.1 us
    ppermute x10, starting transfers between devices, shifted(): return lax.ppermute(x, axis, [(i, (i + shift) % n) for i in range(n)])  26.3 us
    all_to_all x5, starting transfers between devices, exchange(): return lax.all_to_all(x, axes, split_axis=0, concat_axis=0, tiled=True)  20.8 us
    ppermute x10, waiting for transfers between devices, shifted(): return lax.ppermute(x, axis, [(i, (i + shift) % n) for i in range(n)])  15.1 us
    pallas_call x1, Pallas kernels, mix_project(): pl.pallas_call(mix_kernel, grid=(LIVE // STEP,), out_shape=jax.ShapeDtype...  13.6 us
    ppermute x4, starting transfers between devices, on_device(): full.append(lax.ppermute(mixed, DP + HD, sends))  11.8 us
    pallas_call x1, Pallas kernels, live_values(): pl.pallas_call(values_kernel, grid=(LIVE // STEP,), out_shape=jax.ShapeDt...  9.27 us
  transfers between devices with their start and end apart: 20, of which 11 were waited for; matrix products, arithmetic and copies ran while one was open for 6% of the time, Pallas kernels for 6%

profile of v4, /device:TPU:1, one launch (start us, length us, event | category | flops | bytes accessed | tf_op | source)
XLA Modules:
  0.0 256.2 jit_solution(16716102472835111339)
XLA Ops:
  0.0 2.2 pack.1
  2.2 3.8 %collective-permute-start = (bf16[96,512]{1,0:T(8,128)(2,1)}, bf16[96,512]{1,0:T(8,128)(2,1)S(1)}, u32[]{:S(2)}, u32[]{:S(2)}) collective-permute-start(bf16[96,512]{1,0:T(8,128)(2,1)} %get-tuple-element.17), channel_id=1, source_target_pairs={{0,64},{64,128},{128,192},{192,0},{1,65},{65,129},{129,193},{193,1... | collective-permute-start | bytes 294920 | tf_op jit(solution)/shard_map/ppermute | solution.py:27
  6.0 5.1 %collective-permute-start.1 = (bf16[96,512]{1,0:T(8,128)(2,1)}, bf16[96,512]{1,0:T(8,128)(2,1)S(1)}, u32[]{:S(2)}, u32[]{:S(2)}) collective-permute-start(bf16[96,512]{1,0:T(8,128)(2,1)} %get-tuple-element.18), channel_id=1, source_target_pairs={{0,128},{64,192},{128,0},{192,64},{1,129},{65,193},{129,1},{193,65... | collective-permute-start | bytes 294920 | tf_op jit(solution)/shard_map/ppermute | solution.py:27
  11.2 2.4 collective-permute-start.2
  13.5 3.7 %score_weights.1 = bf16[64,512]{1,0:T(8,128)(2,1)} custom-call(s32[32]{0:T(128)} %counts_ref.3, bf16[64,2048]{1,0:T(8,128)(2,1)} %qn_ref.1, bf16[64,1024]{1,0:T(8,128)(2,1)} %qr_ref.1, bf16[64,512]{1,0:T(8,128)(2,1)} %lat_ref.3, bf16[64,64]{1,0:T(8,128)(2,1)} %kr_ref.1, bf16[512,2048]{1,0:T(8,128)(2,1)} %ku_ref.1, s32[1,64]{1,0:T(1,128)} %req_ref.1), custom_call_target="tpu_custom_call" | custom-call | flops 4000000000 | bytes 12000000 | tf_op jit(solution)/shard_map/score_weights/pallas_call | solution.py:162
  17.3 1.6 broadcast_in_dim.62
  18.8 3.4 %all-to-all-start = ((bf16[4,64,512]{2,1,0:T(8,128)(2,1)}), bf16[4,64,512]{2,1,0:T(8,128)(2,1)S(1)}, u32[]{:S(2)}, u32[]{:S(2)}) async-start(bf16[4,64,512]{2,1,0:T(8,128)(2,1)} %broadcast_in_dim.62), calls=%async_computation | async-start | bytes 524288 | tf_op jit(solution)/shard_map/all_to_all | solution.py:320
  22.4 0.6 copy-done.8
  23.1 2.1 repack.1
  25.2 1.3 collective-permute-start.3
  26.5 2.6 %collective-permute-start.4 = (bf16[288,512]{1,0:T(8,128)(2,1)}, bf16[288,512]{1,0:T(8,128)(2,1)S(1)}, u32[]{:S(2)}, u32[]{:S(2)}) collective-permute-start(bf16[288,512]{1,0:T(8,128)(2,1)} %get-tuple-element.22), channel_id=1, source_target_pairs={{0,32},{16,48},{32,0},{48,16},{1,33},{17,49},{33,1},{49,17},{2,34}... | collective-permute-start | bytes 884744 | tf_op jit(solution)/shard_map/ppermute | solution.py:27
  29.2 1.1 collective-permute-start.5
  30.3 1.0 constant_dynamic-update-slice_fusion.3
  31.3 2.5 collective-permute-done.3
  33.7 7.4 %collective-permute-done.4 = bf16[288,512]{1,0:T(8,128)(2,1)S(1)} collective-permute-done((bf16[288,512]{1,0:T(8,128)(2,1)}, bf16[288,512]{1,0:T(8,128)(2,1)S(1)}, u32[]{:S(2)}, u32[]{:S(2)}) %collective-permute-start.4) | collective-permute-done | bytes 294944 | tf_op jit(solution)/shard_map/ppermute | solution.py:27
  41.2 0.4 collective-permute-done.5
  41.6 2.1 collective-permute-start.6
  43.8 0.7 select_reduce_fusion.3
  45.6 0.7 reshape.417.goes_ref
  46.5 1.1 broadcast_in_dim.63
  47.5 3.5 %all-to-all-start.1 = ((bf16[4,4,64,512]{3,2,1,0:T(8,128)(2,1)}), bf16[4,4,64,512]{3,2,1,0:T(8,128)(2,1)S(1)}, u32[]{:S(2)}, u32[]{:S(2)}) async-start(bf16[4,4,64,512]{3,2,1,0:T(8,128)(2,1)} %broadcast_in_dim.63), calls=%async_computation.1 | async-start | bytes 2097152 | tf_op jit(solution)/shard_map/all_to_all | solution.py:320
  51.1 0.9 slice.42
  52.2 0.2 convolution_add_fusion.1
  52.5 0.7 collective-permute-start.7
  53.1 9.3 %live_values.1.prev_ref.cur_ref = bf16[1024,2048]{1,0:T(8,128)(2,1)} custom-call(s32[2,1,1152]{2,1,0:T(1,128)} %reshape.417.goes_ref, bf16[1152,512]{1,0:T(8,128)(2,1)} %copy-done.3, bf16[1152,512]{1,0:T(8,128)(2,1)} %collective-permute-done.6.other_ref, bf16[512,2048]{1,0:T(8,128)(2,1)} %up_ref.1), custom_call_target="tpu_custom_call" | custom-call | flops 6000000000 | bytes 18000000 | tf_op jit(solution)/shard_map/live_values/pallas_call | solution.py:187
  62.4 3.6 %all-to-all-done.1 = bf16[4,4,64,512]{3,2,1,0:T(8,128)(2,1)S(1)} async-done(((bf16[4,4,64,512]{3,2,1,0:T(8,128)(2,1)}), bf16[4,4,64,512]{3,2,1,0:T(8,128)(2,1)S(1)}, u32[]{:S(2)}, u32[]{:S(2)}) %all-to-all-start.1) | async-done | bytes 1048608 | tf_op jit(solution)/shard_map/all_to_all | solution.py:320
  66.0 1.1 collective-permute-start.8
  67.5 0.6 compare_select_fusion.goes_ref
  68.2 1.3 collective-permute-done.8.other_ref
  69.4 1.0 copy-done.7
  70.4 13.6 %mix_project.1 = bf16[8,224,128]{2,1,0:T(8,128)(2,1)} custom-call(s32[2,1,1024]{2,1,0:T(1,128)} %compare_select_fusion.goes_ref, bf16[1024,512]{1,0:T(8,128)(2,1)} %bitcast.71, bf16[1024,512]{1,0:T(8,128)(2,1)} %copy-done.7, bf16[1024,2048]{1,0:T(8,128)(2,1)} %live_values.1.prev_ref.cur_ref, bf16[1024,2048]{1,0:T(8,128)(2,1)} %live_values.1.prev_ref.cur_ref, ...), custom_call_target="tpu_custom_call" | custom-call | flops 8999999488 | bytes 27000000 | tf_op jit(solution)/shard_map/mix_project/pallas_call | solution.py:255
  84.0 18.3 %all_to_all.40 = bf16[8,224,128]{2,1,0:T(8,128)(2,1)S(1)} all-to-all(bf16[8,224,128]{2,1,0:T(8,128)(2,1)} %mix_project.1), channel_id=1, replica_groups=mesh['zh'=4,'y'=4,'c'=2,'x'=4,'zl'=2] {'x','zl'}, dimensions={0} | all-to-all | bytes 917504 | tf_op jit(solution)/shard_map/all_to_all | solution.py:320
  102.4 0.7 collective-permute-start.9
  103.0 3.3 %collective-permute-start.10 = (bf16[224,128]{1,0:T(8,128)(2,1)S(1)}, bf16[224,128]{1,0:T(8,128)(2,1)S(1)}, u32[]{:S(2)}, u32[]{:S(2)}) collective-permute-start(bf16[224,128]{1,0:T(8,128)(2,1)S(1)} %add_convert_fusion.1), channel_id=1, source_target_pairs={{0,64},{1,96},{2,128},{3,160},{4,192},{5,224},{6,0},{7,32},{8,72},... | collective-permute-start | bytes 172040 | tf_op jit(solution)/shard_map/ppermute | solution.py:427
  106.3 4.3 %collective-permute-start.11 = (bf16[224,128]{1,0:T(8,128)(2,1)S(1)}, bf16[224,128]{1,0:T(8,128)(2,1)S(1)}, u32[]{:S(2)}, u32[]{:S(2)}) collective-permute-start(bf16[224,128]{1,0:T(8,128)(2,1)S(1)} %add_convert_fusion.1), channel_id=1, source_target_pairs={{0,128},{1,160},{2,192},{3,224},{4,0},{5,32},{6,64},{7,96},{8,136}... | collective-permute-start | bytes 172040 | tf_op jit(solution)/shard_map/ppermute | solution.py:427
  110.6 3.6 %collective-permute-start.12 = (bf16[224,128]{1,0:T(8,128)(2,1)S(1)}, bf16[224,128]{1,0:T(8,128)(2,1)S(1)}, u32[]{:S(2)}, u32[]{:S(2)}) collective-permute-start(bf16[224,128]{1,0:T(8,128)(2,1)S(1)} %add_convert_fusion.1), channel_id=1, source_target_pairs={{0,192},{1,224},{2,0},{3,32},{4,64},{5,96},{6,128},{7,160},{8,200}... | collective-permute-start | bytes 172040 | tf_op jit(solution)/shard_map/ppermute | solution.py:427
  114.2 1.8 collective-permute-done.12
  116.2 19.6 %all_to_all.41 = bf16[4,4,224,128]{3,2,1,0:T(8,128)(2,1)S(1)} all-to-all(bf16[4,4,224,128]{3,2,1,0:T(8,128)(2,1)S(1)} %broadcast_in_dim.73), channel_id=1, replica_groups=mesh['zh'=4,'y'=4,'c'=2,'x'=4,'zl'=2] {'y'}, dimensions={0} | all-to-all | bytes 1835008 | tf_op jit(solution)/shard_map/all_to_all | solution.py:320
  135.8 4.1 %collective-permute-start.13 = (bf16[2,2,4,224,128]{4,3,2,1,0:T(8,128)(2,1)S(1)}, bf16[2,2,4,224,128]{4,3,2,1,0:T(8,128)(2,1)S(1)}, u32[]{:S(2)}, u32[]{:S(2)}) collective-permute-start(bf16[2,2,4,224,128]{4,3,2,1,0:T(8,128)(2,1)S(1)} %bitcast.66), channel_id=1, source_target_pairs={{0,8},{8,0},{1,9},{9,1},{2,10},{10,2},{3,11},{11,3},{4,12},{12,4},... | collective-permute-start | bytes 2752520 | tf_op jit(solution)/shard_map/ppermute | solution.py:27
  139.9 0.6 broadcast_in_dim.74.gain_ref
  140.5 1.5 collective-permute-done.13.other_ref
  142.0 0.9 copy-done.4
  142.9 7.6 %gate_up.1 = bf16[8,1168,128]{2,1,0:T(8,128)(2,1)} custom-call(bf16[2,2,4,224,128]{4,3,2,1,0:T(8,128)(2,1)} %bitcast.67, bf16[2,2,4,224,128]{4,3,2,1,0:T(8,128)(2,1)} %copy-done.4, f32[1,896]{1,0:T(1,128)} %broadcast_in_dim.74.gain_ref, bf16[576,896]{1,0:T(8,128)(2,1)} %bitcast.80, bf16[576,896]{1,0:T(8,128)(2,1)} %bitcast.81), custom_call_target="tpu_custom_call" | custom-call | flops 6000000000 | bytes 18000000 | tf_op jit(solution)/shard_map/gate_up/pallas_call | solution.py:307
  150.5 33.3 %all_to_all.42 = bf16[8,1168,128]{2,1,0:T(8,128)(2,1)S(1)} all-to-all(bf16[8,1168,128]{2,1,0:T(8,128)(2,1)} %gate_up.1), channel_id=1, replica_groups=mesh['zh'=4,'y'=4,'c'=2,'x'=4,'zl'=2] {'x','zl'}, dimensions={0} | all-to-all | bytes 4784128 | tf_op jit(solution)/shard_map/all_to_all | solution.py:320
  183.8 0.3 convert_reduce_fusion
  184.3 1.2 broadcast_in_dim.75
  185.4 3.6 %all-to-all-start.5 = ((bf16[8,576,128]{2,1,0:T(8,128)(2,1)}), bf16[8,576,128]{2,1,0:T(8,128)(2,1)S(1)}, u32[]{:S(2)}, u32[]{:S(2)}) async-start(bf16[8,576,128]{2,1,0:T(8,128)(2,1)} %broadcast_in_dim.75), calls=%async_computation.5 | async-start | bytes 2359296 | tf_op jit(solution)/shard_map/all_to_all | solution.py:320
  189.0 15.3 %all-to-all-done.5 = bf16[8,576,128]{2,1,0:T(8,128)(2,1)S(1)} async-done(((bf16[8,576,128]{2,1,0:T(8,128)(2,1)}), bf16[8,576,128]{2,1,0:T(8,128)(2,1)S(1)}, u32[]{:S(2)}, u32[]{:S(2)}) %all-to-all-start.5) | async-done | bytes 1179680 | tf_op jit(solution)/shard_map/all_to_all | solution.py:320
  204.3 1.9 convolution_convert_fusion
  206.2 2.7 %collective-permute-start.14 = (bf16[4,128,896]{2,1,0:T(8,128)(2,1)}, bf16[4,128,896]{2,1,0:T(8,128)(2,1)S(1)}, u32[]{:S(2)}, u32[]{:S(2)}) collective-permute-start(bf16[4,128,896]{2,1,0:T(8,128)(2,1)} %convolution_convert_fusion), channel_id=1, source_target_pairs={{0,8},{8,0},{1,9},{9,1},{2,10},{10,2},{3,11},{11,3},{4,12},{12,4},... | collective-permute-start | bytes 2752520 | tf_op jit(solution)/shard_map/ppermute | solution.py:27
  209.2 2.0 collective-permute-done.14
  211.2 1.9 add_convert_fusion
  213.1 3.5 %all-to-all-start.6 = ((bf16[4,128,896]{2,1,0:T(8,128)(2,1)}), bf16[4,128,896]{2,1,0:T(8,128)(2,1)S(1)}, u32[]{:S(2)}, u32[]{:S(2)}) async-start(bf16[4,128,896]{2,1,0:T(8,128)(2,1)} %add_convert_fusion), calls=%async_computation.6 | async-start | bytes 1835008 | tf_op jit(solution)/shard_map/all_to_all | solution.py:320
  216.7 1.0 fusion.20
  217.6 1.0 fusion.18
  218.7 0.3 fusion.22
  219.0 11.0 %all-to-all-done.6 = bf16[4,128,896]{2,1,0:T(8,128)(2,1)S(1)} async-done(((bf16[4,128,896]{2,1,0:T(8,128)(2,1)}), bf16[4,128,896]{2,1,0:T(8,128)(2,1)S(1)}, u32[]{:S(2)}, u32[]{:S(2)}) %all-to-all-start.6) | async-done | bytes 917536 | tf_op jit(solution)/shard_map/all_to_all | solution.py:320
  230.2 1.1 fusion.1
  231.3 6.8 %all-to-all-start.7 = ((bf16[32,8,896]{2,1,0:T(8,128)(2,1)}), bf16[32,8,896]{2,1,0:T(8,128)(2,1)S(1)}, u32[]{:S(2)}, u32[]{:S(2)}) async-start(bf16[32,8,896]{2,1,0:T(8,128)(2,1)} %fusion.1), calls=%async_computation.7 | async-start | bytes 917504 | tf_op jit(solution)/shard_map/all_to_all | solution.py:320
  238.1 0.7 fusion.41
  238.8 0.6 add_and_fusion
  239.4 0.6 iota_compare_fusion.9
  240.2 15.2 %all-to-all-done.7 = bf16[32,8,896]{2,1,0:T(8,128)(2,1)S(1)} async-done(((bf16[32,8,896]{2,1,0:T(8,128)(2,1)}), bf16[32,8,896]{2,1,0:T(8,128)(2,1)S(1)}, u32[]{:S(2)}, u32[]{:S(2)}) %all-to-all-start.7) | async-done | bytes 458784 | tf_op jit(solution)/shard_map/all_to_all | solution.py:320
  255.3 0.9 fusion.2
  (84 shorter events, 3.1 us)
Async XLA Ops:
  0.0 204.3 %copy-start = (bf16[576,896]{1,0:T(8,128)(2,1)S(1)}, bf16[576,896]{1,0:T(8,128)(2,1)}, u32[]{:S(2)}) copy-start(bf16[576,896]{1,0:T(8,128)(2,1)} %param.25) | copy-start | bytes 3096580
  2.2 20.1 %collective-permute-start = (bf16[96,512]{1,0:T(8,128)(2,1)}, bf16[96,512]{1,0:T(8,128)(2,1)S(1)}, u32[]{:S(2)}, u32[]{:S(2)}) collective-permute-start(bf16[96,512]{1,0:T(8,128)(2,1)} %get-tuple-element.17), channel_id=1, source_target_pairs={{0,64},{64,128},{128,192},{192,0},{1,65},{65,129},{129,193},{193,1... | collective-permute-start | bytes 294920 | tf_op jit(solution)/shard_map/ppermute | solution.py:27
  6.0 16.3 %collective-permute-start.1 = (bf16[96,512]{1,0:T(8,128)(2,1)}, bf16[96,512]{1,0:T(8,128)(2,1)S(1)}, u32[]{:S(2)}, u32[]{:S(2)}) collective-permute-start(bf16[96,512]{1,0:T(8,128)(2,1)} %get-tuple-element.18), channel_id=1, source_target_pairs={{0,128},{64,192},{128,0},{192,64},{1,129},{65,193},{129,1},{193,65... | collective-permute-start | bytes 294920 | tf_op jit(solution)/shard_map/ppermute | solution.py:27
  11.2 11.2 %collective-permute-start.2 = (bf16[96,512]{1,0:T(8,128)(2,1)}, bf16[96,512]{1,0:T(8,128)(2,1)S(1)}, u32[]{:S(2)}, u32[]{:S(2)}) collective-permute-start(bf16[96,512]{1,0:T(8,128)(2,1)} %get-tuple-element.19), channel_id=1, source_target_pairs={{0,192},{64,0},{128,64},{192,128},{1,193},{65,1},{129,65},{193,129... | collective-permute-start | bytes 294920 | tf_op jit(solution)/shard_map/ppermute | solution.py:27
  18.8 27.6 %all-to-all-start = ((bf16[4,64,512]{2,1,0:T(8,128)(2,1)}), bf16[4,64,512]{2,1,0:T(8,128)(2,1)S(1)}, u32[]{:S(2)}, u32[]{:S(2)}) async-start(bf16[4,64,512]{2,1,0:T(8,128)(2,1)} %broadcast_in_dim.62), calls=%async_computation | async-start | bytes 524288 | tf_op jit(solution)/shard_map/all_to_all | solution.py:320
  22.4 0.6 copy-start.8
  22.4 0.7 copy-start.9
  22.4 0.7 copy-start.10
  25.2 8.5 %collective-permute-start.3 = (bf16[288,512]{1,0:T(8,128)(2,1)}, bf16[288,512]{1,0:T(8,128)(2,1)S(1)}, u32[]{:S(2)}, u32[]{:S(2)}) collective-permute-start(bf16[288,512]{1,0:T(8,128)(2,1)} %get-tuple-element.21), channel_id=1, source_target_pairs={{0,16},{16,32},{32,48},{48,0},{1,17},{17,33},{33,49},{49,1},{2,18}... | collective-permute-start | bytes 884744 | tf_op jit(solution)/shard_map/ppermute | solution.py:27
  26.5 14.7 %collective-permute-start.4 = (bf16[288,512]{1,0:T(8,128)(2,1)}, bf16[288,512]{1,0:T(8,128)(2,1)S(1)}, u32[]{:S(2)}, u32[]{:S(2)}) collective-permute-start(bf16[288,512]{1,0:T(8,128)(2,1)} %get-tuple-element.22), channel_id=1, source_target_pairs={{0,32},{16,48},{32,0},{48,16},{1,33},{17,49},{33,1},{49,17},{2,34}... | collective-permute-start | bytes 884744 | tf_op jit(solution)/shard_map/ppermute | solution.py:27
  29.2 12.4 %collective-permute-start.5 = (bf16[288,512]{1,0:T(8,128)(2,1)}, bf16[288,512]{1,0:T(8,128)(2,1)S(1)}, u32[]{:S(2)}, u32[]{:S(2)}) collective-permute-start(bf16[288,512]{1,0:T(8,128)(2,1)} %get-tuple-element.23), channel_id=1, source_target_pairs={{0,48},{16,0},{32,16},{48,32},{1,49},{17,1},{33,17},{49,33},{2,50}... | collective-permute-start | bytes 884744 | tf_op jit(solution)/shard_map/ppermute | solution.py:27
  30.3 13.6 %copy-start.5 = (s32[32]{0:T(128)S(1)}, s32[32]{0:T(128)}, u32[]{:S(2)}) copy-start(s32[32]{0:T(128)} %counts_ref.3) | copy-start | bytes 388
  41.6 5.9 %copy-start.3 = (bf16[1152,512]{1,0:T(8,128)(2,1)}, bf16[1152,512]{1,0:T(8,128)(2,1)S(1)}, u32[]{:S(2)}) copy-start(bf16[1152,512]{1,0:T(8,128)(2,1)S(1)} %constant_dynamic-update-slice_fusion.own_ref) | copy-start | bytes 3538948
  41.6 9.4 %collective-permute-start.6 = (bf16[1152,512]{1,0:T(8,128)(2,1)S(1)}, bf16[1152,512]{1,0:T(8,128)(2,1)}, u32[]{:S(2)}, u32[]{:S(2)}) collective-permute-start(bf16[1152,512]{1,0:T(8,128)(2,1)S(1)} %constant_dynamic-update-slice_fusion.own_ref), channel_id=1, source_target_pairs={{0,8},{8,0},{1,9},{9,1},{2,10},{10,2},{3,11},{11,3},{4,12},{12,4},... | collective-permute-start | bytes 3538952 | tf_op jit(solution)/shard_map/ppermute | solution.py:27
  47.5 18.5 %all-to-all-start.1 = ((bf16[4,4,64,512]{3,2,1,0:T(8,128)(2,1)}), bf16[4,4,64,512]{3,2,1,0:T(8,128)(2,1)S(1)}, u32[]{:S(2)}, u32[]{:S(2)}) async-start(bf16[4,4,64,512]{3,2,1,0:T(8,128)(2,1)} %broadcast_in_dim.63), calls=%async_computation.1 | async-start | bytes 2097152 | tf_op jit(solution)/shard_map/all_to_all | solution.py:320
  52.5 13.6 %collective-permute-start.7 = (bf16[224,128]{1,0:T(8,128)(2,1)S(1)}, bf16[224,128]{1,0:T(8,128)(2,1)S(1)}, u32[]{:S(2)}, u32[]{:S(2)}) collective-permute-start(bf16[224,128]{1,0:T(8,128)(2,1)S(1)} %fusion.19), channel_id=1, source_target_pairs={{0,0},{1,32},{2,64},{3,96},{4,128},{5,160},{6,192},{7,224},{8,8},{... | collective-permute-start | bytes 172040 | tf_op jit(solution)/shard_map/ppermute | solution.py:410
  66.0 3.4 %copy-start.2 = (bf16[4,4,64,512]{3,2,1,0:T(8,128)(2,1)}, bf16[4,4,64,512]{3,2,1,0:T(8,128)(2,1)S(1)}, u32[]{:S(2)}) copy-start(bf16[4,4,64,512]{3,2,1,0:T(8,128)(2,1)S(1)} %all-to-all-done.1) | copy-start | bytes 3145732
  66.0 3.4 %collective-permute-start.8 = (bf16[1024,512]{1,0:T(8,128)(2,1)S(1)}, bf16[1024,512]{1,0:T(8,128)(2,1)S(1)}, u32[]{:S(2)}, u32[]{:S(2)}) collective-permute-start(bf16[1024,512]{1,0:T(8,128)(2,1)S(1)} %bitcast.70), channel_id=1, source_target_pairs={{0,8},{8,0},{1,9},{9,1},{2,10},{10,2},{3,11},{11,3},{4,12},{12,4},... | collective-permute-start | bytes 3145736 | tf_op jit(solution)/shard_map/ppermute | solution.py:27
  69.4 1.0 copy-start.7
  102.4 11.8 %collective-permute-start.9 = (bf16[224,128]{1,0:T(8,128)(2,1)S(1)}, bf16[224,128]{1,0:T(8,128)(2,1)S(1)}, u32[]{:S(2)}, u32[]{:S(2)}) collective-permute-start(bf16[224,128]{1,0:T(8,128)(2,1)S(1)} %add_convert_fusion.1), channel_id=1, source_target_pairs={{0,0},{1,32},{2,64},{3,96},{4,128},{5,160},{6,192},{7,224},{8,8},{... | collective-permute-start | bytes 172040 | tf_op jit(solution)/shard_map/ppermute | solution.py:427
  103.0 11.2 %collective-permute-start.10 = (bf16[224,128]{1,0:T(8,128)(2,1)S(1)}, bf16[224,128]{1,0:T(8,128)(2,1)S(1)}, u32[]{:S(2)}, u32[]{:S(2)}) collective-permute-start(bf16[224,128]{1,0:T(8,128)(2,1)S(1)} %add_convert_fusion.1), channel_id=1, source_target_pairs={{0,64},{1,96},{2,128},{3,160},{4,192},{5,224},{6,0},{7,32},{8,72},... | collective-permute-start | bytes 172040 | tf_op jit(solution)/shard_map/ppermute | solution.py:427
  106.3 7.9 %collective-permute-start.11 = (bf16[224,128]{1,0:T(8,128)(2,1)S(1)}, bf16[224,128]{1,0:T(8,128)(2,1)S(1)}, u32[]{:S(2)}, u32[]{:S(2)}) collective-permute-start(bf16[224,128]{1,0:T(8,128)(2,1)S(1)} %add_convert_fusion.1), channel_id=1, source_target_pairs={{0,128},{1,160},{2,192},{3,224},{4,0},{5,32},{6,64},{7,96},{8,136}... | collective-permute-start | bytes 172040 | tf_op jit(solution)/shard_map/ppermute | solution.py:427
  110.6 5.4 %collective-permute-start.12 = (bf16[224,128]{1,0:T(8,128)(2,1)S(1)}, bf16[224,128]{1,0:T(8,128)(2,1)S(1)}, u32[]{:S(2)}, u32[]{:S(2)}) collective-permute-start(bf16[224,128]{1,0:T(8,128)(2,1)S(1)} %add_convert_fusion.1), channel_id=1, source_target_pairs={{0,192},{1,224},{2,0},{3,32},{4,64},{5,96},{6,128},{7,160},{8,200}... | collective-permute-start | bytes 172040 | tf_op jit(solution)/shard_map/ppermute | solution.py:427
  116.2 23.7 %copy-start.6 = (f32[896]{0:T(1024)S(1)}, f32[896]{0:T(1024)}, u32[]{:S(2)}) copy-start(f32[896]{0:T(1024)} %param.22) | copy-start | bytes 10756
  135.8 6.2 %copy-start.1 = (bf16[4,4,224,128]{3,2,1,0:T(8,128)(2,1)}, bf16[4,4,224,128]{3,2,1,0:T(8,128)(2,1)S(1)}, u32[]{:S(2)}) copy-start(bf16[4,4,224,128]{3,2,1,0:T(8,128)(2,1)S(1)} %all_to_all.41) | copy-start | bytes 2752516
  135.8 6.2 %collective-permute-start.13 = (bf16[2,2,4,224,128]{4,3,2,1,0:T(8,128)(2,1)S(1)}, bf16[2,2,4,224,128]{4,3,2,1,0:T(8,128)(2,1)S(1)}, u32[]{:S(2)}, u32[]{:S(2)}) collective-permute-start(bf16[2,2,4,224,128]{4,3,2,1,0:T(8,128)(2,1)S(1)} %bitcast.66), channel_id=1, source_target_pairs={{0,8},{8,0},{1,9},{9,1},{2,10},{10,2},{3,11},{11,3},{4,12},{12,4},... | collective-permute-start | bytes 2752520 | tf_op jit(solution)/shard_map/ppermute | solution.py:27
  142.0 0.9 copy-start.4
  185.4 18.9 %all-to-all-start.5 = ((bf16[8,576,128]{2,1,0:T(8,128)(2,1)}), bf16[8,576,128]{2,1,0:T(8,128)(2,1)S(1)}, u32[]{:S(2)}, u32[]{:S(2)}) async-start(bf16[8,576,128]{2,1,0:T(8,128)(2,1)} %broadcast_in_dim.75), calls=%async_computation.5 | async-start | bytes 2359296 | tf_op jit(solution)/shard_map/all_to_all | solution.py:320
  206.2 5.0 %collective-permute-start.14 = (bf16[4,128,896]{2,1,0:T(8,128)(2,1)}, bf16[4,128,896]{2,1,0:T(8,128)(2,1)S(1)}, u32[]{:S(2)}, u32[]{:S(2)}) collective-permute-start(bf16[4,128,896]{2,1,0:T(8,128)(2,1)} %convolution_convert_fusion), channel_id=1, source_target_pairs={{0,8},{8,0},{1,9},{9,1},{2,10},{10,2},{3,11},{11,3},{4,12},{12,4},... | collective-permute-start | bytes 2752520 | tf_op jit(solution)/shard_map/ppermute | solution.py:27
  213.1 16.9 %all-to-all-start.6 = ((bf16[4,128,896]{2,1,0:T(8,128)(2,1)}), bf16[4,128,896]{2,1,0:T(8,128)(2,1)S(1)}, u32[]{:S(2)}, u32[]{:S(2)}) async-start(bf16[4,128,896]{2,1,0:T(8,128)(2,1)} %add_convert_fusion), calls=%async_computation.6 | async-start | bytes 1835008 | tf_op jit(solution)/shard_map/all_to_all | solution.py:320
  231.3 24.0 %all-to-all-start.7 = ((bf16[32,8,896]{2,1,0:T(8,128)(2,1)}), bf16[32,8,896]{2,1,0:T(8,128)(2,1)S(1)}, u32[]{:S(2)}, u32[]{:S(2)}) async-start(bf16[32,8,896]{2,1,0:T(8,128)(2,1)} %fusion.1), calls=%async_computation.7 | async-start | bytes 917504 | tf_op jit(solution)/shard_map/all_to_all | solution.py:320

commit v5 on v4

--- a/solution.py
+++ b/solution.py
@@ -57,73 +57,70 @@
     )
 
 
-def pack_kernel(counts_ref, lat_ref, res_ref, *refs):
-    outs, rows_ref = refs[:4], refs[4]
+def pack_kernel(counts_ref, lat_ref, res_ref, out_ref, rows_ref):
     slots, width = res_ref.shape
     half, lanes = width // 2, lat_ref.shape[1]
-    zh = lax.axis_index("zh")
     start = live_before(counts_ref)
     i_at, slot = iota((slots, slots), 0), iota((slots, slots), 1)
     roll = ((((i_at >> 3) - start) & 7) + 8 * (i_at & 7)) == slot
     rows_ref[...] = dot(jnp.where(roll, 1.0, 0.0).astype(BF), res_ref[...])
     fill = jnp.zeros((16, lanes - half), F32)
     for s in range(4):
-        outs[s][:slots, :] = lat_ref[...]
+        out_ref[s, :slots, :] = lat_ref[...]
         for high in range(2):
-            m = ((zh + s) & 3) * 2 + high
-            piece = rows_ref[pl.ds(pl.multiple_of(m * 8, 8), 8), :]
+            piece = rows_ref[(s * 2 + high) * 8 : (s * 2 + high + 1) * 8, :]
             piece = jnp.concatenate([piece[:, :half], piece[:, half:]], axis=0)
             piece = jnp.concatenate([piece, fill], axis=1)
-            outs[s][slots + 16 * high : slots + 16 * (high + 1), :] = piece.astype(BF)
+            out_ref[s, slots + 16 * high : slots + 16 * (high + 1), :] = piece.astype(BF)
 
 
 def pack(counts, latent, residual):
     slots, lanes = latent.shape
-    shape = (slots + 32, lanes)
+    shape = (4, slots + 32, lanes)
     return pl.pallas_call(
         pack_kernel,
         grid=(1,),
-        out_shape=[jax.ShapeDtypeStruct(shape, BF)] * 4,
+        out_shape=jax.ShapeDtypeStruct(shape, BF),
         in_specs=[
             pl.BlockSpec(memory_space=pltpu.SMEM),
             whole(latent.shape),
             whole(residual.shape),
         ],
-        out_specs=[whole(shape)] * 4,
+        out_specs=whole(shape),
         scratch_shapes=[pltpu.VMEM(residual.shape, F32)],
         cost_estimate=cost(2),
         name="pack",
     )(counts, latent, residual)
 
 
-def repack_kernel(*refs):
-    ins, outs, rows_ref = refs[:4], refs[4:8], refs[8]
-    slots = ins[0].shape[0] - 32
+def repack_kernel(in_ref, *refs):
+    outs, rows_ref = refs[:4], refs[4]
+    slots = in_ref.shape[1] - 32
     y = lax.axis_index("y")
     for t in range(4):
-        rows_ref[t] = ins[t][slots:, :].astype(F32)
+        rows_ref[t] = in_ref[t, slots:, :].astype(F32)
     for s in range(4):
         at = pl.ds(pl.multiple_of(((y + s) & 3) * 8, 8), 8)
         for t in range(4):
-            outs[s][t * slots : (t + 1) * slots, :] = ins[t][:slots, :]
+            outs[s][t * slots : (t + 1) * slots, :] = in_ref[t, :slots, :]
         for t in (0, 2):
             pair = jnp.concatenate([rows_ref[t, at, :], rows_ref[t + 1, at, :]], axis=0)
             outs[s][4 * slots + 8 * t : 4 * slots + 8 * t + 16, :] = pair.astype(BF)
 
 
-def repack(*pieces):
-    rows, lanes = pieces[0].shape
+def repack(packed):
+    _, rows, lanes = packed.shape
     shape = (4 * (rows - 32) + 32, lanes)
     return pl.pallas_call(
         repack_kernel,
         grid=(1,),
         out_shape=[jax.ShapeDtypeStruct(shape, BF)] * 4,
-        in_specs=[whole(pieces[0].shape)] * 4,
+        in_specs=[whole(packed.shape)],
         out_specs=[whole(shape)] * 4,
         scratch_shapes=[pltpu.VMEM((4, 32, lanes), F32)],
         cost_estimate=cost(2),
         name="repack",
-    )(*pieces)
+    )(packed)
 
 
 def score_kernel(counts_ref, qn_ref, qr_ref, lat_ref, kr_ref, ku_ref, req_ref, out_ref, s_ref):
@@ -153,12 +150,13 @@
         for i in range(1, per):
             h = group * per + i
             out = jnp.where((lane >> 5) == i, folded[h * slots : (h + 1) * slots], out)
-        out_ref[:, group * BLK : (group + 1) * BLK] = out.astype(BF)
+        for copy in range(out_ref.shape[0]):
+            out_ref[copy, :, group * BLK : (group + 1) * BLK] = out.astype(BF)
 
 
 def score_weights(counts, *arrays):
     slots, heads = arrays[2].shape[0], arrays[4].shape[1] // NOPE
-    shape = (slots, heads * WIN)
+    shape = (4, slots, heads * WIN)
     return pl.pallas_call(
         score_kernel,
         grid=(1,),
@@ -171,31 +169,30 @@
     )(counts, *arrays)
 
 
-def live_rows(goes_ref, own_ref, other_ref):
-    row = iota((STEP, own_ref.shape[0]), 0) + pl.program_id(0) * STEP
-    out = dot(jnp.where(goes_ref[0] == row, 1.0, 0.0).astype(BF), own_ref[...])
-    out = out + dot(jnp.where(goes_ref[1] == row, 1.0, 0.0).astype(BF), other_ref[...])
-    return out.astype(BF)
-
-
-def values_kernel(goes_ref, own_ref, other_ref, up_ref, out_ref):
-    out_ref[...] = dot(live_rows(goes_ref, own_ref, other_ref), up_ref[...]).astype(BF)
-
-
-def live_values(goes, own, other, up):
+def live_rows(goes_ref, slots_ref):
+    row = iota((STEP, slots_ref.shape[0]), 0) + pl.program_id(0) * STEP
+    return dot(jnp.where(goes_ref[...] == row, 1.0, 0.0).astype(BF), slots_ref[...]).astype(BF)
+
+
+def values_kernel(goes_ref, slots_ref, up_ref, out_ref):
+    out_ref[...] = dot(live_rows(goes_ref, slots_ref), up_ref[...]).astype(BF)
+
+
+def live_values(goes, slots, up):
     width = up.shape[1]
     return pl.pallas_call(
         values_kernel,
         grid=(LIVE // STEP,),
         out_shape=jax.ShapeDtypeStruct((LIVE, width), BF),
-        in_specs=[whole(a.shape) for a in (goes, own, other, up)],
+        in_specs=[whole(a.shape) for a in (goes, slots, up)],
         out_specs=pl.BlockSpec((STEP, width), lambda b: (b, 0)),
-        cost_estimate=cost(6),
+        cost_estimate=cost(0),
         name="live_values",
-    )(goes, own, other, up)
-
-
-def mix_kernel(goes_ref, own_ref, other_ref, prev_ref, cur_ref, wo_ref, out_ref, att_ref, all_ref):
+    )(goes, slots, up)
+
+
+def mix_kernel(goes_ref, slots_ref, prev_ref, cur_ref, *refs):
+    att_ref, all_ref = refs[4:]
     b = pl.program_id(0)
     heads = cur_ref.shape[1] // VH
     r_at, l_at = iota((BLK, BLK), 0), iota((BLK, BLK), 1)
@@ -205,8 +202,8 @@
     masks = [jnp.where(near & ((l_at >> 5) == q), 1.0, 0.0).astype(BF) for q in range(per)]
     r_at, l_at = iota((WIN, BLK), 0), iota((WIN, BLK), 1)
     before = jnp.where((BLK + r_at - l_at) < WIN, 1.0, 0.0).astype(BF)
-    blank = jnp.zeros((BLK, BLK), BF)
-    packed = live_rows(goes_ref, own_ref, other_ref)
+    blank = jnp.zeros((BLK - WIN, BLK), BF)
+    packed = live_rows(goes_ref, slots_ref)
     for group in range(heads // per):
         one = packed[:, group * BLK : (group + 1) * BLK].astype(F32)
         turned = [one.astype(BF)]
@@ -214,61 +211,57 @@
             turned.append(pltpu.roll(one, q * WIN, 1).astype(BF))
         for i in range(per):
             cols = slice((group * per + i) * VH, (group * per + i + 1) * VH)
-            bands = []
-            for rows in (slice(0, BLK), slice(BLK, STEP)):
+            last = turned[(per - 1 - i) % per]
+            olds = [prev_ref[:, cols], cur_ref[:BLK, cols]]
+            for t in range(STEP // BLK):
+                rows = slice(t * BLK, (t + 1) * BLK)
                 band = turned[(-i) % per][rows] * masks[0]
                 for q in range(1, per):
                     band = band + turned[(q - i) % per][rows] * masks[q]
-                bands.append(band)
-            last = turned[(per - 1 - i) % per]
-            corner = jnp.concatenate([last[BLK : BLK + WIN] * before, blank[WIN:]], axis=0)
-            band = jnp.concatenate(
-                [
-                    jnp.concatenate([bands[0], blank], axis=1),
-                    jnp.concatenate([corner, bands[1]], axis=1),
-                ],
-                axis=0,
-            )
-            att = dot(band, cur_ref[:, cols])
-            old = dot(last[:WIN] * before, prev_ref[:, cols])
-            att_ref[:WIN, cols] = (att[:WIN] + old).astype(BF)
-            att_ref[WIN:, cols] = att[WIN:].astype(BF)
-    part = nt(att_ref[...], wo_ref[...]).astype(BF)
+                corner = jnp.concatenate([last[rows][:WIN] * before, blank], axis=0)
+                att = dot(
+                    jnp.concatenate([corner, band], axis=1),
+                    jnp.concatenate([olds[t], cur_ref[rows, cols]], axis=0),
+                )
+                att_ref[rows, cols] = att.astype(BF)
     share = STEP // 8
     r_at, l_at = iota((STEP, STEP), 0), iota((STEP, STEP), 1)
     order = ((r_at & (share - 1)) * 8 + (r_at >> 5)) == l_at
-    part = dot(jnp.where(order, 1.0, 0.0).astype(BF), part)
+    order = jnp.where(order, 1.0, 0.0).astype(BF)
     rows = pl.ds(pl.multiple_of(b * share, share), share)
-    for m in range(8):
-        all_ref[m, rows, :] = part[m * share : (m + 1) * share]
+    for which in range(2):
+        part = dot(order, nt(att_ref[...], refs[which][...]).astype(BF))
+        for m in range(8):
+            all_ref[which, m, rows, :] = part[m * share : (m + 1) * share]
 
     @pl.when(b == pl.num_programs(0) - 1)
     def _():
-        for m in range(8):
-            out_ref[m] = all_ref[m].T.astype(BF)
-
-
-def mix_project(goes, own, other, values, wo):
+        for which in range(2):
+            for m in range(8):
+                refs[2 + which][m] = all_ref[which, m].T.astype(BF)
+
+
+def mix_project(goes, slots, values, wo, wo_other):
     width = values.shape[1]
     n = wo.shape[0]
     shape = (8, n, LIVE // 8)
     return pl.pallas_call(
         mix_kernel,
         grid=(LIVE // STEP,),
-        out_shape=jax.ShapeDtypeStruct(shape, BF),
+        out_shape=[jax.ShapeDtypeStruct(shape, BF)] * 2,
         in_specs=[
             whole(goes.shape),
-            whole(own.shape),
-            whole(other.shape),
+            whole(slots.shape),
             pl.BlockSpec((BLK, width), lambda b: (jnp.maximum(b * (STEP // BLK) - 1, 0), 0)),
             pl.BlockSpec((STEP, width), lambda b: (b, 0)),
             whole(wo.shape),
+            whole(wo.shape),
         ],
-        out_specs=whole(shape),
-        scratch_shapes=[pltpu.VMEM((STEP, width), BF), pltpu.VMEM((8, LIVE // 8, n), F32)],
+        out_specs=[whole(shape)] * 2,
+        scratch_shapes=[pltpu.VMEM((STEP, width), BF), pltpu.VMEM((2, 8, LIVE // 8, n), F32)],
         cost_estimate=cost(9),
         name="mix_project",
-    )(goes, own, other, values, values, wo)
+    )(goes, slots, values, values, wo, wo_other)
 
 
 def gate_up_kernel(own_ref, other_ref, gain_ref, gate_ref, up_ref, out_ref, x_ref, gain_at):
@@ -365,30 +358,30 @@
     own_start, own_length = starts(rank), lengths(rank)
     slot = jnp.arange(slots, dtype=jnp.int32)
 
-    pieces = pack(rank_tokens, latent, residual)
-    pieces = [pieces[0]] + [shifted(pieces[s], "zh", s) for s in (1, 2, 3)]
+    packed = exchange(pack(rank_tokens, latent, residual), "zh")
 
     weights = score_weights(
         rank_tokens, query_nope, query_rope, latent, key_rope, key_up, request_ids
     )
-    weights = gather(weights, "zh")
-    pieces = repack(*pieces)
+    weights, packed = lax.optimization_barrier((weights, packed))
+    weights = exchange(weights, "zh")
+    pieces = repack(packed)
+    weights, _ = lax.optimization_barrier((weights, pieces))
     pieces = [pieces[0]] + [shifted(pieces[s], "y", s) for s in (1, 2, 3)]
     got = jnp.concatenate(pieces, axis=0)
-    got_other = shifted(got, "c", 1)
     weights = gather(weights, "y").reshape(-1, weights.shape[2])
 
     four = jnp.arange(4, dtype=jnp.int32)
     eight = jnp.arange(8, dtype=jnp.int32)
+    ahead = (four[None, :] * 4 + four[:, None]) * 2 + c
+    goes = jnp.where(slot < lengths(ahead)[..., None], starts(ahead)[..., None] + slot, -1)
+    goes = goes.reshape(1, -1)
     core = jnp.stack([c, 1 - c])[:, None, None]
-    ahead = (four[None, None, :] * 4 + four[None, :, None]) * 2 + core
-    goes = jnp.where(slot < lengths(ahead)[..., None], starts(ahead)[..., None] + slot, -1)
-    goes = goes.reshape(2, 1, -1)
-    back = (((zh - four) & 3)[None, None, :] * 4 + ((y - four) & 3)[None, :, None]) * 2 + core
+    back = (four[None, None, :] * 4 + ((y - four) & 3)[None, :, None]) * 2 + core
     back_start, back_count = starts(back)[..., None], lengths(back)[..., None]
-    goes_back = jnp.where(slot < back_count, back_start + slot, -1).reshape(2, 4, -1)
-    goes_back = jnp.pad(goes_back, ((0, 0), (0, 0), (0, 32)), constant_values=-1).reshape(2, 1, -1)
-    values = live_values(goes_back, got, got_other, value_up)
+    goes_back = jnp.where(slot < back_count[0], back_start[0] + slot, -1).reshape(4, -1)
+    goes_back = jnp.pad(goes_back, ((0, 0), (0, 32)), constant_values=-1).reshape(1, -1)
+    values = live_values(goes_back, got, value_up)
 
     swap = []
     for a in range(4):
@@ -404,14 +397,16 @@
     def tn(a, b):
         return lax.dot_general(a, b, (((0,), (0,)), ((), ())), preferred_element_type=F32)
 
-    rows = [a.reshape(4, -1, a.shape[1])[:, 4 * slots :].reshape(-1, a.shape[1]) for a in (got, got_other)]
+    rows = got.reshape(4, -1, got.shape[1])[:, 4 * slots :].reshape(-1, got.shape[1])
+    rows = [rows, shifted(rows, "c", 1)]
     rows = tn(rows[0], come[0]) + tn(rows[1], come[1])
     rows = jnp.where(c == 0, rows[:quarter], rows[quarter : 2 * quarter]).astype(BF)
+    rows, values = lax.optimization_barrier((rows, values))
     rows = lax.ppermute(rows, DP + HD, swap)
 
-    weights, values, rows = lax.optimization_barrier((weights, values, rows))
-    weights_other = shifted(weights, "c", 1)
-    part = mix_project(goes, weights, weights_other, values, output_weight.T)
+    wo = output_weight.T
+    part, sent = mix_project(goes, weights, values, wo, shifted(wo, "c", 1))
+    part = part + shifted(sent, "c", 1)
     projected = jnp.sum(exchange(part, HD).astype(F32), axis=0)
     mixed = (rows.astype(F32) + projected).astype(BF)
 

time: 257 us -> 259 us (level)
  blocking collectives: 71.2 us -> 52.9 us
  starting transfers between devices: 59.5 us -> 76.5 us
  other arithmetic: 6.63 us -> 9.83 us
    all_to_all x3 -> x2, blocking collectives: 71.2 us -> 52.9 us  [exchange(): return lax.all_to_all(x, axes, split_axis=0, concat_axis=0, tiled=True)]
    all_to_all x5 -> x7, starting transfers between devices: 20.8 us -> 36 us  [exchange(): return lax.all_to_all(x, axes, split_axis=0, concat_axis=0, tiled=True)]
    all_to_all x5 -> x7, waiting for transfers between devices: 45.1 us -> 54.2 us  [exchange(): return lax.all_to_all(x, axes, split_axis=0, concat_axis=0, tiled=True)]
    ppermute x10 -> x8, waiting for transfers between devices: 15.1 us -> 6.92 us  [shifted(): return lax.ppermute(x, axis, [(i, (i + shift) % n) for i in range(n)])]
    ppermute x4, starting transfers between devices: 11.8 us -> 16.5 us  [on_device(): full.append(lax.ppermute(mixed, DP + HD, sends))]
    ppermute x10 -> x8, starting transfers between devices: 26.3 us -> 23.5 us  [shifted(): return lax.ppermute(x, axis, [(i, (i + shift) % n) for i in range(n)])]
  transfers between devices with their start and end apart: 20 -> 20, of which waited for: 11 -> 12; matrix products, arithmetic and copies ran while one was open for 6% -> 6% of each run, Pallas kernels for 6% -> 5%
where the time goes in v5:
time: 259 us; the launch traced here: 258 us
  starting transfers between devices  76.5 us (30%)
  waiting for transfers between devices  63.4 us (24%)
  blocking collectives  52.9 us (20%)
  Pallas kernels  37.5 us (14%)
  local copies, waits for them, and re-layouts  10.9 us (4%)
  other arithmetic  9.83 us (4%)
  matrix products  6.58 us (3%)
    all_to_all x7, waiting for transfers between devices, exchange(): return lax.all_to_all(x, axes, split_axis=0, concat_axis=0, tiled=True)  54.2 us
    all_to_all x2, blocking collectives, exchange(): return lax.all_to_all(x, axes, split_axis=0, concat_axis=0, tiled=True)  52.9 us
    all_to_all x7, starting transfers between devices, exchange(): return lax.all_to_all(x, axes, split_axis=0, concat_axis=0, tiled=True)  36 us
    ppermute x8, starting transfers between devices, shifted(): return lax.ppermute(x, axis, [(i, (i + shift) % n) for i in range(n)])  23.5 us
    ppermute x4, starting transfers between devices, on_device(): full.append(lax.ppermute(mixed, DP + HD, sends))  16.5 us
    pallas_call x1, Pallas kernels, mix_project(): pl.pallas_call(mix_kernel, grid=(LIVE // STEP,), out_shape=[jax.ShapeDtyp...  14.2 us
    pallas_call x1, Pallas kernels, gate_up(): pl.pallas_call(gate_up_kernel, grid=(highs * planes // blocks,), out_shap...  7.57 us
    pallas_call x1, Pallas kernels, live_values(): pl.pallas_call(values_kernel, grid=(LIVE // STEP,), out_shape=jax.ShapeDt...  7.55 us
  transfers between devices with their start and end apart: 20, of which 12 were waited for; matrix products, arithmetic and copies ran while one was open for 6% of the time, Pallas kernels for 5%

profile of v5, /device:TPU:1, one launch (start us, length us, event | category | flops | bytes accessed | tf_op | source)
XLA Modules:
  0.0 257.9 jit_solution(17946665281488150547)
XLA Ops:
  0.0 2.2 pack.1
  2.2 9.0 %all-to-all-start = ((bf16[4,96,512]{2,1,0:T(8,128)(2,1)}), bf16[4,96,512]{2,1,0:T(8,128)(2,1)S(1)}, u32[]{:S(2)}, u32[]{:S(2)}) async-start(bf16[4,96,512]{2,1,0:T(8,128)(2,1)} %pack.1), calls=%async_computation | async-start | bytes 786432 | tf_op jit(solution)/shard_map/all_to_all | solution.py:313
  11.2 1.0 collective-permute-start.5
  12.4 0.4 select_reduce_fusion.1
  14.1 3.8 %score_weights.1 = bf16[4,64,512]{2,1,0:T(8,128)(2,1)} custom-call(s32[32]{0:T(128)} %counts_ref.3, bf16[64,2048]{1,0:T(8,128)(2,1)} %qn_ref.1, bf16[64,1024]{1,0:T(8,128)(2,1)} %qr_ref.1, bf16[64,512]{1,0:T(8,128)(2,1)} %lat_ref.3, bf16[64,64]{1,0:T(8,128)(2,1)} %kr_ref.1, bf16[512,2048]{1,0:T(8,128)(2,1)} %ku_ref.1, s32[1,64]{1,0:T(1,128)} %req_ref.1), custom_call_target="tpu_custom_call" | custom-call | flops 4000000000 | bytes 12000000 | tf_op jit(solution)/shard_map/score_weights/pallas_call | solution.py:160
  17.9 3.9 %all-to-all-done.in_ref = bf16[4,96,512]{2,1,0:T(8,128)(2,1)S(1)} async-done(((bf16[4,96,512]{2,1,0:T(8,128)(2,1)}), bf16[4,96,512]{2,1,0:T(8,128)(2,1)S(1)}, u32[]{:S(2)}, u32[]{:S(2)}) %all-to-all-start) | async-done | bytes 393248 | tf_op jit(solution)/shard_map/all_to_all | solution.py:313
  21.8 0.8 copy-done.4
  22.6 2.1 repack.1
  24.7 1.2 collective-permute-start
  25.9 0.6 add_select_fusion.1
  26.5 2.6 %collective-permute-start.1 = (bf16[288,512]{1,0:T(8,128)(2,1)}, bf16[288,512]{1,0:T(8,128)(2,1)S(1)}, u32[]{:S(2)}, u32[]{:S(2)}) collective-permute-start(bf16[288,512]{1,0:T(8,128)(2,1)} %get-tuple-element.19), channel_id=1, source_target_pairs={{0,32},{16,48},{32,0},{48,16},{1,33},{17,49},{33,1},{49,17},{2,34}... | collective-permute-start | bytes 884744 | tf_op jit(solution)/shard_map/ppermute | solution.py:27
  29.1 0.9 select_reduce_fusion.4
  30.0 1.1 collective-permute-start.2
  31.1 4.4 %all-to-all-start.1 = ((bf16[4,64,512]{2,1,0:T(8,128)(2,1)}), bf16[4,64,512]{2,1,0:T(8,128)(2,1)S(1)}, u32[]{:S(2)}, u32[]{:S(2)}) async-start(bf16[4,64,512]{2,1,0:T(8,128)(2,1)} %score_weights.1), calls=%async_computation.1 | async-start | bytes 524288 | tf_op jit(solution)/shard_map/all_to_all | solution.py:313
  35.5 1.0 constant_dynamic-update-slice_fusion.3
  36.5 1.7 collective-permute-done.1
  38.3 1.0 constant_dynamic-update-slice_fusion.slots_ref
  39.3 5.0 %collective-permute-start.3 = (bf16[128,512]{1,0:T(8,128)(2,1)S(1)}, bf16[128,512]{1,0:T(8,128)(2,1)S(1)}, u32[]{:S(2)}, u32[]{:S(2)}) collective-permute-start(bf16[128,512]{1,0:T(8,128)(2,1)S(1)} %bitcast.75), channel_id=1, source_target_pairs={{0,8},{8,0},{1,9},{9,1},{2,10},{10,2},{3,11},{11,3},{4,12},{12,4},... | collective-permute-start | bytes 393224 | tf_op jit(solution)/shard_map/ppermute | solution.py:27
  44.3 1.1 broadcast_in_dim.77
  45.4 4.1 %all-to-all-start.2 = ((bf16[4,4,64,512]{3,2,1,0:T(8,128)(2,1)}), bf16[4,4,64,512]{3,2,1,0:T(8,128)(2,1)S(1)}, u32[]{:S(2)}, u32[]{:S(2)}) async-start(bf16[4,4,64,512]{3,2,1,0:T(8,128)(2,1)} %broadcast_in_dim.77), calls=%async_computation.2 | async-start | bytes 2097152 | tf_op jit(solution)/shard_map/all_to_all | solution.py:313
  49.5 0.8 add_select_fusion
  50.3 0.7 pad.4
  51.0 0.7 reshape.387.goes_ref
  51.6 0.7 select_n.141.goes_ref
  52.3 7.6 %live_values.1.prev_ref.cur_ref = bf16[1024,2048]{1,0:T(8,128)(2,1)} custom-call(s32[1,1152]{1,0:T(1,128)} %reshape.387.goes_ref, bf16[1152,512]{1,0:T(8,128)(2,1)} %copy-done.1, bf16[512,2048]{1,0:T(8,128)(2,1)} %up_ref.1), custom_call_target="tpu_custom_call" | custom-call | tf_op jit(solution)/shard_map/live_values/pallas_call | solution.py:183
  60.3 0.5 all-to-all-done.2
  60.9 1.0 copy-done.3
  61.9 14.2 %mix_project.1 = (bf16[8,224,128]{2,1,0:T(8,128)(2,1)}, bf16[8,224,128]{2,1,0:T(8,128)(2,1)}) custom-call(s32[1,1024]{1,0:T(1,128)} %select_n.141.goes_ref, bf16[1024,512]{1,0:T(8,128)(2,1)} %bitcast.73, bf16[1024,2048]{1,0:T(8,128)(2,1)} %live_values.1.prev_ref.cur_ref, bf16[1024,2048]{1,0:T(8,128)(2,1)} %live_values.1.prev_ref.cur_ref, ...), custom_call_target="tpu_custom_call" | custom-call | flops 8999999488 | bytes 27000000 | tf_op jit(solution)/shard_map/mix_project/pallas_call | solution.py:248
  76.0 4.7 %collective-permute-start.6 = (bf16[8,224,128]{2,1,0:T(8,128)(2,1)}, bf16[8,224,128]{2,1,0:T(8,128)(2,1)S(1)}, u32[]{:S(2)}, u32[]{:S(2)}) collective-permute-start(bf16[8,224,128]{2,1,0:T(8,128)(2,1)} %get-tuple-element.26), channel_id=1, source_target_pairs={{0,8},{8,0},{1,9},{9,1},{2,10},{10,2},{3,11},{11,3},{4,12},{12,4},... | collective-permute-start | bytes 1376264 | tf_op jit(solution)/shard_map/ppermute | solution.py:27
  80.7 1.7 collective-permute-done.6
  82.4 1.9 add.294
  84.3 4.9 %all-to-all-start.3 = ((bf16[8,224,128]{2,1,0:T(8,128)(2,1)}), bf16[8,224,128]{2,1,0:T(8,128)(2,1)S(1)}, u32[]{:S(2)}, u32[]{:S(2)}) async-start(bf16[8,224,128]{2,1,0:T(8,128)(2,1)} %add.294), calls=%async_computation.3 | async-start | bytes 917504 | tf_op jit(solution)/shard_map/all_to_all | solution.py:313
  89.1 0.7 collective-permute-start.4
  89.8 8.1 %all-to-all-done.3 = bf16[8,224,128]{2,1,0:T(8,128)(2,1)S(1)} async-done(((bf16[8,224,128]{2,1,0:T(8,128)(2,1)}), bf16[8,224,128]{2,1,0:T(8,128)(2,1)S(1)}, u32[]{:S(2)}, u32[]{:S(2)}) %all-to-all-start.3) | async-done | bytes 458784 | tf_op jit(solution)/shard_map/all_to_all | solution.py:313
  98.0 0.7 collective-permute-start.7
  98.7 3.2 %collective-permute-start.8 = (bf16[224,128]{1,0:T(8,128)(2,1)S(1)}, bf16[224,128]{1,0:T(8,128)(2,1)S(1)}, u32[]{:S(2)}, u32[]{:S(2)}) collective-permute-start(bf16[224,128]{1,0:T(8,128)(2,1)S(1)} %add_convert_fusion.1), channel_id=1, source_target_pairs={{0,64},{1,96},{2,128},{3,160},{4,192},{5,224},{6,0},{7,32},{8,72},... | collective-permute-start | bytes 172040 | tf_op jit(solution)/shard_map/ppermute | solution.py:422
  101.9 10.2 %collective-permute-start.9 = (bf16[224,128]{1,0:T(8,128)(2,1)S(1)}, bf16[224,128]{1,0:T(8,128)(2,1)S(1)}, u32[]{:S(2)}, u32[]{:S(2)}) collective-permute-start(bf16[224,128]{1,0:T(8,128)(2,1)S(1)} %add_convert_fusion.1), channel_id=1, source_target_pairs={{0,128},{1,160},{2,192},{3,224},{4,0},{5,32},{6,64},{7,96},{8,136}... | collective-permute-start | bytes 172040 | tf_op jit(solution)/shard_map/ppermute | solution.py:422
  112.1 2.4 collective-permute-start.10
  114.5 2.2 collective-permute-done.10
  116.9 18.8 %all_to_all.45 = bf16[4,4,224,128]{3,2,1,0:T(8,128)(2,1)S(1)} all-to-all(bf16[4,4,224,128]{3,2,1,0:T(8,128)(2,1)S(1)} %broadcast_in_dim.130), channel_id=1, replica_groups=mesh['zh'=4,'y'=4,'c'=2,'x'=4,'zl'=2] {'y'}, dimensions={0} | all-to-all | bytes 1835008 | tf_op jit(solution)/shard_map/all_to_all | solution.py:313
  135.7 5.3 %collective-permute-start.11 = (bf16[2,2,4,224,128]{4,3,2,1,0:T(8,128)(2,1)S(1)}, bf16[2,2,4,224,128]{4,3,2,1,0:T(8,128)(2,1)S(1)}, u32[]{:S(2)}, u32[]{:S(2)}) collective-permute-start(bf16[2,2,4,224,128]{4,3,2,1,0:T(8,128)(2,1)S(1)} %bitcast.69), channel_id=1, source_target_pairs={{0,8},{8,0},{1,9},{9,1},{2,10},{10,2},{3,11},{11,3},{4,12},{12,4},... | collective-permute-start | bytes 2752520 | tf_op jit(solution)/shard_map/ppermute | solution.py:27
  141.0 0.6 broadcast_in_dim.131.gain_ref
  141.6 1.5 collective-permute-done.11.other_ref
  143.1 0.9 copy-done.5
  144.0 7.6 %gate_up.1 = bf16[8,1168,128]{2,1,0:T(8,128)(2,1)} custom-call(bf16[2,2,4,224,128]{4,3,2,1,0:T(8,128)(2,1)} %bitcast.70, bf16[2,2,4,224,128]{4,3,2,1,0:T(8,128)(2,1)} %copy-done.5, f32[1,896]{1,0:T(1,128)} %broadcast_in_dim.131.gain_ref, bf16[576,896]{1,0:T(8,128)(2,1)} %bitcast.81, bf16[576,896]{1,0:T(8,128)(2,1)} %bitcast.82), custom_call_target="tpu_custom_call" | custom-call | flops 6000000000 | bytes 18000000 | tf_op jit(solution)/shard_map/gate_up/pallas_call | solution.py:300
  151.6 34.1 %all_to_all.46 = bf16[8,1168,128]{2,1,0:T(8,128)(2,1)S(1)} all-to-all(bf16[8,1168,128]{2,1,0:T(8,128)(2,1)} %gate_up.1), channel_id=1, replica_groups=mesh['zh'=4,'y'=4,'c'=2,'x'=4,'zl'=2] {'x','zl'}, dimensions={0} | all-to-all | bytes 4784128 | tf_op jit(solution)/shard_map/all_to_all | solution.py:313
  186.2 1.2 broadcast_in_dim.132
  187.4 3.7 %all-to-all-start.6 = ((bf16[8,576,128]{2,1,0:T(8,128)(2,1)}), bf16[8,576,128]{2,1,0:T(8,128)(2,1)S(1)}, u32[]{:S(2)}, u32[]{:S(2)}) async-start(bf16[8,576,128]{2,1,0:T(8,128)(2,1)} %broadcast_in_dim.132), calls=%async_computation.6 | async-start | bytes 2359296 | tf_op jit(solution)/shard_map/all_to_all | solution.py:313
  191.0 15.4 %all-to-all-done.6 = bf16[8,576,128]{2,1,0:T(8,128)(2,1)S(1)} async-done(((bf16[8,576,128]{2,1,0:T(8,128)(2,1)}), bf16[8,576,128]{2,1,0:T(8,128)(2,1)S(1)}, u32[]{:S(2)}, u32[]{:S(2)}) %all-to-all-start.6) | async-done | bytes 1179680 | tf_op jit(solution)/shard_map/all_to_all | solution.py:313
  206.4 1.9 convolution_convert_fusion
  208.3 2.7 %collective-permute-start.12 = (bf16[4,128,896]{2,1,0:T(8,128)(2,1)}, bf16[4,128,896]{2,1,0:T(8,128)(2,1)S(1)}, u32[]{:S(2)}, u32[]{:S(2)}) collective-permute-start(bf16[4,128,896]{2,1,0:T(8,128)(2,1)} %convolution_convert_fusion), channel_id=1, source_target_pairs={{0,8},{8,0},{1,9},{9,1},{2,10},{10,2},{3,11},{11,3},{4,12},{12,4},... | collective-permute-start | bytes 2752520 | tf_op jit(solution)/shard_map/ppermute | solution.py:27
  211.3 2.0 collective-permute-done.12
  213.3 1.9 add_convert_fusion
  215.2 3.5 %all-to-all-start.7 = ((bf16[4,128,896]{2,1,0:T(8,128)(2,1)}), bf16[4,128,896]{2,1,0:T(8,128)(2,1)S(1)}, u32[]{:S(2)}, u32[]{:S(2)}) async-start(bf16[4,128,896]{2,1,0:T(8,128)(2,1)} %add_convert_fusion), calls=%async_computation.7 | async-start | bytes 1835008 | tf_op jit(solution)/shard_map/all_to_all | solution.py:313
  218.7 1.0 fusion.20
  219.7 1.0 fusion.18
  221.1 11.0 %all-to-all-done.7 = bf16[4,128,896]{2,1,0:T(8,128)(2,1)S(1)} async-done(((bf16[4,128,896]{2,1,0:T(8,128)(2,1)}), bf16[4,128,896]{2,1,0:T(8,128)(2,1)S(1)}, u32[]{:S(2)}, u32[]{:S(2)}) %all-to-all-start.7) | async-done | bytes 917536 | tf_op jit(solution)/shard_map/all_to_all | solution.py:313
  232.3 1.1 fusion.1
  233.4 6.4 %all-to-all-start.8 = ((bf16[32,8,896]{2,1,0:T(8,128)(2,1)}), bf16[32,8,896]{2,1,0:T(8,128)(2,1)S(1)}, u32[]{:S(2)}, u32[]{:S(2)}) async-start(bf16[32,8,896]{2,1,0:T(8,128)(2,1)} %fusion.1), calls=%async_computation.8 | async-start | bytes 917504 | tf_op jit(solution)/shard_map/all_to_all | solution.py:313
  239.8 0.6 fusion.41
  240.4 0.6 add_and_fusion
  241.1 0.6 iota_compare_fusion.10
  241.8 15.2 %all-to-all-done.8 = bf16[32,8,896]{2,1,0:T(8,128)(2,1)S(1)} async-done(((bf16[32,8,896]{2,1,0:T(8,128)(2,1)}), bf16[32,8,896]{2,1,0:T(8,128)(2,1)S(1)}, u32[]{:S(2)}, u32[]{:S(2)}) %all-to-all-start.8) | async-done | bytes 458784 | tf_op jit(solution)/shard_map/all_to_all | solution.py:313
  257.0 0.9 fusion.2
  (80 shorter events, 3.6 us)
Async XLA Ops:
  0.0 206.4 %copy-start = (bf16[576,896]{1,0:T(8,128)(2,1)S(1)}, bf16[576,896]{1,0:T(8,128)(2,1)}, u32[]{:S(2)}) copy-start(bf16[576,896]{1,0:T(8,128)(2,1)} %param.25) | copy-start | bytes 3096580
  0.0 12.4 %copy-start.6 = (s32[32]{0:T(128)S(1)}, s32[32]{0:T(128)}, u32[]{:S(2)}) copy-start(s32[32]{0:T(128)} %counts_ref.3) | copy-start | bytes 388
  2.2 19.6 %all-to-all-start = ((bf16[4,96,512]{2,1,0:T(8,128)(2,1)}), bf16[4,96,512]{2,1,0:T(8,128)(2,1)S(1)}, u32[]{:S(2)}, u32[]{:S(2)}) async-start(bf16[4,96,512]{2,1,0:T(8,128)(2,1)} %pack.1), calls=%async_computation | async-start | bytes 786432 | tf_op jit(solution)/shard_map/all_to_all | solution.py:313
  11.2 49.1 %collective-permute-start.5 = (bf16[224,2048]{1,0:T(8,128)(2,1)}, bf16[224,2048]{1,0:T(8,128)(2,1)}, u32[]{:S(2)}, u32[]{:S(2)}) collective-permute-start(bf16[224,2048]{1,0:T(8,128)(2,1)} %bitcast.9.refs_0_), channel_id=1, source_target_pairs={{0,8},{8,0},{1,9},{9,1},{2,10},{10,2},{3,11},{11,3},{4,12},{12,4},... | collective-permute-start | bytes 2752520 | tf_op jit(solution)/shard_map/ppermute | solution.py:27
  12.2 5.7 %copy-start.10 = (s32[8]{0:T(128)}, s32[8]{0:T(128)S(1)}, u32[]{:S(2)}) copy-start(s32[8]{0:T(128)S(1)} %iota_multiply_fusion.1) | copy-start | bytes 100
  17.9 11.2 %copy-start.7 = (s32[32]{0:T(128)S(1)}, s32[32]{0:T(128)}, u32[]{:S(2)}) copy-start(s32[32]{0:T(128)} %counts_ref.3) | copy-start | bytes 388
  21.8 0.8 copy-start.4
  24.7 11.8 %collective-permute-start = (bf16[288,512]{1,0:T(8,128)(2,1)}, bf16[288,512]{1,0:T(8,128)(2,1)S(1)}, u32[]{:S(2)}, u32[]{:S(2)}) collective-permute-start(bf16[288,512]{1,0:T(8,128)(2,1)} %get-tuple-element.18), channel_id=1, source_target_pairs={{0,16},{16,32},{32,48},{48,0},{1,17},{17,33},{33,49},{49,1},{2,18}... | collective-permute-start | bytes 884744 | tf_op jit(solution)/shard_map/ppermute | solution.py:27
  26.5 11.7 %collective-permute-start.1 = (bf16[288,512]{1,0:T(8,128)(2,1)}, bf16[288,512]{1,0:T(8,128)(2,1)S(1)}, u32[]{:S(2)}, u32[]{:S(2)}) collective-permute-start(bf16[288,512]{1,0:T(8,128)(2,1)} %get-tuple-element.19), channel_id=1, source_target_pairs={{0,32},{16,48},{32,0},{48,16},{1,33},{17,49},{33,1},{49,17},{2,34}... | collective-permute-start | bytes 884744 | tf_op jit(solution)/shard_map/ppermute | solution.py:27
  30.0 8.3 %collective-permute-start.2 = (bf16[288,512]{1,0:T(8,128)(2,1)}, bf16[288,512]{1,0:T(8,128)(2,1)}, u32[]{:S(2)}, u32[]{:S(2)}) collective-permute-start(bf16[288,512]{1,0:T(8,128)(2,1)} %get-tuple-element.20), channel_id=1, source_target_pairs={{0,48},{16,0},{32,16},{48,32},{1,49},{17,1},{33,17},{49,33},{2,50}... | collective-permute-start | bytes 884744 | tf_op jit(solution)/shard_map/ppermute | solution.py:27
  31.1 13.2 %all-to-all-start.1 = ((bf16[4,64,512]{2,1,0:T(8,128)(2,1)}), bf16[4,64,512]{2,1,0:T(8,128)(2,1)S(1)}, u32[]{:S(2)}, u32[]{:S(2)}) async-start(bf16[4,64,512]{2,1,0:T(8,128)(2,1)} %score_weights.1), calls=%async_computation.1 | async-start | bytes 524288 | tf_op jit(solution)/shard_map/all_to_all | solution.py:313
  39.3 6.1 %copy-start.1 = (bf16[1152,512]{1,0:T(8,128)(2,1)}, bf16[1152,512]{1,0:T(8,128)(2,1)S(1)}, u32[]{:S(2)}) copy-start(bf16[1152,512]{1,0:T(8,128)(2,1)S(1)} %constant_dynamic-update-slice_fusion.slots_ref) | copy-start | bytes 3538948
  39.3 20.6 %collective-permute-start.3 = (bf16[128,512]{1,0:T(8,128)(2,1)S(1)}, bf16[128,512]{1,0:T(8,128)(2,1)S(1)}, u32[]{:S(2)}, u32[]{:S(2)}) collective-permute-start(bf16[128,512]{1,0:T(8,128)(2,1)S(1)} %bitcast.75), channel_id=1, source_target_pairs={{0,8},{8,0},{1,9},{9,1},{2,10},{10,2},{3,11},{11,3},{4,12},{12,4},... | collective-permute-start | bytes 393224 | tf_op jit(solution)/shard_map/ppermute | solution.py:27
  45.4 15.5 %all-to-all-start.2 = ((bf16[4,4,64,512]{3,2,1,0:T(8,128)(2,1)}), bf16[4,4,64,512]{3,2,1,0:T(8,128)(2,1)S(1)}, u32[]{:S(2)}, u32[]{:S(2)}) async-start(bf16[4,4,64,512]{3,2,1,0:T(8,128)(2,1)} %broadcast_in_dim.77), calls=%async_computation.2 | async-start | bytes 2097152 | tf_op jit(solution)/shard_map/all_to_all | solution.py:313
  60.9 1.0 copy-start.3
  76.0 6.3 %collective-permute-start.6 = (bf16[8,224,128]{2,1,0:T(8,128)(2,1)}, bf16[8,224,128]{2,1,0:T(8,128)(2,1)S(1)}, u32[]{:S(2)}, u32[]{:S(2)}) collective-permute-start(bf16[8,224,128]{2,1,0:T(8,128)(2,1)} %get-tuple-element.26), channel_id=1, source_target_pairs={{0,8},{8,0},{1,9},{9,1},{2,10},{10,2},{3,11},{11,3},{4,12},{12,4},... | collective-permute-start | bytes 1376264 | tf_op jit(solution)/shard_map/ppermute | solution.py:27
  84.3 13.7 %all-to-all-start.3 = ((bf16[8,224,128]{2,1,0:T(8,128)(2,1)}), bf16[8,224,128]{2,1,0:T(8,128)(2,1)S(1)}, u32[]{:S(2)}, u32[]{:S(2)}) async-start(bf16[8,224,128]{2,1,0:T(8,128)(2,1)} %add.294), calls=%async_computation.3 | async-start | bytes 917504 | tf_op jit(solution)/shard_map/all_to_all | solution.py:313
  89.1 8.9 %collective-permute-start.4 = (bf16[224,128]{1,0:T(8,128)(2,1)S(1)}, bf16[224,128]{1,0:T(8,128)(2,1)S(1)}, u32[]{:S(2)}, u32[]{:S(2)}) collective-permute-start(bf16[224,128]{1,0:T(8,128)(2,1)S(1)} %fusion.19), channel_id=1, source_target_pairs={{0,0},{1,32},{2,64},{3,96},{4,128},{5,160},{6,192},{7,224},{8,8},{... | collective-permute-start | bytes 172040 | tf_op jit(solution)/shard_map/ppermute | solution.py:405
  98.0 16.5 %collective-permute-start.7 = (bf16[224,128]{1,0:T(8,128)(2,1)S(1)}, bf16[224,128]{1,0:T(8,128)(2,1)S(1)}, u32[]{:S(2)}, u32[]{:S(2)}) collective-permute-start(bf16[224,128]{1,0:T(8,128)(2,1)S(1)} %add_convert_fusion.1), channel_id=1, source_target_pairs={{0,0},{1,32},{2,64},{3,96},{4,128},{5,160},{6,192},{7,224},{8,8},{... | collective-permute-start | bytes 172040 | tf_op jit(solution)/shard_map/ppermute | solution.py:422
  98.7 15.8 %collective-permute-start.8 = (bf16[224,128]{1,0:T(8,128)(2,1)S(1)}, bf16[224,128]{1,0:T(8,128)(2,1)S(1)}, u32[]{:S(2)}, u32[]{:S(2)}) collective-permute-start(bf16[224,128]{1,0:T(8,128)(2,1)S(1)} %add_convert_fusion.1), channel_id=1, source_target_pairs={{0,64},{1,96},{2,128},{3,160},{4,192},{5,224},{6,0},{7,32},{8,72},... | collective-permute-start | bytes 172040 | tf_op jit(solution)/shard_map/ppermute | solution.py:422
  101.9 12.6 %collective-permute-start.9 = (bf16[224,128]{1,0:T(8,128)(2,1)S(1)}, bf16[224,128]{1,0:T(8,128)(2,1)S(1)}, u32[]{:S(2)}, u32[]{:S(2)}) collective-permute-start(bf16[224,128]{1,0:T(8,128)(2,1)S(1)} %add_convert_fusion.1), channel_id=1, source_target_pairs={{0,128},{1,160},{2,192},{3,224},{4,0},{5,32},{6,64},{7,96},{8,136}... | collective-permute-start | bytes 172040 | tf_op jit(solution)/shard_map/ppermute | solution.py:422
  112.1 4.6 %collective-permute-start.10 = (bf16[224,128]{1,0:T(8,128)(2,1)S(1)}, bf16[224,128]{1,0:T(8,128)(2,1)S(1)}, u32[]{:S(2)}, u32[]{:S(2)}) collective-permute-start(bf16[224,128]{1,0:T(8,128)(2,1)S(1)} %add_convert_fusion.1), channel_id=1, source_target_pairs={{0,192},{1,224},{2,0},{3,32},{4,64},{5,96},{6,128},{7,160},{8,200}... | collective-permute-start | bytes 172040 | tf_op jit(solution)/shard_map/ppermute | solution.py:422
  116.9 24.1 %copy-start.9 = (f32[896]{0:T(1024)S(1)}, f32[896]{0:T(1024)}, u32[]{:S(2)}) copy-start(f32[896]{0:T(1024)} %param.22) | copy-start | bytes 10756
  135.7 7.4 %copy-start.2 = (bf16[4,4,224,128]{3,2,1,0:T(8,128)(2,1)}, bf16[4,4,224,128]{3,2,1,0:T(8,128)(2,1)S(1)}, u32[]{:S(2)}) copy-start(bf16[4,4,224,128]{3,2,1,0:T(8,128)(2,1)S(1)} %all_to_all.45) | copy-start | bytes 2752516
  135.7 7.4 %collective-permute-start.11 = (bf16[2,2,4,224,128]{4,3,2,1,0:T(8,128)(2,1)S(1)}, bf16[2,2,4,224,128]{4,3,2,1,0:T(8,128)(2,1)S(1)}, u32[]{:S(2)}, u32[]{:S(2)}) collective-permute-start(bf16[2,2,4,224,128]{4,3,2,1,0:T(8,128)(2,1)S(1)} %bitcast.69), channel_id=1, source_target_pairs={{0,8},{8,0},{1,9},{9,1},{2,10},{10,2},{3,11},{11,3},{4,12},{12,4},... | collective-permute-start | bytes 2752520 | tf_op jit(solution)/shard_map/ppermute | solution.py:27
  143.1 0.9 copy-start.5
  187.4 19.1 %all-to-all-start.6 = ((bf16[8,576,128]{2,1,0:T(8,128)(2,1)}), bf16[8,576,128]{2,1,0:T(8,128)(2,1)S(1)}, u32[]{:S(2)}, u32[]{:S(2)}) async-start(bf16[8,576,128]{2,1,0:T(8,128)(2,1)} %broadcast_in_dim.132), calls=%async_computation.6 | async-start | bytes 2359296 | tf_op jit(solution)/shard_map/all_to_all | solution.py:313
  206.4 4.6 %copy-start.8 = (s32[32]{0:T(128)S(1)}, s32[32]{0:T(128)}, u32[]{:S(2)}) copy-start(s32[32]{0:T(128)} %counts_ref.3) | copy-start | bytes 388
  206.4 4.7 %copy-start.11 = (s32[8]{0:T(128)S(1)}, s32[8]{0:T(128)}, u32[]{:S(2)}) copy-start(s32[8]{0:T(128)} %copy-done.10) | copy-start | bytes 100
  208.3 5.0 %collective-permute-start.12 = (bf16[4,128,896]{2,1,0:T(8,128)(2,1)}, bf16[4,128,896]{2,1,0:T(8,128)(2,1)S(1)}, u32[]{:S(2)}, u32[]{:S(2)}) collective-permute-start(bf16[4,128,896]{2,1,0:T(8,128)(2,1)} %convolution_convert_fusion), channel_id=1, source_target_pairs={{0,8},{8,0},{1,9},{9,1},{2,10},{10,2},{3,11},{11,3},{4,12},{12,4},... | collective-permute-start | bytes 2752520 | tf_op jit(solution)/shard_map/ppermute | solution.py:27
  215.2 16.9 %all-to-all-start.7 = ((bf16[4,128,896]{2,1,0:T(8,128)(2,1)}), bf16[4,128,896]{2,1,0:T(8,128)(2,1)S(1)}, u32[]{:S(2)}, u32[]{:S(2)}) async-start(bf16[4,128,896]{2,1,0:T(8,128)(2,1)} %add_convert_fusion), calls=%async_computation.7 | async-start | bytes 1835008 | tf_op jit(solution)/shard_map/all_to_all | solution.py:313
  233.4 23.6 %all-to-all-start.8 = ((bf16[32,8,896]{2,1,0:T(8,128)(2,1)}), bf16[32,8,896]{2,1,0:T(8,128)(2,1)S(1)}, u32[]{:S(2)}, u32[]{:S(2)}) async-start(bf16[32,8,896]{2,1,0:T(8,128)(2,1)} %fusion.1), calls=%async_computation.8 | async-start | bytes 917504 | tf_op jit(solution)/shard_map/all_to_all | solution.py:313

commit v6 on v4

--- a/solution.py
+++ b/solution.py
@@ -153,12 +153,13 @@
         for i in range(1, per):
             h = group * per + i
             out = jnp.where((lane >> 5) == i, folded[h * slots : (h + 1) * slots], out)
-        out_ref[:, group * BLK : (group + 1) * BLK] = out.astype(BF)
+        for copy in range(out_ref.shape[0]):
+            out_ref[copy, :, group * BLK : (group + 1) * BLK] = out.astype(BF)
 
 
 def score_weights(counts, *arrays):
     slots, heads = arrays[2].shape[0], arrays[4].shape[1] // NOPE
-    shape = (slots, heads * WIN)
+    shape = (4, slots, heads * WIN)
     return pl.pallas_call(
         score_kernel,
         grid=(1,),
@@ -190,7 +191,7 @@
         out_shape=jax.ShapeDtypeStruct((LIVE, width), BF),
         in_specs=[whole(a.shape) for a in (goes, own, other, up)],
         out_specs=pl.BlockSpec((STEP, width), lambda b: (b, 0)),
-        cost_estimate=cost(6),
+        cost_estimate=cost(0),
         name="live_values",
     )(goes, own, other, up)
 
@@ -205,7 +206,7 @@
     masks = [jnp.where(near & ((l_at >> 5) == q), 1.0, 0.0).astype(BF) for q in range(per)]
     r_at, l_at = iota((WIN, BLK), 0), iota((WIN, BLK), 1)
     before = jnp.where((BLK + r_at - l_at) < WIN, 1.0, 0.0).astype(BF)
-    blank = jnp.zeros((BLK, BLK), BF)
+    blank = jnp.zeros((BLK - WIN, BLK), BF)
     packed = live_rows(goes_ref, own_ref, other_ref)
     for group in range(heads // per):
         one = packed[:, group * BLK : (group + 1) * BLK].astype(F32)
@@ -214,25 +215,19 @@
             turned.append(pltpu.roll(one, q * WIN, 1).astype(BF))
         for i in range(per):
             cols = slice((group * per + i) * VH, (group * per + i + 1) * VH)
-            bands = []
-            for rows in (slice(0, BLK), slice(BLK, STEP)):
+            last = turned[(per - 1 - i) % per]
+            olds = [prev_ref[:, cols], cur_ref[:BLK, cols]]
+            for t in range(STEP // BLK):
+                rows = slice(t * BLK, (t + 1) * BLK)
                 band = turned[(-i) % per][rows] * masks[0]
                 for q in range(1, per):
                     band = band + turned[(q - i) % per][rows] * masks[q]
-                bands.append(band)
-            last = turned[(per - 1 - i) % per]
-            corner = jnp.concatenate([last[BLK : BLK + WIN] * before, blank[WIN:]], axis=0)
-            band = jnp.concatenate(
-                [
-                    jnp.concatenate([bands[0], blank], axis=1),
-                    jnp.concatenate([corner, bands[1]], axis=1),
-                ],
-                axis=0,
-            )
-            att = dot(band, cur_ref[:, cols])
-            old = dot(last[:WIN] * before, prev_ref[:, cols])
-            att_ref[:WIN, cols] = (att[:WIN] + old).astype(BF)
-            att_ref[WIN:, cols] = att[WIN:].astype(BF)
+                corner = jnp.concatenate([last[rows][:WIN] * before, blank], axis=0)
+                att = dot(
+                    jnp.concatenate([corner, band], axis=1),
+                    jnp.concatenate([olds[t], cur_ref[rows, cols]], axis=0),
+                )
+                att_ref[rows, cols] = att.astype(BF)
     part = nt(att_ref[...], wo_ref[...]).astype(BF)
     share = STEP // 8
     r_at, l_at = iota((STEP, STEP), 0), iota((STEP, STEP), 1)
@@ -272,15 +267,20 @@
 
 
 def gate_up_kernel(own_ref, other_ref, gain_ref, gate_ref, up_ref, out_ref, x_ref, gain_at):
-    core = lax.axis_index("c")
-    _, lows, blocks, k, chunk = own_ref.shape
+    core, y = lax.axis_index("c"), lax.axis_index("y")
+    b = pl.program_id(0)
+    blocks = out_ref.shape[0]
+    _, planes, k, chunk = own_ref.shape
     ff = gate_ref.shape[0]
+    steps = planes // blocks
+    high, first = b // steps, (b % steps) * blocks
     squares = jnp.zeros((1, blocks * chunk), F32)
     gain_at[...] = jnp.broadcast_to(gain_ref[...], (8, gain_ref.shape[1])).T
     for ref, flip in ((own_ref, core), (other_ref, 1 - core)):
-        for low in range(lows):
+        for low in range(2):
             rows = pl.ds(pl.multiple_of((low * 2 + flip) * k, 32), k)
-            x = jnp.concatenate([ref[0, low, i] for i in range(blocks)], axis=1).astype(F32)
+            s = (y - high * 2 - low) & 3
+            x = jnp.concatenate([ref[s, first + i] for i in range(blocks)], axis=1).astype(F32)
             squares = squares + jnp.sum(x * x, axis=0, keepdims=True)
             x_ref[rows, :] = (x * gain_at[rows, :1]).astype(BF)
     x = x_ref[...]
@@ -297,18 +297,20 @@
 
 
 def gate_up(own, other, gain, gate_weight, up_weight):
-    highs, lows, planes, k, chunk = own.shape
+    _, planes, k, chunk = own.shape
     ff, width = gate_weight.shape
     blocks = 2
-    spec = pl.BlockSpec(
-        (1, lows, blocks, k, chunk),
-        lambda b: (b // (planes // blocks), 0, b % (planes // blocks), 0, 0),
-    )
     return pl.pallas_call(
         gate_up_kernel,
-        grid=(highs * planes // blocks,),
-        out_shape=jax.ShapeDtypeStruct((highs * planes, 2 * ff + 16, chunk), BF),
-        in_specs=[spec, spec, whole((1, width)), whole((ff, width)), whole((ff, width))],
+        grid=(2 * planes // blocks,),
+        out_shape=jax.ShapeDtypeStruct((2 * planes, 2 * ff + 16, chunk), BF),
+        in_specs=[
+            whole(own.shape),
+            whole(own.shape),
+            whole((1, width)),
+            whole((ff, width)),
+            whole((ff, width)),
+        ],
         out_specs=pl.BlockSpec((blocks, 2 * ff + 16, chunk), lambda b: (b, 0, 0)),
         scratch_shapes=[pltpu.VMEM((width, blocks * chunk), BF), pltpu.VMEM((width, 8), F32)],
         cost_estimate=cost(6),
@@ -371,12 +373,15 @@
     weights = score_weights(
         rank_tokens, query_nope, query_rope, latent, key_rope, key_up, request_ids
     )
-    weights = gather(weights, "zh")
+    weights = exchange(weights, "zh")
     pieces = repack(*pieces)
+    weights, gain, _ = lax.optimization_barrier((weights, norm_gain[None, :], pieces))
+    weights = jnp.broadcast_to(weights[None], (4,) + weights.shape)
     pieces = [pieces[0]] + [shifted(pieces[s], "y", s) for s in (1, 2, 3)]
+    pieces, weights = lax.optimization_barrier((pieces, weights))
     got = jnp.concatenate(pieces, axis=0)
     got_other = shifted(got, "c", 1)
-    weights = gather(weights, "y").reshape(-1, weights.shape[2])
+    weights = exchange(weights, "y").reshape(-1, weights.shape[3])
 
     four = jnp.arange(4, dtype=jnp.int32)
     eight = jnp.arange(8, dtype=jnp.int32)
@@ -407,9 +412,10 @@
     rows = [a.reshape(4, -1, a.shape[1])[:, 4 * slots :].reshape(-1, a.shape[1]) for a in (got, got_other)]
     rows = tn(rows[0], come[0]) + tn(rows[1], come[1])
     rows = jnp.where(c == 0, rows[:quarter], rows[quarter : 2 * quarter]).astype(BF)
+    rows, values = lax.optimization_barrier((rows, values))
     rows = lax.ppermute(rows, DP + HD, swap)
 
-    weights, values, rows = lax.optimization_barrier((weights, values, rows))
+    weights, values = lax.optimization_barrier((weights, values))
     weights_other = shifted(weights, "c", 1)
     part = mix_project(goes, weights, weights_other, values, output_weight.T)
     projected = jnp.sum(exchange(part, HD).astype(F32), axis=0)
@@ -427,10 +433,10 @@
         full.append(lax.ppermute(mixed, DP + HD, sends))
     full = jnp.stack(full)
 
-    full = gather(full, "y").reshape(2, 2, 4, quarter, chunk)
+    full = jnp.stack([full] + [shifted(full, "y", s) for s in (1, 2, 3)])
     full_other = shifted(full, "c", 1)
     ff = down_weight.shape[0]
-    part = gate_up(full, full_other, norm_gain[None, :], gate_weight.T, up_weight.T)
+    part = gate_up(full, full_other, gain, gate_weight.T, up_weight.T)
     total = jnp.sum(exchange(part, HD).astype(F32), axis=0)
     scale = lax.rsqrt((total[2 * ff : 2 * ff + 1] + total[2 * ff + 1 : 2 * ff + 2]) / model + 1e-06)
     hidden = (jax.nn.silu(total[:ff] * scale) * (total[ff : 2 * ff] * scale)).astype(BF)
@@ -443,16 +449,19 @@
         )
 
     sent = shifted(down(1 - c).astype(BF), "c", 1)
-    total = (down(c) + sent.astype(F32)).astype(BF)
-    total = jnp.sum(exchange(total, "y").astype(F32), axis=0)
+    total = down(c) + sent.astype(F32)
+    pieces = [pick(total, (y + s) & 3) for s in range(4)]
+    total = pieces[0]
+    for s in (1, 2, 3):
+        total = total + shifted(pieces[s].astype(BF), "y", s).astype(F32)
     spot = y * 2 + c
     begin = starts(every)
     m = ((zh - (spot & 3)) & 3) * 2 + (spot >> 2)
     place = ((m - begin[:, None]) & 7) + 8 * eight[None, :]
     comes = jnp.where(place < rank_tokens[:, None], (begin[:, None] + place) >> 3, -1)
     expand = (comes.reshape(ranks * 8, 1) == jnp.arange(chunk, dtype=jnp.int32)).astype(BF)
-    pair = [pick(a.reshape(2, 2, 4, quarter, chunk), spot >> 2) for a in (full, full_other)]
-    pair = [lax.dynamic_index_in_dim(a, spot & 3, 1, keepdims=False) for a in pair]
+    at = [(y - (spot >> 2) * 2 - low) & 3 for low in range(2)]
+    pair = [jnp.stack([pick(pick(a, s), spot & 3) for s in at]) for a in (full, full_other)]
     low = jnp.where(c == 0, pair[0], pair[1])
     high = jnp.where(c == 0, pair[1], pair[0])
     own = jnp.stack([low, high], axis=1).reshape(width, chunk)

time: 257 us -> 249 us (0.969)
  blocking collectives: 71.2 us -> 36.7 us
  waiting for transfers between devices: 62 us -> 82.3 us
  starting transfers between devices: 59.5 us -> 69.9 us
    all_to_all x3 -> x1, blocking collectives: 71.2 us -> 36.7 us  [exchange(): return lax.all_to_all(x, axes, split_axis=0, concat_axis=0, tiled=True)]
    ppermute x10 -> x16, waiting for transfers between devices: 15.1 us -> 37.8 us  [shifted(): return lax.ppermute(x, axis, [(i, (i + shift) % n) for i in range(n)])]
    ppermute x10 -> x16, starting transfers between devices: 26.3 us -> 37.7 us  [shifted(): return lax.ppermute(x, axis, [(i, (i + shift) % n) for i in range(n)])]
    all_to_all x5, waiting for transfers between devices: 45.1 us -> 41.4 us  [exchange(): return lax.all_to_all(x, axes, split_axis=0, concat_axis=0, tiled=True)]
    broadcast_in_dim x4 -> x1, local copies, waits for them, and re-layouts: 3.95 us -> 1.2 us  [gather(): return exchange(jnp.broadcast_to(x[None], (n,) + x.shape), axes)]
  transfers between devices with their start and end apart: 20 -> 26, of which waited for: 11 -> 16; matrix products, arithmetic and copies ran while one was open for 6% -> 4% of each run, Pallas kernels for 6% -> 6%
where the time goes in v6:
time: 249 us; the launch traced here: 248 us
  waiting for transfers between devices  82.3 us (33%)
  starting transfers between devices  69.9 us (28%)
  Pallas kernels  37.2 us (15%)
  blocking collectives  36.7 us (15%)
  local copies, waits for them, and re-layouts  10.8 us (4%)
  matrix products  6.42 us (3%)
  other arithmetic  4.75 us (2%)
    all_to_all x5, waiting for transfers between devices, exchange(): return lax.all_to_all(x, axes, split_axis=0, concat_axis=0, tiled=True)  41.4 us
    ppermute x16, waiting for transfers between devices, shifted(): return lax.ppermute(x, axis, [(i, (i + shift) % n) for i in range(n)])  37.8 us
    ppermute x16, starting transfers between devices, shifted(): return lax.ppermute(x, axis, [(i, (i + shift) % n) for i in range(n)])  37.7 us
    all_to_all x1, blocking collectives, exchange(): return lax.all_to_all(x, axes, split_axis=0, concat_axis=0, tiled=True)  36.7 us
    all_to_all x5, starting transfers between devices, exchange(): return lax.all_to_all(x, axes, split_axis=0, concat_axis=0, tiled=True)  19.7 us
    pallas_call x1, Pallas kernels, mix_project(): pl.pallas_call(mix_kernel, grid=(LIVE // STEP,), out_shape=jax.ShapeDtype...  12 us
    ppermute x4, starting transfers between devices, on_device(): full.append(lax.ppermute(mixed, DP + HD, sends))  11.8 us
    pallas_call x1, Pallas kernels, live_values(): pl.pallas_call(values_kernel, grid=(LIVE // STEP,), out_shape=jax.ShapeDt...  9.24 us
  transfers between devices with their start and end apart: 26, of which 16 were waited for; matrix products, arithmetic and copies ran while one was open for 4% of the time, Pallas kernels for 6%

profile of v6, /device:TPU:1, one launch (start us, length us, event | category | flops | bytes accessed | tf_op | source)
XLA Modules:
  0.0 248.5 jit_solution(15817294695913328190)
XLA Ops:
  0.0 2.2 pack.1
  2.2 3.8 %collective-permute-start = (bf16[96,512]{1,0:T(8,128)(2,1)}, bf16[96,512]{1,0:T(8,128)(2,1)S(1)}, u32[]{:S(2)}, u32[]{:S(2)}) collective-permute-start(bf16[96,512]{1,0:T(8,128)(2,1)} %get-tuple-element.25), channel_id=1, source_target_pairs={{0,64},{64,128},{128,192},{192,0},{1,65},{65,129},{129,193},{193,1... | collective-permute-start | bytes 294920 | tf_op jit(solution)/shard_map/ppermute | solution.py:27
  6.1 5.1 %collective-permute-start.1 = (bf16[96,512]{1,0:T(8,128)(2,1)}, bf16[96,512]{1,0:T(8,128)(2,1)S(1)}, u32[]{:S(2)}, u32[]{:S(2)}) collective-permute-start(bf16[96,512]{1,0:T(8,128)(2,1)} %get-tuple-element.26), channel_id=1, source_target_pairs={{0,128},{64,192},{128,0},{192,64},{1,129},{65,193},{129,1},{193,65... | collective-permute-start | bytes 294920 | tf_op jit(solution)/shard_map/ppermute | solution.py:27
  11.2 2.4 collective-permute-start.2
  13.6 3.8 %score_weights.1 = bf16[4,64,512]{2,1,0:T(8,128)(2,1)} custom-call(s32[32]{0:T(128)} %counts_ref.3, bf16[64,2048]{1,0:T(8,128)(2,1)} %qn_ref.1, bf16[64,1024]{1,0:T(8,128)(2,1)} %qr_ref.1, bf16[64,512]{1,0:T(8,128)(2,1)} %lat_ref.3, bf16[64,64]{1,0:T(8,128)(2,1)} %kr_ref.1, bf16[512,2048]{1,0:T(8,128)(2,1)} %ku_ref.1, s32[1,64]{1,0:T(1,128)} %req_ref.1), custom_call_target="tpu_custom_call" | custom-call | flops 4000000000 | bytes 12000000 | tf_op jit(solution)/shard_map/score_weights/pallas_call | solution.py:163
  17.4 3.4 %all-to-all-start = ((bf16[4,64,512]{2,1,0:T(8,128)(2,1)}), bf16[4,64,512]{2,1,0:T(8,128)(2,1)S(1)}, u32[]{:S(2)}, u32[]{:S(2)}) async-start(bf16[4,64,512]{2,1,0:T(8,128)(2,1)} %score_weights.1), calls=%async_computation | async-start | bytes 524288 | tf_op jit(solution)/shard_map/all_to_all | solution.py:322
  21.6 0.6 copy-done.10
  22.3 2.2 repack.1
  24.5 1.3 collective-permute-start.3
  25.8 2.6 %collective-permute-start.4 = (bf16[288,512]{1,0:T(8,128)(2,1)}, bf16[288,512]{1,0:T(8,128)(2,1)S(1)}, u32[]{:S(2)}, u32[]{:S(2)}) collective-permute-start(bf16[288,512]{1,0:T(8,128)(2,1)} %get-tuple-element.30), channel_id=1, source_target_pairs={{0,32},{16,48},{32,0},{48,16},{1,33},{17,49},{33,1},{49,17},{2,34}... | collective-permute-start | bytes 884744 | tf_op jit(solution)/shard_map/ppermute | solution.py:27
  28.4 1.1 collective-permute-start.5
  29.5 0.7 select_reduce_fusion.3
  30.6 2.4 collective-permute-done.3
  33.0 7.4 %collective-permute-done.4 = bf16[288,512]{1,0:T(8,128)(2,1)S(1)} collective-permute-done((bf16[288,512]{1,0:T(8,128)(2,1)}, bf16[288,512]{1,0:T(8,128)(2,1)S(1)}, u32[]{:S(2)}, u32[]{:S(2)}) %collective-permute-start.4) | collective-permute-done | bytes 294944 | tf_op jit(solution)/shard_map/ppermute | solution.py:27
  40.9 1.2 broadcast_in_dim.60
  42.2 2.1 collective-permute-start.6
  45.1 4.3 %all-to-all-start.1 = ((bf16[4,4,64,512]{3,2,1,0:T(8,128)(2,1)}), bf16[4,4,64,512]{3,2,1,0:T(8,128)(2,1)}, u32[]{:S(2)}, u32[]{:S(2)}) async-start(bf16[4,4,64,512]{3,2,1,0:T(8,128)(2,1)} %broadcast_in_dim.60), calls=%async_computation.1 | async-start | bytes 2097152 | tf_op jit(solution)/shard_map/all_to_all | solution.py:322
  49.4 0.7 reshape.474.goes_ref
  50.1 0.9 fusion.32
  51.1 1.0 copy-done.2
  52.1 9.2 %live_values.1.prev_ref.cur_ref = bf16[1024,2048]{1,0:T(8,128)(2,1)} custom-call(s32[2,1,1152]{2,1,0:T(1,128)} %reshape.474.goes_ref, bf16[1152,512]{1,0:T(8,128)(2,1)} %copy-done.1, bf16[1152,512]{1,0:T(8,128)(2,1)} %copy-done.2, bf16[512,2048]{1,0:T(8,128)(2,1)} %up_ref.1), custom_call_target="tpu_custom_call" | custom-call | tf_op jit(solution)/shard_map/live_values/pallas_call | solution.py:188
  61.6 3.1 %all-to-all-done.1 = bf16[4,4,64,512]{3,2,1,0:T(8,128)(2,1)} async-done(((bf16[4,4,64,512]{3,2,1,0:T(8,128)(2,1)}), bf16[4,4,64,512]{3,2,1,0:T(8,128)(2,1)}, u32[]{:S(2)}, u32[]{:S(2)}) %all-to-all-start.1) | async-done | bytes 1048608 | tf_op jit(solution)/shard_map/all_to_all | solution.py:322
  64.7 0.8 collective-permute-start.8
  65.9 0.6 compare_select_fusion.goes_ref
  66.5 1.5 collective-permute-done.8.other_ref
  68.0 1.0 copy-done.9
  69.0 12.0 %mix_project.1 = bf16[8,224,128]{2,1,0:T(8,128)(2,1)} custom-call(s32[2,1,1024]{2,1,0:T(1,128)} %compare_select_fusion.goes_ref, bf16[1024,512]{1,0:T(8,128)(2,1)} %bitcast.8.own_ref, bf16[1024,512]{1,0:T(8,128)(2,1)} %copy-done.9, bf16[1024,2048]{1,0:T(8,128)(2,1)} %live_values.1.prev_ref.cur_ref, bf16[1024,2048]{1,0:T(8,128)(2,1)} %live_values.1.prev_ref.cur_ref, ...), custom_call_target="tpu_custom_call" | custom-call | flops 8999999488 | bytes 27000000 | tf_op jit(solution)/shard_map/mix_project/pallas_call | solution.py:250
  81.0 4.5 %all-to-all-start.2 = ((bf16[8,224,128]{2,1,0:T(8,128)(2,1)}), bf16[8,224,128]{2,1,0:T(8,128)(2,1)S(1)}, u32[]{:S(2)}, u32[]{:S(2)}) async-start(bf16[8,224,128]{2,1,0:T(8,128)(2,1)} %mix_project.1), calls=%async_computation.2 | async-start | bytes 917504 | tf_op jit(solution)/shard_map/all_to_all | solution.py:322
  85.4 0.7 collective-permute-start.7
  86.1 8.2 %all-to-all-done.2 = bf16[8,224,128]{2,1,0:T(8,128)(2,1)S(1)} async-done(((bf16[8,224,128]{2,1,0:T(8,128)(2,1)}), bf16[8,224,128]{2,1,0:T(8,128)(2,1)S(1)}, u32[]{:S(2)}, u32[]{:S(2)}) %all-to-all-start.2) | async-done | bytes 458784 | tf_op jit(solution)/shard_map/all_to_all | solution.py:322
  94.4 4.1 %collective-permute-start.12 = (bf16[224,128]{1,0:T(8,128)(2,1)S(1)}, bf16[224,128]{1,0:T(8,128)(2,1)S(1)}, u32[]{:S(2)}, u32[]{:S(2)}) collective-permute-start(bf16[224,128]{1,0:T(8,128)(2,1)S(1)} %add_convert_fusion), channel_id=1, source_target_pairs={{0,192},{1,224},{2,0},{3,32},{4,64},{5,96},{6,128},{7,160},{8,200}... | collective-permute-start | bytes 172040 | tf_op jit(solution)/shard_map/ppermute | solution.py:433
  98.5 5.0 %collective-permute-start.11 = (bf16[224,128]{1,0:T(8,128)(2,1)S(1)}, bf16[224,128]{1,0:T(8,128)(2,1)S(1)}, u32[]{:S(2)}, u32[]{:S(2)}) collective-permute-start(bf16[224,128]{1,0:T(8,128)(2,1)S(1)} %add_convert_fusion), channel_id=1, source_target_pairs={{0,128},{1,160},{2,192},{3,224},{4,0},{5,32},{6,64},{7,96},{8,136}... | collective-permute-start | bytes 172040 | tf_op jit(solution)/shard_map/ppermute | solution.py:433
  103.4 2.0 collective-permute-start.10
  105.5 0.7 collective-permute-start.9
  106.2 3.0 %collective-permute-done.10 = bf16[224,128]{1,0:T(8,128)(2,1)S(1)} collective-permute-done((bf16[224,128]{1,0:T(8,128)(2,1)S(1)}, bf16[224,128]{1,0:T(8,128)(2,1)S(1)}, u32[]{:S(2)}, u32[]{:S(2)}) %collective-permute-start.10) | collective-permute-done | bytes 57376 | tf_op jit(solution)/shard_map/ppermute | solution.py:433
  109.2 10.6 %collective-permute-start.15 = (bf16[4,224,128]{2,1,0:T(8,128)(2,1)S(1)}, bf16[4,224,128]{2,1,0:T(8,128)(2,1)S(1)}, u32[]{:S(2)}, u32[]{:S(2)}) collective-permute-start(bf16[4,224,128]{2,1,0:T(8,128)(2,1)S(1)} %get-tuple-element.61), channel_id=1, source_target_pairs={{0,48},{16,0},{32,16},{48,32},{1,49},{17,1},{33,17},{49,33},{2,50}... | collective-permute-start | bytes 688136 | tf_op jit(solution)/shard_map/ppermute | solution.py:27
  119.9 0.8 collective-permute-start.13
  120.7 8.5 %collective-permute-done.15 = bf16[4,224,128]{2,1,0:T(8,128)(2,1)S(1)} collective-permute-done((bf16[4,224,128]{2,1,0:T(8,128)(2,1)S(1)}, bf16[4,224,128]{2,1,0:T(8,128)(2,1)S(1)}, u32[]{:S(2)}, u32[]{:S(2)}) %collective-permute-start.15) | collective-permute-done | bytes 229408 | tf_op jit(solution)/shard_map/ppermute | solution.py:27
  129.2 3.2 %collective-permute-done.13 = bf16[4,224,128]{2,1,0:T(8,128)(2,1)S(1)} collective-permute-done((bf16[4,224,128]{2,1,0:T(8,128)(2,1)S(1)}, bf16[4,224,128]{2,1,0:T(8,128)(2,1)S(1)}, u32[]{:S(2)}, u32[]{:S(2)}) %collective-permute-start.13) | collective-permute-done | bytes 229408 | tf_op jit(solution)/shard_map/ppermute | solution.py:27
  132.5 1.8 collective-permute-start.16
  134.3 2.1 collective-permute-done.16.other_ref
  136.4 0.9 copy-done.6
  137.3 7.8 %gate_up.1 = bf16[8,1168,128]{2,1,0:T(8,128)(2,1)} custom-call(bf16[4,4,224,128]{3,2,1,0:T(8,128)(2,1)} %copy-done.3, bf16[4,4,224,128]{3,2,1,0:T(8,128)(2,1)} %copy-done.6, f32[1,896]{1,0:T(1,128)} %broadcast_in_dim.59.gain_ref, bf16[576,896]{1,0:T(8,128)(2,1)} %bitcast.80, bf16[576,896]{1,0:T(8,128)(2,1)} %bitcast.81), custom_call_target="tpu_custom_call" | custom-call | flops 6000000000 | bytes 18000000 | tf_op jit(solution)/shard_map/gate_up/pallas_call | solution.py:303
  145.1 36.7 %all_to_all.30 = bf16[8,1168,128]{2,1,0:T(8,128)(2,1)S(1)} all-to-all(bf16[8,1168,128]{2,1,0:T(8,128)(2,1)} %gate_up.1), channel_id=1, replica_groups=mesh['zh'=4,'y'=4,'c'=2,'x'=4,'zl'=2] {'x','zl'}, dimensions={0} | all-to-all | bytes 4784128 | tf_op jit(solution)/shard_map/all_to_all | solution.py:322
  182.3 1.2 broadcast_in_dim.69
  183.5 3.6 %all-to-all-start.4 = ((bf16[8,576,128]{2,1,0:T(8,128)(2,1)}), bf16[8,576,128]{2,1,0:T(8,128)(2,1)S(1)}, u32[]{:S(2)}, u32[]{:S(2)}) async-start(bf16[8,576,128]{2,1,0:T(8,128)(2,1)} %broadcast_in_dim.69), calls=%async_computation.4 | async-start | bytes 2359296 | tf_op jit(solution)/shard_map/all_to_all | solution.py:322
  187.2 15.0 %all-to-all-done.4 = bf16[8,576,128]{2,1,0:T(8,128)(2,1)S(1)} async-done(((bf16[8,576,128]{2,1,0:T(8,128)(2,1)}), bf16[8,576,128]{2,1,0:T(8,128)(2,1)S(1)}, u32[]{:S(2)}, u32[]{:S(2)}) %all-to-all-start.4) | async-done | bytes 1179680 | tf_op jit(solution)/shard_map/all_to_all | solution.py:322
  202.2 1.9 convolution_convert_fusion
  204.2 2.8 %collective-permute-start.17 = (bf16[4,128,896]{2,1,0:T(8,128)(2,1)}, bf16[4,128,896]{2,1,0:T(8,128)(2,1)S(1)}, u32[]{:S(2)}, u32[]{:S(2)}) collective-permute-start(bf16[4,128,896]{2,1,0:T(8,128)(2,1)} %convolution_convert_fusion), channel_id=1, source_target_pairs={{0,8},{8,0},{1,9},{9,1},{2,10},{10,2},{3,11},{11,3},{4,12},{12,4},... | collective-permute-start | bytes 2752520 | tf_op jit(solution)/shard_map/ppermute | solution.py:27
  207.2 0.9 constant_dynamic-slice_fusion.3
  208.1 0.9 constant_dynamic-slice_fusion.1
  209.3 1.0 convert_add_fusion
  210.4 0.9 collective-permute-start.20
  211.3 1.6 collective-permute-start.19
  213.2 4.1 %collective-permute-done.20 = bf16[128,896]{1,0:T(8,128)(2,1)S(1)} collective-permute-done((bf16[128,896]{1,0:T(8,128)(2,1)S(1)}, bf16[128,896]{1,0:T(8,128)(2,1)S(1)}, u32[]{:S(2)}, u32[]{:S(2)}) %collective-permute-start.20) | collective-permute-done | bytes 229408 | tf_op jit(solution)/shard_map/ppermute | solution.py:27
  217.3 2.0 collective-permute-done.19
  219.3 5.9 %collective-permute-done.18 = bf16[128,896]{1,0:T(8,128)(2,1)S(1)} collective-permute-done((bf16[128,896]{1,0:T(8,128)(2,1)S(1)}, bf16[128,896]{1,0:T(8,128)(2,1)S(1)}, u32[]{:S(2)}, u32[]{:S(2)}) %collective-permute-start.18) | collective-permute-done | bytes 229408 | tf_op jit(solution)/shard_map/ppermute | solution.py:27
  225.2 1.1 fusion.1
  226.3 4.0 %all-to-all-start.5 = ((bf16[32,8,896]{2,1,0:T(8,128)(2,1)}), bf16[32,8,896]{2,1,0:T(8,128)(2,1)S(1)}, u32[]{:S(2)}, u32[]{:S(2)}) async-start(bf16[32,8,896]{2,1,0:T(8,128)(2,1)} %fusion.1), calls=%async_computation.5 | async-start | bytes 917504 | tf_op jit(solution)/shard_map/all_to_all | solution.py:322
  230.4 0.7 fusion.47
  231.1 0.7 iota_compare_fusion.9
  231.8 0.7 add_and_fusion
  232.5 15.1 %all-to-all-done.5 = bf16[32,8,896]{2,1,0:T(8,128)(2,1)S(1)} async-done(((bf16[32,8,896]{2,1,0:T(8,128)(2,1)}), bf16[32,8,896]{2,1,0:T(8,128)(2,1)S(1)}, u32[]{:S(2)}, u32[]{:S(2)}) %all-to-all-start.5) | async-done | bytes 458784 | tf_op jit(solution)/shard_map/all_to_all | solution.py:322
  247.6 0.9 fusion.2
  (97 shorter events, 5.3 us)
Async XLA Ops:
  0.0 202.2 %copy-start = (bf16[576,896]{1,0:T(8,128)(2,1)S(1)}, bf16[576,896]{1,0:T(8,128)(2,1)}, u32[]{:S(2)}) copy-start(bf16[576,896]{1,0:T(8,128)(2,1)} %param.25) | copy-start | bytes 3096580
  2.2 19.3 %collective-permute-start = (bf16[96,512]{1,0:T(8,128)(2,1)}, bf16[96,512]{1,0:T(8,128)(2,1)S(1)}, u32[]{:S(2)}, u32[]{:S(2)}) collective-permute-start(bf16[96,512]{1,0:T(8,128)(2,1)} %get-tuple-element.25), channel_id=1, source_target_pairs={{0,64},{64,128},{128,192},{192,0},{1,65},{65,129},{129,193},{193,1... | collective-permute-start | bytes 294920 | tf_op jit(solution)/shard_map/ppermute | solution.py:27
  6.1 15.5 %collective-permute-start.1 = (bf16[96,512]{1,0:T(8,128)(2,1)}, bf16[96,512]{1,0:T(8,128)(2,1)S(1)}, u32[]{:S(2)}, u32[]{:S(2)}) collective-permute-start(bf16[96,512]{1,0:T(8,128)(2,1)} %get-tuple-element.26), channel_id=1, source_target_pairs={{0,128},{64,192},{128,0},{192,64},{1,129},{65,193},{129,1},{193,65... | collective-permute-start | bytes 294920 | tf_op jit(solution)/shard_map/ppermute | solution.py:27
  11.2 9.7 %copy-start.8 = (f32[896]{0:T(1024)S(1)}, f32[896]{0:T(1024)}, u32[]{:S(2)}) copy-start(f32[896]{0:T(1024)} %param.22) | copy-start | bytes 10756
  11.2 10.4 %collective-permute-start.2 = (bf16[96,512]{1,0:T(8,128)(2,1)}, bf16[96,512]{1,0:T(8,128)(2,1)S(1)}, u32[]{:S(2)}, u32[]{:S(2)}) collective-permute-start(bf16[96,512]{1,0:T(8,128)(2,1)} %get-tuple-element.27), channel_id=1, source_target_pairs={{0,192},{64,0},{128,64},{192,128},{1,193},{65,1},{129,65},{193,129... | collective-permute-start | bytes 294920 | tf_op jit(solution)/shard_map/ppermute | solution.py:27
  17.4 13.2 %all-to-all-start = ((bf16[4,64,512]{2,1,0:T(8,128)(2,1)}), bf16[4,64,512]{2,1,0:T(8,128)(2,1)S(1)}, u32[]{:S(2)}, u32[]{:S(2)}) async-start(bf16[4,64,512]{2,1,0:T(8,128)(2,1)} %score_weights.1), calls=%async_computation | async-start | bytes 524288 | tf_op jit(solution)/shard_map/all_to_all | solution.py:322
  21.6 0.6 copy-start.10
  21.6 0.7 copy-start.11
  21.6 0.7 copy-start.12
  22.3 7.2 %copy-start.7 = (s32[32]{0:T(128)S(1)}, s32[32]{0:T(128)}, u32[]{:S(2)}) copy-start(s32[32]{0:T(128)} %counts_ref.3) | copy-start | bytes 388
  24.5 17.6 %copy-start.5 = (bf16[288,512]{1,0:T(8,128)(2,1)S(1)}, bf16[288,512]{1,0:T(8,128)(2,1)}, u32[]{:S(2)}) copy-start(bf16[288,512]{1,0:T(8,128)(2,1)} %get-tuple-element.33) | copy-start | bytes 884740
  24.5 8.5 %collective-permute-start.3 = (bf16[288,512]{1,0:T(8,128)(2,1)}, bf16[288,512]{1,0:T(8,128)(2,1)S(1)}, u32[]{:S(2)}, u32[]{:S(2)}) collective-permute-start(bf16[288,512]{1,0:T(8,128)(2,1)} %get-tuple-element.29), channel_id=1, source_target_pairs={{0,16},{16,32},{32,48},{48,0},{1,17},{17,33},{33,49},{49,1},{2,18}... | collective-permute-start | bytes 884744 | tf_op jit(solution)/shard_map/ppermute | solution.py:27
  25.8 14.7 %collective-permute-start.4 = (bf16[288,512]{1,0:T(8,128)(2,1)}, bf16[288,512]{1,0:T(8,128)(2,1)S(1)}, u32[]{:S(2)}, u32[]{:S(2)}) collective-permute-start(bf16[288,512]{1,0:T(8,128)(2,1)} %get-tuple-element.30), channel_id=1, source_target_pairs={{0,32},{16,48},{32,0},{48,16},{1,33},{17,49},{33,1},{49,17},{2,34}... | collective-permute-start | bytes 884744 | tf_op jit(solution)/shard_map/ppermute | solution.py:27
  28.4 12.5 %collective-permute-start.5 = (bf16[288,512]{1,0:T(8,128)(2,1)}, bf16[288,512]{1,0:T(8,128)(2,1)S(1)}, u32[]{:S(2)}, u32[]{:S(2)}) collective-permute-start(bf16[288,512]{1,0:T(8,128)(2,1)} %get-tuple-element.31), channel_id=1, source_target_pairs={{0,48},{16,0},{32,16},{48,32},{1,49},{17,1},{33,17},{49,33},{2,50}... | collective-permute-start | bytes 884744 | tf_op jit(solution)/shard_map/ppermute | solution.py:27
  42.2 7.9 %copy-start.1 = (bf16[1152,512]{1,0:T(8,128)(2,1)}, bf16[1152,512]{1,0:T(8,128)(2,1)S(1)}, u32[]{:S(2)}) copy-start(bf16[1152,512]{1,0:T(8,128)(2,1)S(1)} %constant_dynamic-update-slice_fusion.own_ref) | copy-start | bytes 3538948
  42.2 8.9 %collective-permute-start.6 = (bf16[1152,512]{1,0:T(8,128)(2,1)S(1)}, bf16[1152,512]{1,0:T(8,128)(2,1)S(1)}, u32[]{:S(2)}, u32[]{:S(2)}) collective-permute-start(bf16[1152,512]{1,0:T(8,128)(2,1)S(1)} %constant_dynamic-update-slice_fusion.own_ref), channel_id=1, source_target_pairs={{0,8},{8,0},{1,9},{9,1},{2,10},{10,2},{3,11},{11,3},{4,12},{12,4},... | collective-permute-start | bytes 3538952 | tf_op jit(solution)/shard_map/ppermute | solution.py:27
  45.1 19.6 %all-to-all-start.1 = ((bf16[4,4,64,512]{3,2,1,0:T(8,128)(2,1)}), bf16[4,4,64,512]{3,2,1,0:T(8,128)(2,1)}, u32[]{:S(2)}, u32[]{:S(2)}) async-start(bf16[4,4,64,512]{3,2,1,0:T(8,128)(2,1)} %broadcast_in_dim.60), calls=%async_computation.1 | async-start | bytes 2097152 | tf_op jit(solution)/shard_map/all_to_all | solution.py:322
  51.0 1.0 copy-start.2
  52.1 9.2 %copy-start.4 = (f32[512,128]{1,0:T(8,128)S(1)}, f32[512,128]{1,0:T(8,128)}, u32[]{:S(2)}) copy-start(f32[512,128]{1,0:T(8,128)} %fusion.32) | copy-start | bytes 786436
  64.7 3.3 %collective-permute-start.8 = (bf16[1024,512]{1,0:T(8,128)(2,1)}, bf16[1024,512]{1,0:T(8,128)(2,1)S(1)}, u32[]{:S(2)}, u32[]{:S(2)}) collective-permute-start(bf16[1024,512]{1,0:T(8,128)(2,1)} %bitcast.8.own_ref), channel_id=1, source_target_pairs={{0,8},{8,0},{1,9},{9,1},{2,10},{10,2},{3,11},{11,3},{4,12},{12,4},... | collective-permute-start | bytes 3145736 | tf_op jit(solution)/shard_map/ppermute | solution.py:27
  68.0 1.0 copy-start.9
  81.0 13.3 %all-to-all-start.2 = ((bf16[8,224,128]{2,1,0:T(8,128)(2,1)}), bf16[8,224,128]{2,1,0:T(8,128)(2,1)S(1)}, u32[]{:S(2)}, u32[]{:S(2)}) async-start(bf16[8,224,128]{2,1,0:T(8,128)(2,1)} %mix_project.1), calls=%async_computation.2 | async-start | bytes 917504 | tf_op jit(solution)/shard_map/all_to_all | solution.py:322
  85.4 8.9 %collective-permute-start.7 = (bf16[224,128]{1,0:T(8,128)(2,1)S(1)}, bf16[224,128]{1,0:T(8,128)(2,1)S(1)}, u32[]{:S(2)}, u32[]{:S(2)}) collective-permute-start(bf16[224,128]{1,0:T(8,128)(2,1)S(1)} %fusion.25), channel_id=1, source_target_pairs={{0,0},{1,32},{2,64},{3,96},{4,128},{5,160},{6,192},{7,224},{8,8},{... | collective-permute-start | bytes 172040 | tf_op jit(solution)/shard_map/ppermute | solution.py:416
  94.4 11.8 %collective-permute-start.12 = (bf16[224,128]{1,0:T(8,128)(2,1)S(1)}, bf16[224,128]{1,0:T(8,128)(2,1)S(1)}, u32[]{:S(2)}, u32[]{:S(2)}) collective-permute-start(bf16[224,128]{1,0:T(8,128)(2,1)S(1)} %add_convert_fusion), channel_id=1, source_target_pairs={{0,192},{1,224},{2,0},{3,32},{4,64},{5,96},{6,128},{7,160},{8,200}... | collective-permute-start | bytes 172040 | tf_op jit(solution)/shard_map/ppermute | solution.py:433
  98.5 7.7 %collective-permute-start.11 = (bf16[224,128]{1,0:T(8,128)(2,1)S(1)}, bf16[224,128]{1,0:T(8,128)(2,1)S(1)}, u32[]{:S(2)}, u32[]{:S(2)}) collective-permute-start(bf16[224,128]{1,0:T(8,128)(2,1)S(1)} %add_convert_fusion), channel_id=1, source_target_pairs={{0,128},{1,160},{2,192},{3,224},{4,0},{5,32},{6,64},{7,96},{8,136}... | collective-permute-start | bytes 172040 | tf_op jit(solution)/shard_map/ppermute | solution.py:433
  103.4 5.7 %collective-permute-start.10 = (bf16[224,128]{1,0:T(8,128)(2,1)S(1)}, bf16[224,128]{1,0:T(8,128)(2,1)S(1)}, u32[]{:S(2)}, u32[]{:S(2)}) collective-permute-start(bf16[224,128]{1,0:T(8,128)(2,1)S(1)} %add_convert_fusion), channel_id=1, source_target_pairs={{0,64},{1,96},{2,128},{3,160},{4,192},{5,224},{6,0},{7,32},{8,72},... | collective-permute-start | bytes 172040 | tf_op jit(solution)/shard_map/ppermute | solution.py:433
  105.5 3.7 %collective-permute-start.9 = (bf16[224,128]{1,0:T(8,128)(2,1)S(1)}, bf16[224,128]{1,0:T(8,128)(2,1)S(1)}, u32[]{:S(2)}, u32[]{:S(2)}) collective-permute-start(bf16[224,128]{1,0:T(8,128)(2,1)S(1)} %add_convert_fusion), channel_id=1, source_target_pairs={{0,0},{1,32},{2,64},{3,96},{4,128},{5,160},{6,192},{7,224},{8,8},{... | collective-permute-start | bytes 172040 | tf_op jit(solution)/shard_map/ppermute | solution.py:433
  109.2 19.9 %collective-permute-start.15 = (bf16[4,224,128]{2,1,0:T(8,128)(2,1)S(1)}, bf16[4,224,128]{2,1,0:T(8,128)(2,1)S(1)}, u32[]{:S(2)}, u32[]{:S(2)}) collective-permute-start(bf16[4,224,128]{2,1,0:T(8,128)(2,1)S(1)} %get-tuple-element.61), channel_id=1, source_target_pairs={{0,48},{16,0},{32,16},{48,32},{1,49},{17,1},{33,17},{49,33},{2,50}... | collective-permute-start | bytes 688136 | tf_op jit(solution)/shard_map/ppermute | solution.py:27
  119.8 9.3 %collective-permute-start.14 = (bf16[4,224,128]{2,1,0:T(8,128)(2,1)S(1)}, bf16[4,224,128]{2,1,0:T(8,128)(2,1)S(1)}, u32[]{:S(2)}, u32[]{:S(2)}) collective-permute-start(bf16[4,224,128]{2,1,0:T(8,128)(2,1)S(1)} %get-tuple-element.61), channel_id=1, source_target_pairs={{0,32},{16,48},{32,0},{48,16},{1,33},{17,49},{33,1},{49,17},{2,34}... | collective-permute-start | bytes 688136 | tf_op jit(solution)/shard_map/ppermute | solution.py:27
  119.9 12.4 %collective-permute-start.13 = (bf16[4,224,128]{2,1,0:T(8,128)(2,1)S(1)}, bf16[4,224,128]{2,1,0:T(8,128)(2,1)S(1)}, u32[]{:S(2)}, u32[]{:S(2)}) collective-permute-start(bf16[4,224,128]{2,1,0:T(8,128)(2,1)S(1)} %get-tuple-element.61), channel_id=1, source_target_pairs={{0,16},{16,32},{32,48},{48,0},{1,17},{17,33},{33,49},{49,1},{2,18}... | collective-permute-start | bytes 688136 | tf_op jit(solution)/shard_map/ppermute | solution.py:27
  132.5 3.9 %copy-start.3 = (bf16[4,4,224,128]{3,2,1,0:T(8,128)(2,1)}, bf16[4,4,224,128]{3,2,1,0:T(8,128)(2,1)S(1)}, u32[]{:S(2)}) copy-start(bf16[4,4,224,128]{3,2,1,0:T(8,128)(2,1)S(1)} %pad_maximum_fusion.own_ref) | copy-start | bytes 2752516
  132.5 3.9 %collective-permute-start.16 = (bf16[4,4,224,128]{3,2,1,0:T(8,128)(2,1)S(1)}, bf16[4,4,224,128]{3,2,1,0:T(8,128)(2,1)S(1)}, u32[]{:S(2)}, u32[]{:S(2)}) collective-permute-start(bf16[4,4,224,128]{3,2,1,0:T(8,128)(2,1)S(1)} %pad_maximum_fusion.own_ref), channel_id=1, source_target_pairs={{0,8},{8,0},{1,9},{9,1},{2,10},{10,2},{3,11},{11,3},{4,12},{12,4},... | collective-permute-start | bytes 2752520 | tf_op jit(solution)/shard_map/ppermute | solution.py:27
  136.4 0.9 copy-start.6
  183.5 18.7 %all-to-all-start.4 = ((bf16[8,576,128]{2,1,0:T(8,128)(2,1)}), bf16[8,576,128]{2,1,0:T(8,128)(2,1)S(1)}, u32[]{:S(2)}, u32[]{:S(2)}) async-start(bf16[8,576,128]{2,1,0:T(8,128)(2,1)} %broadcast_in_dim.69), calls=%async_computation.4 | async-start | bytes 2359296 | tf_op jit(solution)/shard_map/all_to_all | solution.py:322
  204.2 5.1 %collective-permute-start.17 = (bf16[4,128,896]{2,1,0:T(8,128)(2,1)}, bf16[4,128,896]{2,1,0:T(8,128)(2,1)S(1)}, u32[]{:S(2)}, u32[]{:S(2)}) collective-permute-start(bf16[4,128,896]{2,1,0:T(8,128)(2,1)} %convolution_convert_fusion), channel_id=1, source_target_pairs={{0,8},{8,0},{1,9},{9,1},{2,10},{10,2},{3,11},{11,3},{4,12},{12,4},... | collective-permute-start | bytes 2752520 | tf_op jit(solution)/shard_map/ppermute | solution.py:27
  210.4 6.9 %collective-permute-start.20 = (bf16[128,896]{1,0:T(8,128)(2,1)S(1)}, bf16[128,896]{1,0:T(8,128)(2,1)S(1)}, u32[]{:S(2)}, u32[]{:S(2)}) collective-permute-start(bf16[128,896]{1,0:T(8,128)(2,1)S(1)} %get-tuple-element.52), channel_id=1, source_target_pairs={{0,48},{16,0},{32,16},{48,32},{1,49},{17,1},{33,17},{49,33},{2,50}... | collective-permute-start | bytes 688136 | tf_op jit(solution)/shard_map/ppermute | solution.py:27
  211.3 8.0 %collective-permute-start.19 = (bf16[128,896]{1,0:T(8,128)(2,1)S(1)}, bf16[128,896]{1,0:T(8,128)(2,1)S(1)}, u32[]{:S(2)}, u32[]{:S(2)}) collective-permute-start(bf16[128,896]{1,0:T(8,128)(2,1)S(1)} %get-tuple-element.53), channel_id=1, source_target_pairs={{0,32},{16,48},{32,0},{48,16},{1,33},{17,49},{33,1},{49,17},{2,34}... | collective-permute-start | bytes 688136 | tf_op jit(solution)/shard_map/ppermute | solution.py:27
  212.9 12.4 %collective-permute-start.18 = (bf16[128,896]{1,0:T(8,128)(2,1)S(1)}, bf16[128,896]{1,0:T(8,128)(2,1)S(1)}, u32[]{:S(2)}, u32[]{:S(2)}) collective-permute-start(bf16[128,896]{1,0:T(8,128)(2,1)S(1)} %get-tuple-element.51), channel_id=1, source_target_pairs={{0,16},{16,32},{32,48},{48,0},{1,17},{17,33},{33,49},{49,1},{2,18}... | collective-permute-start | bytes 688136 | tf_op jit(solution)/shard_map/ppermute | solution.py:27
  226.3 21.2 %all-to-all-start.5 = ((bf16[32,8,896]{2,1,0:T(8,128)(2,1)}), bf16[32,8,896]{2,1,0:T(8,128)(2,1)S(1)}, u32[]{:S(2)}, u32[]{:S(2)}) async-start(bf16[32,8,896]{2,1,0:T(8,128)(2,1)} %fusion.1), calls=%async_computation.5 | async-start | bytes 917504 | tf_op jit(solution)/shard_map/all_to_all | solution.py:322

commit v7 on v6

--- a/solution.py
+++ b/solution.py
@@ -1,3 +1,5 @@
+import functools
+
 import jax
 import jax.numpy as jnp
 from jax import lax
@@ -192,6 +194,7 @@
         in_specs=[whole(a.shape) for a in (goes, own, other, up)],
         out_specs=pl.BlockSpec((STEP, width), lambda b: (b, 0)),
         cost_estimate=cost(0),
+        compiler_params=pltpu.CompilerParams(vmem_limit_bytes=24 * 2**20),
         name="live_values",
     )(goes, own, other, up)
 
@@ -262,60 +265,65 @@
         out_specs=whole(shape),
         scratch_shapes=[pltpu.VMEM((STEP, width), BF), pltpu.VMEM((8, LIVE // 8, n), F32)],
         cost_estimate=cost(9),
+        compiler_params=pltpu.CompilerParams(vmem_limit_bytes=50 * 2**20),
         name="mix_project",
     )(goes, own, other, values, values, wo)
 
 
-def gate_up_kernel(own_ref, other_ref, gain_ref, gate_ref, up_ref, out_ref, x_ref, gain_at):
+def gate_up_kernel(steps, own_ref, other_ref, gain_ref, gate_ref, up_ref, *refs):
+    outs, x_ref = refs[:-1], refs[-1]
     core, y = lax.axis_index("c"), lax.axis_index("y")
-    b = pl.program_id(0)
-    blocks = out_ref.shape[0]
-    _, planes, k, chunk = own_ref.shape
+    x_at, zl = lax.axis_index("x"), lax.axis_index("zl")
+    k, chunk = own_ref.shape[2:]
     ff = gate_ref.shape[0]
-    steps = planes // blocks
-    high, first = b // steps, (b % steps) * blocks
-    squares = jnp.zeros((1, blocks * chunk), F32)
-    gain_at[...] = jnp.broadcast_to(gain_ref[...], (8, gain_ref.shape[1])).T
-    for ref, flip in ((own_ref, core), (other_ref, 1 - core)):
+    gain = jnp.broadcast_to(gain_ref[...], (8, gain_ref.shape[1])).T
+    x_ref[:, :8] = gain.astype(F32)
+    squares = []
+    scaled = []
+    for dx, dz in steps:
+        spot = ((x_at + dx) & 3) * 2 + (zl ^ dz)
+        total = jnp.zeros((1, chunk), F32)
         for low in range(2):
-            rows = pl.ds(pl.multiple_of((low * 2 + flip) * k, 32), k)
-            s = (y - high * 2 - low) & 3
-            x = jnp.concatenate([ref[s, first + i] for i in range(blocks)], axis=1).astype(F32)
-            squares = squares + jnp.sum(x * x, axis=0, keepdims=True)
-            x_ref[rows, :] = (x * gain_at[rows, :1]).astype(BF)
-    x = x_ref[...]
+            s = (y - (spot >> 2) * 2 - low) & 3
+            one, two = own_ref[s, spot & 3], other_ref[s, spot & 3]
+            for half in range(2):
+                x = jnp.where(core == half, one, two).astype(F32)
+                total = total + jnp.sum(x * x, axis=0, keepdims=True)
+                rows = slice((low * 2 + half) * k, (low * 2 + half + 1) * k)
+                scaled.append((x * x_ref[rows, :1]).astype(BF))
+        squares.append(total)
+    columns = [
+        jnp.concatenate(scaled[4 * i : 4 * i + 4], axis=0) for i in range(len(steps))
+    ]
+    x = jnp.concatenate(columns, axis=1)
     gate = dot(gate_ref[...], x).astype(BF)
     up = dot(up_ref[...], x).astype(BF)
-    row = iota((16, blocks * chunk), 0)
-    high = squares.astype(BF).astype(F32)
-    extra = jnp.where(row == 0, high, jnp.where(row == 1, squares - high, 0.0)).astype(BF)
-    for i in range(blocks):
+    row = iota((16, chunk), 0)
+    for i, out_ref in enumerate(outs):
         cols = slice(i * chunk, (i + 1) * chunk)
-        out_ref[i, :ff, :] = gate[:, cols]
-        out_ref[i, ff : 2 * ff, :] = up[:, cols]
-        out_ref[i, 2 * ff :, :] = extra[:, cols]
-
-
-def gate_up(own, other, gain, gate_weight, up_weight):
-    _, planes, k, chunk = own.shape
+        high = squares[i].astype(BF).astype(F32)
+        extra = jnp.where(row == 0, high, jnp.where(row == 1, squares[i] - high, 0.0))
+        out_ref[:ff, :] = gate[:, cols]
+        out_ref[ff : 2 * ff, :] = up[:, cols]
+        out_ref[2 * ff :, :] = extra.astype(BF)
+
+
+def gate_up(steps, own, other, gain, gate_weight, up_weight):
+    k, chunk = own.shape[2:]
     ff, width = gate_weight.shape
-    blocks = 2
+    shape = (2 * ff + 16, chunk)
+    arrays = (own, other, gain, gate_weight, up_weight)
     return pl.pallas_call(
-        gate_up_kernel,
-        grid=(2 * planes // blocks,),
-        out_shape=jax.ShapeDtypeStruct((2 * planes, 2 * ff + 16, chunk), BF),
-        in_specs=[
-            whole(own.shape),
-            whole(own.shape),
-            whole((1, width)),
-            whole((ff, width)),
-            whole((ff, width)),
-        ],
-        out_specs=pl.BlockSpec((blocks, 2 * ff + 16, chunk), lambda b: (b, 0, 0)),
-        scratch_shapes=[pltpu.VMEM((width, blocks * chunk), BF), pltpu.VMEM((width, 8), F32)],
-        cost_estimate=cost(6),
+        functools.partial(gate_up_kernel, steps),
+        grid=(1,),
+        out_shape=[jax.ShapeDtypeStruct(shape, BF)] * len(steps),
+        in_specs=[whole(a.shape) for a in arrays],
+        out_specs=[whole(shape)] * len(steps),
+        scratch_shapes=[pltpu.VMEM((width, BLK), F32)],
+        cost_estimate=cost(4),
+        compiler_params=pltpu.CompilerParams(vmem_limit_bytes=24 * 2**20),
         name="gate_up",
-    )(own, other, gain, gate_weight, up_weight)
+    )(*arrays)
 
 
 def exchange(x, axes):
@@ -436,8 +444,14 @@
     full = jnp.stack([full] + [shifted(full, "y", s) for s in (1, 2, 3)])
     full_other = shifted(full, "c", 1)
     ff = down_weight.shape[0]
-    part = gate_up(full, full_other, gain, gate_weight.T, up_weight.T)
-    total = jnp.sum(exchange(part, HD).astype(F32), axis=0)
+    arrays = (full, full_other, gain, gate_weight.T, up_weight.T)
+    near = [(0, 0), (1, 0), (3, 0), (2, 0)]
+    far = [(0, 1), (1, 1), (3, 1), (2, 1)]
+    parts = list(zip(near, gate_up(near, *arrays))) + list(zip(far, gate_up(far, *arrays)))
+    total = parts[0][1].astype(F32)
+    for (dx, dz), part in parts[1:]:
+        sends = [(i, ((i // 2 + dx) % 4) * 2 + ((i % 2) ^ dz)) for i in range(8)]
+        total = total + lax.ppermute(part, HD, sends).astype(F32)
     scale = lax.rsqrt((total[2 * ff : 2 * ff + 1] + total[2 * ff + 1 : 2 * ff + 2]) / model + 1e-06)
     hidden = (jax.nn.silu(total[:ff] * scale) * (total[ff : 2 * ff] * scale)).astype(BF)
     hidden = gather(hidden, HD).reshape(4, 2, ff, chunk)

time: 249 us -> 242 us (0.972)
  blocking collectives: 36.7 us -> 0 us
  waiting for transfers between devices: 82.3 us -> 108 us
  starting transfers between devices: 69.9 us -> 81.6 us
  Pallas kernels: 37.2 us -> 29.1 us
    all_to_all x1 -> x0, blocking collectives: 36.7 us -> none  [exchange(): return lax.all_to_all(x, axes, split_axis=0, concat_axis=0, tiled=True)]
    ppermute x0 -> x7, waiting for transfers between devices: none -> 19.6 us  [on_device(): total = total + lax.ppermute(part, HD, sends).astype(F32)]
    ppermute x0 -> x7, starting transfers between devices: none -> 12.5 us  [on_device(): total = total + lax.ppermute(part, HD, sends).astype(F32)]
    pallas_call x1 -> x2, Pallas kernels: 7.79 us -> 3.48 us  [gate_up(): pl.pallas_call(functools.partial(gate_up_kernel, steps), grid=(1,), out_s...]
    all_to_all x5, waiting for transfers between devices: 41.4 us -> 45 us  [exchange(): return lax.all_to_all(x, axes, split_axis=0, concat_axis=0, tiled=True)]
    pallas_call x1, Pallas kernels: 9.24 us -> 5.88 us  [live_values(): pl.pallas_call(values_kernel, grid=(LIVE // STEP,), out_shape=jax.ShapeDt...]
    ppermute x16, waiting for transfers between devices: 37.8 us -> 40.8 us  [shifted(): return lax.ppermute(x, axis, [(i, (i + shift) % n) for i in range(n)])]
    unnamed x29 -> x27, local copies, waits for them, and re-layouts: 3.75 us -> 5.47 us
  transfers between devices with their start and end apart: 26 -> 33, of which waited for: 16 -> 23; matrix products, arithmetic and copies ran while one was open for 4% -> 2% of each run, Pallas kernels for 6% -> 6%
where the time goes in v7:
time: 242 us; the launch traced here: 241 us
  waiting for transfers between devices  108 us (45%)
  starting transfers between devices  81.6 us (34%)
  Pallas kernels  29.1 us (12%)
  local copies, waits for them, and re-layouts  9.52 us (4%)
  matrix products  8.08 us (3%)
  other arithmetic  3.95 us (2%)
    all_to_all x5, waiting for transfers between devices, exchange(): return lax.all_to_all(x, axes, split_axis=0, concat_axis=0, tiled=True)  45 us
    ppermute x16, waiting for transfers between devices, shifted(): return lax.ppermute(x, axis, [(i, (i + shift) % n) for i in range(n)])  40.8 us
    ppermute x16, starting transfers between devices, shifted(): return lax.ppermute(x, axis, [(i, (i + shift) % n) for i in range(n)])  36.1 us
    all_to_all x5, starting transfers between devices, exchange(): return lax.all_to_all(x, axes, split_axis=0, concat_axis=0, tiled=True)  20.6 us
    ppermute x7, waiting for transfers between devices, on_device(): total = total + lax.ppermute(part, HD, sends).astype(F32)  19.6 us
    ppermute x7, starting transfers between devices, on_device(): total = total + lax.ppermute(part, HD, sends).astype(F32)  12.5 us
    ppermute x4, starting transfers between devices, on_device(): full.append(lax.ppermute(mixed, DP + HD, sends))  11.8 us
    pallas_call x1, Pallas kernels, mix_project(): pl.pallas_call(mix_kernel, grid=(LIVE // STEP,), out_shape=jax.ShapeDtype...  11.5 us
  transfers between devices with their start and end apart: 33, of which 23 were waited for; matrix products, arithmetic and copies ran while one was open for 2% of the time, Pallas kernels for 6%

profile of v7, /device:TPU:1, one launch (start us, length us, event | category | flops | bytes accessed | tf_op | source)
XLA Modules:
  0.0 241.2 jit_solution(7931416070110659785)
XLA Ops:
  0.0 2.2 pack.1
  2.2 3.8 %collective-permute-start = (bf16[96,512]{1,0:T(8,128)(2,1)}, bf16[96,512]{1,0:T(8,128)(2,1)S(1)}, u32[]{:S(2)}, u32[]{:S(2)}) collective-permute-start(bf16[96,512]{1,0:T(8,128)(2,1)} %get-tuple-element.33), channel_id=1, source_target_pairs={{0,64},{64,128},{128,192},{192,0},{1,65},{65,129},{129,193},{193,1... | collective-permute-start | bytes 294920 | tf_op jit(solution)/shard_map/ppermute | solution.py:29
  6.1 5.1 %collective-permute-start.1 = (bf16[96,512]{1,0:T(8,128)(2,1)}, bf16[96,512]{1,0:T(8,128)(2,1)S(1)}, u32[]{:S(2)}, u32[]{:S(2)}) collective-permute-start(bf16[96,512]{1,0:T(8,128)(2,1)} %get-tuple-element.34), channel_id=1, source_target_pairs={{0,128},{64,192},{128,0},{192,64},{1,129},{65,193},{129,1},{193,65... | collective-permute-start | bytes 294920 | tf_op jit(solution)/shard_map/ppermute | solution.py:29
  11.2 2.4 collective-permute-start.2
  13.5 3.8 %score_weights.1 = bf16[4,64,512]{2,1,0:T(8,128)(2,1)} custom-call(s32[32]{0:T(128)} %counts_ref.3, bf16[64,2048]{1,0:T(8,128)(2,1)} %qn_ref.1, bf16[64,1024]{1,0:T(8,128)(2,1)} %qr_ref.1, bf16[64,512]{1,0:T(8,128)(2,1)} %lat_ref.3, bf16[64,64]{1,0:T(8,128)(2,1)} %kr_ref.1, bf16[512,2048]{1,0:T(8,128)(2,1)} %ku_ref.1, s32[1,64]{1,0:T(1,128)} %req_ref.1), custom_call_target="tpu_custom_call" | custom-call | flops 4000000000 | bytes 12000000 | tf_op jit(solution)/shard_map/score_weights/pallas_call | solution.py:165
  17.4 3.4 %all-to-all-start = ((bf16[4,64,512]{2,1,0:T(8,128)(2,1)}), bf16[4,64,512]{2,1,0:T(8,128)(2,1)S(1)}, u32[]{:S(2)}, u32[]{:S(2)}) async-start(bf16[4,64,512]{2,1,0:T(8,128)(2,1)} %score_weights.1), calls=%async_computation | async-start | bytes 524288 | tf_op jit(solution)/shard_map/all_to_all | solution.py:330
  22.1 2.2 repack.1
  24.3 1.3 collective-permute-start.3
  25.6 2.6 %collective-permute-start.4 = (bf16[288,512]{1,0:T(8,128)(2,1)}, bf16[288,512]{1,0:T(8,128)(2,1)S(1)}, u32[]{:S(2)}, u32[]{:S(2)}) collective-permute-start(bf16[288,512]{1,0:T(8,128)(2,1)} %get-tuple-element.38), channel_id=1, source_target_pairs={{0,32},{16,48},{32,0},{48,16},{1,33},{17,49},{33,1},{49,17},{2,34}... | collective-permute-start | bytes 884744 | tf_op jit(solution)/shard_map/ppermute | solution.py:29
  28.2 1.1 collective-permute-start.5
  29.4 0.7 select_reduce_fusion.3
  30.5 2.8 %collective-permute-done.3 = bf16[288,512]{1,0:T(8,128)(2,1)S(1)} collective-permute-done((bf16[288,512]{1,0:T(8,128)(2,1)}, bf16[288,512]{1,0:T(8,128)(2,1)S(1)}, u32[]{:S(2)}, u32[]{:S(2)}) %collective-permute-start.3) | collective-permute-done | bytes 294944 | tf_op jit(solution)/shard_map/ppermute | solution.py:29
  33.2 7.4 %collective-permute-done.4 = bf16[288,512]{1,0:T(8,128)(2,1)S(1)} collective-permute-done((bf16[288,512]{1,0:T(8,128)(2,1)}, bf16[288,512]{1,0:T(8,128)(2,1)S(1)}, u32[]{:S(2)}, u32[]{:S(2)}) %collective-permute-start.4) | collective-permute-done | bytes 294944 | tf_op jit(solution)/shard_map/ppermute | solution.py:29
  40.8 1.1 broadcast_in_dim.60
  42.0 2.0 collective-permute-start.6
  44.9 4.3 %all-to-all-start.1 = ((bf16[4,4,64,512]{3,2,1,0:T(8,128)(2,1)}), bf16[4,4,64,512]{3,2,1,0:T(8,128)(2,1)}, u32[]{:S(2)}, u32[]{:S(2)}) async-start(bf16[4,4,64,512]{3,2,1,0:T(8,128)(2,1)} %broadcast_in_dim.60), calls=%async_computation.1 | async-start | bytes 2097152 | tf_op jit(solution)/shard_map/all_to_all | solution.py:330
  49.6 1.6 copy-done.2
  51.1 5.9 %live_values.1.prev_ref.cur_ref = bf16[1024,2048]{1,0:T(8,128)(2,1)S(1)} custom-call(s32[2,1,1152]{2,1,0:T(1,128)S(1)} %reshape.474.goes_ref, bf16[1152,512]{1,0:T(8,128)(2,1)S(1)} %constant_dynamic-update-slice_fusion.own_ref, bf16[1152,512]{1,0:T(8,128)(2,1)S(1)} %collective-permute-done.6.other_ref, bf16[512,2048]{1,0:T(8,128)(2,1)S(1)} %copy-done.2), custom_call_target="tpu_custom_call" | custom-call | tf_op jit(solution)/shard_map/live_values/pallas_call | solution.py:190
  57.0 2.0 copy-done.1
  59.3 5.2 %all-to-all-done.1 = bf16[4,4,64,512]{3,2,1,0:T(8,128)(2,1)} async-done(((bf16[4,4,64,512]{3,2,1,0:T(8,128)(2,1)}), bf16[4,4,64,512]{3,2,1,0:T(8,128)(2,1)}, u32[]{:S(2)}, u32[]{:S(2)}) %all-to-all-start.1) | async-done | bytes 1048608 | tf_op jit(solution)/shard_map/all_to_all | solution.py:330
  64.5 0.8 collective-permute-start.8
  65.7 2.1 collective-permute-done.8.other_ref
  67.8 1.2 copy-done.5
  69.0 11.5 %mix_project.1 = bf16[8,224,128]{2,1,0:T(8,128)(2,1)} custom-call(s32[2,1,1024]{2,1,0:T(1,128)S(1)} %compare_select_fusion.goes_ref, bf16[1024,512]{1,0:T(8,128)(2,1)} %bitcast.8.own_ref, bf16[1024,512]{1,0:T(8,128)(2,1)S(1)} %collective-permute-done.8.other_ref, bf16[1024,2048]{1,0:T(8,128)(2,1)} %copy-done.1, bf16[1024,2048]{1,0:T(8,128)(2,1)} %copy-done.1, ...), custom_call_target="tpu_custom_call" | custom-call | flops 8999999488 | bytes 27000000 | tf_op jit(solution)/shard_map/mix_project/pallas_call | solution.py:253
  80.4 4.1 %all-to-all-start.2 = ((bf16[8,224,128]{2,1,0:T(8,128)(2,1)}), bf16[8,224,128]{2,1,0:T(8,128)(2,1)S(1)}, u32[]{:S(2)}, u32[]{:S(2)}) async-start(bf16[8,224,128]{2,1,0:T(8,128)(2,1)} %mix_project.1), calls=%async_computation.2 | async-start | bytes 917504 | tf_op jit(solution)/shard_map/all_to_all | solution.py:330
  84.5 0.7 collective-permute-start.7
  85.2 8.1 %all-to-all-done.2 = bf16[8,224,128]{2,1,0:T(8,128)(2,1)S(1)} async-done(((bf16[8,224,128]{2,1,0:T(8,128)(2,1)}), bf16[8,224,128]{2,1,0:T(8,128)(2,1)S(1)}, u32[]{:S(2)}, u32[]{:S(2)}) %all-to-all-start.2) | async-done | bytes 458784 | tf_op jit(solution)/shard_map/all_to_all | solution.py:330
  93.4 4.1 %collective-permute-start.12 = (bf16[224,128]{1,0:T(8,128)(2,1)S(1)}, bf16[224,128]{1,0:T(8,128)(2,1)S(1)}, u32[]{:S(2)}, u32[]{:S(2)}) collective-permute-start(bf16[224,128]{1,0:T(8,128)(2,1)S(1)} %add_convert_fusion), channel_id=1, source_target_pairs={{0,192},{1,224},{2,0},{3,32},{4,64},{5,96},{6,128},{7,160},{8,200}... | collective-permute-start | bytes 172040 | tf_op jit(solution)/shard_map/ppermute | solution.py:441
  97.5 5.0 %collective-permute-start.11 = (bf16[224,128]{1,0:T(8,128)(2,1)S(1)}, bf16[224,128]{1,0:T(8,128)(2,1)S(1)}, u32[]{:S(2)}, u32[]{:S(2)}) collective-permute-start(bf16[224,128]{1,0:T(8,128)(2,1)S(1)} %add_convert_fusion), channel_id=1, source_target_pairs={{0,128},{1,160},{2,192},{3,224},{4,0},{5,32},{6,64},{7,96},{8,136}... | collective-permute-start | bytes 172040 | tf_op jit(solution)/shard_map/ppermute | solution.py:441
  102.5 2.0 collective-permute-start.10
  104.5 0.7 collective-permute-start.9
  105.2 3.0 %collective-permute-done.10 = bf16[224,128]{1,0:T(8,128)(2,1)S(1)} collective-permute-done((bf16[224,128]{1,0:T(8,128)(2,1)S(1)}, bf16[224,128]{1,0:T(8,128)(2,1)S(1)}, u32[]{:S(2)}, u32[]{:S(2)}) %collective-permute-start.10) | collective-permute-done | bytes 57376 | tf_op jit(solution)/shard_map/ppermute | solution.py:441
  108.3 10.6 %collective-permute-start.15 = (bf16[4,224,128]{2,1,0:T(8,128)(2,1)S(1)}, bf16[4,224,128]{2,1,0:T(8,128)(2,1)S(1)}, u32[]{:S(2)}, u32[]{:S(2)}) collective-permute-start(bf16[4,224,128]{2,1,0:T(8,128)(2,1)S(1)} %get-tuple-element.77), channel_id=1, source_target_pairs={{0,48},{16,0},{32,16},{48,32},{1,49},{17,1},{33,17},{49,33},{2,50}... | collective-permute-start | bytes 688136 | tf_op jit(solution)/shard_map/ppermute | solution.py:29
  119.0 0.8 collective-permute-start.13
  119.8 8.4 %collective-permute-done.15 = bf16[4,224,128]{2,1,0:T(8,128)(2,1)S(1)} collective-permute-done((bf16[4,224,128]{2,1,0:T(8,128)(2,1)S(1)}, bf16[4,224,128]{2,1,0:T(8,128)(2,1)S(1)}, u32[]{:S(2)}, u32[]{:S(2)}) %collective-permute-start.15) | collective-permute-done | bytes 229408 | tf_op jit(solution)/shard_map/ppermute | solution.py:29
  128.2 3.2 %collective-permute-done.13 = bf16[4,224,128]{2,1,0:T(8,128)(2,1)S(1)} collective-permute-done((bf16[4,224,128]{2,1,0:T(8,128)(2,1)S(1)}, bf16[4,224,128]{2,1,0:T(8,128)(2,1)S(1)}, u32[]{:S(2)}, u32[]{:S(2)}) %collective-permute-start.13) | collective-permute-done | bytes 229408 | tf_op jit(solution)/shard_map/ppermute | solution.py:29
  131.6 1.8 collective-permute-start.16
  133.4 2.1 collective-permute-done.16.other_ref
  135.5 1.7 gate_up.3
  137.2 5.9 %collective-permute-start.23 = (bf16[1168,128]{1,0:T(8,128)(2,1)S(1)}, bf16[1168,128]{1,0:T(8,128)(2,1)S(1)}, u32[]{:S(2)}, u32[]{:S(2)}) collective-permute-start(bf16[1168,128]{1,0:T(8,128)(2,1)S(1)} %get-tuple-element.58), channel_id=1, source_target_pairs={{0,5},{1,4},{2,7},{3,6},{4,1},{5,0},{6,3},{7,2},{8,13},{9,12},{10,... | collective-permute-start | bytes 897032 | tf_op jit(solution)/shard_map/ppermute | solution.py:454
  143.7 1.7 collective-permute-start.21
  145.9 1.7 gate_up.2
  147.7 2.5 %collective-permute-done.23 = bf16[1168,128]{1,0:T(8,128)(2,1)S(1)} collective-permute-done((bf16[1168,128]{1,0:T(8,128)(2,1)S(1)}, bf16[1168,128]{1,0:T(8,128)(2,1)S(1)}, u32[]{:S(2)}, u32[]{:S(2)}) %collective-permute-start.23) | collective-permute-done | bytes 299040 | tf_op jit(solution)/shard_map/ppermute | solution.py:454
  150.3 2.8 %collective-permute-start.18 = (bf16[1168,128]{1,0:T(8,128)(2,1)S(1)}, bf16[1168,128]{1,0:T(8,128)(2,1)S(1)}, u32[]{:S(2)}, u32[]{:S(2)}) collective-permute-start(bf16[1168,128]{1,0:T(8,128)(2,1)S(1)} %get-tuple-element.53), channel_id=1, source_target_pairs={{0,6},{1,7},{2,0},{3,1},{4,2},{5,3},{6,4},{7,5},{8,14},{9,15},{10,... | collective-permute-start | bytes 897032 | tf_op jit(solution)/shard_map/ppermute | solution.py:454
  153.1 4.1 %collective-permute-done.22 = bf16[1168,128]{1,0:T(8,128)(2,1)S(1)} collective-permute-done((bf16[1168,128]{1,0:T(8,128)(2,1)S(1)}, bf16[1168,128]{1,0:T(8,128)(2,1)S(1)}, u32[]{:S(2)}, u32[]{:S(2)}) %collective-permute-start.22) | collective-permute-done | bytes 299040 | tf_op jit(solution)/shard_map/ppermute | solution.py:454
  157.2 0.9 collective-permute-start.17
  158.0 5.9 %collective-permute-done.21 = bf16[1168,128]{1,0:T(8,128)(2,1)S(1)} collective-permute-done((bf16[1168,128]{1,0:T(8,128)(2,1)S(1)}, bf16[1168,128]{1,0:T(8,128)(2,1)S(1)}, u32[]{:S(2)}, u32[]{:S(2)}) %collective-permute-start.21) | collective-permute-done | bytes 299040 | tf_op jit(solution)/shard_map/ppermute | solution.py:454
  164.0 6.2 %collective-permute-done.20 = bf16[1168,128]{1,0:T(8,128)(2,1)S(1)} collective-permute-done((bf16[1168,128]{1,0:T(8,128)(2,1)S(1)}, bf16[1168,128]{1,0:T(8,128)(2,1)S(1)}, u32[]{:S(2)}, u32[]{:S(2)}) %collective-permute-start.20) | collective-permute-done | bytes 299040 | tf_op jit(solution)/shard_map/ppermute | solution.py:454
  171.5 1.2 broadcast_in_dim.69
  172.6 4.5 %all-to-all-start.3 = ((bf16[8,576,128]{2,1,0:T(8,128)(2,1)}), bf16[8,576,128]{2,1,0:T(8,128)(2,1)}, u32[]{:S(2)}, u32[]{:S(2)}) async-start(bf16[8,576,128]{2,1,0:T(8,128)(2,1)} %broadcast_in_dim.69), calls=%async_computation.3 | async-start | bytes 2359296 | tf_op jit(solution)/shard_map/all_to_all | solution.py:330
  177.2 16.3 %all-to-all-done.3 = bf16[8,576,128]{2,1,0:T(8,128)(2,1)} async-done(((bf16[8,576,128]{2,1,0:T(8,128)(2,1)}), bf16[8,576,128]{2,1,0:T(8,128)(2,1)}, u32[]{:S(2)}, u32[]{:S(2)}) %all-to-all-start.3) | async-done | bytes 1179680 | tf_op jit(solution)/shard_map/all_to_all | solution.py:330
  193.6 3.0 %convolution_convert_fusion = bf16[4,128,896]{2,1,0:T(8,128)(2,1)} fusion(bf16[576,896]{1,0:T(8,128)(2,1)S(1)} %copy-done, bf16[4,2,576,128]{3,2,1,0:T(8,128)(2,1)} %bitcast.21, s32[]{:T(128)S(6)} %select_n.153), kind=kOutput, calls=%fused_computation.1 | convolution fusion | flops 528941056 | bytes 2539524 | tf_op jit(solution)/shard_map/dot_general | solution.py:461
  196.6 1.4 collective-permute-start.24
  198.3 2.1 collective-permute-done.24
  200.4 2.3 convert_add_fusion
  202.9 0.7 collective-permute-start.27
  203.6 1.5 collective-permute-start.26
  205.5 4.3 %collective-permute-done.27 = bf16[128,896]{1,0:T(8,128)(2,1)S(1)} collective-permute-done((bf16[128,896]{1,0:T(8,128)(2,1)S(1)}, bf16[128,896]{1,0:T(8,128)(2,1)S(1)}, u32[]{:S(2)}, u32[]{:S(2)}) %collective-permute-start.27) | collective-permute-done | bytes 229408 | tf_op jit(solution)/shard_map/ppermute | solution.py:29
  209.8 1.9 collective-permute-done.26
  211.7 5.9 %collective-permute-done.25 = bf16[128,896]{1,0:T(8,128)(2,1)S(1)} collective-permute-done((bf16[128,896]{1,0:T(8,128)(2,1)S(1)}, bf16[128,896]{1,0:T(8,128)(2,1)S(1)}, u32[]{:S(2)}, u32[]{:S(2)}) %collective-permute-start.25) | collective-permute-done | bytes 229408 | tf_op jit(solution)/shard_map/ppermute | solution.py:29
  217.6 1.1 fusion.1
  218.7 4.4 %all-to-all-start.4 = ((bf16[32,8,896]{2,1,0:T(8,128)(2,1)}), bf16[32,8,896]{2,1,0:T(8,128)(2,1)S(1)}, u32[]{:S(2)}, u32[]{:S(2)}) async-start(bf16[32,8,896]{2,1,0:T(8,128)(2,1)} %fusion.1), calls=%async_computation.4 | async-start | bytes 917504 | tf_op jit(solution)/shard_map/all_to_all | solution.py:330
  225.0 15.3 %all-to-all-done.4 = bf16[32,8,896]{2,1,0:T(8,128)(2,1)S(1)} async-done(((bf16[32,8,896]{2,1,0:T(8,128)(2,1)}), bf16[32,8,896]{2,1,0:T(8,128)(2,1)S(1)}, u32[]{:S(2)}, u32[]{:S(2)}) %all-to-all-start.4) | async-done | bytes 458784 | tf_op jit(solution)/shard_map/all_to_all | solution.py:330
  240.3 0.9 fusion.2
  (109 shorter events, 9.3 us)
Async XLA Ops:
  0.0 193.6 %copy-start = (bf16[576,896]{1,0:T(8,128)(2,1)S(1)}, bf16[576,896]{1,0:T(8,128)(2,1)}, u32[]{:S(2)}) copy-start(bf16[576,896]{1,0:T(8,128)(2,1)} %param.25) | copy-start | bytes 3096580
  2.2 18.8 %collective-permute-start = (bf16[96,512]{1,0:T(8,128)(2,1)}, bf16[96,512]{1,0:T(8,128)(2,1)S(1)}, u32[]{:S(2)}, u32[]{:S(2)}) collective-permute-start(bf16[96,512]{1,0:T(8,128)(2,1)} %get-tuple-element.33), channel_id=1, source_target_pairs={{0,64},{64,128},{128,192},{192,0},{1,65},{65,129},{129,193},{193,1... | collective-permute-start | bytes 294920 | tf_op jit(solution)/shard_map/ppermute | solution.py:29
  6.1 14.9 %collective-permute-start.1 = (bf16[96,512]{1,0:T(8,128)(2,1)}, bf16[96,512]{1,0:T(8,128)(2,1)S(1)}, u32[]{:S(2)}, u32[]{:S(2)}) collective-permute-start(bf16[96,512]{1,0:T(8,128)(2,1)} %get-tuple-element.34), channel_id=1, source_target_pairs={{0,128},{64,192},{128,0},{192,64},{1,129},{65,193},{129,1},{193,65... | collective-permute-start | bytes 294920 | tf_op jit(solution)/shard_map/ppermute | solution.py:29
  11.2 9.7 %copy-start.8 = (f32[896]{0:T(1024)S(1)}, f32[896]{0:T(1024)}, u32[]{:S(2)}) copy-start(f32[896]{0:T(1024)} %param.22) | copy-start | bytes 10756
  11.2 10.3 %collective-permute-start.2 = (bf16[96,512]{1,0:T(8,128)(2,1)}, bf16[96,512]{1,0:T(8,128)(2,1)S(1)}, u32[]{:S(2)}, u32[]{:S(2)}) collective-permute-start(bf16[96,512]{1,0:T(8,128)(2,1)} %get-tuple-element.35), channel_id=1, source_target_pairs={{0,192},{64,0},{128,64},{192,128},{1,193},{65,1},{129,65},{193,129... | collective-permute-start | bytes 294920 | tf_op jit(solution)/shard_map/ppermute | solution.py:29
  17.4 13.1 %all-to-all-start = ((bf16[4,64,512]{2,1,0:T(8,128)(2,1)}), bf16[4,64,512]{2,1,0:T(8,128)(2,1)S(1)}, u32[]{:S(2)}, u32[]{:S(2)}) async-start(bf16[4,64,512]{2,1,0:T(8,128)(2,1)} %score_weights.1), calls=%async_computation | async-start | bytes 524288 | tf_op jit(solution)/shard_map/all_to_all | solution.py:330
  21.0 0.6 copy-start.9
  21.0 0.7 copy-start.10
  21.5 0.6 copy-start.11
  22.1 7.2 %copy-start.7 = (s32[32]{0:T(128)S(1)}, s32[32]{0:T(128)}, u32[]{:S(2)}) copy-start(s32[32]{0:T(128)} %counts_ref.3) | copy-start | bytes 388
  24.3 17.6 %copy-start.6 = (bf16[288,512]{1,0:T(8,128)(2,1)S(1)}, bf16[288,512]{1,0:T(8,128)(2,1)}, u32[]{:S(2)}) copy-start(bf16[288,512]{1,0:T(8,128)(2,1)} %get-tuple-element.41) | copy-start | bytes 884740
  24.3 8.9 %collective-permute-start.3 = (bf16[288,512]{1,0:T(8,128)(2,1)}, bf16[288,512]{1,0:T(8,128)(2,1)S(1)}, u32[]{:S(2)}, u32[]{:S(2)}) collective-permute-start(bf16[288,512]{1,0:T(8,128)(2,1)} %get-tuple-element.37), channel_id=1, source_target_pairs={{0,16},{16,32},{32,48},{48,0},{1,17},{17,33},{33,49},{49,1},{2,18}... | collective-permute-start | bytes 884744 | tf_op jit(solution)/shard_map/ppermute | solution.py:29
  25.6 15.1 %collective-permute-start.4 = (bf16[288,512]{1,0:T(8,128)(2,1)}, bf16[288,512]{1,0:T(8,128)(2,1)S(1)}, u32[]{:S(2)}, u32[]{:S(2)}) collective-permute-start(bf16[288,512]{1,0:T(8,128)(2,1)} %get-tuple-element.38), channel_id=1, source_target_pairs={{0,32},{16,48},{32,0},{48,16},{1,33},{17,49},{33,1},{49,17},{2,34}... | collective-permute-start | bytes 884744 | tf_op jit(solution)/shard_map/ppermute | solution.py:29
  28.2 12.6 %collective-permute-start.5 = (bf16[288,512]{1,0:T(8,128)(2,1)}, bf16[288,512]{1,0:T(8,128)(2,1)S(1)}, u32[]{:S(2)}, u32[]{:S(2)}) collective-permute-start(bf16[288,512]{1,0:T(8,128)(2,1)} %get-tuple-element.39), channel_id=1, source_target_pairs={{0,48},{16,0},{32,16},{48,32},{1,49},{17,1},{33,17},{49,33},{2,50}... | collective-permute-start | bytes 884744 | tf_op jit(solution)/shard_map/ppermute | solution.py:29
  42.0 7.5 %collective-permute-start.6 = (bf16[1152,512]{1,0:T(8,128)(2,1)S(1)}, bf16[1152,512]{1,0:T(8,128)(2,1)S(1)}, u32[]{:S(2)}, u32[]{:S(2)}) collective-permute-start(bf16[1152,512]{1,0:T(8,128)(2,1)S(1)} %constant_dynamic-update-slice_fusion.own_ref), channel_id=1, source_target_pairs={{0,8},{8,0},{1,9},{9,1},{2,10},{10,2},{3,11},{11,3},{4,12},{12,4},... | collective-permute-start | bytes 3538952 | tf_op jit(solution)/shard_map/ppermute | solution.py:29
  44.9 19.6 %all-to-all-start.1 = ((bf16[4,4,64,512]{3,2,1,0:T(8,128)(2,1)}), bf16[4,4,64,512]{3,2,1,0:T(8,128)(2,1)}, u32[]{:S(2)}, u32[]{:S(2)}) async-start(bf16[4,4,64,512]{3,2,1,0:T(8,128)(2,1)} %broadcast_in_dim.60), calls=%async_computation.1 | async-start | bytes 2097152 | tf_op jit(solution)/shard_map/all_to_all | solution.py:330
  49.6 1.6 copy-start.2
  57.0 2.0 copy-start.1
  64.5 3.3 %collective-permute-start.8 = (bf16[1024,512]{1,0:T(8,128)(2,1)}, bf16[1024,512]{1,0:T(8,128)(2,1)S(1)}, u32[]{:S(2)}, u32[]{:S(2)}) collective-permute-start(bf16[1024,512]{1,0:T(8,128)(2,1)} %bitcast.8.own_ref), channel_id=1, source_target_pairs={{0,8},{8,0},{1,9},{9,1},{2,10},{10,2},{3,11},{11,3},{4,12},{12,4},... | collective-permute-start | bytes 3145736 | tf_op jit(solution)/shard_map/ppermute | solution.py:29
  67.8 1.2 copy-start.5
  80.4 12.9 %all-to-all-start.2 = ((bf16[8,224,128]{2,1,0:T(8,128)(2,1)}), bf16[8,224,128]{2,1,0:T(8,128)(2,1)S(1)}, u32[]{:S(2)}, u32[]{:S(2)}) async-start(bf16[8,224,128]{2,1,0:T(8,128)(2,1)} %mix_project.1), calls=%async_computation.2 | async-start | bytes 917504 | tf_op jit(solution)/shard_map/all_to_all | solution.py:330
  84.5 8.9 %collective-permute-start.7 = (bf16[224,128]{1,0:T(8,128)(2,1)S(1)}, bf16[224,128]{1,0:T(8,128)(2,1)S(1)}, u32[]{:S(2)}, u32[]{:S(2)}) collective-permute-start(bf16[224,128]{1,0:T(8,128)(2,1)S(1)} %fusion.25), channel_id=1, source_target_pairs={{0,0},{1,32},{2,64},{3,96},{4,128},{5,160},{6,192},{7,224},{8,8},{... | collective-permute-start | bytes 172040 | tf_op jit(solution)/shard_map/ppermute | solution.py:424
  93.4 11.8 %collective-permute-start.12 = (bf16[224,128]{1,0:T(8,128)(2,1)S(1)}, bf16[224,128]{1,0:T(8,128)(2,1)S(1)}, u32[]{:S(2)}, u32[]{:S(2)}) collective-permute-start(bf16[224,128]{1,0:T(8,128)(2,1)S(1)} %add_convert_fusion), channel_id=1, source_target_pairs={{0,192},{1,224},{2,0},{3,32},{4,64},{5,96},{6,128},{7,160},{8,200}... | collective-permute-start | bytes 172040 | tf_op jit(solution)/shard_map/ppermute | solution.py:441
  97.5 7.7 %collective-permute-start.11 = (bf16[224,128]{1,0:T(8,128)(2,1)S(1)}, bf16[224,128]{1,0:T(8,128)(2,1)S(1)}, u32[]{:S(2)}, u32[]{:S(2)}) collective-permute-start(bf16[224,128]{1,0:T(8,128)(2,1)S(1)} %add_convert_fusion), channel_id=1, source_target_pairs={{0,128},{1,160},{2,192},{3,224},{4,0},{5,32},{6,64},{7,96},{8,136}... | collective-permute-start | bytes 172040 | tf_op jit(solution)/shard_map/ppermute | solution.py:441
  102.5 5.7 %collective-permute-start.10 = (bf16[224,128]{1,0:T(8,128)(2,1)S(1)}, bf16[224,128]{1,0:T(8,128)(2,1)S(1)}, u32[]{:S(2)}, u32[]{:S(2)}) collective-permute-start(bf16[224,128]{1,0:T(8,128)(2,1)S(1)} %add_convert_fusion), channel_id=1, source_target_pairs={{0,64},{1,96},{2,128},{3,160},{4,192},{5,224},{6,0},{7,32},{8,72},... | collective-permute-start | bytes 172040 | tf_op jit(solution)/shard_map/ppermute | solution.py:441
  104.5 3.7 %collective-permute-start.9 = (bf16[224,128]{1,0:T(8,128)(2,1)S(1)}, bf16[224,128]{1,0:T(8,128)(2,1)S(1)}, u32[]{:S(2)}, u32[]{:S(2)}) collective-permute-start(bf16[224,128]{1,0:T(8,128)(2,1)S(1)} %add_convert_fusion), channel_id=1, source_target_pairs={{0,0},{1,32},{2,64},{3,96},{4,128},{5,160},{6,192},{7,224},{8,8},{... | collective-permute-start | bytes 172040 | tf_op jit(solution)/shard_map/ppermute | solution.py:441
  108.2 27.2 %copy-start.3 = (bf16[896,576]{0,1:T(8,128)(2,1)S(1)}, bf16[896,576]{0,1:T(8,128)(2,1)}, u32[]{:S(2)}) copy-start(bf16[896,576]{0,1:T(8,128)(2,1)} %param.23) | copy-start | bytes 3096580
  108.2 27.2 %copy-start.4 = (bf16[896,576]{0,1:T(8,128)(2,1)S(1)}, bf16[896,576]{0,1:T(8,128)(2,1)}, u32[]{:S(2)}) copy-start(bf16[896,576]{0,1:T(8,128)(2,1)} %param.24) | copy-start | bytes 3096580
  108.3 19.9 %collective-permute-start.15 = (bf16[4,224,128]{2,1,0:T(8,128)(2,1)S(1)}, bf16[4,224,128]{2,1,0:T(8,128)(2,1)S(1)}, u32[]{:S(2)}, u32[]{:S(2)}) collective-permute-start(bf16[4,224,128]{2,1,0:T(8,128)(2,1)S(1)} %get-tuple-element.77), channel_id=1, source_target_pairs={{0,48},{16,0},{32,16},{48,32},{1,49},{17,1},{33,17},{49,33},{2,50}... | collective-permute-start | bytes 688136 | tf_op jit(solution)/shard_map/ppermute | solution.py:29
  118.9 9.3 %collective-permute-start.14 = (bf16[4,224,128]{2,1,0:T(8,128)(2,1)S(1)}, bf16[4,224,128]{2,1,0:T(8,128)(2,1)S(1)}, u32[]{:S(2)}, u32[]{:S(2)}) collective-permute-start(bf16[4,224,128]{2,1,0:T(8,128)(2,1)S(1)} %get-tuple-element.77), channel_id=1, source_target_pairs={{0,32},{16,48},{32,0},{48,16},{1,33},{17,49},{33,1},{49,17},{2,34}... | collective-permute-start | bytes 688136 | tf_op jit(solution)/shard_map/ppermute | solution.py:29
  119.0 12.4 %collective-permute-start.13 = (bf16[4,224,128]{2,1,0:T(8,128)(2,1)S(1)}, bf16[4,224,128]{2,1,0:T(8,128)(2,1)S(1)}, u32[]{:S(2)}, u32[]{:S(2)}) collective-permute-start(bf16[4,224,128]{2,1,0:T(8,128)(2,1)S(1)} %get-tuple-element.77), channel_id=1, source_target_pairs={{0,16},{16,32},{32,48},{48,0},{1,17},{17,33},{33,49},{49,1},{2,18}... | collective-permute-start | bytes 688136 | tf_op jit(solution)/shard_map/ppermute | solution.py:29
  131.6 3.9 %collective-permute-start.16 = (bf16[4,4,224,128]{3,2,1,0:T(8,128)(2,1)S(1)}, bf16[4,4,224,128]{3,2,1,0:T(8,128)(2,1)S(1)}, u32[]{:S(2)}, u32[]{:S(2)}) collective-permute-start(bf16[4,4,224,128]{3,2,1,0:T(8,128)(2,1)S(1)} %pad_maximum_fusion.own_ref), channel_id=1, source_target_pairs={{0,8},{8,0},{1,9},{9,1},{2,10},{10,2},{3,11},{11,3},{4,12},{12,4},... | collective-permute-start | bytes 2752520 | tf_op jit(solution)/shard_map/ppermute | solution.py:29
  137.2 13.0 %collective-permute-start.23 = (bf16[1168,128]{1,0:T(8,128)(2,1)S(1)}, bf16[1168,128]{1,0:T(8,128)(2,1)S(1)}, u32[]{:S(2)}, u32[]{:S(2)}) collective-permute-start(bf16[1168,128]{1,0:T(8,128)(2,1)S(1)} %get-tuple-element.58), channel_id=1, source_target_pairs={{0,5},{1,4},{2,7},{3,6},{4,1},{5,0},{6,3},{7,2},{8,13},{9,12},{10,... | collective-permute-start | bytes 897032 | tf_op jit(solution)/shard_map/ppermute | solution.py:454
  143.1 14.1 %collective-permute-start.22 = (bf16[1168,128]{1,0:T(8,128)(2,1)S(1)}, bf16[1168,128]{1,0:T(8,128)(2,1)S(1)}, u32[]{:S(2)}, u32[]{:S(2)}) collective-permute-start(bf16[1168,128]{1,0:T(8,128)(2,1)S(1)} %get-tuple-element.57), channel_id=1, source_target_pairs={{0,7},{1,6},{2,1},{3,0},{4,3},{5,2},{6,5},{7,4},{8,15},{9,14},{10,... | collective-permute-start | bytes 897032 | tf_op jit(solution)/shard_map/ppermute | solution.py:454
  143.7 20.2 %collective-permute-start.21 = (bf16[1168,128]{1,0:T(8,128)(2,1)S(1)}, bf16[1168,128]{1,0:T(8,128)(2,1)S(1)}, u32[]{:S(2)}, u32[]{:S(2)}) collective-permute-start(bf16[1168,128]{1,0:T(8,128)(2,1)S(1)} %get-tuple-element.56), channel_id=1, source_target_pairs={{0,3},{1,2},{2,5},{3,4},{4,7},{5,6},{6,1},{7,0},{8,11},{9,10},{10,... | collective-permute-start | bytes 897032 | tf_op jit(solution)/shard_map/ppermute | solution.py:454
  145.5 24.7 %collective-permute-start.20 = (bf16[1168,128]{1,0:T(8,128)(2,1)S(1)}, bf16[1168,128]{1,0:T(8,128)(2,1)S(1)}, u32[]{:S(2)}, u32[]{:S(2)}) collective-permute-start(bf16[1168,128]{1,0:T(8,128)(2,1)S(1)} %get-tuple-element.55), channel_id=1, source_target_pairs={{0,1},{1,0},{2,3},{3,2},{4,5},{5,4},{6,7},{7,6},{8,9},{9,8},{10,11... | collective-permute-start | bytes 897032 | tf_op jit(solution)/shard_map/ppermute | solution.py:454
  147.6 22.5 %collective-permute-start.19 = (bf16[1168,128]{1,0:T(8,128)(2,1)S(1)}, bf16[1168,128]{1,0:T(8,128)(2,1)S(1)}, u32[]{:S(2)}, u32[]{:S(2)}) collective-permute-start(bf16[1168,128]{1,0:T(8,128)(2,1)S(1)} %get-tuple-element.54), channel_id=1, source_target_pairs={{0,4},{1,5},{2,6},{3,7},{4,0},{5,1},{6,2},{7,3},{8,12},{9,13},{10,... | collective-permute-start | bytes 897032 | tf_op jit(solution)/shard_map/ppermute | solution.py:454
  150.3 20.4 %collective-permute-start.18 = (bf16[1168,128]{1,0:T(8,128)(2,1)S(1)}, bf16[1168,128]{1,0:T(8,128)(2,1)S(1)}, u32[]{:S(2)}, u32[]{:S(2)}) collective-permute-start(bf16[1168,128]{1,0:T(8,128)(2,1)S(1)} %get-tuple-element.53), channel_id=1, source_target_pairs={{0,6},{1,7},{2,0},{3,1},{4,2},{5,3},{6,4},{7,5},{8,14},{9,15},{10,... | collective-permute-start | bytes 897032 | tf_op jit(solution)/shard_map/ppermute | solution.py:454
  157.2 13.9 %collective-permute-start.17 = (bf16[1168,128]{1,0:T(8,128)(2,1)S(1)}, bf16[1168,128]{1,0:T(8,128)(2,1)S(1)}, u32[]{:S(2)}, u32[]{:S(2)}) collective-permute-start(bf16[1168,128]{1,0:T(8,128)(2,1)S(1)} %get-tuple-element.52), channel_id=1, source_target_pairs={{0,2},{1,3},{2,4},{3,5},{4,6},{5,7},{6,0},{7,1},{8,10},{9,11},{10,... | collective-permute-start | bytes 897032 | tf_op jit(solution)/shard_map/ppermute | solution.py:454
  172.6 20.9 %all-to-all-start.3 = ((bf16[8,576,128]{2,1,0:T(8,128)(2,1)}), bf16[8,576,128]{2,1,0:T(8,128)(2,1)}, u32[]{:S(2)}, u32[]{:S(2)}) async-start(bf16[8,576,128]{2,1,0:T(8,128)(2,1)} %broadcast_in_dim.69), calls=%async_computation.3 | async-start | bytes 2359296 | tf_op jit(solution)/shard_map/all_to_all | solution.py:330
  196.6 3.9 %collective-permute-start.24 = (bf16[4,128,896]{2,1,0:T(8,128)(2,1)}, bf16[4,128,896]{2,1,0:T(8,128)(2,1)}, u32[]{:S(2)}, u32[]{:S(2)}) collective-permute-start(bf16[4,128,896]{2,1,0:T(8,128)(2,1)} %convolution_convert_fusion), channel_id=1, source_target_pairs={{0,8},{8,0},{1,9},{9,1},{2,10},{10,2},{3,11},{11,3},{4,12},{12,4},... | collective-permute-start | bytes 2752520 | tf_op jit(solution)/shard_map/ppermute | solution.py:29
  202.9 6.9 %collective-permute-start.27 = (bf16[128,896]{1,0:T(8,128)(2,1)S(1)}, bf16[128,896]{1,0:T(8,128)(2,1)S(1)}, u32[]{:S(2)}, u32[]{:S(2)}) collective-permute-start(bf16[128,896]{1,0:T(8,128)(2,1)S(1)} %get-tuple-element.68), channel_id=1, source_target_pairs={{0,48},{16,0},{32,16},{48,32},{1,49},{17,1},{33,17},{49,33},{2,50}... | collective-permute-start | bytes 688136 | tf_op jit(solution)/shard_map/ppermute | solution.py:29
  203.6 8.0 %collective-permute-start.26 = (bf16[128,896]{1,0:T(8,128)(2,1)S(1)}, bf16[128,896]{1,0:T(8,128)(2,1)S(1)}, u32[]{:S(2)}, u32[]{:S(2)}) collective-permute-start(bf16[128,896]{1,0:T(8,128)(2,1)S(1)} %get-tuple-element.69), channel_id=1, source_target_pairs={{0,32},{16,48},{32,0},{48,16},{1,33},{17,49},{33,1},{49,17},{2,34}... | collective-permute-start | bytes 688136 | tf_op jit(solution)/shard_map/ppermute | solution.py:29
  205.2 12.4 %collective-permute-start.25 = (bf16[128,896]{1,0:T(8,128)(2,1)S(1)}, bf16[128,896]{1,0:T(8,128)(2,1)S(1)}, u32[]{:S(2)}, u32[]{:S(2)}) collective-permute-start(bf16[128,896]{1,0:T(8,128)(2,1)S(1)} %get-tuple-element.67), channel_id=1, source_target_pairs={{0,16},{16,32},{32,48},{48,0},{1,17},{17,33},{33,49},{49,1},{2,18}... | collective-permute-start | bytes 688136 | tf_op jit(solution)/shard_map/ppermute | solution.py:29
  218.7 21.6 %all-to-all-start.4 = ((bf16[32,8,896]{2,1,0:T(8,128)(2,1)}), bf16[32,8,896]{2,1,0:T(8,128)(2,1)S(1)}, u32[]{:S(2)}, u32[]{:S(2)}) async-start(bf16[32,8,896]{2,1,0:T(8,128)(2,1)} %fusion.1), calls=%async_computation.4 | async-start | bytes 917504 | tf_op jit(solution)/shard_map/all_to_all | solution.py:330

commit v8 on v7

--- a/solution.py
+++ b/solution.py
@@ -170,6 +170,7 @@
         out_specs=whole(shape),
         scratch_shapes=[pltpu.VMEM((slots * heads, slots), F32)],
         cost_estimate=cost(4),
+        compiler_params=pltpu.CompilerParams(vmem_limit_bytes=16 * 2**20),
         name="score_weights",
     )(counts, *arrays)
 
@@ -423,23 +424,14 @@
     rows, values = lax.optimization_barrier((rows, values))
     rows = lax.ppermute(rows, DP + HD, swap)
 
-    weights, values = lax.optimization_barrier((weights, values))
+    weights, values, rows = lax.optimization_barrier((weights, values, rows))
     weights_other = shifted(weights, "c", 1)
     part = mix_project(goes, weights, weights_other, values, output_weight.T)
     projected = jnp.sum(exchange(part, HD).astype(F32), axis=0)
     mixed = (rows.astype(F32) + projected).astype(BF)
 
-    full = []
-    for k in range(4):
-        sends = []
-        for a in range(4):
-            for b in range(8):
-                for e in range(4):
-                    for f in range(2):
-                        to = (((e + k) & 3) * 8 + (f * 4 + (b & 3))) * 8 + a * 2 + (b >> 2)
-                        sends.append(((a * 8 + b) * 8 + e * 2 + f, to))
-        full.append(lax.ppermute(mixed, DP + HD, sends))
-    full = jnp.stack(full)
+    full = jnp.stack([mixed] + [shifted(mixed, "x", k) for k in (1, 2, 3)])
+    full = lax.ppermute(full, DP + HD, swap)
 
     full = jnp.stack([full] + [shifted(full, "y", s) for s in (1, 2, 3)])
     full_other = shifted(full, "c", 1)

time: 242 us -> 257 us (1.062)
  blocking collectives: 0 us -> 20.8 us
  waiting for transfers between devices: 108 us -> 100 us
  starting transfers between devices: 81.6 us -> 85.4 us
    all_to_all x0 -> x1, blocking collectives: none -> 20.8 us  [exchange(): return lax.all_to_all(x, axes, split_axis=0, concat_axis=0, tiled=True)]
    ppermute x16 -> x19, starting transfers between devices: 36.1 us -> 48.6 us  [shifted(): return lax.ppermute(x, axis, [(i, (i + shift) % n) for i in range(n)])]
    ppermute x4 -> x1, starting transfers between devices: 11.8 us -> 0.68 us  [on_device(): full = lax.ppermute(full, DP + HD, swap)]
    all_to_all x5 -> x4, waiting for transfers between devices: 45 us -> 36.5 us  [exchange(): return lax.all_to_all(x, axes, split_axis=0, concat_axis=0, tiled=True)]
    ppermute x7, starting transfers between devices: 12.5 us -> 17.8 us  [on_device(): total = total + lax.ppermute(part, HD, sends).astype(F32)]
    ppermute x16 -> x19, waiting for transfers between devices: 40.8 us -> 45.9 us  [shifted(): return lax.ppermute(x, axis, [(i, (i + shift) % n) for i in range(n)])]
    ppermute x4 -> x1, waiting for transfers between devices: 3.02 us -> 0.01 us  [on_device(): full = lax.ppermute(full, DP + HD, swap)]
    all_to_all x5 -> x4, starting transfers between devices: 20.6 us -> 17.6 us  [exchange(): return lax.all_to_all(x, axes, split_axis=0, concat_axis=0, tiled=True)]
  transfers between devices with their start and end apart: 33 -> 32, of which waited for: 23 -> 22; matrix products, arithmetic and copies ran while one was open for 2% -> 2% of each run, Pallas kernels for 6% -> 5%
where the time goes in v8:
time: 257 us; the launch traced here: 256 us
  waiting for transfers between devices  100 us (39%)
  starting transfers between devices  85.4 us (33%)
  Pallas kernels  27.2 us (11%)
  blocking collectives  20.8 us (8%)
  local copies, waits for them, and re-layouts  9.76 us (4%)
  matrix products  8.09 us (3%)
  other arithmetic  3.94 us (2%)
    ppermute x19, starting transfers between devices, shifted(): return lax.ppermute(x, axis, [(i, (i + shift) % n) for i in range(n)])  48.6 us
    ppermute x19, waiting for transfers between devices, shifted(): return lax.ppermute(x, axis, [(i, (i + shift) % n) for i in range(n)])  45.9 us
    all_to_all x4, waiting for transfers between devices, exchange(): return lax.all_to_all(x, axes, split_axis=0, concat_axis=0, tiled=True)  36.5 us
    all_to_all x1, blocking collectives, exchange(): return lax.all_to_all(x, axes, split_axis=0, concat_axis=0, tiled=True)  20.8 us
    ppermute x7, starting transfers between devices, on_device(): total = total + lax.ppermute(part, HD, sends).astype(F32)  17.8 us
    ppermute x7, waiting for transfers between devices, on_device(): total = total + lax.ppermute(part, HD, sends).astype(F32)  17.7 us
    all_to_all x4, starting transfers between devices, exchange(): return lax.all_to_all(x, axes, split_axis=0, concat_axis=0, tiled=True)  17.6 us
    pallas_call x1, Pallas kernels, mix_project(): pl.pallas_call(mix_kernel, grid=(LIVE // STEP,), out_shape=jax.ShapeDtype...  10.8 us
  transfers between devices with their start and end apart: 32, of which 22 were waited for; matrix products, arithmetic and copies ran while one was open for 2% of the time, Pallas kernels for 5%

profile of v8, /device:TPU:1, one launch (start us, length us, event | category | flops | bytes accessed | tf_op | source)
XLA Modules:
  0.0 255.9 jit_solution(7433947607073138437)
XLA Ops:
  0.1 2.3 pack.1
  2.3 3.8 %collective-permute-start = (bf16[96,512]{1,0:T(8,128)(2,1)}, bf16[96,512]{1,0:T(8,128)(2,1)}, u32[]{:S(2)}, u32[]{:S(2)}) collective-permute-start(bf16[96,512]{1,0:T(8,128)(2,1)} %get-tuple-element.34), channel_id=1, source_target_pairs={{0,64},{64,128},{128,192},{192,0},{1,65},{65,129},{129,193},{193,1... | collective-permute-start | bytes 294920 | tf_op jit(solution)/shard_map/ppermute | solution.py:29
  6.2 5.1 %collective-permute-start.1 = (bf16[96,512]{1,0:T(8,128)(2,1)}, bf16[96,512]{1,0:T(8,128)(2,1)}, u32[]{:S(2)}, u32[]{:S(2)}) collective-permute-start(bf16[96,512]{1,0:T(8,128)(2,1)} %get-tuple-element.35), channel_id=1, source_target_pairs={{0,128},{64,192},{128,0},{192,64},{1,129},{65,193},{129,1},{193,65... | collective-permute-start | bytes 294920 | tf_op jit(solution)/shard_map/ppermute | solution.py:29
  11.3 2.4 collective-permute-start.2
  13.7 0.8 copy-done.10
  14.5 2.6 %score_weights.1 = bf16[4,64,512]{2,1,0:T(8,128)(2,1)} custom-call(s32[32]{0:T(128)S(1)} %copy-done.3, bf16[64,2048]{1,0:T(8,128)(2,1)S(1)} %copy-done.8, bf16[64,1024]{1,0:T(8,128)(2,1)S(1)} %copy-done.9, bf16[64,512]{1,0:T(8,128)(2,1)S(1)} %copy-done.10, bf16[64,64]{1,0:T(8,128)(2,1)S(1)} %copy-done.11, bf16[512,2048]{1,0:T(8,128)(2,1)S(1)} %copy-done.4, ...), custom_call_target="tpu_custom_call" | custom-call | flops 4000000000 | bytes 12000000 | tf_op jit(solution)/shard_map/score_weights/pallas_call | solution.py:165
  17.1 3.4 %all-to-all-start = ((bf16[4,64,512]{2,1,0:T(8,128)(2,1)}), bf16[4,64,512]{2,1,0:T(8,128)(2,1)S(1)}, u32[]{:S(2)}, u32[]{:S(2)}) async-start(bf16[4,64,512]{2,1,0:T(8,128)(2,1)} %score_weights.1), calls=%async_computation | async-start | bytes 524288 | tf_op jit(solution)/shard_map/all_to_all | solution.py:331
  20.7 1.0 collective-permute-done.2.refs_3_
  21.7 2.2 repack.1
  23.9 1.3 collective-permute-start.3
  25.2 2.6 %collective-permute-start.4 = (bf16[288,512]{1,0:T(8,128)(2,1)}, bf16[288,512]{1,0:T(8,128)(2,1)S(1)}, u32[]{:S(2)}, u32[]{:S(2)}) collective-permute-start(bf16[288,512]{1,0:T(8,128)(2,1)} %get-tuple-element.39), channel_id=1, source_target_pairs={{0,32},{16,48},{32,0},{48,16},{1,33},{17,49},{33,1},{49,17},{2,34}... | collective-permute-start | bytes 884744 | tf_op jit(solution)/shard_map/ppermute | solution.py:29
  27.8 1.1 collective-permute-start.5
  28.9 0.7 select_reduce_fusion.3
  30.0 3.4 %collective-permute-done.3 = bf16[288,512]{1,0:T(8,128)(2,1)S(1)} collective-permute-done((bf16[288,512]{1,0:T(8,128)(2,1)}, bf16[288,512]{1,0:T(8,128)(2,1)S(1)}, u32[]{:S(2)}, u32[]{:S(2)}) %collective-permute-start.3) | collective-permute-done | bytes 294944 | tf_op jit(solution)/shard_map/ppermute | solution.py:29
  33.4 7.4 %collective-permute-done.4 = bf16[288,512]{1,0:T(8,128)(2,1)S(1)} collective-permute-done((bf16[288,512]{1,0:T(8,128)(2,1)}, bf16[288,512]{1,0:T(8,128)(2,1)S(1)}, u32[]{:S(2)}, u32[]{:S(2)}) %collective-permute-start.4) | collective-permute-done | bytes 294944 | tf_op jit(solution)/shard_map/ppermute | solution.py:29
  40.9 1.1 broadcast_in_dim.60
  42.1 1.5 collective-permute-start.6
  44.4 4.2 %all-to-all-start.1 = ((bf16[4,4,64,512]{3,2,1,0:T(8,128)(2,1)}), bf16[4,4,64,512]{3,2,1,0:T(8,128)(2,1)}, u32[]{:S(2)}, u32[]{:S(2)}) async-start(bf16[4,4,64,512]{3,2,1,0:T(8,128)(2,1)} %broadcast_in_dim.60), calls=%async_computation.1 | async-start | bytes 2097152 | tf_op jit(solution)/shard_map/all_to_all | solution.py:331
  49.1 1.6 copy-done.2
  50.7 5.9 %live_values.1.prev_ref.cur_ref = bf16[1024,2048]{1,0:T(8,128)(2,1)S(1)} custom-call(s32[2,1,1152]{2,1,0:T(1,128)S(1)} %reshape.475.goes_ref, bf16[1152,512]{1,0:T(8,128)(2,1)S(1)} %constant_dynamic-update-slice_fusion.own_ref, bf16[1152,512]{1,0:T(8,128)(2,1)S(1)} %collective-permute-done.6.other_ref, bf16[512,2048]{1,0:T(8,128)(2,1)S(1)} %copy-done.2), custom_call_target="tpu_custom_call" | custom-call | tf_op jit(solution)/shard_map/live_values/pallas_call | solution.py:191
  56.6 2.0 copy-done.1
  59.5 4.5 %all-to-all-done.1 = bf16[4,4,64,512]{3,2,1,0:T(8,128)(2,1)} async-done(((bf16[4,4,64,512]{3,2,1,0:T(8,128)(2,1)}), bf16[4,4,64,512]{3,2,1,0:T(8,128)(2,1)}, u32[]{:S(2)}, u32[]{:S(2)}) %all-to-all-start.1) | async-done | bytes 1048608 | tf_op jit(solution)/shard_map/all_to_all | solution.py:331
  64.0 0.8 collective-permute-start.8
  65.3 2.1 collective-permute-done.8.other_ref
  67.3 1.2 copy-done.7
  68.5 10.8 %mix_project.1 = bf16[8,224,128]{2,1,0:T(8,128)(2,1)S(1)} custom-call(s32[2,1,1024]{2,1,0:T(1,128)S(1)} %compare_select_fusion.goes_ref, bf16[1024,512]{1,0:T(8,128)(2,1)} %bitcast.own_ref, bf16[1024,512]{1,0:T(8,128)(2,1)S(1)} %collective-permute-done.8.other_ref, bf16[1024,2048]{1,0:T(8,128)(2,1)} %copy-done.1, bf16[1024,2048]{1,0:T(8,128)(2,1)} %copy-done.1, ...), custom_call_target="tpu_custom_call" | custom-call | flops 8999999488 | bytes 27000000 | tf_op jit(solution)/shard_map/mix_project/pallas_call | solution.py:254
  79.3 20.8 %all_to_all.25 = bf16[8,224,128]{2,1,0:T(8,128)(2,1)S(1)} all-to-all(bf16[8,224,128]{2,1,0:T(8,128)(2,1)S(1)} %mix_project.1), channel_id=1, replica_groups=mesh['zh'=4,'y'=4,'c'=2,'x'=4,'zl'=2] {'x','zl'}, dimensions={0} | all-to-all | bytes 917504 | tf_op jit(solution)/shard_map/all_to_all | solution.py:331
  100.2 0.8 collective-permute-start.11
  101.0 1.0 collective-permute-start.10
  102.0 1.5 collective-permute-done.11
  103.5 2.0 collective-permute-done.10
  105.5 0.7 collective-permute-done.9
  107.0 22.1 %collective-permute-start.15 = (bf16[4,224,128]{2,1,0:T(8,128)(2,1)S(1)}, bf16[4,224,128]{2,1,0:T(8,128)(2,1)S(1)}, u32[]{:S(2)}, u32[]{:S(2)}) collective-permute-start(bf16[4,224,128]{2,1,0:T(8,128)(2,1)S(1)} %collective-permute-done.12), channel_id=1, source_target_pairs={{0,48},{16,0},{32,16},{48,32},{1,49},{17,1},{33,17},{49,33},{2,50}... | collective-permute-start | bytes 688136 | tf_op jit(solution)/shard_map/ppermute | solution.py:29
  129.7 9.4 %collective-permute-done.15 = bf16[4,224,128]{2,1,0:T(8,128)(2,1)S(1)} collective-permute-done((bf16[4,224,128]{2,1,0:T(8,128)(2,1)S(1)}, bf16[4,224,128]{2,1,0:T(8,128)(2,1)S(1)}, u32[]{:S(2)}, u32[]{:S(2)}) %collective-permute-start.15) | collective-permute-done | bytes 229408 | tf_op jit(solution)/shard_map/ppermute | solution.py:29
  139.0 3.4 %collective-permute-done.13 = bf16[4,224,128]{2,1,0:T(8,128)(2,1)S(1)} collective-permute-done((bf16[4,224,128]{2,1,0:T(8,128)(2,1)S(1)}, bf16[4,224,128]{2,1,0:T(8,128)(2,1)S(1)}, u32[]{:S(2)}, u32[]{:S(2)}) %collective-permute-start.13) | collective-permute-done | bytes 229408 | tf_op jit(solution)/shard_map/ppermute | solution.py:29
  142.5 0.9 collective-permute-start.16
  143.4 2.1 collective-permute-done.16.other_ref
  145.5 1.7 gate_up.3
  147.3 1.4 collective-permute-start.23
  148.7 5.5 %collective-permute-start.22 = (bf16[1168,128]{1,0:T(8,128)(2,1)S(1)}, bf16[1168,128]{1,0:T(8,128)(2,1)S(1)}, u32[]{:S(2)}, u32[]{:S(2)}) collective-permute-start(bf16[1168,128]{1,0:T(8,128)(2,1)S(1)} %get-tuple-element.59), channel_id=1, source_target_pairs={{0,7},{1,6},{2,1},{3,0},{4,3},{5,2},{6,5},{7,4},{8,15},{9,14},{10,... | collective-permute-start | bytes 897032 | tf_op jit(solution)/shard_map/ppermute | solution.py:446
  154.2 2.2 collective-permute-start.21
  156.3 2.1 collective-permute-start.20
  158.4 1.7 gate_up.2
  160.3 5.3 %collective-permute-start.18 = (bf16[1168,128]{1,0:T(8,128)(2,1)S(1)}, bf16[1168,128]{1,0:T(8,128)(2,1)S(1)}, u32[]{:S(2)}, u32[]{:S(2)}) collective-permute-start(bf16[1168,128]{1,0:T(8,128)(2,1)S(1)} %get-tuple-element.55), channel_id=1, source_target_pairs={{0,6},{1,7},{2,0},{3,1},{4,2},{5,3},{6,4},{7,5},{8,14},{9,15},{10,... | collective-permute-start | bytes 897032 | tf_op jit(solution)/shard_map/ppermute | solution.py:446
  165.6 4.1 %collective-permute-done.22 = bf16[1168,128]{1,0:T(8,128)(2,1)S(1)} collective-permute-done((bf16[1168,128]{1,0:T(8,128)(2,1)S(1)}, bf16[1168,128]{1,0:T(8,128)(2,1)S(1)}, u32[]{:S(2)}, u32[]{:S(2)}) %collective-permute-start.22) | collective-permute-done | bytes 299040 | tf_op jit(solution)/shard_map/ppermute | solution.py:446
  169.6 1.3 collective-permute-start.17
  170.9 5.4 %collective-permute-done.21 = bf16[1168,128]{1,0:T(8,128)(2,1)S(1)} collective-permute-done((bf16[1168,128]{1,0:T(8,128)(2,1)S(1)}, bf16[1168,128]{1,0:T(8,128)(2,1)S(1)}, u32[]{:S(2)}, u32[]{:S(2)}) %collective-permute-start.21) | collective-permute-done | bytes 299040 | tf_op jit(solution)/shard_map/ppermute | solution.py:446
  176.3 6.3 %collective-permute-done.20 = bf16[1168,128]{1,0:T(8,128)(2,1)S(1)} collective-permute-done((bf16[1168,128]{1,0:T(8,128)(2,1)S(1)}, bf16[1168,128]{1,0:T(8,128)(2,1)S(1)}, u32[]{:S(2)}, u32[]{:S(2)}) %collective-permute-start.20) | collective-permute-done | bytes 299040 | tf_op jit(solution)/shard_map/ppermute | solution.py:446
  183.2 1.4 collective-permute-done.17
  185.0 1.2 broadcast_in_dim.69
  186.2 4.5 %all-to-all-start.3 = ((bf16[8,576,128]{2,1,0:T(8,128)(2,1)}), bf16[8,576,128]{2,1,0:T(8,128)(2,1)}, u32[]{:S(2)}, u32[]{:S(2)}) async-start(bf16[8,576,128]{2,1,0:T(8,128)(2,1)} %broadcast_in_dim.69), calls=%async_computation.3 | async-start | bytes 2359296 | tf_op jit(solution)/shard_map/all_to_all | solution.py:331
  190.8 16.7 %all-to-all-done.3 = bf16[8,576,128]{2,1,0:T(8,128)(2,1)} async-done(((bf16[8,576,128]{2,1,0:T(8,128)(2,1)}), bf16[8,576,128]{2,1,0:T(8,128)(2,1)}, u32[]{:S(2)}, u32[]{:S(2)}) %all-to-all-start.3) | async-done | bytes 1179680 | tf_op jit(solution)/shard_map/all_to_all | solution.py:331
  207.5 3.0 %convolution_convert_fusion = bf16[4,128,896]{2,1,0:T(8,128)(2,1)} fusion(bf16[576,896]{1,0:T(8,128)(2,1)S(1)} %copy-done, bf16[4,2,576,128]{3,2,1,0:T(8,128)(2,1)} %bitcast.21, s32[]{:T(128)S(6)} %select_n.153), kind=kOutput, calls=%fused_computation.1 | convolution fusion | flops 528941056 | bytes 2539524 | tf_op jit(solution)/shard_map/dot_general | solution.py:453
  210.5 1.3 collective-permute-start.24
  212.1 2.1 collective-permute-done.24
  214.2 2.3 convert_add_fusion
  217.1 2.8 %collective-permute-start.26 = (bf16[128,896]{1,0:T(8,128)(2,1)S(1)}, bf16[128,896]{1,0:T(8,128)(2,1)S(1)}, u32[]{:S(2)}, u32[]{:S(2)}) collective-permute-start(bf16[128,896]{1,0:T(8,128)(2,1)S(1)} %get-tuple-element.71), channel_id=1, source_target_pairs={{0,32},{16,48},{32,0},{48,16},{1,33},{17,49},{33,1},{49,17},{2,34}... | collective-permute-start | bytes 688136 | tf_op jit(solution)/shard_map/ppermute | solution.py:29
  220.3 3.3 %collective-permute-done.27 = bf16[128,896]{1,0:T(8,128)(2,1)S(1)} collective-permute-done((bf16[128,896]{1,0:T(8,128)(2,1)S(1)}, bf16[128,896]{1,0:T(8,128)(2,1)S(1)}, u32[]{:S(2)}, u32[]{:S(2)}) %collective-permute-start.27) | collective-permute-done | bytes 229408 | tf_op jit(solution)/shard_map/ppermute | solution.py:29
  223.6 1.6 collective-permute-done.26
  225.1 5.9 %collective-permute-done.25 = bf16[128,896]{1,0:T(8,128)(2,1)S(1)} collective-permute-done((bf16[128,896]{1,0:T(8,128)(2,1)S(1)}, bf16[128,896]{1,0:T(8,128)(2,1)S(1)}, u32[]{:S(2)}, u32[]{:S(2)}) %collective-permute-start.25) | collective-permute-done | bytes 229408 | tf_op jit(solution)/shard_map/ppermute | solution.py:29
  231.1 1.1 fusion.1
  232.2 5.5 %all-to-all-start.4 = ((bf16[32,8,896]{2,1,0:T(8,128)(2,1)}), bf16[32,8,896]{2,1,0:T(8,128)(2,1)S(1)}, u32[]{:S(2)}, u32[]{:S(2)}) async-start(bf16[32,8,896]{2,1,0:T(8,128)(2,1)} %fusion.1), calls=%async_computation.4 | async-start | bytes 917504 | tf_op jit(solution)/shard_map/all_to_all | solution.py:331
  239.7 15.3 %all-to-all-done.4 = bf16[32,8,896]{2,1,0:T(8,128)(2,1)S(1)} async-done(((bf16[32,8,896]{2,1,0:T(8,128)(2,1)}), bf16[32,8,896]{2,1,0:T(8,128)(2,1)S(1)}, u32[]{:S(2)}, u32[]{:S(2)}) %all-to-all-start.4) | async-done | bytes 458784 | tf_op jit(solution)/shard_map/all_to_all | solution.py:331
  255.0 0.9 fusion.2
  (114 shorter events, 9.0 us)
Async XLA Ops:
  0.0 207.5 %copy-start = (bf16[576,896]{1,0:T(8,128)(2,1)S(1)}, bf16[576,896]{1,0:T(8,128)(2,1)}, u32[]{:S(2)}) copy-start(bf16[576,896]{1,0:T(8,128)(2,1)} %param.25) | copy-start | bytes 3096580
  0.0 13.7 %copy-start.3 = (s32[32]{0:T(128)S(1)}, s32[32]{0:T(128)}, u32[]{:S(2)}) copy-start(s32[32]{0:T(128)} %counts_ref.3) | copy-start | bytes 388
  0.0 13.7 %copy-start.8 = (bf16[64,2048]{1,0:T(8,128)(2,1)S(1)}, bf16[64,2048]{1,0:T(8,128)(2,1)}, u32[]{:S(2)}) copy-start(bf16[64,2048]{1,0:T(8,128)(2,1)} %qn_ref.1) | copy-start | bytes 786436
  0.0 13.7 %copy-start.9 = (bf16[64,1024]{1,0:T(8,128)(2,1)S(1)}, bf16[64,1024]{1,0:T(8,128)(2,1)}, u32[]{:S(2)}) copy-start(bf16[64,1024]{1,0:T(8,128)(2,1)} %qr_ref.1) | copy-start | bytes 393220
  0.0 13.6 %copy-start.11 = (bf16[64,64]{1,0:T(8,128)(2,1)S(1)}, bf16[64,64]{1,0:T(8,128)(2,1)}, u32[]{:S(2)}) copy-start(bf16[64,64]{1,0:T(8,128)(2,1)} %kr_ref.1) | copy-start | bytes 24580
  0.0 13.6 %copy-start.4 = (bf16[512,2048]{1,0:T(8,128)(2,1)S(1)}, bf16[512,2048]{1,0:T(8,128)(2,1)}, u32[]{:S(2)}) copy-start(bf16[512,2048]{1,0:T(8,128)(2,1)} %ku_ref.1) | copy-start | bytes 6291460
  0.0 13.6 %copy-start.12 = (s32[1,64]{1,0:T(1,128)S(1)}, s32[1,64]{1,0:T(1,128)}, u32[]{:S(2)}) copy-start(s32[1,64]{1,0:T(1,128)} %req_ref.1) | copy-start | bytes 772
  2.3 18.4 %collective-permute-start = (bf16[96,512]{1,0:T(8,128)(2,1)}, bf16[96,512]{1,0:T(8,128)(2,1)}, u32[]{:S(2)}, u32[]{:S(2)}) collective-permute-start(bf16[96,512]{1,0:T(8,128)(2,1)} %get-tuple-element.34), channel_id=1, source_target_pairs={{0,64},{64,128},{128,192},{192,0},{1,65},{65,129},{129,193},{193,1... | collective-permute-start | bytes 294920 | tf_op jit(solution)/shard_map/ppermute | solution.py:29
  6.2 14.6 %collective-permute-start.1 = (bf16[96,512]{1,0:T(8,128)(2,1)}, bf16[96,512]{1,0:T(8,128)(2,1)}, u32[]{:S(2)}, u32[]{:S(2)}) collective-permute-start(bf16[96,512]{1,0:T(8,128)(2,1)} %get-tuple-element.35), channel_id=1, source_target_pairs={{0,128},{64,192},{128,0},{192,64},{1,129},{65,193},{129,1},{193,65... | collective-permute-start | bytes 294920 | tf_op jit(solution)/shard_map/ppermute | solution.py:29
  11.3 10.5 %collective-permute-start.2 = (bf16[96,512]{1,0:T(8,128)(2,1)}, bf16[96,512]{1,0:T(8,128)(2,1)}, u32[]{:S(2)}, u32[]{:S(2)}) collective-permute-start(bf16[96,512]{1,0:T(8,128)(2,1)} %get-tuple-element.36), channel_id=1, source_target_pairs={{0,192},{64,0},{128,64},{192,128},{1,193},{65,1},{129,65},{193,129... | collective-permute-start | bytes 294920 | tf_op jit(solution)/shard_map/ppermute | solution.py:29
  13.7 0.8 copy-start.10
  14.5 6.0 %copy-start.14 = (f32[896]{0:T(1024)S(1)}, f32[896]{0:T(1024)}, u32[]{:S(2)}) copy-start(f32[896]{0:T(1024)} %param.22) | copy-start | bytes 10756
  17.1 12.9 %all-to-all-start = ((bf16[4,64,512]{2,1,0:T(8,128)(2,1)}), bf16[4,64,512]{2,1,0:T(8,128)(2,1)S(1)}, u32[]{:S(2)}, u32[]{:S(2)}) async-start(bf16[4,64,512]{2,1,0:T(8,128)(2,1)} %score_weights.1), calls=%async_computation | async-start | bytes 524288 | tf_op jit(solution)/shard_map/all_to_all | solution.py:331
  23.9 18.1 %copy-start.13 = (bf16[288,512]{1,0:T(8,128)(2,1)S(1)}, bf16[288,512]{1,0:T(8,128)(2,1)}, u32[]{:S(2)}) copy-start(bf16[288,512]{1,0:T(8,128)(2,1)} %get-tuple-element.43) | copy-start | bytes 884740
  23.9 9.6 %collective-permute-start.3 = (bf16[288,512]{1,0:T(8,128)(2,1)}, bf16[288,512]{1,0:T(8,128)(2,1)S(1)}, u32[]{:S(2)}, u32[]{:S(2)}) collective-permute-start(bf16[288,512]{1,0:T(8,128)(2,1)} %get-tuple-element.38), channel_id=1, source_target_pairs={{0,16},{16,32},{32,48},{48,0},{1,17},{17,33},{33,49},{49,1},{2,18}... | collective-permute-start | bytes 884744 | tf_op jit(solution)/shard_map/ppermute | solution.py:29
  25.2 15.7 %collective-permute-start.4 = (bf16[288,512]{1,0:T(8,128)(2,1)}, bf16[288,512]{1,0:T(8,128)(2,1)S(1)}, u32[]{:S(2)}, u32[]{:S(2)}) collective-permute-start(bf16[288,512]{1,0:T(8,128)(2,1)} %get-tuple-element.39), channel_id=1, source_target_pairs={{0,32},{16,48},{32,0},{48,16},{1,33},{17,49},{33,1},{49,17},{2,34}... | collective-permute-start | bytes 884744 | tf_op jit(solution)/shard_map/ppermute | solution.py:29
  27.8 13.1 %collective-permute-start.5 = (bf16[288,512]{1,0:T(8,128)(2,1)}, bf16[288,512]{1,0:T(8,128)(2,1)S(1)}, u32[]{:S(2)}, u32[]{:S(2)}) collective-permute-start(bf16[288,512]{1,0:T(8,128)(2,1)} %get-tuple-element.40), channel_id=1, source_target_pairs={{0,48},{16,0},{32,16},{48,32},{1,49},{17,1},{33,17},{49,33},{2,50}... | collective-permute-start | bytes 884744 | tf_op jit(solution)/shard_map/ppermute | solution.py:29
  42.1 6.9 %collective-permute-start.6 = (bf16[1152,512]{1,0:T(8,128)(2,1)S(1)}, bf16[1152,512]{1,0:T(8,128)(2,1)S(1)}, u32[]{:S(2)}, u32[]{:S(2)}) collective-permute-start(bf16[1152,512]{1,0:T(8,128)(2,1)S(1)} %constant_dynamic-update-slice_fusion.own_ref), channel_id=1, source_target_pairs={{0,8},{8,0},{1,9},{9,1},{2,10},{10,2},{3,11},{11,3},{4,12},{12,4},... | collective-permute-start | bytes 3538952 | tf_op jit(solution)/shard_map/ppermute | solution.py:29
  44.4 19.6 %all-to-all-start.1 = ((bf16[4,4,64,512]{3,2,1,0:T(8,128)(2,1)}), bf16[4,4,64,512]{3,2,1,0:T(8,128)(2,1)}, u32[]{:S(2)}, u32[]{:S(2)}) async-start(bf16[4,4,64,512]{3,2,1,0:T(8,128)(2,1)} %broadcast_in_dim.60), calls=%async_computation.1 | async-start | bytes 2097152 | tf_op jit(solution)/shard_map/all_to_all | solution.py:331
  49.1 1.6 copy-start.2
  56.6 2.0 copy-start.1
  58.8 5.2 %collective-permute-start.7 = (bf16[224,128]{1,0:T(8,128)(2,1)S(1)}, bf16[224,128]{1,0:T(8,128)(2,1)S(1)}, u32[]{:S(2)}, u32[]{:S(2)}) collective-permute-start(bf16[224,128]{1,0:T(8,128)(2,1)S(1)} %fusion.25), channel_id=1, source_target_pairs={{0,0},{1,32},{2,64},{3,96},{4,128},{5,160},{6,192},{7,224},{8,8},{... | collective-permute-start | bytes 172040 | tf_op jit(solution)/shard_map/ppermute | solution.py:425
  64.0 3.3 %collective-permute-start.8 = (bf16[1024,512]{1,0:T(8,128)(2,1)}, bf16[1024,512]{1,0:T(8,128)(2,1)S(1)}, u32[]{:S(2)}, u32[]{:S(2)}) collective-permute-start(bf16[1024,512]{1,0:T(8,128)(2,1)} %bitcast.own_ref), channel_id=1, source_target_pairs={{0,8},{8,0},{1,9},{9,1},{2,10},{10,2},{3,11},{11,3},{4,12},{12,4},... | collective-permute-start | bytes 3145736 | tf_op jit(solution)/shard_map/ppermute | solution.py:29
  67.3 1.2 copy-start.7
  100.2 45.4 %copy-start.5 = (bf16[896,576]{0,1:T(8,128)(2,1)S(1)}, bf16[896,576]{0,1:T(8,128)(2,1)}, u32[]{:S(2)}) copy-start(bf16[896,576]{0,1:T(8,128)(2,1)} %param.23) | copy-start | bytes 3096580
  100.2 45.4 %copy-start.6 = (bf16[896,576]{0,1:T(8,128)(2,1)S(1)}, bf16[896,576]{0,1:T(8,128)(2,1)}, u32[]{:S(2)}) copy-start(bf16[896,576]{0,1:T(8,128)(2,1)} %param.24) | copy-start | bytes 3096580
  100.2 3.3 %collective-permute-start.11 = (bf16[224,128]{1,0:T(8,128)(2,1)S(1)}, bf16[224,128]{1,0:T(8,128)(2,1)S(1)}, u32[]{:S(2)}, u32[]{:S(2)}) collective-permute-start(bf16[224,128]{1,0:T(8,128)(2,1)S(1)} %add_convert_fusion), channel_id=1, source_target_pairs={{0,6},{2,0},{4,2},{6,4},{1,7},{3,1},{5,3},{7,5},{8,14},{10,8},{12,... | collective-permute-start | bytes 172040 | tf_op jit(solution)/shard_map/ppermute | solution.py:29
  101.0 4.5 %collective-permute-start.10 = (bf16[224,128]{1,0:T(8,128)(2,1)S(1)}, bf16[224,128]{1,0:T(8,128)(2,1)S(1)}, u32[]{:S(2)}, u32[]{:S(2)}) collective-permute-start(bf16[224,128]{1,0:T(8,128)(2,1)S(1)} %add_convert_fusion), channel_id=1, source_target_pairs={{0,4},{2,6},{4,0},{6,2},{1,5},{3,7},{5,1},{7,3},{8,12},{10,14},{12... | collective-permute-start | bytes 172040 | tf_op jit(solution)/shard_map/ppermute | solution.py:29
  102.0 4.2 %collective-permute-start.9 = (bf16[224,128]{1,0:T(8,128)(2,1)S(1)}, bf16[224,128]{1,0:T(8,128)(2,1)S(1)}, u32[]{:S(2)}, u32[]{:S(2)}) collective-permute-start(bf16[224,128]{1,0:T(8,128)(2,1)S(1)} %add_convert_fusion), channel_id=1, source_target_pairs={{0,2},{2,4},{4,6},{6,0},{1,3},{3,5},{5,7},{7,1},{8,10},{10,12},{12... | collective-permute-start | bytes 172040 | tf_op jit(solution)/shard_map/ppermute | solution.py:29
  106.3 0.7 collective-permute-start.12
  107.0 32.1 %collective-permute-start.15 = (bf16[4,224,128]{2,1,0:T(8,128)(2,1)S(1)}, bf16[4,224,128]{2,1,0:T(8,128)(2,1)S(1)}, u32[]{:S(2)}, u32[]{:S(2)}) collective-permute-start(bf16[4,224,128]{2,1,0:T(8,128)(2,1)S(1)} %collective-permute-done.12), channel_id=1, source_target_pairs={{0,48},{16,0},{32,16},{48,32},{1,49},{17,1},{33,17},{49,33},{2,50}... | collective-permute-start | bytes 688136 | tf_op jit(solution)/shard_map/ppermute | solution.py:29
  129.1 9.9 %collective-permute-start.14 = (bf16[4,224,128]{2,1,0:T(8,128)(2,1)S(1)}, bf16[4,224,128]{2,1,0:T(8,128)(2,1)S(1)}, u32[]{:S(2)}, u32[]{:S(2)}) collective-permute-start(bf16[4,224,128]{2,1,0:T(8,128)(2,1)S(1)} %collective-permute-done.12), channel_id=1, source_target_pairs={{0,32},{16,48},{32,0},{48,16},{1,33},{17,49},{33,1},{49,17},{2,34}... | collective-permute-start | bytes 688136 | tf_op jit(solution)/shard_map/ppermute | solution.py:29
  129.1 13.3 %collective-permute-start.13 = (bf16[4,224,128]{2,1,0:T(8,128)(2,1)S(1)}, bf16[4,224,128]{2,1,0:T(8,128)(2,1)S(1)}, u32[]{:S(2)}, u32[]{:S(2)}) collective-permute-start(bf16[4,224,128]{2,1,0:T(8,128)(2,1)S(1)} %collective-permute-done.12), channel_id=1, source_target_pairs={{0,16},{16,32},{32,48},{48,0},{1,17},{17,33},{33,49},{49,1},{2,18}... | collective-permute-start | bytes 688136 | tf_op jit(solution)/shard_map/ppermute | solution.py:29
  142.5 3.0 %collective-permute-start.16 = (bf16[4,4,224,128]{3,2,1,0:T(8,128)(2,1)S(1)}, bf16[4,4,224,128]{3,2,1,0:T(8,128)(2,1)S(1)}, u32[]{:S(2)}, u32[]{:S(2)}) collective-permute-start(bf16[4,4,224,128]{3,2,1,0:T(8,128)(2,1)S(1)} %pad_maximum_fusion.own_ref), channel_id=1, source_target_pairs={{0,8},{8,0},{1,9},{9,1},{2,10},{10,2},{3,11},{11,3},{4,12},{12,4},... | collective-permute-start | bytes 2752520 | tf_op jit(solution)/shard_map/ppermute | solution.py:29
  147.3 13.0 %collective-permute-start.23 = (bf16[1168,128]{1,0:T(8,128)(2,1)S(1)}, bf16[1168,128]{1,0:T(8,128)(2,1)S(1)}, u32[]{:S(2)}, u32[]{:S(2)}) collective-permute-start(bf16[1168,128]{1,0:T(8,128)(2,1)S(1)} %get-tuple-element.60), channel_id=1, source_target_pairs={{0,5},{1,4},{2,7},{3,6},{4,1},{5,0},{6,3},{7,2},{8,13},{9,12},{10,... | collective-permute-start | bytes 897032 | tf_op jit(solution)/shard_map/ppermute | solution.py:446
  148.7 20.9 %collective-permute-start.22 = (bf16[1168,128]{1,0:T(8,128)(2,1)S(1)}, bf16[1168,128]{1,0:T(8,128)(2,1)S(1)}, u32[]{:S(2)}, u32[]{:S(2)}) collective-permute-start(bf16[1168,128]{1,0:T(8,128)(2,1)S(1)} %get-tuple-element.59), channel_id=1, source_target_pairs={{0,7},{1,6},{2,1},{3,0},{4,3},{5,2},{6,5},{7,4},{8,15},{9,14},{10,... | collective-permute-start | bytes 897032 | tf_op jit(solution)/shard_map/ppermute | solution.py:446
  154.2 22.1 %collective-permute-start.21 = (bf16[1168,128]{1,0:T(8,128)(2,1)S(1)}, bf16[1168,128]{1,0:T(8,128)(2,1)S(1)}, u32[]{:S(2)}, u32[]{:S(2)}) collective-permute-start(bf16[1168,128]{1,0:T(8,128)(2,1)S(1)} %get-tuple-element.58), channel_id=1, source_target_pairs={{0,3},{1,2},{2,5},{3,4},{4,7},{5,6},{6,1},{7,0},{8,11},{9,10},{10,... | collective-permute-start | bytes 897032 | tf_op jit(solution)/shard_map/ppermute | solution.py:446
  156.3 26.2 %collective-permute-start.20 = (bf16[1168,128]{1,0:T(8,128)(2,1)S(1)}, bf16[1168,128]{1,0:T(8,128)(2,1)S(1)}, u32[]{:S(2)}, u32[]{:S(2)}) collective-permute-start(bf16[1168,128]{1,0:T(8,128)(2,1)S(1)} %get-tuple-element.57), channel_id=1, source_target_pairs={{0,1},{1,0},{2,3},{3,2},{4,5},{5,4},{6,7},{7,6},{8,9},{9,8},{10,11... | collective-permute-start | bytes 897032 | tf_op jit(solution)/shard_map/ppermute | solution.py:446
  160.2 22.4 %collective-permute-start.19 = (bf16[1168,128]{1,0:T(8,128)(2,1)S(1)}, bf16[1168,128]{1,0:T(8,128)(2,1)S(1)}, u32[]{:S(2)}, u32[]{:S(2)}) collective-permute-start(bf16[1168,128]{1,0:T(8,128)(2,1)S(1)} %get-tuple-element.56), channel_id=1, source_target_pairs={{0,4},{1,5},{2,6},{3,7},{4,0},{5,1},{6,2},{7,3},{8,12},{9,13},{10,... | collective-permute-start | bytes 897032 | tf_op jit(solution)/shard_map/ppermute | solution.py:446
  160.3 22.9 %collective-permute-start.18 = (bf16[1168,128]{1,0:T(8,128)(2,1)S(1)}, bf16[1168,128]{1,0:T(8,128)(2,1)S(1)}, u32[]{:S(2)}, u32[]{:S(2)}) collective-permute-start(bf16[1168,128]{1,0:T(8,128)(2,1)S(1)} %get-tuple-element.55), channel_id=1, source_target_pairs={{0,6},{1,7},{2,0},{3,1},{4,2},{5,3},{6,4},{7,5},{8,14},{9,15},{10,... | collective-permute-start | bytes 897032 | tf_op jit(solution)/shard_map/ppermute | solution.py:446
  169.6 15.0 %collective-permute-start.17 = (bf16[1168,128]{1,0:T(8,128)(2,1)S(1)}, bf16[1168,128]{1,0:T(8,128)(2,1)S(1)}, u32[]{:S(2)}, u32[]{:S(2)}) collective-permute-start(bf16[1168,128]{1,0:T(8,128)(2,1)S(1)} %get-tuple-element.54), channel_id=1, source_target_pairs={{0,2},{1,3},{2,4},{3,5},{4,6},{5,7},{6,0},{7,1},{8,10},{9,11},{10,... | collective-permute-start | bytes 897032 | tf_op jit(solution)/shard_map/ppermute | solution.py:446
  186.2 21.3 %all-to-all-start.3 = ((bf16[8,576,128]{2,1,0:T(8,128)(2,1)}), bf16[8,576,128]{2,1,0:T(8,128)(2,1)}, u32[]{:S(2)}, u32[]{:S(2)}) async-start(bf16[8,576,128]{2,1,0:T(8,128)(2,1)} %broadcast_in_dim.69), calls=%async_computation.3 | async-start | bytes 2359296 | tf_op jit(solution)/shard_map/all_to_all | solution.py:331
  210.5 3.8 %collective-permute-start.24 = (bf16[4,128,896]{2,1,0:T(8,128)(2,1)}, bf16[4,128,896]{2,1,0:T(8,128)(2,1)}, u32[]{:S(2)}, u32[]{:S(2)}) collective-permute-start(bf16[4,128,896]{2,1,0:T(8,128)(2,1)} %convolution_convert_fusion), channel_id=1, source_target_pairs={{0,8},{8,0},{1,9},{9,1},{2,10},{10,2},{3,11},{11,3},{4,12},{12,4},... | collective-permute-start | bytes 2752520 | tf_op jit(solution)/shard_map/ppermute | solution.py:29
  216.7 6.9 %collective-permute-start.27 = (bf16[128,896]{1,0:T(8,128)(2,1)S(1)}, bf16[128,896]{1,0:T(8,128)(2,1)S(1)}, u32[]{:S(2)}, u32[]{:S(2)}) collective-permute-start(bf16[128,896]{1,0:T(8,128)(2,1)S(1)} %get-tuple-element.70), channel_id=1, source_target_pairs={{0,48},{16,0},{32,16},{48,32},{1,49},{17,1},{33,17},{49,33},{2,50}... | collective-permute-start | bytes 688136 | tf_op jit(solution)/shard_map/ppermute | solution.py:29
  217.1 8.0 %collective-permute-start.26 = (bf16[128,896]{1,0:T(8,128)(2,1)S(1)}, bf16[128,896]{1,0:T(8,128)(2,1)S(1)}, u32[]{:S(2)}, u32[]{:S(2)}) collective-permute-start(bf16[128,896]{1,0:T(8,128)(2,1)S(1)} %get-tuple-element.71), channel_id=1, source_target_pairs={{0,32},{16,48},{32,0},{48,16},{1,33},{17,49},{33,1},{49,17},{2,34}... | collective-permute-start | bytes 688136 | tf_op jit(solution)/shard_map/ppermute | solution.py:29
  219.9 11.2 %collective-permute-start.25 = (bf16[128,896]{1,0:T(8,128)(2,1)S(1)}, bf16[128,896]{1,0:T(8,128)(2,1)S(1)}, u32[]{:S(2)}, u32[]{:S(2)}) collective-permute-start(bf16[128,896]{1,0:T(8,128)(2,1)S(1)} %get-tuple-element.69), channel_id=1, source_target_pairs={{0,16},{16,32},{32,48},{48,0},{1,17},{17,33},{33,49},{49,1},{2,18}... | collective-permute-start | bytes 688136 | tf_op jit(solution)/shard_map/ppermute | solution.py:29
  232.2 22.8 %all-to-all-start.4 = ((bf16[32,8,896]{2,1,0:T(8,128)(2,1)}), bf16[32,8,896]{2,1,0:T(8,128)(2,1)S(1)}, u32[]{:S(2)}, u32[]{:S(2)}) async-start(bf16[32,8,896]{2,1,0:T(8,128)(2,1)} %fusion.1), calls=%async_computation.4 | async-start | bytes 917504 | tf_op jit(solution)/shard_map/all_to_all | solution.py:331

commit v9 on v7

--- a/solution.py
+++ b/solution.py
@@ -57,75 +57,6 @@
         lambda i, a: a + jnp.where(i < place, counts_ref[i], 0),
         jnp.int32(0),
     )
-
-
-def pack_kernel(counts_ref, lat_ref, res_ref, *refs):
-    outs, rows_ref = refs[:4], refs[4]
-    slots, width = res_ref.shape
-    half, lanes = width // 2, lat_ref.shape[1]
-    zh = lax.axis_index("zh")
-    start = live_before(counts_ref)
-    i_at, slot = iota((slots, slots), 0), iota((slots, slots), 1)
-    roll = ((((i_at >> 3) - start) & 7) + 8 * (i_at & 7)) == slot
-    rows_ref[...] = dot(jnp.where(roll, 1.0, 0.0).astype(BF), res_ref[...])
-    fill = jnp.zeros((16, lanes - half), F32)
-    for s in range(4):
-        outs[s][:slots, :] = lat_ref[...]
-        for high in range(2):
-            m = ((zh + s) & 3) * 2 + high
-            piece = rows_ref[pl.ds(pl.multiple_of(m * 8, 8), 8), :]
-            piece = jnp.concatenate([piece[:, :half], piece[:, half:]], axis=0)
-            piece = jnp.concatenate([piece, fill], axis=1)
-            outs[s][slots + 16 * high : slots + 16 * (high + 1), :] = piece.astype(BF)
-
-
-def pack(counts, latent, residual):
-    slots, lanes = latent.shape
-    shape = (slots + 32, lanes)
-    return pl.pallas_call(
-        pack_kernel,
-        grid=(1,),
-        out_shape=[jax.ShapeDtypeStruct(shape, BF)] * 4,
-        in_specs=[
-            pl.BlockSpec(memory_space=pltpu.SMEM),
-            whole(latent.shape),
-            whole(residual.shape),
-        ],
-        out_specs=[whole(shape)] * 4,
-        scratch_shapes=[pltpu.VMEM(residual.shape, F32)],
-        cost_estimate=cost(2),
-        name="pack",
-    )(counts, latent, residual)
-
-
-def repack_kernel(*refs):
-    ins, outs, rows_ref = refs[:4], refs[4:8], refs[8]
-    slots = ins[0].shape[0] - 32
-    y = lax.axis_index("y")
-    for t in range(4):
-        rows_ref[t] = ins[t][slots:, :].astype(F32)
-    for s in range(4):
-        at = pl.ds(pl.multiple_of(((y + s) & 3) * 8, 8), 8)
-        for t in range(4):
-            outs[s][t * slots : (t + 1) * slots, :] = ins[t][:slots, :]
-        for t in (0, 2):
-            pair = jnp.concatenate([rows_ref[t, at, :], rows_ref[t + 1, at, :]], axis=0)
-            outs[s][4 * slots + 8 * t : 4 * slots + 8 * t + 16, :] = pair.astype(BF)
-
-
-def repack(*pieces):
-    rows, lanes = pieces[0].shape
-    shape = (4 * (rows - 32) + 32, lanes)
-    return pl.pallas_call(
-        repack_kernel,
-        grid=(1,),
-        out_shape=[jax.ShapeDtypeStruct(shape, BF)] * 4,
-        in_specs=[whole(pieces[0].shape)] * 4,
-        out_specs=[whole(shape)] * 4,
-        scratch_shapes=[pltpu.VMEM((4, 32, lanes), F32)],
-        cost_estimate=cost(2),
-        name="repack",
-    )(*pieces)
 
 
 def score_kernel(counts_ref, qn_ref, qr_ref, lat_ref, kr_ref, ku_ref, req_ref, out_ref, s_ref):
@@ -181,22 +112,24 @@
     return out.astype(BF)
 
 
-def values_kernel(goes_ref, own_ref, other_ref, up_ref, out_ref):
-    out_ref[...] = dot(live_rows(goes_ref, own_ref, other_ref), up_ref[...]).astype(BF)
-
-
-def live_values(goes, own, other, up):
+def values_kernel(goes_ref, slots_ref, up_ref, out_ref):
+    row = iota((STEP, slots_ref.shape[0]), 0) + pl.program_id(0) * STEP
+    live = dot(jnp.where(goes_ref[...] == row, 1.0, 0.0).astype(BF), slots_ref[...])
+    out_ref[...] = dot(live.astype(BF), up_ref[...]).astype(BF)
+
+
+def live_values(goes, slots, up):
     width = up.shape[1]
     return pl.pallas_call(
         values_kernel,
         grid=(LIVE // STEP,),
         out_shape=jax.ShapeDtypeStruct((LIVE, width), BF),
-        in_specs=[whole(a.shape) for a in (goes, own, other, up)],
+        in_specs=[whole(a.shape) for a in (goes, slots, up)],
         out_specs=pl.BlockSpec((STEP, width), lambda b: (b, 0)),
         cost_estimate=cost(0),
         compiler_params=pltpu.CompilerParams(vmem_limit_bytes=24 * 2**20),
         name="live_values",
-    )(goes, own, other, up)
+    )(goes, slots, up)
 
 
 def mix_kernel(goes_ref, own_ref, other_ref, prev_ref, cur_ref, wo_ref, out_ref, att_ref, all_ref):
@@ -375,33 +308,21 @@
     own_start, own_length = starts(rank), lengths(rank)
     slot = jnp.arange(slots, dtype=jnp.int32)
 
-    pieces = pack(rank_tokens, latent, residual)
-    pieces = [pieces[0]] + [shifted(pieces[s], "zh", s) for s in (1, 2, 3)]
+    latents = lax.all_gather(latent, DP, axis=0, tiled=True)
+    begin = starts(every)
+    slots_go = jnp.where(slot < rank_tokens[:, None], begin[:, None] + slot, -1)
+    values = live_values(slots_go.reshape(1, -1), latents, value_up)
+
+    eight = jnp.arange(8, dtype=jnp.int32)
+    spread = ((eight[:, None] - own_start) & 7) + 8 * eight
+    roll = (spread.reshape(slots, 1) == slot).astype(BF)
+    rows = dot(roll, residual).astype(BF).reshape(8, 8, 4, quarter)
+    rows = exchange(rows.transpose(0, 2, 1, 3).reshape(ranks, 8, quarter), DP)
 
     weights = score_weights(
         rank_tokens, query_nope, query_rope, latent, key_rope, key_up, request_ids
     )
     weights = exchange(weights, "zh")
-    pieces = repack(*pieces)
-    weights, gain, _ = lax.optimization_barrier((weights, norm_gain[None, :], pieces))
-    weights = jnp.broadcast_to(weights[None], (4,) + weights.shape)
-    pieces = [pieces[0]] + [shifted(pieces[s], "y", s) for s in (1, 2, 3)]
-    pieces, weights = lax.optimization_barrier((pieces, weights))
-    got = jnp.concatenate(pieces, axis=0)
-    got_other = shifted(got, "c", 1)
-    weights = exchange(weights, "y").reshape(-1, weights.shape[3])
-
-    four = jnp.arange(4, dtype=jnp.int32)
-    eight = jnp.arange(8, dtype=jnp.int32)
-    core = jnp.stack([c, 1 - c])[:, None, None]
-    ahead = (four[None, None, :] * 4 + four[None, :, None]) * 2 + core
-    goes = jnp.where(slot < lengths(ahead)[..., None], starts(ahead)[..., None] + slot, -1)
-    goes = goes.reshape(2, 1, -1)
-    back = (((zh - four) & 3)[None, None, :] * 4 + ((y - four) & 3)[None, :, None]) * 2 + core
-    back_start, back_count = starts(back)[..., None], lengths(back)[..., None]
-    goes_back = jnp.where(slot < back_count, back_start + slot, -1).reshape(2, 4, -1)
-    goes_back = jnp.pad(goes_back, ((0, 0), (0, 0), (0, 32)), constant_values=-1).reshape(2, 1, -1)
-    values = live_values(goes_back, got, got_other, value_up)
 
     swap = []
     for a in range(4):
@@ -410,21 +331,20 @@
                 for f in range(2):
                     to = (e * 8 + (f * 4 + (b & 3))) * 8 + a * 2 + (b >> 2)
                     swap.append(((a * 8 + b) * 8 + e * 2 + f, to))
-    place = (((zh * 2 + (y >> 1)) - back_start) & 7) + 8 * eight
-    come = jnp.where(place < back_count, (back_start + place) >> 3, -1)
-    come = (come.reshape(2, -1, 1) == jnp.arange(chunk, dtype=jnp.int32)).astype(BF)
-
-    def tn(a, b):
-        return lax.dot_general(a, b, (((0,), (0,)), ((), ())), preferred_element_type=F32)
-
-    rows = [a.reshape(4, -1, a.shape[1])[:, 4 * slots :].reshape(-1, a.shape[1]) for a in (got, got_other)]
-    rows = tn(rows[0], come[0]) + tn(rows[1], come[1])
-    rows = jnp.where(c == 0, rows[:quarter], rows[quarter : 2 * quarter]).astype(BF)
-    rows, values = lax.optimization_barrier((rows, values))
-    rows = lax.ppermute(rows, DP + HD, swap)
-
-    weights, values = lax.optimization_barrier((weights, values))
+    place = (((zh * 2 + (y >> 1)) - begin[:, None]) & 7) + 8 * eight
+    come = jnp.where(place < rank_tokens[:, None], (begin[:, None] + place) >> 3, -1)
+    come = (come.reshape(-1, 1) == jnp.arange(chunk, dtype=jnp.int32)).astype(BF)
+    rows = lax.dot_general(
+        rows.reshape(ranks * 8, quarter), come, (((0,), (0,)), ((), ())), preferred_element_type=F32
+    )
+    rows = lax.ppermute(rows.astype(BF), DP + HD, swap)
+    weights, gain, _ = lax.optimization_barrier((weights, norm_gain[None, :], rows))
+    weights = gather(weights, "y").reshape(-1, weights.shape[2])
     weights_other = shifted(weights, "c", 1)
+
+    goes = slots_go.reshape(4, 4, 2, slots).transpose(2, 1, 0, 3)
+    goes = jnp.where(c == 0, goes, goes[::-1]).reshape(2, 1, -1)
+
     part = mix_project(goes, weights, weights_other, values, output_weight.T)
     projected = jnp.sum(exchange(part, HD).astype(F32), axis=0)
     mixed = (rows.astype(F32) + projected).astype(BF)
@@ -469,7 +389,6 @@
     for s in (1, 2, 3):
         total = total + shifted(pieces[s].astype(BF), "y", s).astype(F32)
     spot = y * 2 + c
-    begin = starts(every)
     m = ((zh - (spot & 3)) & 3) * 2 + (spot >> 2)
     place = ((m - begin[:, None]) & 7) + 8 * eight[None, :]
     comes = jnp.where(place < rank_tokens[:, None], (begin[:, None] + place) >> 3, -1)

time: 242 us -> 264 us (1.091)
  blocking collectives: 0 us -> 38 us
  between operations: 0.55 us -> 13.8 us
  waiting for transfers between devices: 108 us -> 96.5 us
  starting transfers between devices: 81.6 us -> 70.2 us
  Pallas kernels: 29.1 us -> 23.6 us
  local copies, waits for them, and re-layouts: 9.52 us -> 6.65 us
    all_to_all x0 -> x2, blocking collectives: none -> 38 us  [exchange(): return lax.all_to_all(x, axes, split_axis=0, concat_axis=0, tiled=True)]
    ppermute x16 -> x9, waiting for transfers between devices: 40.8 us -> 21.1 us  [shifted(): return lax.ppermute(x, axis, [(i, (i + shift) % n) for i in range(n)])]
    ppermute x16 -> x9, starting transfers between devices: 36.1 us -> 21.5 us  [shifted(): return lax.ppermute(x, axis, [(i, (i + shift) % n) for i in range(n)])]
    all_to_all x5 -> x4, starting transfers between devices: 20.6 us -> 28.5 us  [exchange(): return lax.all_to_all(x, axes, split_axis=0, concat_axis=0, tiled=True)]
    ppermute x7, waiting for transfers between devices: 19.6 us -> 25.1 us  [on_device(): total = total + lax.ppermute(part, HD, sends).astype(F32)]
    ppermute x4, starting transfers between devices: 11.8 us -> 6.45 us  [on_device(): full.append(lax.ppermute(mixed, DP + HD, sends))]
    pallas_call x2 -> x0, Pallas kernels: 4.4 us -> none  [the longest x1 2.23 us: pack(): pl.pallas_call(pack_kernel, grid=(1,), out_shape=[jax.ShapeDtypeStruct(sh...]
    unnamed x27 -> x18, local copies, waits for them, and re-layouts: 5.47 us -> 3.59 us
  transfers between devices with their start and end apart: 33 -> 26, of which waited for: 23 -> 16; matrix products, arithmetic and copies ran while one was open for 2% -> 3% of each run, Pallas kernels for 6% -> 4%
where the time goes in v9:
time: 264 us; the launch traced here: 263 us
  waiting for transfers between devices  96.5 us (37%)
  starting transfers between devices  70.2 us (27%)
  blocking collectives  38 us (14%)
  Pallas kernels  23.6 us (9%)
  between operations  13.8 us (5%)
  matrix products  9.08 us (3%)
  local copies, waits for them, and re-layouts  6.65 us (3%)
  other arithmetic  5.08 us (2%)
    all_to_all x4, waiting for transfers between devices, exchange(): return lax.all_to_all(x, axes, split_axis=0, concat_axis=0, tiled=True)  46 us
    all_to_all x2, blocking collectives, exchange(): return lax.all_to_all(x, axes, split_axis=0, concat_axis=0, tiled=True)  38 us
    all_to_all x4, starting transfers between devices, exchange(): return lax.all_to_all(x, axes, split_axis=0, concat_axis=0, tiled=True)  28.5 us
    ppermute x7, waiting for transfers between devices, on_device(): total = total + lax.ppermute(part, HD, sends).astype(F32)  25.1 us
    ppermute x9, starting transfers between devices, shifted(): return lax.ppermute(x, axis, [(i, (i + shift) % n) for i in range(n)])  21.5 us
    ppermute x9, waiting for transfers between devices, shifted(): return lax.ppermute(x, axis, [(i, (i + shift) % n) for i in range(n)])  21.1 us
    ppermute x7, starting transfers between devices, on_device(): total = total + lax.ppermute(part, HD, sends).astype(F32)  13.1 us
    pallas_call x1, Pallas kernels, mix_project(): pl.pallas_call(mix_kernel, grid=(LIVE // STEP,), out_shape=jax.ShapeDtype...  11 us
  transfers between devices with their start and end apart: 26, of which 16 were waited for; matrix products, arithmetic and copies ran while one was open for 3% of the time, Pallas kernels for 4%

profile of v9, /device:TPU:1, one launch (start us, length us, event | category | flops | bytes accessed | tf_op | source)
XLA Modules:
  0.0 263.0 jit_solution(9549861647049538721)
XLA Ops:
  6.5 0.7 all-gather.2.cloned.1.call-update
  7.3 1.3 fusion.51
  8.6 0.6 subtract_and_fusion.1
  9.4 1.1 convolution_convert_fusion.1
  10.7 0.7 copy.26
  11.3 12.8 %all-to-all-start = ((bf16[32,8,224]{2,1,0:T(8,128)(2,1)}), bf16[32,8,224]{2,1,0:T(8,128)(2,1)S(1)}, u32[]{:S(2)}, u32[]{:S(2)}) async-start(bf16[32,8,224]{2,1,0:T(8,128)(2,1)} %bitcast.1), calls=%async_computation | async-start | bytes 262144 | tf_op jit(solution)/shard_map/all_to_all | solution.py:263
  24.1 0.8 select_reduce_fusion
  24.9 3.9 %score_weights.1 = bf16[4,64,512]{2,1,0:T(8,128)(2,1)} custom-call(s32[32]{0:T(128)} %counts_ref.1, bf16[64,2048]{1,0:T(8,128)(2,1)} %qn_ref.1, bf16[64,1024]{1,0:T(8,128)(2,1)} %qr_ref.1, bf16[64,512]{1,0:T(8,128)(2,1)} %lat_ref.1, bf16[64,64]{1,0:T(8,128)(2,1)} %kr_ref.1, bf16[512,2048]{1,0:T(8,128)(2,1)} %ku_ref.1, s32[1,64]{1,0:T(1,128)} %req_ref.1), custom_call_target="tpu_custom_call" | custom-call | flops 4000000000 | bytes 12000000 | tf_op jit(solution)/shard_map/score_weights/pallas_call | solution.py:96
  28.8 6.3 %all-to-all-done = bf16[32,8,224]{2,1,0:T(8,128)(2,1)S(1)} async-done(((bf16[32,8,224]{2,1,0:T(8,128)(2,1)}), bf16[32,8,224]{2,1,0:T(8,128)(2,1)S(1)}, u32[]{:S(2)}, u32[]{:S(2)}) %all-to-all-start) | async-done | bytes 114720 | tf_op jit(solution)/shard_map/all_to_all | solution.py:263
  35.1 3.4 %all-to-all-start.1 = ((bf16[4,64,512]{2,1,0:T(8,128)(2,1)}), bf16[4,64,512]{2,1,0:T(8,128)(2,1)S(1)}, u32[]{:S(2)}, u32[]{:S(2)}) async-start(bf16[4,64,512]{2,1,0:T(8,128)(2,1)} %score_weights.1), calls=%async_computation.1 | async-start | bytes 524288 | tf_op jit(solution)/shard_map/all_to_all | solution.py:263
  38.7 0.3 convolution_convert_fusion.2
  39.0 0.8 collective-permute-start
  39.8 8.1 %all-to-all-done.1 = bf16[4,64,512]{2,1,0:T(8,128)(2,1)S(1)} async-done(((bf16[4,64,512]{2,1,0:T(8,128)(2,1)}), bf16[4,64,512]{2,1,0:T(8,128)(2,1)S(1)}, u32[]{:S(2)}, u32[]{:S(2)}) %all-to-all-start.1) | async-done | bytes 262176 | tf_op jit(solution)/shard_map/all_to_all | solution.py:263
  48.1 21.8 %all_to_all.30 = bf16[4,4,64,512]{3,2,1,0:T(8,128)(2,1)} all-to-all(bf16[4,4,64,512]{3,2,1,0:T(8,128)(2,1)S(1)} %broadcast_in_dim.43), channel_id=1, replica_groups=mesh['zh'=4,'y'=4,'c'=2,'x'=4,'zl'=2] {'y'}, dimensions={0} | all-to-all | bytes 2097152 | tf_op jit(solution)/shard_map/all_to_all | solution.py:263
  69.8 1.8 collective-permute-start.1
  72.5 1.6 copy-done.3
  74.0 5.3 %live_values.1.prev_ref.cur_ref = bf16[1024,2048]{1,0:T(8,128)(2,1)S(1)} custom-call(s32[1,2048]{1,0:T(1,128)S(1)} %select_n.141.goes_ref, bf16[2048,512]{1,0:T(8,128)(2,1)S(1)} %copy-done.3, bf16[512,2048]{1,0:T(8,128)(2,1)S(1)} %copy-done.2), custom_call_target="tpu_custom_call" | custom-call | tf_op jit(solution)/shard_map/live_values/pallas_call | solution.py:123
  79.4 2.0 copy-done.1
  81.4 11.0 %mix_project.1 = bf16[8,224,128]{2,1,0:T(8,128)(2,1)S(1)} custom-call(s32[2,1,1024]{2,1,0:T(1,128)S(1)} %reshape.399.goes_ref, bf16[1024,512]{1,0:T(8,128)(2,1)} %bitcast.5.own_ref, bf16[1024,512]{1,0:T(8,128)(2,1)} %collective-permute-done.1.other_ref, bf16[1024,2048]{1,0:T(8,128)(2,1)} %copy-done.1, bf16[1024,2048]{1,0:T(8,128)(2,1)} %copy-done.1, ...), custom_call_target="tpu_custom_call" | custom-call | flops 8999999488 | bytes 27000000 | tf_op jit(solution)/shard_map/mix_project/pallas_call | solution.py:186
  92.4 16.2 %all_to_all.31 = bf16[8,224,128]{2,1,0:T(8,128)(2,1)S(1)} all-to-all(bf16[8,224,128]{2,1,0:T(8,128)(2,1)S(1)} %mix_project.1), channel_id=1, replica_groups=mesh['zh'=4,'y'=4,'c'=2,'x'=4,'zl'=2] {'x','zl'}, dimensions={0} | all-to-all | bytes 917504 | tf_op jit(solution)/shard_map/all_to_all | solution.py:263
  108.7 2.2 collective-permute-start.5
  110.9 2.7 %collective-permute-start.4 = (bf16[224,128]{1,0:T(8,128)(2,1)S(1)}, bf16[224,128]{1,0:T(8,128)(2,1)S(1)}, u32[]{:S(2)}, u32[]{:S(2)}) collective-permute-start(bf16[224,128]{1,0:T(8,128)(2,1)S(1)} %add_convert_fusion), channel_id=1, source_target_pairs={{0,128},{1,160},{2,192},{3,224},{4,0},{5,32},{6,64},{7,96},{8,136}... | collective-permute-start | bytes 172040 | tf_op jit(solution)/shard_map/ppermute | solution.py:361
  113.6 0.8 collective-permute-start.3
  114.5 0.7 collective-permute-start.2
  115.2 0.4 collective-permute-done.4
  115.6 3.2 %collective-permute-done.3 = bf16[224,128]{1,0:T(8,128)(2,1)S(1)} collective-permute-done((bf16[224,128]{1,0:T(8,128)(2,1)S(1)}, bf16[224,128]{1,0:T(8,128)(2,1)S(1)}, u32[]{:S(2)}, u32[]{:S(2)}) %collective-permute-start.3) | collective-permute-done | bytes 57376 | tf_op jit(solution)/shard_map/ppermute | solution.py:361
  118.9 7.8 %collective-permute-start.7 = (bf16[4,224,128]{2,1,0:T(8,128)(2,1)S(1)}, bf16[4,224,128]{2,1,0:T(8,128)(2,1)S(1)}, u32[]{:S(2)}, u32[]{:S(2)}) collective-permute-start(bf16[4,224,128]{2,1,0:T(8,128)(2,1)S(1)} %get-tuple-element.37), channel_id=1, source_target_pairs={{0,32},{16,48},{32,0},{48,16},{1,33},{17,49},{33,1},{49,17},{2,34}... | collective-permute-start | bytes 688136 | tf_op jit(solution)/shard_map/ppermute | solution.py:29
  126.6 0.6 collective-permute-start.6
  127.3 2.0 collective-permute-start.8
  129.3 0.7 collective-permute-done.7
  130.0 6.1 %collective-permute-done.6 = bf16[4,224,128]{2,1,0:T(8,128)(2,1)S(1)} collective-permute-done((bf16[4,224,128]{2,1,0:T(8,128)(2,1)S(1)}, bf16[4,224,128]{2,1,0:T(8,128)(2,1)S(1)}, u32[]{:S(2)}, u32[]{:S(2)}) %collective-permute-start.6) | collective-permute-done | bytes 229408 | tf_op jit(solution)/shard_map/ppermute | solution.py:29
  136.2 2.9 %collective-permute-start.9 = (bf16[4,4,224,128]{3,2,1,0:T(8,128)(2,1)S(1)}, bf16[4,4,224,128]{3,2,1,0:T(8,128)(2,1)S(1)}, u32[]{:S(2)}, u32[]{:S(2)}) collective-permute-start(bf16[4,4,224,128]{3,2,1,0:T(8,128)(2,1)S(1)} %pad_maximum_fusion.own_ref), channel_id=1, source_target_pairs={{0,8},{8,0},{1,9},{9,1},{2,10},{10,2},{3,11},{11,3},{4,12},{12,4},... | collective-permute-start | bytes 2752520 | tf_op jit(solution)/shard_map/ppermute | solution.py:29
  139.1 2.1 collective-permute-done.9.other_ref
  141.2 1.7 gate_up.3
  143.0 0.7 collective-permute-start.13
  143.6 5.0 %collective-permute-start.14 = (bf16[1168,128]{1,0:T(8,128)(2,1)S(1)}, bf16[1168,128]{1,0:T(8,128)(2,1)S(1)}, u32[]{:S(2)}, u32[]{:S(2)}) collective-permute-start(bf16[1168,128]{1,0:T(8,128)(2,1)S(1)} %get-tuple-element.22), channel_id=1, source_target_pairs={{0,3},{1,2},{2,5},{3,4},{4,7},{5,6},{6,1},{7,0},{8,11},{9,10},{10,... | collective-permute-start | bytes 897032 | tf_op jit(solution)/shard_map/ppermute | solution.py:374
  148.6 1.8 collective-permute-start.15
  150.5 2.8 %collective-permute-start.16 = (bf16[1168,128]{1,0:T(8,128)(2,1)S(1)}, bf16[1168,128]{1,0:T(8,128)(2,1)S(1)}, u32[]{:S(2)}, u32[]{:S(2)}) collective-permute-start(bf16[1168,128]{1,0:T(8,128)(2,1)S(1)} %get-tuple-element.24), channel_id=1, source_target_pairs={{0,5},{1,4},{2,7},{3,6},{4,1},{5,0},{6,3},{7,2},{8,13},{9,12},{10,... | collective-permute-start | bytes 897032 | tf_op jit(solution)/shard_map/ppermute | solution.py:374
  153.3 1.7 gate_up.2
  155.1 2.6 %collective-permute-start.11 = (bf16[1168,128]{1,0:T(8,128)(2,1)S(1)}, bf16[1168,128]{1,0:T(8,128)(2,1)S(1)}, u32[]{:S(2)}, u32[]{:S(2)}) collective-permute-start(bf16[1168,128]{1,0:T(8,128)(2,1)S(1)} %get-tuple-element.19), channel_id=1, source_target_pairs={{0,6},{1,7},{2,0},{3,1},{4,2},{5,3},{6,4},{7,5},{8,14},{9,15},{10,... | collective-permute-start | bytes 897032 | tf_op jit(solution)/shard_map/ppermute | solution.py:374
  157.7 6.2 %collective-permute-done.14 = bf16[1168,128]{1,0:T(8,128)(2,1)S(1)} collective-permute-done((bf16[1168,128]{1,0:T(8,128)(2,1)S(1)}, bf16[1168,128]{1,0:T(8,128)(2,1)S(1)}, u32[]{:S(2)}, u32[]{:S(2)}) %collective-permute-start.14) | collective-permute-done | bytes 299040 | tf_op jit(solution)/shard_map/ppermute | solution.py:374
  163.9 4.5 %collective-permute-done.15 = bf16[1168,128]{1,0:T(8,128)(2,1)S(1)} collective-permute-done((bf16[1168,128]{1,0:T(8,128)(2,1)S(1)}, bf16[1168,128]{1,0:T(8,128)(2,1)S(1)}, u32[]{:S(2)}, u32[]{:S(2)}) %collective-permute-start.15) | collective-permute-done | bytes 299040 | tf_op jit(solution)/shard_map/ppermute | solution.py:374
  168.4 8.7 %collective-permute-done.16 = bf16[1168,128]{1,0:T(8,128)(2,1)S(1)} collective-permute-done((bf16[1168,128]{1,0:T(8,128)(2,1)S(1)}, bf16[1168,128]{1,0:T(8,128)(2,1)S(1)}, u32[]{:S(2)}, u32[]{:S(2)}) %collective-permute-start.16) | collective-permute-done | bytes 299040 | tf_op jit(solution)/shard_map/ppermute | solution.py:374
  177.1 5.7 %collective-permute-done.11 = bf16[1168,128]{1,0:T(8,128)(2,1)S(1)} collective-permute-done((bf16[1168,128]{1,0:T(8,128)(2,1)S(1)}, bf16[1168,128]{1,0:T(8,128)(2,1)S(1)}, u32[]{:S(2)}, u32[]{:S(2)}) %collective-permute-start.11) | collective-permute-done | bytes 299040 | tf_op jit(solution)/shard_map/ppermute | solution.py:374
  182.8 0.3 convert_add_fusion.1
  183.2 1.2 broadcast_in_dim.48
  184.4 4.8 %all-to-all-start.4 = ((bf16[8,576,128]{2,1,0:T(8,128)(2,1)}), bf16[8,576,128]{2,1,0:T(8,128)(2,1)}, u32[]{:S(2)}, u32[]{:S(2)}) async-start(bf16[8,576,128]{2,1,0:T(8,128)(2,1)} %broadcast_in_dim.48), calls=%async_computation.4 | async-start | bytes 2359296 | tf_op jit(solution)/shard_map/all_to_all | solution.py:263
  189.2 15.7 %all-to-all-done.4 = bf16[8,576,128]{2,1,0:T(8,128)(2,1)} async-done(((bf16[8,576,128]{2,1,0:T(8,128)(2,1)}), bf16[8,576,128]{2,1,0:T(8,128)(2,1)}, u32[]{:S(2)}, u32[]{:S(2)}) %all-to-all-start.4) | async-done | bytes 1179680 | tf_op jit(solution)/shard_map/all_to_all | solution.py:263
  204.9 3.0 %convolution_convert_fusion = bf16[4,128,896]{2,1,0:T(8,128)(2,1)} fusion(bf16[576,896]{1,0:T(8,128)(2,1)S(1)} %copy-done, bf16[4,2,576,128]{3,2,1,0:T(8,128)(2,1)} %bitcast.18, s32[]{:T(128)S(6)} %select_n.143), kind=kOutput, calls=%fused_computation.1 | convolution fusion | flops 528941056 | bytes 2539524 | tf_op jit(solution)/shard_map/dot_general | solution.py:381
  207.9 2.5 collective-permute-start.17
  210.6 2.2 collective-permute-done.17
  212.8 2.3 convert_add_fusion
  215.3 1.1 collective-permute-start.18
  216.4 1.7 collective-permute-start.20
  218.0 1.1 collective-permute-start.19
  219.1 0.3 fusion.27
  219.5 3.9 %collective-permute-done.18 = bf16[128,896]{1,0:T(8,128)(2,1)S(1)} collective-permute-done((bf16[128,896]{1,0:T(8,128)(2,1)S(1)}, bf16[128,896]{1,0:T(8,128)(2,1)S(1)}, u32[]{:S(2)}, u32[]{:S(2)}) %collective-permute-start.18) | collective-permute-done | bytes 229408 | tf_op jit(solution)/shard_map/ppermute | solution.py:29
  223.4 6.0 %collective-permute-done.19 = bf16[128,896]{1,0:T(8,128)(2,1)S(1)} collective-permute-done((bf16[128,896]{1,0:T(8,128)(2,1)S(1)}, bf16[128,896]{1,0:T(8,128)(2,1)S(1)}, u32[]{:S(2)}, u32[]{:S(2)}) %collective-permute-start.19) | collective-permute-done | bytes 229408 | tf_op jit(solution)/shard_map/ppermute | solution.py:29
  229.4 1.1 fusion.1
  230.5 7.5 %all-to-all-start.5 = ((bf16[32,8,896]{2,1,0:T(8,128)(2,1)}), bf16[32,8,896]{2,1,0:T(8,128)(2,1)S(1)}, u32[]{:S(2)}, u32[]{:S(2)}) async-start(bf16[32,8,896]{2,1,0:T(8,128)(2,1)} %fusion.1), calls=%async_computation.5 | async-start | bytes 917504 | tf_op jit(solution)/shard_map/all_to_all | solution.py:263
  238.0 0.6 add_and_fusion
  238.6 0.7 iota_compare_fusion.10
  239.4 15.9 %all-to-all-done.5 = bf16[32,8,896]{2,1,0:T(8,128)(2,1)S(1)} async-done(((bf16[32,8,896]{2,1,0:T(8,128)(2,1)}), bf16[32,8,896]{2,1,0:T(8,128)(2,1)S(1)}, u32[]{:S(2)}, u32[]{:S(2)}) %all-to-all-start.5) | async-done | bytes 458784 | tf_op jit(solution)/shard_map/all_to_all | solution.py:263
  255.2 0.9 fusion.2
  (63 shorter events, 2.2 us)
Async XLA Ops:
  6.5 198.4 %copy-start = (bf16[576,896]{1,0:T(8,128)(2,1)S(1)}, bf16[576,896]{1,0:T(8,128)(2,1)}, u32[]{:S(2)}) copy-start(bf16[576,896]{1,0:T(8,128)(2,1)} %param.25) | copy-start | bytes 3096580
  6.5 65.9 %all-gather.2.cloned.1.call-start = ((), (), s32[]{:S(2)}) async-start(), calls=%async_computation.6 | async-start | bytes 2162688 | tf_op jit(solution)/shard_map/all_gather | solution.py:311
  11.3 23.8 %all-to-all-start = ((bf16[32,8,224]{2,1,0:T(8,128)(2,1)}), bf16[32,8,224]{2,1,0:T(8,128)(2,1)S(1)}, u32[]{:S(2)}, u32[]{:S(2)}) async-start(bf16[32,8,224]{2,1,0:T(8,128)(2,1)} %bitcast.1), calls=%async_computation | async-start | bytes 262144 | tf_op jit(solution)/shard_map/all_to_all | solution.py:263
  24.9 13.6 %copy-start.7 = (s32[32]{0:T(128)S(1)}, s32[32]{0:T(128)}, u32[]{:S(2)}) copy-start(s32[32]{0:T(128)} %counts_ref.1) | copy-start | bytes 388
  24.9 14.9 %copy-start.8 = (f32[896]{0:T(1024)S(1)}, f32[896]{0:T(1024)}, u32[]{:S(2)}) copy-start(f32[896]{0:T(1024)} %param.22) | copy-start | bytes 10756
  35.1 12.9 %all-to-all-start.1 = ((bf16[4,64,512]{2,1,0:T(8,128)(2,1)}), bf16[4,64,512]{2,1,0:T(8,128)(2,1)S(1)}, u32[]{:S(2)}, u32[]{:S(2)}) async-start(bf16[4,64,512]{2,1,0:T(8,128)(2,1)} %score_weights.1), calls=%async_computation.1 | async-start | bytes 524288 | tf_op jit(solution)/shard_map/all_to_all | solution.py:263
  39.0 33.5 %copy-start.2 = (bf16[512,2048]{1,0:T(8,128)(2,1)S(1)}, bf16[512,2048]{1,0:T(8,128)(2,1)}, u32[]{:S(2)}) copy-start(bf16[512,2048]{1,0:T(8,128)(2,1)} %up_ref.1) | copy-start | bytes 6291460
  39.0 0.8 collective-permute-start
  69.8 11.5 %collective-permute-start.1 = (bf16[1024,512]{1,0:T(8,128)(2,1)}, bf16[1024,512]{1,0:T(8,128)(2,1)}, u32[]{:S(2)}, u32[]{:S(2)}) collective-permute-start(bf16[1024,512]{1,0:T(8,128)(2,1)} %bitcast.5.own_ref), channel_id=1, source_target_pairs={{0,8},{8,0},{1,9},{9,1},{2,10},{10,2},{3,11},{11,3},{4,12},{12,4},... | collective-permute-start | bytes 3145736 | tf_op jit(solution)/shard_map/ppermute | solution.py:29
  72.5 1.6 copy-start.3
  74.0 7.3 %copy-start.6 = (bf16[2048,224]{0,1:T(8,128)(2,1)S(1)}, bf16[2048,224]{0,1:T(8,128)(2,1)}, u32[]{:S(2)}) copy-start(bf16[2048,224]{0,1:T(8,128)(2,1)} %param.20) | copy-start | bytes 2752516
  79.4 2.0 copy-start.1
  108.6 32.6 %copy-start.4 = (bf16[896,576]{0,1:T(8,128)(2,1)S(1)}, bf16[896,576]{0,1:T(8,128)(2,1)}, u32[]{:S(2)}) copy-start(bf16[896,576]{0,1:T(8,128)(2,1)} %param.23) | copy-start | bytes 3096580
  108.6 32.6 %copy-start.5 = (bf16[896,576]{0,1:T(8,128)(2,1)S(1)}, bf16[896,576]{0,1:T(8,128)(2,1)}, u32[]{:S(2)}) copy-start(bf16[896,576]{0,1:T(8,128)(2,1)} %param.24) | copy-start | bytes 3096580
  108.7 6.5 %collective-permute-start.5 = (bf16[224,128]{1,0:T(8,128)(2,1)S(1)}, bf16[224,128]{1,0:T(8,128)(2,1)S(1)}, u32[]{:S(2)}, u32[]{:S(2)}) collective-permute-start(bf16[224,128]{1,0:T(8,128)(2,1)S(1)} %add_convert_fusion), channel_id=1, source_target_pairs={{0,192},{1,224},{2,0},{3,32},{4,64},{5,96},{6,128},{7,160},{8,200}... | collective-permute-start | bytes 172040 | tf_op jit(solution)/shard_map/ppermute | solution.py:361
  110.9 4.7 %collective-permute-start.4 = (bf16[224,128]{1,0:T(8,128)(2,1)S(1)}, bf16[224,128]{1,0:T(8,128)(2,1)S(1)}, u32[]{:S(2)}, u32[]{:S(2)}) collective-permute-start(bf16[224,128]{1,0:T(8,128)(2,1)S(1)} %add_convert_fusion), channel_id=1, source_target_pairs={{0,128},{1,160},{2,192},{3,224},{4,0},{5,32},{6,64},{7,96},{8,136}... | collective-permute-start | bytes 172040 | tf_op jit(solution)/shard_map/ppermute | solution.py:361
  113.6 5.2 %collective-permute-start.3 = (bf16[224,128]{1,0:T(8,128)(2,1)S(1)}, bf16[224,128]{1,0:T(8,128)(2,1)S(1)}, u32[]{:S(2)}, u32[]{:S(2)}) collective-permute-start(bf16[224,128]{1,0:T(8,128)(2,1)S(1)} %add_convert_fusion), channel_id=1, source_target_pairs={{0,64},{1,96},{2,128},{3,160},{4,192},{5,224},{6,0},{7,32},{8,72},... | collective-permute-start | bytes 172040 | tf_op jit(solution)/shard_map/ppermute | solution.py:361
  114.5 4.3 %collective-permute-start.2 = (bf16[224,128]{1,0:T(8,128)(2,1)S(1)}, bf16[224,128]{1,0:T(8,128)(2,1)S(1)}, u32[]{:S(2)}, u32[]{:S(2)}) collective-permute-start(bf16[224,128]{1,0:T(8,128)(2,1)S(1)} %add_convert_fusion), channel_id=1, source_target_pairs={{0,0},{1,32},{2,64},{3,96},{4,128},{5,160},{6,192},{7,224},{8,8},{... | collective-permute-start | bytes 172040 | tf_op jit(solution)/shard_map/ppermute | solution.py:361
  118.9 11.2 %collective-permute-start.7 = (bf16[4,224,128]{2,1,0:T(8,128)(2,1)S(1)}, bf16[4,224,128]{2,1,0:T(8,128)(2,1)S(1)}, u32[]{:S(2)}, u32[]{:S(2)}) collective-permute-start(bf16[4,224,128]{2,1,0:T(8,128)(2,1)S(1)} %get-tuple-element.37), channel_id=1, source_target_pairs={{0,32},{16,48},{32,0},{48,16},{1,33},{17,49},{33,1},{49,17},{2,34}... | collective-permute-start | bytes 688136 | tf_op jit(solution)/shard_map/ppermute | solution.py:29
  126.6 9.5 %collective-permute-start.6 = (bf16[4,224,128]{2,1,0:T(8,128)(2,1)S(1)}, bf16[4,224,128]{2,1,0:T(8,128)(2,1)S(1)}, u32[]{:S(2)}, u32[]{:S(2)}) collective-permute-start(bf16[4,224,128]{2,1,0:T(8,128)(2,1)S(1)} %get-tuple-element.37), channel_id=1, source_target_pairs={{0,16},{16,32},{32,48},{48,0},{1,17},{17,33},{33,49},{49,1},{2,18}... | collective-permute-start | bytes 688136 | tf_op jit(solution)/shard_map/ppermute | solution.py:29
  127.3 8.9 %collective-permute-start.8 = (bf16[4,224,128]{2,1,0:T(8,128)(2,1)S(1)}, bf16[4,224,128]{2,1,0:T(8,128)(2,1)S(1)}, u32[]{:S(2)}, u32[]{:S(2)}) collective-permute-start(bf16[4,224,128]{2,1,0:T(8,128)(2,1)S(1)} %get-tuple-element.37), channel_id=1, source_target_pairs={{0,48},{16,0},{32,16},{48,32},{1,49},{17,1},{33,17},{49,33},{2,50}... | collective-permute-start | bytes 688136 | tf_op jit(solution)/shard_map/ppermute | solution.py:29
  136.2 5.0 %collective-permute-start.9 = (bf16[4,4,224,128]{3,2,1,0:T(8,128)(2,1)S(1)}, bf16[4,4,224,128]{3,2,1,0:T(8,128)(2,1)S(1)}, u32[]{:S(2)}, u32[]{:S(2)}) collective-permute-start(bf16[4,4,224,128]{3,2,1,0:T(8,128)(2,1)S(1)} %pad_maximum_fusion.own_ref), channel_id=1, source_target_pairs={{0,8},{8,0},{1,9},{9,1},{2,10},{10,2},{3,11},{11,3},{4,12},{12,4},... | collective-permute-start | bytes 2752520 | tf_op jit(solution)/shard_map/ppermute | solution.py:29
  143.0 12.1 %collective-permute-start.13 = (bf16[1168,128]{1,0:T(8,128)(2,1)S(1)}, bf16[1168,128]{1,0:T(8,128)(2,1)S(1)}, u32[]{:S(2)}, u32[]{:S(2)}) collective-permute-start(bf16[1168,128]{1,0:T(8,128)(2,1)S(1)} %get-tuple-element.21), channel_id=1, source_target_pairs={{0,1},{1,0},{2,3},{3,2},{4,5},{5,4},{6,7},{7,6},{8,9},{9,8},{10,11... | collective-permute-start | bytes 897032 | tf_op jit(solution)/shard_map/ppermute | solution.py:374
  143.6 20.3 %collective-permute-start.14 = (bf16[1168,128]{1,0:T(8,128)(2,1)S(1)}, bf16[1168,128]{1,0:T(8,128)(2,1)S(1)}, u32[]{:S(2)}, u32[]{:S(2)}) collective-permute-start(bf16[1168,128]{1,0:T(8,128)(2,1)S(1)} %get-tuple-element.22), channel_id=1, source_target_pairs={{0,3},{1,2},{2,5},{3,4},{4,7},{5,6},{6,1},{7,0},{8,11},{9,10},{10,... | collective-permute-start | bytes 897032 | tf_op jit(solution)/shard_map/ppermute | solution.py:374
  148.6 19.7 %collective-permute-start.15 = (bf16[1168,128]{1,0:T(8,128)(2,1)S(1)}, bf16[1168,128]{1,0:T(8,128)(2,1)S(1)}, u32[]{:S(2)}, u32[]{:S(2)}) collective-permute-start(bf16[1168,128]{1,0:T(8,128)(2,1)S(1)} %get-tuple-element.23), channel_id=1, source_target_pairs={{0,7},{1,6},{2,1},{3,0},{4,3},{5,2},{6,5},{7,4},{8,15},{9,14},{10,... | collective-permute-start | bytes 897032 | tf_op jit(solution)/shard_map/ppermute | solution.py:374
  150.5 26.6 %collective-permute-start.16 = (bf16[1168,128]{1,0:T(8,128)(2,1)S(1)}, bf16[1168,128]{1,0:T(8,128)(2,1)S(1)}, u32[]{:S(2)}, u32[]{:S(2)}) collective-permute-start(bf16[1168,128]{1,0:T(8,128)(2,1)S(1)} %get-tuple-element.24), channel_id=1, source_target_pairs={{0,5},{1,4},{2,7},{3,6},{4,1},{5,0},{6,3},{7,2},{8,13},{9,12},{10,... | collective-permute-start | bytes 897032 | tf_op jit(solution)/shard_map/ppermute | solution.py:374
  155.0 22.1 %collective-permute-start.10 = (bf16[1168,128]{1,0:T(8,128)(2,1)S(1)}, bf16[1168,128]{1,0:T(8,128)(2,1)S(1)}, u32[]{:S(2)}, u32[]{:S(2)}) collective-permute-start(bf16[1168,128]{1,0:T(8,128)(2,1)S(1)} %get-tuple-element.18), channel_id=1, source_target_pairs={{0,2},{1,3},{2,4},{3,5},{4,6},{5,7},{6,0},{7,1},{8,10},{9,11},{10,... | collective-permute-start | bytes 897032 | tf_op jit(solution)/shard_map/ppermute | solution.py:374
  155.1 27.7 %collective-permute-start.11 = (bf16[1168,128]{1,0:T(8,128)(2,1)S(1)}, bf16[1168,128]{1,0:T(8,128)(2,1)S(1)}, u32[]{:S(2)}, u32[]{:S(2)}) collective-permute-start(bf16[1168,128]{1,0:T(8,128)(2,1)S(1)} %get-tuple-element.19), channel_id=1, source_target_pairs={{0,6},{1,7},{2,0},{3,1},{4,2},{5,3},{6,4},{7,5},{8,14},{9,15},{10,... | collective-permute-start | bytes 897032 | tf_op jit(solution)/shard_map/ppermute | solution.py:374
  163.9 18.9 %collective-permute-start.12 = (bf16[1168,128]{1,0:T(8,128)(2,1)S(1)}, bf16[1168,128]{1,0:T(8,128)(2,1)S(1)}, u32[]{:S(2)}, u32[]{:S(2)}) collective-permute-start(bf16[1168,128]{1,0:T(8,128)(2,1)S(1)} %get-tuple-element.20), channel_id=1, source_target_pairs={{0,4},{1,5},{2,6},{3,7},{4,0},{5,1},{6,2},{7,3},{8,12},{9,13},{10,... | collective-permute-start | bytes 897032 | tf_op jit(solution)/shard_map/ppermute | solution.py:374
  184.4 20.5 %all-to-all-start.4 = ((bf16[8,576,128]{2,1,0:T(8,128)(2,1)}), bf16[8,576,128]{2,1,0:T(8,128)(2,1)}, u32[]{:S(2)}, u32[]{:S(2)}) async-start(bf16[8,576,128]{2,1,0:T(8,128)(2,1)} %broadcast_in_dim.48), calls=%async_computation.4 | async-start | bytes 2359296 | tf_op jit(solution)/shard_map/all_to_all | solution.py:263
  207.9 4.9 %collective-permute-start.17 = (bf16[4,128,896]{2,1,0:T(8,128)(2,1)}, bf16[4,128,896]{2,1,0:T(8,128)(2,1)}, u32[]{:S(2)}, u32[]{:S(2)}) collective-permute-start(bf16[4,128,896]{2,1,0:T(8,128)(2,1)} %convolution_convert_fusion), channel_id=1, source_target_pairs={{0,8},{8,0},{1,9},{9,1},{2,10},{10,2},{3,11},{11,3},{4,12},{12,4},... | collective-permute-start | bytes 2752520 | tf_op jit(solution)/shard_map/ppermute | solution.py:29
  215.3 8.1 %collective-permute-start.18 = (bf16[128,896]{1,0:T(8,128)(2,1)S(1)}, bf16[128,896]{1,0:T(8,128)(2,1)S(1)}, u32[]{:S(2)}, u32[]{:S(2)}) collective-permute-start(bf16[128,896]{1,0:T(8,128)(2,1)S(1)} %get-tuple-element.27), channel_id=1, source_target_pairs={{0,16},{16,32},{32,48},{48,0},{1,17},{17,33},{33,49},{49,1},{2,18}... | collective-permute-start | bytes 688136 | tf_op jit(solution)/shard_map/ppermute | solution.py:29
  216.4 7.0 %collective-permute-start.20 = (bf16[128,896]{1,0:T(8,128)(2,1)S(1)}, bf16[128,896]{1,0:T(8,128)(2,1)S(1)}, u32[]{:S(2)}, u32[]{:S(2)}) collective-permute-start(bf16[128,896]{1,0:T(8,128)(2,1)S(1)} %get-tuple-element.28), channel_id=1, source_target_pairs={{0,48},{16,0},{32,16},{48,32},{1,49},{17,1},{33,17},{49,33},{2,50}... | collective-permute-start | bytes 688136 | tf_op jit(solution)/shard_map/ppermute | solution.py:29
  218.0 11.3 %collective-permute-start.19 = (bf16[128,896]{1,0:T(8,128)(2,1)S(1)}, bf16[128,896]{1,0:T(8,128)(2,1)S(1)}, u32[]{:S(2)}, u32[]{:S(2)}) collective-permute-start(bf16[128,896]{1,0:T(8,128)(2,1)S(1)} %get-tuple-element.29), channel_id=1, source_target_pairs={{0,32},{16,48},{32,0},{48,16},{1,33},{17,49},{33,1},{49,17},{2,34}... | collective-permute-start | bytes 688136 | tf_op jit(solution)/shard_map/ppermute | solution.py:29
  230.5 24.7 %all-to-all-start.5 = ((bf16[32,8,896]{2,1,0:T(8,128)(2,1)}), bf16[32,8,896]{2,1,0:T(8,128)(2,1)S(1)}, u32[]{:S(2)}, u32[]{:S(2)}) async-start(bf16[32,8,896]{2,1,0:T(8,128)(2,1)} %fusion.1), calls=%async_computation.5 | async-start | bytes 917504 | tf_op jit(solution)/shard_map/all_to_all | solution.py:263
Sparse Core Ops, SparseCore 0:
  9.9 60.9 all-gather.1

commit v10 on v7

--- a/solution.py
+++ b/solution.py
@@ -326,6 +326,40 @@
     )(*arrays)
 
 
+def down_kernel(flip, *refs):
+    pieces, (w_ref, out_ref) = refs[:8], refs[8:]
+    swapped = lax.axis_index("zl") ^ lax.axis_index("c") ^ flip
+    x = jnp.concatenate(
+        [
+            jnp.where(swapped == 0, pieces[2 * dx][...], pieces[2 * dx + 1][...])
+            for dx in range(4)
+        ],
+        axis=1,
+    )
+    out = lax.dot_general(
+        x, w_ref[...], (((0,), (0,)), ((), ())), preferred_element_type=F32
+    )
+    out_ref[...] = out.reshape(out_ref.shape).astype(out_ref.dtype)
+
+
+def down(flip, pieces, weight, kind):
+    shape = (4, pieces[0].shape[1], weight.shape[1])
+    return pl.pallas_call(
+        functools.partial(down_kernel, flip),
+        grid=(1,),
+        out_shape=jax.ShapeDtypeStruct(shape, kind),
+        in_specs=[whole(p.shape) for p in pieces] + [whole(weight.shape)],
+        out_specs=whole(shape),
+        compiler_params=pltpu.CompilerParams(vmem_limit_bytes=24 * 2**20),
+        cost_estimate=cost(2),
+        name="down",
+    )(*pieces, weight)
+
+
+def sent_along_hd(x, dx, dz):
+    return lax.ppermute(x, HD, [(i, ((i // 2 + dx) % 4) * 2 + ((i % 2) ^ dz)) for i in range(8)])
+
+
 def exchange(x, axes):
     return lax.all_to_all(x, axes, split_axis=0, concat_axis=0, tiled=True)
 
@@ -445,26 +479,22 @@
     full_other = shifted(full, "c", 1)
     ff = down_weight.shape[0]
     arrays = (full, full_other, gain, gate_weight.T, up_weight.T)
-    near = [(0, 0), (1, 0), (3, 0), (2, 0)]
-    far = [(0, 1), (1, 1), (3, 1), (2, 1)]
-    parts = list(zip(near, gate_up(near, *arrays))) + list(zip(far, gate_up(far, *arrays)))
+    late = [(0, 0), (2, 1), (3, 1), (2, 0)]
+    soon = [(1, 1), (3, 0), (1, 0), (0, 1)]
+    parts = list(zip(late, gate_up(late, *arrays))) + list(zip(soon, gate_up(soon, *arrays)))
     total = parts[0][1].astype(F32)
     for (dx, dz), part in parts[1:]:
-        sends = [(i, ((i // 2 + dx) % 4) * 2 + ((i % 2) ^ dz)) for i in range(8)]
-        total = total + lax.ppermute(part, HD, sends).astype(F32)
+        total = total + sent_along_hd(part, dx, dz).astype(F32)
     scale = lax.rsqrt((total[2 * ff : 2 * ff + 1] + total[2 * ff + 1 : 2 * ff + 2]) / model + 1e-06)
     hidden = (jax.nn.silu(total[:ff] * scale) * (total[ff : 2 * ff] * scale)).astype(BF)
-    hidden = gather(hidden, HD).reshape(4, 2, ff, chunk)
-
-    def down(core):
-        piece = lax.dynamic_index_in_dim(hidden, core, 1, keepdims=False)
-        return lax.dot_general(
-            piece, down_weight, (((1,), (0,)), ((), ())), preferred_element_type=F32
-        )
-
-    sent = shifted(down(1 - c).astype(BF), "c", 1)
-    total = down(c) + sent.astype(F32)
-    pieces = [pick(total, (y + s) & 3) for s in range(4)]
+    hidden = [
+        hidden if r == 0 else sent_along_hd(hidden, r // 2, r % 2) for r in range(8)
+    ]
+
+    sent = shifted(down(1, hidden, down_weight, BF), "c", 1)
+    total = down(0, hidden, down_weight, F32) + sent.astype(F32)
+    turn = lax.axis_index("x") - y
+    pieces = [pick(total, (turn - s) & 3) for s in range(4)]
     total = pieces[0]
     for s in (1, 2, 3):
         total = total + shifted(pieces[s].astype(BF), "y", s).astype(F32)

time: 242 us -> 242 us (level)
  starting transfers between devices: 81.6 us -> 101 us
  waiting for transfers between devices: 108 us -> 89.3 us
  matrix products: 8.08 us -> 2.77 us
  Pallas kernels: 29.1 us -> 33.2 us
    all_to_all x5 -> x4, waiting for transfers between devices: 45 us -> 28 us  [exchange(): return lax.all_to_all(x, axes, split_axis=0, concat_axis=0, tiled=True)]
    ppermute x7 -> x14, starting transfers between devices: 12.5 us -> 28.8 us  [sent_along_hd(): lax.ppermute(x, HD, [(i, (i // 2 + dx) % 4 * 2 + (i % 2 ^ dz)) for i in r...]
    dot_general x2 -> x0, matrix products: 5.33 us -> none  [down(): lax.dot_general(piece, down_weight, (((1,), (0,)), ((), ())), preferred_e...]
    ppermute x16, starting transfers between devices: 36.1 us -> 39.3 us  [shifted(): return lax.ppermute(x, axis, [(i, (i + shift) % n) for i in range(n)])]
    pallas_call x0 -> x2, Pallas kernels: none -> 2.97 us  [down(): pl.pallas_call(functools.partial(down_kernel, flip), grid=(1,), out_shape...]
    ppermute x16, waiting for transfers between devices: 40.8 us -> 38.3 us  [shifted(): return lax.ppermute(x, axis, [(i, (i + shift) % n) for i in range(n)])]
    unnamed x27 -> x43, local copies, waits for them, and re-layouts: 5.47 us -> 4.84 us
    ppermute x7 -> x14, waiting for transfers between devices: 19.6 us -> 20 us  [sent_along_hd(): lax.ppermute(x, HD, [(i, (i // 2 + dx) % 4 * 2 + (i % 2 ^ dz)) for i in r...]
  transfers between devices with their start and end apart: 33 -> 39, of which waited for: 23 -> 22; matrix products, arithmetic and copies ran while one was open for 2% -> 3% of each run, Pallas kernels for 6% -> 7%
where the time goes in v10:
time: 242 us; the launch traced here: 241 us
  starting transfers between devices  101 us (42%)
  waiting for transfers between devices  89.3 us (37%)
  Pallas kernels  33.2 us (14%)
  local copies, waits for them, and re-layouts  8.63 us (4%)
  other arithmetic  5.35 us (2%)
  matrix products  2.77 us (1%)
    ppermute x16, starting transfers between devices, shifted(): return lax.ppermute(x, axis, [(i, (i + shift) % n) for i in range(n)])  39.3 us
    ppermute x16, waiting for transfers between devices, shifted(): return lax.ppermute(x, axis, [(i, (i + shift) % n) for i in range(n)])  38.3 us
    ppermute x14, starting transfers between devices, sent_along_hd(): lax.ppermute(x, HD, [(i, (i // 2 + dx) % 4 * 2 + (i % 2 ^ dz)) for i in r...  28.8 us
    all_to_all x4, waiting for transfers between devices, exchange(): return lax.all_to_all(x, axes, split_axis=0, concat_axis=0, tiled=True)  28 us
    all_to_all x4, starting transfers between devices, exchange(): return lax.all_to_all(x, axes, split_axis=0, concat_axis=0, tiled=True)  20.8 us
    ppermute x14, waiting for transfers between devices, sent_along_hd(): lax.ppermute(x, HD, [(i, (i // 2 + dx) % 4 * 2 + (i % 2 ^ dz)) for i in r...  20 us
    ppermute x4, starting transfers between devices, on_device(): full.append(lax.ppermute(mixed, DP + HD, sends))  11.8 us
    pallas_call x1, Pallas kernels, mix_project(): pl.pallas_call(mix_kernel, grid=(LIVE // STEP,), out_shape=jax.ShapeDtype...  11.4 us
  transfers between devices with their start and end apart: 39, of which 22 were waited for; matrix products, arithmetic and copies ran while one was open for 3% of the time, Pallas kernels for 7%

profile of v10, /device:TPU:1, one launch (start us, length us, event | category | flops | bytes accessed | tf_op | source)
XLA Modules:
  0.0 241.3 jit_solution(9832800979908303275)
XLA Ops:
  0.0 2.1 pack.1
  2.1 3.8 %collective-permute-start = (bf16[96,512]{1,0:T(8,128)(2,1)}, bf16[96,512]{1,0:T(8,128)(2,1)S(1)}, u32[]{:S(2)}, u32[]{:S(2)}) collective-permute-start(bf16[96,512]{1,0:T(8,128)(2,1)} %get-tuple-element.33), channel_id=1, source_target_pairs={{0,64},{64,128},{128,192},{192,0},{1,65},{65,129},{129,193},{193,1... | collective-permute-start | bytes 294920 | tf_op jit(solution)/shard_map/ppermute | solution.py:29
  6.0 5.1 %collective-permute-start.1 = (bf16[96,512]{1,0:T(8,128)(2,1)}, bf16[96,512]{1,0:T(8,128)(2,1)S(1)}, u32[]{:S(2)}, u32[]{:S(2)}) collective-permute-start(bf16[96,512]{1,0:T(8,128)(2,1)} %get-tuple-element.34), channel_id=1, source_target_pairs={{0,128},{64,192},{128,0},{192,64},{1,129},{65,193},{129,1},{193,65... | collective-permute-start | bytes 294920 | tf_op jit(solution)/shard_map/ppermute | solution.py:29
  11.1 2.4 collective-permute-start.2
  13.5 3.8 %score_weights.1 = bf16[4,64,512]{2,1,0:T(8,128)(2,1)} custom-call(s32[32]{0:T(128)} %counts_ref.3, bf16[64,2048]{1,0:T(8,128)(2,1)} %qn_ref.1, bf16[64,1024]{1,0:T(8,128)(2,1)} %qr_ref.1, bf16[64,512]{1,0:T(8,128)(2,1)} %lat_ref.3, bf16[64,64]{1,0:T(8,128)(2,1)} %kr_ref.1, bf16[512,2048]{1,0:T(8,128)(2,1)} %ku_ref.1, s32[1,64]{1,0:T(1,128)} %req_ref.1), custom_call_target="tpu_custom_call" | custom-call | flops 4000000000 | bytes 12000000 | tf_op jit(solution)/shard_map/score_weights/pallas_call | solution.py:165
  17.3 3.4 %all-to-all-start = ((bf16[4,64,512]{2,1,0:T(8,128)(2,1)}), bf16[4,64,512]{2,1,0:T(8,128)(2,1)S(1)}, u32[]{:S(2)}, u32[]{:S(2)}) async-start(bf16[4,64,512]{2,1,0:T(8,128)(2,1)} %score_weights.1), calls=%async_computation | async-start | bytes 524288 | tf_op jit(solution)/shard_map/all_to_all | solution.py:364
  22.1 2.2 repack.1
  24.2 1.3 collective-permute-start.3
  25.5 2.6 %collective-permute-start.4 = (bf16[288,512]{1,0:T(8,128)(2,1)}, bf16[288,512]{1,0:T(8,128)(2,1)S(1)}, u32[]{:S(2)}, u32[]{:S(2)}) collective-permute-start(bf16[288,512]{1,0:T(8,128)(2,1)} %get-tuple-element.38), channel_id=1, source_target_pairs={{0,32},{16,48},{32,0},{48,16},{1,33},{17,49},{33,1},{49,17},{2,34}... | collective-permute-start | bytes 884744 | tf_op jit(solution)/shard_map/ppermute | solution.py:29
  28.1 1.1 collective-permute-start.5
  30.4 2.8 %collective-permute-done.3 = bf16[288,512]{1,0:T(8,128)(2,1)S(1)} collective-permute-done((bf16[288,512]{1,0:T(8,128)(2,1)}, bf16[288,512]{1,0:T(8,128)(2,1)S(1)}, u32[]{:S(2)}, u32[]{:S(2)}) %collective-permute-start.3) | collective-permute-done | bytes 294944 | tf_op jit(solution)/shard_map/ppermute | solution.py:29
  33.2 7.4 %collective-permute-done.4 = bf16[288,512]{1,0:T(8,128)(2,1)S(1)} collective-permute-done((bf16[288,512]{1,0:T(8,128)(2,1)}, bf16[288,512]{1,0:T(8,128)(2,1)S(1)}, u32[]{:S(2)}, u32[]{:S(2)}) %collective-permute-start.4) | collective-permute-done | bytes 294944 | tf_op jit(solution)/shard_map/ppermute | solution.py:29
  40.7 1.1 broadcast_in_dim.61
  41.9 2.0 collective-permute-start.6
  44.8 4.4 %all-to-all-start.1 = ((bf16[4,4,64,512]{3,2,1,0:T(8,128)(2,1)}), bf16[4,4,64,512]{3,2,1,0:T(8,128)(2,1)}, u32[]{:S(2)}, u32[]{:S(2)}) async-start(bf16[4,4,64,512]{3,2,1,0:T(8,128)(2,1)} %broadcast_in_dim.61), calls=%async_computation.1 | async-start | bytes 2097152 | tf_op jit(solution)/shard_map/all_to_all | solution.py:364
  49.6 0.9 slice.42
  50.5 7.2 %live_values.1.prev_ref.cur_ref = bf16[1024,2048]{1,0:T(8,128)(2,1)S(1)} custom-call(s32[2,1,1152]{2,1,0:T(1,128)S(1)} %reshape.470.goes_ref, bf16[1152,512]{1,0:T(8,128)(2,1)S(1)} %constant_dynamic-update-slice_fusion.own_ref, bf16[1152,512]{1,0:T(8,128)(2,1)} %collective-permute-done.6.other_ref, bf16[512,2048]{1,0:T(8,128)(2,1)S(1)} %copy-done.1), custom_call_target="tpu_custom_call" | custom-call | tf_op jit(solution)/shard_map/live_values/pallas_call | solution.py:190
  57.7 2.0 copy-done
  59.9 4.6 %all-to-all-done.1 = bf16[4,4,64,512]{3,2,1,0:T(8,128)(2,1)} async-done(((bf16[4,4,64,512]{3,2,1,0:T(8,128)(2,1)}), bf16[4,4,64,512]{3,2,1,0:T(8,128)(2,1)}, u32[]{:S(2)}, u32[]{:S(2)}) %all-to-all-start.1) | async-done | bytes 1048608 | tf_op jit(solution)/shard_map/all_to_all | solution.py:364
  64.5 0.8 collective-permute-start.8
  65.7 2.1 collective-permute-done.8.other_ref
  67.8 1.2 copy-done.5
  69.0 11.4 %mix_project.1 = bf16[8,224,128]{2,1,0:T(8,128)(2,1)} custom-call(s32[2,1,1024]{2,1,0:T(1,128)S(1)} %compare_select_fusion.goes_ref, bf16[1024,512]{1,0:T(8,128)(2,1)} %bitcast.8.own_ref, bf16[1024,512]{1,0:T(8,128)(2,1)S(1)} %collective-permute-done.8.other_ref, bf16[1024,2048]{1,0:T(8,128)(2,1)} %copy-done, bf16[1024,2048]{1,0:T(8,128)(2,1)} %copy-done, ...), custom_call_target="tpu_custom_call" | custom-call | flops 8999999488 | bytes 27000000 | tf_op jit(solution)/shard_map/mix_project/pallas_call | solution.py:253
  80.4 4.1 %all-to-all-start.2 = ((bf16[8,224,128]{2,1,0:T(8,128)(2,1)}), bf16[8,224,128]{2,1,0:T(8,128)(2,1)S(1)}, u32[]{:S(2)}, u32[]{:S(2)}) async-start(bf16[8,224,128]{2,1,0:T(8,128)(2,1)} %mix_project.1), calls=%async_computation.2 | async-start | bytes 917504 | tf_op jit(solution)/shard_map/all_to_all | solution.py:364
  85.1 8.1 %all-to-all-done.2 = bf16[8,224,128]{2,1,0:T(8,128)(2,1)S(1)} async-done(((bf16[8,224,128]{2,1,0:T(8,128)(2,1)}), bf16[8,224,128]{2,1,0:T(8,128)(2,1)S(1)}, u32[]{:S(2)}, u32[]{:S(2)}) %all-to-all-start.2) | async-done | bytes 458784 | tf_op jit(solution)/shard_map/all_to_all | solution.py:364
  93.4 4.1 %collective-permute-start.12 = (bf16[224,128]{1,0:T(8,128)(2,1)S(1)}, bf16[224,128]{1,0:T(8,128)(2,1)S(1)}, u32[]{:S(2)}, u32[]{:S(2)}) collective-permute-start(bf16[224,128]{1,0:T(8,128)(2,1)S(1)} %add_convert_fusion), channel_id=1, source_target_pairs={{0,192},{1,224},{2,0},{3,32},{4,64},{5,96},{6,128},{7,160},{8,200}... | collective-permute-start | bytes 172040 | tf_op jit(solution)/shard_map/ppermute | solution.py:475
  97.5 5.0 %collective-permute-start.11 = (bf16[224,128]{1,0:T(8,128)(2,1)S(1)}, bf16[224,128]{1,0:T(8,128)(2,1)S(1)}, u32[]{:S(2)}, u32[]{:S(2)}) collective-permute-start(bf16[224,128]{1,0:T(8,128)(2,1)S(1)} %add_convert_fusion), channel_id=1, source_target_pairs={{0,128},{1,160},{2,192},{3,224},{4,0},{5,32},{6,64},{7,96},{8,136}... | collective-permute-start | bytes 172040 | tf_op jit(solution)/shard_map/ppermute | solution.py:475
  102.4 2.0 collective-permute-start.10
  105.2 3.0 %collective-permute-done.10 = bf16[224,128]{1,0:T(8,128)(2,1)S(1)} collective-permute-done((bf16[224,128]{1,0:T(8,128)(2,1)S(1)}, bf16[224,128]{1,0:T(8,128)(2,1)S(1)}, u32[]{:S(2)}, u32[]{:S(2)}) %collective-permute-start.10) | collective-permute-done | bytes 57376 | tf_op jit(solution)/shard_map/ppermute | solution.py:475
  108.2 10.6 %collective-permute-start.15 = (bf16[4,224,128]{2,1,0:T(8,128)(2,1)S(1)}, bf16[4,224,128]{2,1,0:T(8,128)(2,1)S(1)}, u32[]{:S(2)}, u32[]{:S(2)}) collective-permute-start(bf16[4,224,128]{2,1,0:T(8,128)(2,1)S(1)} %get-tuple-element.77), channel_id=1, source_target_pairs={{0,48},{16,0},{32,16},{48,32},{1,49},{17,1},{33,17},{49,33},{2,50}... | collective-permute-start | bytes 688136 | tf_op jit(solution)/shard_map/ppermute | solution.py:29
  118.9 0.8 collective-permute-start.13
  119.7 8.5 %collective-permute-done.15 = bf16[4,224,128]{2,1,0:T(8,128)(2,1)S(1)} collective-permute-done((bf16[4,224,128]{2,1,0:T(8,128)(2,1)S(1)}, bf16[4,224,128]{2,1,0:T(8,128)(2,1)S(1)}, u32[]{:S(2)}, u32[]{:S(2)}) %collective-permute-start.15) | collective-permute-done | bytes 229408 | tf_op jit(solution)/shard_map/ppermute | solution.py:29
  128.2 3.2 %collective-permute-done.13 = bf16[4,224,128]{2,1,0:T(8,128)(2,1)S(1)} collective-permute-done((bf16[4,224,128]{2,1,0:T(8,128)(2,1)S(1)}, bf16[4,224,128]{2,1,0:T(8,128)(2,1)S(1)}, u32[]{:S(2)}, u32[]{:S(2)}) %collective-permute-start.13) | collective-permute-done | bytes 229408 | tf_op jit(solution)/shard_map/ppermute | solution.py:29
  131.5 1.8 collective-permute-start.16
  133.3 2.1 collective-permute-done.16.other_ref
  135.4 1.8 gate_up.3
  137.3 3.2 %collective-permute-start.22 = (bf16[1168,128]{1,0:T(8,128)(2,1)S(1)}, bf16[1168,128]{1,0:T(8,128)(2,1)S(1)}, u32[]{:S(2)}, u32[]{:S(2)}) collective-permute-start(bf16[1168,128]{1,0:T(8,128)(2,1)S(1)} %get-tuple-element.57), channel_id=1, source_target_pairs={{0,2},{1,3},{2,4},{3,5},{4,6},{5,7},{6,0},{7,1},{8,10},{9,11},{10,... | collective-permute-start | bytes 897032 | tf_op jit(solution)/shard_map/ppermute | solution.py:360
  140.5 2.0 collective-permute-start.21
  143.1 1.7 gate_up.2
  144.9 3.1 %collective-permute-start.19 = (bf16[1168,128]{1,0:T(8,128)(2,1)S(1)}, bf16[1168,128]{1,0:T(8,128)(2,1)S(1)}, u32[]{:S(2)}, u32[]{:S(2)}) collective-permute-start(bf16[1168,128]{1,0:T(8,128)(2,1)S(1)} %get-tuple-element.54), channel_id=1, source_target_pairs={{0,4},{1,5},{2,6},{3,7},{4,0},{5,1},{6,2},{7,3},{8,12},{9,13},{10,... | collective-permute-start | bytes 897032 | tf_op jit(solution)/shard_map/ppermute | solution.py:360
  148.0 2.7 %collective-permute-start.18 = (bf16[1168,128]{1,0:T(8,128)(2,1)S(1)}, bf16[1168,128]{1,0:T(8,128)(2,1)S(1)}, u32[]{:S(2)}, u32[]{:S(2)}) collective-permute-start(bf16[1168,128]{1,0:T(8,128)(2,1)S(1)} %get-tuple-element.53), channel_id=1, source_target_pairs={{0,7},{1,6},{2,1},{3,0},{4,3},{5,2},{6,5},{7,4},{8,15},{9,14},{10,... | collective-permute-start | bytes 897032 | tf_op jit(solution)/shard_map/ppermute | solution.py:360
  150.7 2.3 collective-permute-done.22
  153.0 5.2 %collective-permute-start.17 = (bf16[1168,128]{1,0:T(8,128)(2,1)S(1)}, bf16[1168,128]{1,0:T(8,128)(2,1)S(1)}, u32[]{:S(2)}, u32[]{:S(2)}) collective-permute-start(bf16[1168,128]{1,0:T(8,128)(2,1)S(1)} %get-tuple-element.52), channel_id=1, source_target_pairs={{0,5},{1,4},{2,7},{3,6},{4,1},{5,0},{6,3},{7,2},{8,13},{9,12},{10,... | collective-permute-start | bytes 897032 | tf_op jit(solution)/shard_map/ppermute | solution.py:360
  158.2 5.0 %collective-permute-done.19 = bf16[1168,128]{1,0:T(8,128)(2,1)S(1)} collective-permute-done((bf16[1168,128]{1,0:T(8,128)(2,1)S(1)}, bf16[1168,128]{1,0:T(8,128)(2,1)S(1)}, u32[]{:S(2)}, u32[]{:S(2)}) %collective-permute-start.19) | collective-permute-done | bytes 299040 | tf_op jit(solution)/shard_map/ppermute | solution.py:360
  163.3 4.6 %collective-permute-done.17 = bf16[1168,128]{1,0:T(8,128)(2,1)S(1)} collective-permute-done((bf16[1168,128]{1,0:T(8,128)(2,1)S(1)}, bf16[1168,128]{1,0:T(8,128)(2,1)S(1)}, u32[]{:S(2)}, u32[]{:S(2)}) %collective-permute-start.17) | collective-permute-done | bytes 299040 | tf_op jit(solution)/shard_map/ppermute | solution.py:360
  168.3 3.6 %collective-permute-start.24 = (bf16[576,128]{1,0:T(8,128)(2,1)S(1)}, bf16[576,128]{1,0:T(8,128)(2,1)S(1)}, u32[]{:S(2)}, u32[]{:S(2)}) collective-permute-start(bf16[576,128]{1,0:T(8,128)(2,1)S(1)} %fusion.8.refs_0_), channel_id=1, source_target_pairs={{0,1},{1,0},{2,3},{3,2},{4,5},{5,4},{6,7},{7,6},{8,9},{9,8},{10,11... | collective-permute-start | bytes 442376 | tf_op jit(solution)/shard_map/ppermute | solution.py:360
  172.0 3.3 %collective-permute-start.26 = (bf16[576,128]{1,0:T(8,128)(2,1)S(1)}, bf16[576,128]{1,0:T(8,128)(2,1)S(1)}, u32[]{:S(2)}, u32[]{:S(2)}) collective-permute-start(bf16[576,128]{1,0:T(8,128)(2,1)S(1)} %fusion.8.refs_0_), channel_id=1, source_target_pairs={{0,3},{1,2},{2,5},{3,4},{4,7},{5,6},{6,1},{7,0},{8,11},{9,10},{10,... | collective-permute-start | bytes 442376 | tf_op jit(solution)/shard_map/ppermute | solution.py:360
  175.7 2.4 collective-permute-start.28
  178.6 1.5 collective-permute-start.30
  180.2 2.5 %collective-permute-done.27.refs_4_ = bf16[576,128]{1,0:T(8,128)(2,1)S(1)} collective-permute-done((bf16[576,128]{1,0:T(8,128)(2,1)S(1)}, bf16[576,128]{1,0:T(8,128)(2,1)S(1)}, u32[]{:S(2)}, u32[]{:S(2)}) %collective-permute-start.27) | collective-permute-done | bytes 147488 | tf_op jit(solution)/shard_map/ppermute | solution.py:360
  182.7 0.9 collective-permute-done.28.refs_5_
  183.6 4.6 %collective-permute-done.29.refs_6_ = bf16[576,128]{1,0:T(8,128)(2,1)S(1)} collective-permute-done((bf16[576,128]{1,0:T(8,128)(2,1)S(1)}, bf16[576,128]{1,0:T(8,128)(2,1)S(1)}, u32[]{:S(2)}, u32[]{:S(2)}) %collective-permute-start.29) | collective-permute-done | bytes 147488 | tf_op jit(solution)/shard_map/ppermute | solution.py:360
  188.2 2.0 down.3
  190.2 4.7 %collective-permute-start.31 = (bf16[4,128,896]{2,1,0:T(8,128)(2,1)}, bf16[4,128,896]{2,1,0:T(8,128)(2,1)}, u32[]{:S(2)}, u32[]{:S(2)}) collective-permute-start(bf16[4,128,896]{2,1,0:T(8,128)(2,1)} %down.3), channel_id=1, source_target_pairs={{0,8},{8,0},{1,9},{9,1},{2,10},{10,2},{3,11},{11,3},{4,12},{12,4},... | collective-permute-start | bytes 2752520 | tf_op jit(solution)/shard_map/ppermute | solution.py:29
  196.3 1.0 down.2
  197.4 1.3 convert_add_fusion
  198.9 2.1 collective-permute-start.33
  201.4 4.3 %collective-permute-done.34 = bf16[128,896]{1,0:T(8,128)(2,1)S(1)} collective-permute-done((bf16[128,896]{1,0:T(8,128)(2,1)S(1)}, bf16[128,896]{1,0:T(8,128)(2,1)S(1)}, u32[]{:S(2)}, u32[]{:S(2)}) %collective-permute-start.34) | collective-permute-done | bytes 229408 | tf_op jit(solution)/shard_map/ppermute | solution.py:29
  205.7 1.6 collective-permute-done.33
  207.3 5.7 %collective-permute-done.32 = bf16[128,896]{1,0:T(8,128)(2,1)S(1)} collective-permute-done((bf16[128,896]{1,0:T(8,128)(2,1)S(1)}, bf16[128,896]{1,0:T(8,128)(2,1)S(1)}, u32[]{:S(2)}, u32[]{:S(2)}) %collective-permute-start.32) | collective-permute-done | bytes 229408 | tf_op jit(solution)/shard_map/ppermute | solution.py:29
  212.9 1.1 fusion.1
  214.0 9.0 %all-to-all-start.3 = ((bf16[32,8,896]{2,1,0:T(8,128)(2,1)}), bf16[32,8,896]{2,1,0:T(8,128)(2,1)S(1)}, u32[]{:S(2)}, u32[]{:S(2)}) async-start(bf16[32,8,896]{2,1,0:T(8,128)(2,1)} %fusion.1), calls=%async_computation.3 | async-start | bytes 917504 | tf_op jit(solution)/shard_map/all_to_all | solution.py:364
  225.1 15.3 %all-to-all-done.3 = bf16[32,8,896]{2,1,0:T(8,128)(2,1)S(1)} async-done(((bf16[32,8,896]{2,1,0:T(8,128)(2,1)}), bf16[32,8,896]{2,1,0:T(8,128)(2,1)S(1)}, u32[]{:S(2)}, u32[]{:S(2)}) %all-to-all-start.3) | async-done | bytes 458784 | tf_op jit(solution)/shard_map/all_to_all | solution.py:364
  240.4 0.9 fusion.2
  (137 shorter events, 12.1 us)
Async XLA Ops:
  2.1 18.8 %collective-permute-start = (bf16[96,512]{1,0:T(8,128)(2,1)}, bf16[96,512]{1,0:T(8,128)(2,1)S(1)}, u32[]{:S(2)}, u32[]{:S(2)}) collective-permute-start(bf16[96,512]{1,0:T(8,128)(2,1)} %get-tuple-element.33), channel_id=1, source_target_pairs={{0,64},{64,128},{128,192},{192,0},{1,65},{65,129},{129,193},{193,1... | collective-permute-start | bytes 294920 | tf_op jit(solution)/shard_map/ppermute | solution.py:29
  6.0 15.0 %collective-permute-start.1 = (bf16[96,512]{1,0:T(8,128)(2,1)}, bf16[96,512]{1,0:T(8,128)(2,1)S(1)}, u32[]{:S(2)}, u32[]{:S(2)}) collective-permute-start(bf16[96,512]{1,0:T(8,128)(2,1)} %get-tuple-element.34), channel_id=1, source_target_pairs={{0,128},{64,192},{128,0},{192,64},{1,129},{65,193},{129,1},{193,65... | collective-permute-start | bytes 294920 | tf_op jit(solution)/shard_map/ppermute | solution.py:29
  11.1 9.7 %copy-start.16 = (f32[896]{0:T(1024)S(1)}, f32[896]{0:T(1024)}, u32[]{:S(2)}) copy-start(f32[896]{0:T(1024)} %param.22) | copy-start | bytes 10756
  11.1 10.3 %collective-permute-start.2 = (bf16[96,512]{1,0:T(8,128)(2,1)}, bf16[96,512]{1,0:T(8,128)(2,1)S(1)}, u32[]{:S(2)}, u32[]{:S(2)}) collective-permute-start(bf16[96,512]{1,0:T(8,128)(2,1)} %get-tuple-element.35), channel_id=1, source_target_pairs={{0,192},{64,0},{128,64},{192,128},{1,193},{65,1},{129,65},{193,129... | collective-permute-start | bytes 294920 | tf_op jit(solution)/shard_map/ppermute | solution.py:29
  17.3 13.1 %all-to-all-start = ((bf16[4,64,512]{2,1,0:T(8,128)(2,1)}), bf16[4,64,512]{2,1,0:T(8,128)(2,1)S(1)}, u32[]{:S(2)}, u32[]{:S(2)}) async-start(bf16[4,64,512]{2,1,0:T(8,128)(2,1)} %score_weights.1), calls=%async_computation | async-start | bytes 524288 | tf_op jit(solution)/shard_map/all_to_all | solution.py:364
  20.9 0.6 copy-start.17
  20.9 0.7 copy-start.18
  21.4 0.6 copy-start.19
  22.1 7.2 %copy-start.15 = (s32[32]{0:T(128)S(1)}, s32[32]{0:T(128)}, u32[]{:S(2)}) copy-start(s32[32]{0:T(128)} %counts_ref.3) | copy-start | bytes 388
  24.2 17.6 %copy-start.14 = (bf16[288,512]{1,0:T(8,128)(2,1)S(1)}, bf16[288,512]{1,0:T(8,128)(2,1)}, u32[]{:S(2)}) copy-start(bf16[288,512]{1,0:T(8,128)(2,1)} %get-tuple-element.41) | copy-start | bytes 884740
  24.2 8.9 %collective-permute-start.3 = (bf16[288,512]{1,0:T(8,128)(2,1)}, bf16[288,512]{1,0:T(8,128)(2,1)S(1)}, u32[]{:S(2)}, u32[]{:S(2)}) collective-permute-start(bf16[288,512]{1,0:T(8,128)(2,1)} %get-tuple-element.37), channel_id=1, source_target_pairs={{0,16},{16,32},{32,48},{48,0},{1,17},{17,33},{33,49},{49,1},{2,18}... | collective-permute-start | bytes 884744 | tf_op jit(solution)/shard_map/ppermute | solution.py:29
  25.5 15.1 %collective-permute-start.4 = (bf16[288,512]{1,0:T(8,128)(2,1)}, bf16[288,512]{1,0:T(8,128)(2,1)S(1)}, u32[]{:S(2)}, u32[]{:S(2)}) collective-permute-start(bf16[288,512]{1,0:T(8,128)(2,1)} %get-tuple-element.38), channel_id=1, source_target_pairs={{0,32},{16,48},{32,0},{48,16},{1,33},{17,49},{33,1},{49,17},{2,34}... | collective-permute-start | bytes 884744 | tf_op jit(solution)/shard_map/ppermute | solution.py:29
  28.1 12.6 %collective-permute-start.5 = (bf16[288,512]{1,0:T(8,128)(2,1)}, bf16[288,512]{1,0:T(8,128)(2,1)S(1)}, u32[]{:S(2)}, u32[]{:S(2)}) collective-permute-start(bf16[288,512]{1,0:T(8,128)(2,1)} %get-tuple-element.39), channel_id=1, source_target_pairs={{0,48},{16,0},{32,16},{48,32},{1,49},{17,1},{33,17},{49,33},{2,50}... | collective-permute-start | bytes 884744 | tf_op jit(solution)/shard_map/ppermute | solution.py:29
  41.9 7.6 %collective-permute-start.6 = (bf16[1152,512]{1,0:T(8,128)(2,1)S(1)}, bf16[1152,512]{1,0:T(8,128)(2,1)}, u32[]{:S(2)}, u32[]{:S(2)}) collective-permute-start(bf16[1152,512]{1,0:T(8,128)(2,1)S(1)} %constant_dynamic-update-slice_fusion.own_ref), channel_id=1, source_target_pairs={{0,8},{8,0},{1,9},{9,1},{2,10},{10,2},{3,11},{11,3},{4,12},{12,4},... | collective-permute-start | bytes 3538952 | tf_op jit(solution)/shard_map/ppermute | solution.py:29
  44.8 5.7 %copy-start.1 = (bf16[512,2048]{1,0:T(8,128)(2,1)S(1)}, bf16[512,2048]{1,0:T(8,128)(2,1)}, u32[]{:S(2)}) copy-start(bf16[512,2048]{1,0:T(8,128)(2,1)} %up_ref.1) | copy-start | bytes 6291460
  44.8 19.7 %all-to-all-start.1 = ((bf16[4,4,64,512]{3,2,1,0:T(8,128)(2,1)}), bf16[4,4,64,512]{3,2,1,0:T(8,128)(2,1)}, u32[]{:S(2)}, u32[]{:S(2)}) async-start(bf16[4,4,64,512]{3,2,1,0:T(8,128)(2,1)} %broadcast_in_dim.61), calls=%async_computation.1 | async-start | bytes 2097152 | tf_op jit(solution)/shard_map/all_to_all | solution.py:364
  57.7 2.0 copy-start
  64.5 3.3 %collective-permute-start.8 = (bf16[1024,512]{1,0:T(8,128)(2,1)}, bf16[1024,512]{1,0:T(8,128)(2,1)S(1)}, u32[]{:S(2)}, u32[]{:S(2)}) collective-permute-start(bf16[1024,512]{1,0:T(8,128)(2,1)} %bitcast.8.own_ref), channel_id=1, source_target_pairs={{0,8},{8,0},{1,9},{9,1},{2,10},{10,2},{3,11},{11,3},{4,12},{12,4},... | collective-permute-start | bytes 3145736 | tf_op jit(solution)/shard_map/ppermute | solution.py:29
  67.8 1.2 copy-start.5
  80.4 12.9 %all-to-all-start.2 = ((bf16[8,224,128]{2,1,0:T(8,128)(2,1)}), bf16[8,224,128]{2,1,0:T(8,128)(2,1)S(1)}, u32[]{:S(2)}, u32[]{:S(2)}) async-start(bf16[8,224,128]{2,1,0:T(8,128)(2,1)} %mix_project.1), calls=%async_computation.2 | async-start | bytes 917504 | tf_op jit(solution)/shard_map/all_to_all | solution.py:364
  84.5 8.9 %collective-permute-start.7 = (bf16[224,128]{1,0:T(8,128)(2,1)S(1)}, bf16[224,128]{1,0:T(8,128)(2,1)S(1)}, u32[]{:S(2)}, u32[]{:S(2)}) collective-permute-start(bf16[224,128]{1,0:T(8,128)(2,1)S(1)} %fusion.16), channel_id=1, source_target_pairs={{0,0},{1,32},{2,64},{3,96},{4,128},{5,160},{6,192},{7,224},{8,8},{... | collective-permute-start | bytes 172040 | tf_op jit(solution)/shard_map/ppermute | solution.py:458
  93.4 11.8 %collective-permute-start.12 = (bf16[224,128]{1,0:T(8,128)(2,1)S(1)}, bf16[224,128]{1,0:T(8,128)(2,1)S(1)}, u32[]{:S(2)}, u32[]{:S(2)}) collective-permute-start(bf16[224,128]{1,0:T(8,128)(2,1)S(1)} %add_convert_fusion), channel_id=1, source_target_pairs={{0,192},{1,224},{2,0},{3,32},{4,64},{5,96},{6,128},{7,160},{8,200}... | collective-permute-start | bytes 172040 | tf_op jit(solution)/shard_map/ppermute | solution.py:475
  97.5 7.7 %collective-permute-start.11 = (bf16[224,128]{1,0:T(8,128)(2,1)S(1)}, bf16[224,128]{1,0:T(8,128)(2,1)S(1)}, u32[]{:S(2)}, u32[]{:S(2)}) collective-permute-start(bf16[224,128]{1,0:T(8,128)(2,1)S(1)} %add_convert_fusion), channel_id=1, source_target_pairs={{0,128},{1,160},{2,192},{3,224},{4,0},{5,32},{6,64},{7,96},{8,136}... | collective-permute-start | bytes 172040 | tf_op jit(solution)/shard_map/ppermute | solution.py:475
  102.4 5.7 %collective-permute-start.10 = (bf16[224,128]{1,0:T(8,128)(2,1)S(1)}, bf16[224,128]{1,0:T(8,128)(2,1)S(1)}, u32[]{:S(2)}, u32[]{:S(2)}) collective-permute-start(bf16[224,128]{1,0:T(8,128)(2,1)S(1)} %add_convert_fusion), channel_id=1, source_target_pairs={{0,64},{1,96},{2,128},{3,160},{4,192},{5,224},{6,0},{7,32},{8,72},... | collective-permute-start | bytes 172040 | tf_op jit(solution)/shard_map/ppermute | solution.py:475
  104.5 3.7 %collective-permute-start.9 = (bf16[224,128]{1,0:T(8,128)(2,1)S(1)}, bf16[224,128]{1,0:T(8,128)(2,1)S(1)}, u32[]{:S(2)}, u32[]{:S(2)}) collective-permute-start(bf16[224,128]{1,0:T(8,128)(2,1)S(1)} %add_convert_fusion), channel_id=1, source_target_pairs={{0,0},{1,32},{2,64},{3,96},{4,128},{5,160},{6,192},{7,224},{8,8},{... | collective-permute-start | bytes 172040 | tf_op jit(solution)/shard_map/ppermute | solution.py:475
  108.2 27.2 %copy-start.2 = (bf16[896,576]{0,1:T(8,128)(2,1)S(1)}, bf16[896,576]{0,1:T(8,128)(2,1)}, u32[]{:S(2)}) copy-start(bf16[896,576]{0,1:T(8,128)(2,1)} %param.23) | copy-start | bytes 3096580
  108.2 27.2 %copy-start.3 = (bf16[896,576]{0,1:T(8,128)(2,1)S(1)}, bf16[896,576]{0,1:T(8,128)(2,1)}, u32[]{:S(2)}) copy-start(bf16[896,576]{0,1:T(8,128)(2,1)} %param.24) | copy-start | bytes 3096580
  108.2 19.9 %collective-permute-start.15 = (bf16[4,224,128]{2,1,0:T(8,128)(2,1)S(1)}, bf16[4,224,128]{2,1,0:T(8,128)(2,1)S(1)}, u32[]{:S(2)}, u32[]{:S(2)}) collective-permute-start(bf16[4,224,128]{2,1,0:T(8,128)(2,1)S(1)} %get-tuple-element.77), channel_id=1, source_target_pairs={{0,48},{16,0},{32,16},{48,32},{1,49},{17,1},{33,17},{49,33},{2,50}... | collective-permute-start | bytes 688136 | tf_op jit(solution)/shard_map/ppermute | solution.py:29
  118.8 9.3 %collective-permute-start.14 = (bf16[4,224,128]{2,1,0:T(8,128)(2,1)S(1)}, bf16[4,224,128]{2,1,0:T(8,128)(2,1)S(1)}, u32[]{:S(2)}, u32[]{:S(2)}) collective-permute-start(bf16[4,224,128]{2,1,0:T(8,128)(2,1)S(1)} %get-tuple-element.77), channel_id=1, source_target_pairs={{0,32},{16,48},{32,0},{48,16},{1,33},{17,49},{33,1},{49,17},{2,34}... | collective-permute-start | bytes 688136 | tf_op jit(solution)/shard_map/ppermute | solution.py:29
  118.9 12.4 %collective-permute-start.13 = (bf16[4,224,128]{2,1,0:T(8,128)(2,1)S(1)}, bf16[4,224,128]{2,1,0:T(8,128)(2,1)S(1)}, u32[]{:S(2)}, u32[]{:S(2)}) collective-permute-start(bf16[4,224,128]{2,1,0:T(8,128)(2,1)S(1)} %get-tuple-element.77), channel_id=1, source_target_pairs={{0,16},{16,32},{32,48},{48,0},{1,17},{17,33},{33,49},{49,1},{2,18}... | collective-permute-start | bytes 688136 | tf_op jit(solution)/shard_map/ppermute | solution.py:29
  131.5 3.9 %collective-permute-start.16 = (bf16[4,4,224,128]{3,2,1,0:T(8,128)(2,1)S(1)}, bf16[4,4,224,128]{3,2,1,0:T(8,128)(2,1)S(1)}, u32[]{:S(2)}, u32[]{:S(2)}) collective-permute-start(bf16[4,4,224,128]{3,2,1,0:T(8,128)(2,1)S(1)} %pad_maximum_fusion.own_ref), channel_id=1, source_target_pairs={{0,8},{8,0},{1,9},{9,1},{2,10},{10,2},{3,11},{11,3},{4,12},{12,4},... | collective-permute-start | bytes 2752520 | tf_op jit(solution)/shard_map/ppermute | solution.py:29
  137.2 10.8 %collective-permute-start.23 = (bf16[1168,128]{1,0:T(8,128)(2,1)S(1)}, bf16[1168,128]{1,0:T(8,128)(2,1)S(1)}, u32[]{:S(2)}, u32[]{:S(2)}) collective-permute-start(bf16[1168,128]{1,0:T(8,128)(2,1)S(1)} %get-tuple-element.58), channel_id=1, source_target_pairs={{0,1},{1,0},{2,3},{3,2},{4,5},{5,4},{6,7},{7,6},{8,9},{9,8},{10,11... | collective-permute-start | bytes 897032 | tf_op jit(solution)/shard_map/ppermute | solution.py:360
  137.3 15.7 %collective-permute-start.22 = (bf16[1168,128]{1,0:T(8,128)(2,1)S(1)}, bf16[1168,128]{1,0:T(8,128)(2,1)S(1)}, u32[]{:S(2)}, u32[]{:S(2)}) collective-permute-start(bf16[1168,128]{1,0:T(8,128)(2,1)S(1)} %get-tuple-element.57), channel_id=1, source_target_pairs={{0,2},{1,3},{2,4},{3,5},{4,6},{5,7},{6,0},{7,1},{8,10},{9,11},{10,... | collective-permute-start | bytes 897032 | tf_op jit(solution)/shard_map/ppermute | solution.py:360
  140.5 17.7 %collective-permute-start.21 = (bf16[1168,128]{1,0:T(8,128)(2,1)S(1)}, bf16[1168,128]{1,0:T(8,128)(2,1)S(1)}, u32[]{:S(2)}, u32[]{:S(2)}) collective-permute-start(bf16[1168,128]{1,0:T(8,128)(2,1)S(1)} %get-tuple-element.56), channel_id=1, source_target_pairs={{0,6},{1,7},{2,0},{3,1},{4,2},{5,3},{6,4},{7,5},{8,14},{9,15},{10,... | collective-permute-start | bytes 897032 | tf_op jit(solution)/shard_map/ppermute | solution.py:360
  142.5 15.7 %collective-permute-start.20 = (bf16[1168,128]{1,0:T(8,128)(2,1)S(1)}, bf16[1168,128]{1,0:T(8,128)(2,1)S(1)}, u32[]{:S(2)}, u32[]{:S(2)}) collective-permute-start(bf16[1168,128]{1,0:T(8,128)(2,1)S(1)} %get-tuple-element.55), channel_id=1, source_target_pairs={{0,3},{1,2},{2,5},{3,4},{4,7},{5,6},{6,1},{7,0},{8,11},{9,10},{10,... | collective-permute-start | bytes 897032 | tf_op jit(solution)/shard_map/ppermute | solution.py:360
  144.9 18.4 %collective-permute-start.19 = (bf16[1168,128]{1,0:T(8,128)(2,1)S(1)}, bf16[1168,128]{1,0:T(8,128)(2,1)S(1)}, u32[]{:S(2)}, u32[]{:S(2)}) collective-permute-start(bf16[1168,128]{1,0:T(8,128)(2,1)S(1)} %get-tuple-element.54), channel_id=1, source_target_pairs={{0,4},{1,5},{2,6},{3,7},{4,0},{5,1},{6,2},{7,3},{8,12},{9,13},{10,... | collective-permute-start | bytes 897032 | tf_op jit(solution)/shard_map/ppermute | solution.py:360
  148.0 15.3 %collective-permute-start.18 = (bf16[1168,128]{1,0:T(8,128)(2,1)S(1)}, bf16[1168,128]{1,0:T(8,128)(2,1)S(1)}, u32[]{:S(2)}, u32[]{:S(2)}) collective-permute-start(bf16[1168,128]{1,0:T(8,128)(2,1)S(1)} %get-tuple-element.53), channel_id=1, source_target_pairs={{0,7},{1,6},{2,1},{3,0},{4,3},{5,2},{6,5},{7,4},{8,15},{9,14},{10,... | collective-permute-start | bytes 897032 | tf_op jit(solution)/shard_map/ppermute | solution.py:360
  153.0 14.9 %collective-permute-start.17 = (bf16[1168,128]{1,0:T(8,128)(2,1)S(1)}, bf16[1168,128]{1,0:T(8,128)(2,1)S(1)}, u32[]{:S(2)}, u32[]{:S(2)}) collective-permute-start(bf16[1168,128]{1,0:T(8,128)(2,1)S(1)} %get-tuple-element.52), channel_id=1, source_target_pairs={{0,5},{1,4},{2,7},{3,6},{4,1},{5,0},{6,3},{7,2},{8,13},{9,12},{10,... | collective-permute-start | bytes 897032 | tf_op jit(solution)/shard_map/ppermute | solution.py:360
  167.8 20.4 %copy-start.4 = (bf16[576,896]{1,0:T(8,128)(2,1)S(1)}, bf16[576,896]{1,0:T(8,128)(2,1)}, u32[]{:S(2)}) copy-start(bf16[576,896]{1,0:T(8,128)(2,1)} %refs_8_.3) | copy-start | bytes 3096580
  168.3 9.8 %collective-permute-start.24 = (bf16[576,128]{1,0:T(8,128)(2,1)S(1)}, bf16[576,128]{1,0:T(8,128)(2,1)S(1)}, u32[]{:S(2)}, u32[]{:S(2)}) collective-permute-start(bf16[576,128]{1,0:T(8,128)(2,1)S(1)} %fusion.8.refs_0_), channel_id=1, source_target_pairs={{0,1},{1,0},{2,3},{3,2},{4,5},{5,4},{6,7},{7,6},{8,9},{9,8},{10,11... | collective-permute-start | bytes 442376 | tf_op jit(solution)/shard_map/ppermute | solution.py:360
  171.9 6.7 %collective-permute-start.25 = (bf16[576,128]{1,0:T(8,128)(2,1)S(1)}, bf16[576,128]{1,0:T(8,128)(2,1)S(1)}, u32[]{:S(2)}, u32[]{:S(2)}) collective-permute-start(bf16[576,128]{1,0:T(8,128)(2,1)S(1)} %fusion.8.refs_0_), channel_id=1, source_target_pairs={{0,2},{1,3},{2,4},{3,5},{4,6},{5,7},{6,0},{7,1},{8,10},{9,11},{10,... | collective-permute-start | bytes 442376 | tf_op jit(solution)/shard_map/ppermute | solution.py:360
  172.0 8.2 %collective-permute-start.26 = (bf16[576,128]{1,0:T(8,128)(2,1)S(1)}, bf16[576,128]{1,0:T(8,128)(2,1)S(1)}, u32[]{:S(2)}, u32[]{:S(2)}) collective-permute-start(bf16[576,128]{1,0:T(8,128)(2,1)S(1)} %fusion.8.refs_0_), channel_id=1, source_target_pairs={{0,3},{1,2},{2,5},{3,4},{4,7},{5,6},{6,1},{7,0},{8,11},{9,10},{10,... | collective-permute-start | bytes 442376 | tf_op jit(solution)/shard_map/ppermute | solution.py:360
  175.3 7.4 %collective-permute-start.27 = (bf16[576,128]{1,0:T(8,128)(2,1)S(1)}, bf16[576,128]{1,0:T(8,128)(2,1)S(1)}, u32[]{:S(2)}, u32[]{:S(2)}) collective-permute-start(bf16[576,128]{1,0:T(8,128)(2,1)S(1)} %fusion.8.refs_0_), channel_id=1, source_target_pairs={{0,4},{1,5},{2,6},{3,7},{4,0},{5,1},{6,2},{7,3},{8,12},{9,13},{10,... | collective-permute-start | bytes 442376 | tf_op jit(solution)/shard_map/ppermute | solution.py:360
  175.7 7.9 %collective-permute-start.28 = (bf16[576,128]{1,0:T(8,128)(2,1)S(1)}, bf16[576,128]{1,0:T(8,128)(2,1)S(1)}, u32[]{:S(2)}, u32[]{:S(2)}) collective-permute-start(bf16[576,128]{1,0:T(8,128)(2,1)S(1)} %fusion.8.refs_0_), channel_id=1, source_target_pairs={{0,5},{1,4},{2,7},{3,6},{4,1},{5,0},{6,3},{7,2},{8,13},{9,12},{10,... | collective-permute-start | bytes 442376 | tf_op jit(solution)/shard_map/ppermute | solution.py:360
  178.1 10.1 %collective-permute-start.29 = (bf16[576,128]{1,0:T(8,128)(2,1)S(1)}, bf16[576,128]{1,0:T(8,128)(2,1)S(1)}, u32[]{:S(2)}, u32[]{:S(2)}) collective-permute-start(bf16[576,128]{1,0:T(8,128)(2,1)S(1)} %fusion.8.refs_0_), channel_id=1, source_target_pairs={{0,6},{1,7},{2,0},{3,1},{4,2},{5,3},{6,4},{7,5},{8,14},{9,15},{10,... | collective-permute-start | bytes 442376 | tf_op jit(solution)/shard_map/ppermute | solution.py:360
  178.6 9.6 %collective-permute-start.30 = (bf16[576,128]{1,0:T(8,128)(2,1)S(1)}, bf16[576,128]{1,0:T(8,128)(2,1)S(1)}, u32[]{:S(2)}, u32[]{:S(2)}) collective-permute-start(bf16[576,128]{1,0:T(8,128)(2,1)S(1)} %fusion.8.refs_0_), channel_id=1, source_target_pairs={{0,7},{1,6},{2,1},{3,0},{4,3},{5,2},{6,5},{7,4},{8,15},{9,14},{10,... | collective-permute-start | bytes 442376 | tf_op jit(solution)/shard_map/ppermute | solution.py:360
  182.7 7.5 %copy-start.6 = (bf16[576,128]{1,0:T(8,128)(2,1)}, bf16[576,128]{1,0:T(8,128)(2,1)S(1)}, u32[]{:S(2)}) copy-start(bf16[576,128]{1,0:T(8,128)(2,1)S(1)} %collective-permute-done.27.refs_4_) | copy-start | bytes 442372
  183.6 6.6 %copy-start.8 = (bf16[576,128]{1,0:T(8,128)(2,1)}, bf16[576,128]{1,0:T(8,128)(2,1)S(1)}, u32[]{:S(2)}) copy-start(bf16[576,128]{1,0:T(8,128)(2,1)S(1)} %collective-permute-done.28.refs_5_) | copy-start | bytes 442372
  188.2 2.0 copy-start.10
  188.2 2.0 copy-start.12
  190.2 7.2 %collective-permute-start.31 = (bf16[4,128,896]{2,1,0:T(8,128)(2,1)}, bf16[4,128,896]{2,1,0:T(8,128)(2,1)}, u32[]{:S(2)}, u32[]{:S(2)}) collective-permute-start(bf16[4,128,896]{2,1,0:T(8,128)(2,1)} %down.3), channel_id=1, source_target_pairs={{0,8},{8,0},{1,9},{9,1},{2,10},{10,2},{3,11},{11,3},{4,12},{12,4},... | collective-permute-start | bytes 2752520 | tf_op jit(solution)/shard_map/ppermute | solution.py:29
  195.1 0.9 copy-start.7
  195.1 1.0 copy-start.9
  195.1 1.0 copy-start.11
  195.2 1.1 copy-start.13
  198.8 6.9 %collective-permute-start.34 = (bf16[128,896]{1,0:T(8,128)(2,1)S(1)}, bf16[128,896]{1,0:T(8,128)(2,1)S(1)}, u32[]{:S(2)}, u32[]{:S(2)}) collective-permute-start(bf16[128,896]{1,0:T(8,128)(2,1)S(1)} %get-tuple-element.68), channel_id=1, source_target_pairs={{0,48},{16,0},{32,16},{48,32},{1,49},{17,1},{33,17},{49,33},{2,50}... | collective-permute-start | bytes 688136 | tf_op jit(solution)/shard_map/ppermute | solution.py:29
  198.9 8.4 %collective-permute-start.33 = (bf16[128,896]{1,0:T(8,128)(2,1)S(1)}, bf16[128,896]{1,0:T(8,128)(2,1)S(1)}, u32[]{:S(2)}, u32[]{:S(2)}) collective-permute-start(bf16[128,896]{1,0:T(8,128)(2,1)S(1)} %get-tuple-element.69), channel_id=1, source_target_pairs={{0,32},{16,48},{32,0},{48,16},{1,33},{17,49},{33,1},{49,17},{2,34}... | collective-permute-start | bytes 688136 | tf_op jit(solution)/shard_map/ppermute | solution.py:29
  201.0 11.9 %collective-permute-start.32 = (bf16[128,896]{1,0:T(8,128)(2,1)S(1)}, bf16[128,896]{1,0:T(8,128)(2,1)S(1)}, u32[]{:S(2)}, u32[]{:S(2)}) collective-permute-start(bf16[128,896]{1,0:T(8,128)(2,1)S(1)} %get-tuple-element.67), channel_id=1, source_target_pairs={{0,16},{16,32},{32,48},{48,0},{1,17},{17,33},{33,49},{49,1},{2,18}... | collective-permute-start | bytes 688136 | tf_op jit(solution)/shard_map/ppermute | solution.py:29
  214.0 26.3 %all-to-all-start.3 = ((bf16[32,8,896]{2,1,0:T(8,128)(2,1)}), bf16[32,8,896]{2,1,0:T(8,128)(2,1)S(1)}, u32[]{:S(2)}, u32[]{:S(2)}) async-start(bf16[32,8,896]{2,1,0:T(8,128)(2,1)} %fusion.1), calls=%async_computation.3 | async-start | bytes 917504 | tf_op jit(solution)/shard_map/all_to_all | solution.py:364

commit v11 on v10

--- a/solution.py
+++ b/solution.py
@@ -331,7 +331,7 @@
     swapped = lax.axis_index("zl") ^ lax.axis_index("c") ^ flip
     x = jnp.concatenate(
         [
-            jnp.where(swapped == 0, pieces[2 * dx][...], pieces[2 * dx + 1][...])
+            jnp.where(swapped == 0, pieces[4 + dx][...], pieces[dx][...])
             for dx in range(4)
         ],
         axis=1,
@@ -437,6 +437,21 @@
     goes_back = jnp.pad(goes_back, ((0, 0), (0, 0), (0, 32)), constant_values=-1).reshape(2, 1, -1)
     values = live_values(goes_back, got, got_other, value_up)
 
+    place = (((zh * 2 + (y >> 1)) - back_start) & 7) + 8 * eight
+    come = jnp.where(place < back_count, (back_start + place) >> 3, -1)
+    come = (come.reshape(2, -1, 1) == jnp.arange(chunk, dtype=jnp.int32)).astype(BF)
+
+    def tn(a, b):
+        return lax.dot_general(a, b, (((0,), (0,)), ((), ())), preferred_element_type=F32)
+
+    rows = [a.reshape(4, -1, a.shape[1])[:, 4 * slots :].reshape(-1, a.shape[1]) for a in (got, got_other)]
+    rows = tn(rows[0], come[0]) + tn(rows[1], come[1])
+    rows = jnp.where(c == 0, rows[:quarter], rows[quarter : 2 * quarter])
+    weights, values = lax.optimization_barrier((weights, values))
+    weights_other = shifted(weights, "c", 1)
+    part = mix_project(goes, weights, weights_other, values, output_weight.T)
+    projected = jnp.sum(exchange(part, HD).astype(F32), axis=0).astype(BF)
+
     swap = []
     for a in range(4):
         for b in range(8):
@@ -444,52 +459,26 @@
                 for f in range(2):
                     to = (e * 8 + (f * 4 + (b & 3))) * 8 + a * 2 + (b >> 2)
                     swap.append(((a * 8 + b) * 8 + e * 2 + f, to))
-    place = (((zh * 2 + (y >> 1)) - back_start) & 7) + 8 * eight
-    come = jnp.where(place < back_count, (back_start + place) >> 3, -1)
-    come = (come.reshape(2, -1, 1) == jnp.arange(chunk, dtype=jnp.int32)).astype(BF)
-
-    def tn(a, b):
-        return lax.dot_general(a, b, (((0,), (0,)), ((), ())), preferred_element_type=F32)
-
-    rows = [a.reshape(4, -1, a.shape[1])[:, 4 * slots :].reshape(-1, a.shape[1]) for a in (got, got_other)]
-    rows = tn(rows[0], come[0]) + tn(rows[1], come[1])
-    rows = jnp.where(c == 0, rows[:quarter], rows[quarter : 2 * quarter]).astype(BF)
-    rows, values = lax.optimization_barrier((rows, values))
-    rows = lax.ppermute(rows, DP + HD, swap)
-
-    weights, values = lax.optimization_barrier((weights, values))
-    weights_other = shifted(weights, "c", 1)
-    part = mix_project(goes, weights, weights_other, values, output_weight.T)
-    projected = jnp.sum(exchange(part, HD).astype(F32), axis=0)
-    mixed = (rows.astype(F32) + projected).astype(BF)
-
-    full = []
-    for k in range(4):
-        sends = []
-        for a in range(4):
-            for b in range(8):
-                for e in range(4):
-                    for f in range(2):
-                        to = (((e + k) & 3) * 8 + (f * 4 + (b & 3))) * 8 + a * 2 + (b >> 2)
-                        sends.append(((a * 8 + b) * 8 + e * 2 + f, to))
-        full.append(lax.ppermute(mixed, DP + HD, sends))
-    full = jnp.stack(full)
+    projected = lax.ppermute(projected, DP + HD, swap)
+    mixed = (rows + projected.astype(F32)).astype(BF)
+    full = jnp.stack([mixed] + [shifted(mixed, "zh", k) for k in (1, 2, 3)])
 
     full = jnp.stack([full] + [shifted(full, "y", s) for s in (1, 2, 3)])
     full_other = shifted(full, "c", 1)
     ff = down_weight.shape[0]
     arrays = (full, full_other, gain, gate_weight.T, up_weight.T)
-    late = [(0, 0), (2, 1), (3, 1), (2, 0)]
-    soon = [(1, 1), (3, 0), (1, 0), (0, 1)]
+    late = [(0, 0), (1, 0), (3, 0), (2, 0)]
+    soon = [(0, 1), (1, 1), (3, 1), (2, 1)]
     parts = list(zip(late, gate_up(late, *arrays))) + list(zip(soon, gate_up(soon, *arrays)))
     total = parts[0][1].astype(F32)
     for (dx, dz), part in parts[1:]:
         total = total + sent_along_hd(part, dx, dz).astype(F32)
     scale = lax.rsqrt((total[2 * ff : 2 * ff + 1] + total[2 * ff + 1 : 2 * ff + 2]) / model + 1e-06)
     hidden = (jax.nn.silu(total[:ff] * scale) * (total[ff : 2 * ff] * scale)).astype(BF)
-    hidden = [
-        hidden if r == 0 else sent_along_hd(hidden, r // 2, r % 2) for r in range(8)
-    ]
+    got_hidden = {(0, 0): hidden}
+    for step in soon + late[1:]:
+        got_hidden[step] = sent_along_hd(hidden, *step)
+    hidden = [got_hidden[r % 4, 1 - r // 4] for r in range(8)]
 
     sent = shifted(down(1, hidden, down_weight, BF), "c", 1)
     total = down(0, hidden, down_weight, F32) + sent.astype(F32)

time: 242 us -> 236 us (0.975)
  starting transfers between devices: 101 us -> 83.2 us
  waiting for transfers between devices: 89.3 us -> 102 us
    ppermute x14, waiting for transfers between devices: 20 us -> 31.9 us  [sent_along_hd(): lax.ppermute(x, HD, [(i, (i // 2 + dx) % 4 * 2 + (i % 2 ^ dz)) for i in r...]
    ppermute x5 -> x1, starting transfers between devices: 12.4 us -> 0.66 us  [on_device(): projected = lax.ppermute(projected, DP + HD, swap)]
    ppermute x14, starting transfers between devices: 28.8 us -> 18.4 us  [sent_along_hd(): lax.ppermute(x, HD, [(i, (i // 2 + dx) % 4 * 2 + (i % 2 ^ dz)) for i in r...]
    ppermute x16 -> x19, starting transfers between devices: 39.3 us -> 46.5 us  [shifted(): return lax.ppermute(x, axis, [(i, (i + shift) % n) for i in range(n)])]
    ppermute x16 -> x19, waiting for transfers between devices: 38.3 us -> 43.5 us  [shifted(): return lax.ppermute(x, axis, [(i, (i + shift) % n) for i in range(n)])]
    all_to_all x4, starting transfers between devices: 20.8 us -> 17.6 us  [exchange(): return lax.all_to_all(x, axes, split_axis=0, concat_axis=0, tiled=True)]
    ppermute x5 -> x1, waiting for transfers between devices: 3.02 us -> 0.01 us  [on_device(): projected = lax.ppermute(projected, DP + HD, swap)]
  transfers between devices with their start and end apart: 39 -> 38, of which waited for: 22 -> 29; matrix products, arithmetic and copies ran while one was open for 3% -> 3% of each run, Pallas kernels for 7% -> 7%
where the time goes in v11:
time: 236 us
  waiting for transfers between devices  102 us (43%)
  starting transfers between devices  83.2 us (35%)
  Pallas kernels  33.3 us (14%)
  local copies, waits for them, and re-layouts  8.62 us (4%)
  other arithmetic  5.42 us (2%)
  matrix products  2.77 us (1%)
    ppermute x19, starting transfers between devices, shifted(): return lax.ppermute(x, axis, [(i, (i + shift) % n) for i in range(n)])  46.5 us
    ppermute x19, waiting for transfers between devices, shifted(): return lax.ppermute(x, axis, [(i, (i + shift) % n) for i in range(n)])  43.5 us
    ppermute x14, waiting for transfers between devices, sent_along_hd(): lax.ppermute(x, HD, [(i, (i // 2 + dx) % 4 * 2 + (i % 2 ^ dz)) for i in r...  31.9 us
    all_to_all x4, waiting for transfers between devices, exchange(): return lax.all_to_all(x, axes, split_axis=0, concat_axis=0, tiled=True)  26.4 us
    ppermute x14, starting transfers between devices, sent_along_hd(): lax.ppermute(x, HD, [(i, (i // 2 + dx) % 4 * 2 + (i % 2 ^ dz)) for i in r...  18.4 us
    all_to_all x4, starting transfers between devices, exchange(): return lax.all_to_all(x, axes, split_axis=0, concat_axis=0, tiled=True)  17.6 us
    pallas_call x1, Pallas kernels, mix_project(): pl.pallas_call(mix_kernel, grid=(LIVE // STEP,), out_shape=jax.ShapeDtype...  11.5 us
    pallas_call x1, Pallas kernels, live_values(): pl.pallas_call(values_kernel, grid=(LIVE // STEP,), out_shape=jax.ShapeDt...  7.21 us
  transfers between devices with their start and end apart: 38, of which 29 were waited for; matrix products, arithmetic and copies ran while one was open for 3% of the time, Pallas kernels for 7%

profile of v11, /device:TPU:1, one launch (start us, length us, event | category | flops | bytes accessed | tf_op | source)
XLA Modules:
  0.0 235.7 jit_solution(15188565135874268757)
XLA Ops:
  0.0 2.1 pack.1
  2.1 3.8 %collective-permute-start = (bf16[96,512]{1,0:T(8,128)(2,1)}, bf16[96,512]{1,0:T(8,128)(2,1)S(1)}, u32[]{:S(2)}, u32[]{:S(2)}) collective-permute-start(bf16[96,512]{1,0:T(8,128)(2,1)} %get-tuple-element.31), channel_id=1, source_target_pairs={{0,64},{64,128},{128,192},{192,0},{1,65},{65,129},{129,193},{193,1... | collective-permute-start | bytes 294920 | tf_op jit(solution)/shard_map/ppermute | solution.py:29
  6.0 5.1 %collective-permute-start.1 = (bf16[96,512]{1,0:T(8,128)(2,1)}, bf16[96,512]{1,0:T(8,128)(2,1)S(1)}, u32[]{:S(2)}, u32[]{:S(2)}) collective-permute-start(bf16[96,512]{1,0:T(8,128)(2,1)} %get-tuple-element.32), channel_id=1, source_target_pairs={{0,128},{64,192},{128,0},{192,64},{1,129},{65,193},{129,1},{193,65... | collective-permute-start | bytes 294920 | tf_op jit(solution)/shard_map/ppermute | solution.py:29
  11.1 2.4 %collective-permute-start.2 = (bf16[96,512]{1,0:T(8,128)(2,1)}, bf16[96,512]{1,0:T(8,128)(2,1)S(1)}, u32[]{:S(2)}, u32[]{:S(2)}) collective-permute-start(bf16[96,512]{1,0:T(8,128)(2,1)} %get-tuple-element.33), channel_id=1, source_target_pairs={{0,192},{64,0},{128,64},{192,128},{1,193},{65,1},{129,65},{193,129... | collective-permute-start | bytes 294920 | tf_op jit(solution)/shard_map/ppermute | solution.py:29
  13.5 3.8 %score_weights.1 = bf16[4,64,512]{2,1,0:T(8,128)(2,1)} custom-call(s32[32]{0:T(128)} %counts_ref.3, bf16[64,2048]{1,0:T(8,128)(2,1)} %qn_ref.1, bf16[64,1024]{1,0:T(8,128)(2,1)} %qr_ref.1, bf16[64,512]{1,0:T(8,128)(2,1)} %lat_ref.3, bf16[64,64]{1,0:T(8,128)(2,1)} %kr_ref.1, bf16[512,2048]{1,0:T(8,128)(2,1)} %ku_ref.1, s32[1,64]{1,0:T(1,128)} %req_ref.1), custom_call_target="tpu_custom_call" | custom-call | flops 4000000000 | bytes 12000000 | tf_op jit(solution)/shard_map/score_weights/pallas_call | solution.py:165
  17.3 3.4 %all-to-all-start = ((bf16[4,64,512]{2,1,0:T(8,128)(2,1)}), bf16[4,64,512]{2,1,0:T(8,128)(2,1)S(1)}, u32[]{:S(2)}, u32[]{:S(2)}) async-start(bf16[4,64,512]{2,1,0:T(8,128)(2,1)} %score_weights.1), calls=%async_computation | async-start | bytes 524288 | tf_op jit(solution)/shard_map/all_to_all | solution.py:364
  22.1 2.2 repack.1
  24.2 1.3 collective-permute-start.3
  25.5 2.6 %collective-permute-start.4 = (bf16[288,512]{1,0:T(8,128)(2,1)}, bf16[288,512]{1,0:T(8,128)(2,1)S(1)}, u32[]{:S(2)}, u32[]{:S(2)}) collective-permute-start(bf16[288,512]{1,0:T(8,128)(2,1)} %get-tuple-element.36), channel_id=1, source_target_pairs={{0,32},{16,48},{32,0},{48,16},{1,33},{17,49},{33,1},{49,17},{2,34}... | collective-permute-start | bytes 884744 | tf_op jit(solution)/shard_map/ppermute | solution.py:29
  28.1 1.1 collective-permute-start.5
  29.2 4.2 %collective-permute-done.3 = bf16[288,512]{1,0:T(8,128)(2,1)S(1)} collective-permute-done((bf16[288,512]{1,0:T(8,128)(2,1)}, bf16[288,512]{1,0:T(8,128)(2,1)S(1)}, u32[]{:S(2)}, u32[]{:S(2)}) %collective-permute-start.3) | collective-permute-done | bytes 294944 | tf_op jit(solution)/shard_map/ppermute | solution.py:29
  33.4 7.4 %collective-permute-done.4 = bf16[288,512]{1,0:T(8,128)(2,1)S(1)} collective-permute-done((bf16[288,512]{1,0:T(8,128)(2,1)}, bf16[288,512]{1,0:T(8,128)(2,1)S(1)}, u32[]{:S(2)}, u32[]{:S(2)}) %collective-permute-start.4) | collective-permute-done | bytes 294944 | tf_op jit(solution)/shard_map/ppermute | solution.py:29
  40.9 1.1 broadcast_in_dim.61
  42.1 1.9 collective-permute-start.6
  44.1 4.3 %all-to-all-start.1 = ((bf16[4,4,64,512]{3,2,1,0:T(8,128)(2,1)}), bf16[4,4,64,512]{3,2,1,0:T(8,128)(2,1)}, u32[]{:S(2)}, u32[]{:S(2)}) async-start(bf16[4,4,64,512]{3,2,1,0:T(8,128)(2,1)} %broadcast_in_dim.61), calls=%async_computation.1 | async-start | bytes 2097152 | tf_op jit(solution)/shard_map/all_to_all | solution.py:364
  49.7 7.2 %live_values.1.prev_ref.cur_ref = bf16[1024,2048]{1,0:T(8,128)(2,1)S(1)} custom-call(s32[2,1,1152]{2,1,0:T(1,128)S(1)} %reshape.471.goes_ref, bf16[1152,512]{1,0:T(8,128)(2,1)S(1)} %constant_dynamic-update-slice_fusion.own_ref, bf16[1152,512]{1,0:T(8,128)(2,1)} %collective-permute-done.6.other_ref, bf16[512,2048]{1,0:T(8,128)(2,1)S(1)} %copy-done.1), custom_call_target="tpu_custom_call" | custom-call | tf_op jit(solution)/shard_map/live_values/pallas_call | solution.py:190
  57.0 2.0 copy-done
  58.9 4.6 %all-to-all-done.1 = bf16[4,4,64,512]{3,2,1,0:T(8,128)(2,1)} async-done(((bf16[4,4,64,512]{3,2,1,0:T(8,128)(2,1)}), bf16[4,4,64,512]{3,2,1,0:T(8,128)(2,1)}, u32[]{:S(2)}, u32[]{:S(2)}) %all-to-all-start.1) | async-done | bytes 1048608 | tf_op jit(solution)/shard_map/all_to_all | solution.py:364
  63.5 1.0 collective-permute-start.7
  64.9 2.1 collective-permute-done.7.other_ref
  67.0 1.2 copy-done.5
  68.2 11.5 %mix_project.1 = bf16[8,224,128]{2,1,0:T(8,128)(2,1)} custom-call(s32[2,1,1024]{2,1,0:T(1,128)S(1)} %compare_select_fusion.goes_ref, bf16[1024,512]{1,0:T(8,128)(2,1)} %bitcast.8.own_ref, bf16[1024,512]{1,0:T(8,128)(2,1)S(1)} %collective-permute-done.7.other_ref, bf16[1024,2048]{1,0:T(8,128)(2,1)} %copy-done, bf16[1024,2048]{1,0:T(8,128)(2,1)} %copy-done, ...), custom_call_target="tpu_custom_call" | custom-call | flops 8999999488 | bytes 27000000 | tf_op jit(solution)/shard_map/mix_project/pallas_call | solution.py:253
  79.6 4.0 %all-to-all-start.2 = ((bf16[8,224,128]{2,1,0:T(8,128)(2,1)}), bf16[8,224,128]{2,1,0:T(8,128)(2,1)S(1)}, u32[]{:S(2)}, u32[]{:S(2)}) async-start(bf16[8,224,128]{2,1,0:T(8,128)(2,1)} %mix_project.1), calls=%async_computation.2 | async-start | bytes 917504 | tf_op jit(solution)/shard_map/all_to_all | solution.py:364
  84.7 0.9 slice.42
  85.6 6.9 %all-to-all-done.2 = bf16[8,224,128]{2,1,0:T(8,128)(2,1)S(1)} async-done(((bf16[8,224,128]{2,1,0:T(8,128)(2,1)}), bf16[8,224,128]{2,1,0:T(8,128)(2,1)S(1)}, u32[]{:S(2)}, u32[]{:S(2)}) %all-to-all-start.2) | async-done | bytes 458784 | tf_op jit(solution)/shard_map/all_to_all | solution.py:364
  93.5 11.8 %collective-permute-start.11 = (bf16[224,128]{1,0:T(8,128)(2,1)S(1)}, bf16[224,128]{1,0:T(8,128)(2,1)S(1)}, u32[]{:S(2)}, u32[]{:S(2)}) collective-permute-start(bf16[224,128]{1,0:T(8,128)(2,1)S(1)} %fusion.17), channel_id=1, source_target_pairs={{0,192},{64,0},{128,64},{192,128},{1,193},{65,1},{129,65},{193,129... | collective-permute-start | bytes 172040 | tf_op jit(solution)/shard_map/ppermute | solution.py:29
  105.3 4.1 %collective-permute-start.10 = (bf16[224,128]{1,0:T(8,128)(2,1)S(1)}, bf16[224,128]{1,0:T(8,128)(2,1)S(1)}, u32[]{:S(2)}, u32[]{:S(2)}) collective-permute-start(bf16[224,128]{1,0:T(8,128)(2,1)S(1)} %fusion.17), channel_id=1, source_target_pairs={{0,128},{64,192},{128,0},{192,64},{1,129},{65,193},{129,1},{193,65... | collective-permute-start | bytes 172040 | tf_op jit(solution)/shard_map/ppermute | solution.py:29
  109.4 2.3 collective-permute-start.9
  112.2 2.9 %collective-permute-done.9 = bf16[224,128]{1,0:T(8,128)(2,1)S(1)} collective-permute-done((bf16[224,128]{1,0:T(8,128)(2,1)S(1)}, bf16[224,128]{1,0:T(8,128)(2,1)S(1)}, u32[]{:S(2)}, u32[]{:S(2)}) %collective-permute-start.9) | collective-permute-done | bytes 57376 | tf_op jit(solution)/shard_map/ppermute | solution.py:29
  115.2 2.8 %collective-permute-start.14 = (bf16[4,224,128]{2,1,0:T(8,128)(2,1)S(1)}, bf16[4,224,128]{2,1,0:T(8,128)(2,1)S(1)}, u32[]{:S(2)}, u32[]{:S(2)}) collective-permute-start(bf16[4,224,128]{2,1,0:T(8,128)(2,1)S(1)} %get-tuple-element.73), channel_id=1, source_target_pairs={{0,48},{16,0},{32,16},{48,32},{1,49},{17,1},{33,17},{49,33},{2,50}... | collective-permute-start | bytes 688136 | tf_op jit(solution)/shard_map/ppermute | solution.py:29
  118.8 4.8 %collective-permute-done.14 = bf16[4,224,128]{2,1,0:T(8,128)(2,1)S(1)} collective-permute-done((bf16[4,224,128]{2,1,0:T(8,128)(2,1)S(1)}, bf16[4,224,128]{2,1,0:T(8,128)(2,1)S(1)}, u32[]{:S(2)}, u32[]{:S(2)}) %collective-permute-start.14) | collective-permute-done | bytes 229408 | tf_op jit(solution)/shard_map/ppermute | solution.py:29
  124.4 5.3 %collective-permute-done.12 = bf16[4,224,128]{2,1,0:T(8,128)(2,1)S(1)} collective-permute-done((bf16[4,224,128]{2,1,0:T(8,128)(2,1)S(1)}, bf16[4,224,128]{2,1,0:T(8,128)(2,1)S(1)}, u32[]{:S(2)}, u32[]{:S(2)}) %collective-permute-start.12) | collective-permute-done | bytes 229408 | tf_op jit(solution)/shard_map/ppermute | solution.py:29
  129.8 2.6 %collective-permute-start.15 = (bf16[4,4,224,128]{3,2,1,0:T(8,128)(2,1)S(1)}, bf16[4,4,224,128]{3,2,1,0:T(8,128)(2,1)S(1)}, u32[]{:S(2)}, u32[]{:S(2)}) collective-permute-start(bf16[4,4,224,128]{3,2,1,0:T(8,128)(2,1)S(1)} %pad_maximum_fusion.own_ref), channel_id=1, source_target_pairs={{0,8},{8,0},{1,9},{9,1},{2,10},{10,2},{3,11},{11,3},{4,12},{12,4},... | collective-permute-start | bytes 2752520 | tf_op jit(solution)/shard_map/ppermute | solution.py:29
  132.4 2.1 collective-permute-done.15.other_ref
  134.5 1.7 gate_up.3
  136.4 2.4 %collective-permute-start.21 = (bf16[1168,128]{1,0:T(8,128)(2,1)S(1)}, bf16[1168,128]{1,0:T(8,128)(2,1)S(1)}, u32[]{:S(2)}, u32[]{:S(2)}) collective-permute-start(bf16[1168,128]{1,0:T(8,128)(2,1)S(1)} %get-tuple-element.53), channel_id=1, source_target_pairs={{0,7},{1,6},{2,1},{3,0},{4,3},{5,2},{6,5},{7,4},{8,15},{9,14},{10,... | collective-permute-start | bytes 897032 | tf_op jit(solution)/shard_map/ppermute | solution.py:360
  140.1 1.7 gate_up.2
  141.8 2.9 %collective-permute-start.18 = (bf16[1168,128]{1,0:T(8,128)(2,1)S(1)}, bf16[1168,128]{1,0:T(8,128)(2,1)S(1)}, u32[]{:S(2)}, u32[]{:S(2)}) collective-permute-start(bf16[1168,128]{1,0:T(8,128)(2,1)S(1)} %get-tuple-element.50), channel_id=1, source_target_pairs={{0,4},{1,5},{2,6},{3,7},{4,0},{5,1},{6,2},{7,3},{8,12},{9,13},{10,... | collective-permute-start | bytes 897032 | tf_op jit(solution)/shard_map/ppermute | solution.py:360
  144.7 2.4 %collective-permute-done.22 = bf16[1168,128]{1,0:T(8,128)(2,1)S(1)} collective-permute-done((bf16[1168,128]{1,0:T(8,128)(2,1)S(1)}, bf16[1168,128]{1,0:T(8,128)(2,1)S(1)}, u32[]{:S(2)}, u32[]{:S(2)}) %collective-permute-start.22) | collective-permute-done | bytes 299040 | tf_op jit(solution)/shard_map/ppermute | solution.py:360
  147.1 4.2 %collective-permute-start.17 = (bf16[1168,128]{1,0:T(8,128)(2,1)S(1)}, bf16[1168,128]{1,0:T(8,128)(2,1)S(1)}, u32[]{:S(2)}, u32[]{:S(2)}) collective-permute-start(bf16[1168,128]{1,0:T(8,128)(2,1)S(1)} %get-tuple-element.49), channel_id=1, source_target_pairs={{0,6},{1,7},{2,0},{3,1},{4,2},{5,3},{6,4},{7,5},{8,14},{9,15},{10,... | collective-permute-start | bytes 897032 | tf_op jit(solution)/shard_map/ppermute | solution.py:360
  151.3 3.5 %collective-permute-done.21 = bf16[1168,128]{1,0:T(8,128)(2,1)S(1)} collective-permute-done((bf16[1168,128]{1,0:T(8,128)(2,1)S(1)}, bf16[1168,128]{1,0:T(8,128)(2,1)S(1)}, u32[]{:S(2)}, u32[]{:S(2)}) %collective-permute-start.21) | collective-permute-done | bytes 299040 | tf_op jit(solution)/shard_map/ppermute | solution.py:360
  154.8 5.1 %collective-permute-done.20 = bf16[1168,128]{1,0:T(8,128)(2,1)S(1)} collective-permute-done((bf16[1168,128]{1,0:T(8,128)(2,1)S(1)}, bf16[1168,128]{1,0:T(8,128)(2,1)S(1)}, u32[]{:S(2)}, u32[]{:S(2)}) %collective-permute-start.20) | collective-permute-done | bytes 299040 | tf_op jit(solution)/shard_map/ppermute | solution.py:360
  159.9 5.9 %collective-permute-done.19 = bf16[1168,128]{1,0:T(8,128)(2,1)S(1)} collective-permute-done((bf16[1168,128]{1,0:T(8,128)(2,1)S(1)}, bf16[1168,128]{1,0:T(8,128)(2,1)S(1)}, u32[]{:S(2)}, u32[]{:S(2)}) %collective-permute-start.19) | collective-permute-done | bytes 299040 | tf_op jit(solution)/shard_map/ppermute | solution.py:360
  165.7 2.5 %collective-permute-done.17 = bf16[1168,128]{1,0:T(8,128)(2,1)S(1)} collective-permute-done((bf16[1168,128]{1,0:T(8,128)(2,1)S(1)}, bf16[1168,128]{1,0:T(8,128)(2,1)S(1)}, u32[]{:S(2)}, u32[]{:S(2)}) %collective-permute-start.17) | collective-permute-done | bytes 299040 | tf_op jit(solution)/shard_map/ppermute | solution.py:360
  169.0 0.8 collective-permute-start.24
  170.0 1.3 collective-permute-start.25
  171.3 1.7 collective-permute-start.26
  174.0 2.4 %collective-permute-start.28 = (bf16[576,128]{1,0:T(8,128)(2,1)S(1)}, bf16[576,128]{1,0:T(8,128)(2,1)S(1)}, u32[]{:S(2)}, u32[]{:S(2)}) collective-permute-start(bf16[576,128]{1,0:T(8,128)(2,1)S(1)} %fusion.8.refs_4_), channel_id=1, source_target_pairs={{0,4},{1,5},{2,6},{3,7},{4,0},{5,1},{6,2},{7,3},{8,12},{9,13},{10,... | collective-permute-start | bytes 442376 | tf_op jit(solution)/shard_map/ppermute | solution.py:360
  176.4 1.6 collective-permute-done.24.refs_1_
  179.0 3.2 %collective-permute-done.26.refs_3_ = bf16[576,128]{1,0:T(8,128)(2,1)S(1)} collective-permute-done((bf16[576,128]{1,0:T(8,128)(2,1)S(1)}, bf16[576,128]{1,0:T(8,128)(2,1)S(1)}, u32[]{:S(2)}, u32[]{:S(2)}) %collective-permute-start.26) | collective-permute-done | bytes 147488 | tf_op jit(solution)/shard_map/ppermute | solution.py:360
  182.2 1.0 collective-permute-done.27.refs_5_
  183.2 3.2 %collective-permute-done.28.refs_6_ = bf16[576,128]{1,0:T(8,128)(2,1)S(1)} collective-permute-done((bf16[576,128]{1,0:T(8,128)(2,1)S(1)}, bf16[576,128]{1,0:T(8,128)(2,1)S(1)}, u32[]{:S(2)}, u32[]{:S(2)}) %collective-permute-start.28) | collective-permute-done | bytes 147488 | tf_op jit(solution)/shard_map/ppermute | solution.py:360
  186.4 2.5 %collective-permute-done.29.refs_7_ = bf16[576,128]{1,0:T(8,128)(2,1)S(1)} collective-permute-done((bf16[576,128]{1,0:T(8,128)(2,1)S(1)}, bf16[576,128]{1,0:T(8,128)(2,1)S(1)}, u32[]{:S(2)}, u32[]{:S(2)}) %collective-permute-start.29) | collective-permute-done | bytes 147488 | tf_op jit(solution)/shard_map/ppermute | solution.py:360
  188.9 2.0 down.3
  190.9 1.4 collective-permute-start.30
  193.6 1.0 down.2
  194.7 1.4 convert_add_fusion
  198.1 5.0 %collective-permute-done.33 = bf16[128,896]{1,0:T(8,128)(2,1)S(1)} collective-permute-done((bf16[128,896]{1,0:T(8,128)(2,1)S(1)}, bf16[128,896]{1,0:T(8,128)(2,1)S(1)}, u32[]{:S(2)}, u32[]{:S(2)}) %collective-permute-start.33) | collective-permute-done | bytes 229408 | tf_op jit(solution)/shard_map/ppermute | solution.py:29
  203.1 1.7 collective-permute-done.32
  204.8 5.9 %collective-permute-done.31 = bf16[128,896]{1,0:T(8,128)(2,1)S(1)} collective-permute-done((bf16[128,896]{1,0:T(8,128)(2,1)S(1)}, bf16[128,896]{1,0:T(8,128)(2,1)S(1)}, u32[]{:S(2)}, u32[]{:S(2)}) %collective-permute-start.31) | collective-permute-done | bytes 229408 | tf_op jit(solution)/shard_map/ppermute | solution.py:29
  210.7 1.1 fusion.1
  211.8 5.9 %all-to-all-start.3 = ((bf16[32,8,896]{2,1,0:T(8,128)(2,1)}), bf16[32,8,896]{2,1,0:T(8,128)(2,1)S(1)}, u32[]{:S(2)}, u32[]{:S(2)}) async-start(bf16[32,8,896]{2,1,0:T(8,128)(2,1)} %fusion.1), calls=%async_computation.3 | async-start | bytes 917504 | tf_op jit(solution)/shard_map/all_to_all | solution.py:364
  219.8 15.0 %all-to-all-done.3 = bf16[32,8,896]{2,1,0:T(8,128)(2,1)S(1)} async-done(((bf16[32,8,896]{2,1,0:T(8,128)(2,1)}), bf16[32,8,896]{2,1,0:T(8,128)(2,1)S(1)}, u32[]{:S(2)}, u32[]{:S(2)}) %all-to-all-start.3) | async-done | bytes 458784 | tf_op jit(solution)/shard_map/all_to_all | solution.py:364
  234.8 0.9 fusion.2
  (134 shorter events, 17.3 us)
Async XLA Ops:
  2.1 18.6 %collective-permute-start = (bf16[96,512]{1,0:T(8,128)(2,1)}, bf16[96,512]{1,0:T(8,128)(2,1)S(1)}, u32[]{:S(2)}, u32[]{:S(2)}) collective-permute-start(bf16[96,512]{1,0:T(8,128)(2,1)} %get-tuple-element.31), channel_id=1, source_target_pairs={{0,64},{64,128},{128,192},{192,0},{1,65},{65,129},{129,193},{193,1... | collective-permute-start | bytes 294920 | tf_op jit(solution)/shard_map/ppermute | solution.py:29
  6.0 14.8 %collective-permute-start.1 = (bf16[96,512]{1,0:T(8,128)(2,1)}, bf16[96,512]{1,0:T(8,128)(2,1)S(1)}, u32[]{:S(2)}, u32[]{:S(2)}) collective-permute-start(bf16[96,512]{1,0:T(8,128)(2,1)} %get-tuple-element.32), channel_id=1, source_target_pairs={{0,128},{64,192},{128,0},{192,64},{1,129},{65,193},{129,1},{193,65... | collective-permute-start | bytes 294920 | tf_op jit(solution)/shard_map/ppermute | solution.py:29
  11.1 10.3 %collective-permute-start.2 = (bf16[96,512]{1,0:T(8,128)(2,1)}, bf16[96,512]{1,0:T(8,128)(2,1)S(1)}, u32[]{:S(2)}, u32[]{:S(2)}) collective-permute-start(bf16[96,512]{1,0:T(8,128)(2,1)} %get-tuple-element.33), channel_id=1, source_target_pairs={{0,192},{64,0},{128,64},{192,128},{1,193},{65,1},{129,65},{193,129... | collective-permute-start | bytes 294920 | tf_op jit(solution)/shard_map/ppermute | solution.py:29
  17.3 11.9 %all-to-all-start = ((bf16[4,64,512]{2,1,0:T(8,128)(2,1)}), bf16[4,64,512]{2,1,0:T(8,128)(2,1)S(1)}, u32[]{:S(2)}, u32[]{:S(2)}) async-start(bf16[4,64,512]{2,1,0:T(8,128)(2,1)} %score_weights.1), calls=%async_computation | async-start | bytes 524288 | tf_op jit(solution)/shard_map/all_to_all | solution.py:364
  20.7 0.7 copy-start.17
  20.7 0.7 copy-start.18
  21.4 0.6 copy-start.19
  22.1 7.2 %copy-start.16 = (f32[896]{0:T(1024)S(1)}, f32[896]{0:T(1024)}, u32[]{:S(2)}) copy-start(f32[896]{0:T(1024)} %param.22) | copy-start | bytes 10756
  24.2 17.7 %copy-start.14 = (bf16[288,512]{1,0:T(8,128)(2,1)S(1)}, bf16[288,512]{1,0:T(8,128)(2,1)}, u32[]{:S(2)}) copy-start(bf16[288,512]{1,0:T(8,128)(2,1)} %get-tuple-element.39) | copy-start | bytes 884740
  24.2 9.2 %collective-permute-start.3 = (bf16[288,512]{1,0:T(8,128)(2,1)}, bf16[288,512]{1,0:T(8,128)(2,1)S(1)}, u32[]{:S(2)}, u32[]{:S(2)}) collective-permute-start(bf16[288,512]{1,0:T(8,128)(2,1)} %get-tuple-element.35), channel_id=1, source_target_pairs={{0,16},{16,32},{32,48},{48,0},{1,17},{17,33},{33,49},{49,1},{2,18}... | collective-permute-start | bytes 884744 | tf_op jit(solution)/shard_map/ppermute | solution.py:29
  25.5 15.3 %collective-permute-start.4 = (bf16[288,512]{1,0:T(8,128)(2,1)}, bf16[288,512]{1,0:T(8,128)(2,1)S(1)}, u32[]{:S(2)}, u32[]{:S(2)}) collective-permute-start(bf16[288,512]{1,0:T(8,128)(2,1)} %get-tuple-element.36), channel_id=1, source_target_pairs={{0,32},{16,48},{32,0},{48,16},{1,33},{17,49},{33,1},{49,17},{2,34}... | collective-permute-start | bytes 884744 | tf_op jit(solution)/shard_map/ppermute | solution.py:29
  28.1 12.7 %collective-permute-start.5 = (bf16[288,512]{1,0:T(8,128)(2,1)}, bf16[288,512]{1,0:T(8,128)(2,1)S(1)}, u32[]{:S(2)}, u32[]{:S(2)}) collective-permute-start(bf16[288,512]{1,0:T(8,128)(2,1)} %get-tuple-element.37), channel_id=1, source_target_pairs={{0,48},{16,0},{32,16},{48,32},{1,49},{17,1},{33,17},{49,33},{2,50}... | collective-permute-start | bytes 884744 | tf_op jit(solution)/shard_map/ppermute | solution.py:29
  42.1 6.4 %copy-start.15 = (s32[32]{0:T(128)S(1)}, s32[32]{0:T(128)}, u32[]{:S(2)}) copy-start(s32[32]{0:T(128)} %counts_ref.3) | copy-start | bytes 388
  42.1 7.6 %copy-start.1 = (bf16[512,2048]{1,0:T(8,128)(2,1)S(1)}, bf16[512,2048]{1,0:T(8,128)(2,1)}, u32[]{:S(2)}) copy-start(bf16[512,2048]{1,0:T(8,128)(2,1)} %up_ref.1) | copy-start | bytes 6291460
  42.1 7.6 %collective-permute-start.6 = (bf16[1152,512]{1,0:T(8,128)(2,1)S(1)}, bf16[1152,512]{1,0:T(8,128)(2,1)}, u32[]{:S(2)}, u32[]{:S(2)}) collective-permute-start(bf16[1152,512]{1,0:T(8,128)(2,1)S(1)} %constant_dynamic-update-slice_fusion.own_ref), channel_id=1, source_target_pairs={{0,8},{8,0},{1,9},{9,1},{2,10},{10,2},{3,11},{11,3},{4,12},{12,4},... | collective-permute-start | bytes 3538952 | tf_op jit(solution)/shard_map/ppermute | solution.py:29
  44.1 19.4 %all-to-all-start.1 = ((bf16[4,4,64,512]{3,2,1,0:T(8,128)(2,1)}), bf16[4,4,64,512]{3,2,1,0:T(8,128)(2,1)}, u32[]{:S(2)}, u32[]{:S(2)}) async-start(bf16[4,4,64,512]{3,2,1,0:T(8,128)(2,1)} %broadcast_in_dim.61), calls=%async_computation.1 | async-start | bytes 2097152 | tf_op jit(solution)/shard_map/all_to_all | solution.py:364
  56.9 2.0 copy-start
  63.5 3.5 %collective-permute-start.7 = (bf16[1024,512]{1,0:T(8,128)(2,1)}, bf16[1024,512]{1,0:T(8,128)(2,1)S(1)}, u32[]{:S(2)}, u32[]{:S(2)}) collective-permute-start(bf16[1024,512]{1,0:T(8,128)(2,1)} %bitcast.8.own_ref), channel_id=1, source_target_pairs={{0,8},{8,0},{1,9},{9,1},{2,10},{10,2},{3,11},{11,3},{4,12},{12,4},... | collective-permute-start | bytes 3145736 | tf_op jit(solution)/shard_map/ppermute | solution.py:29
  67.0 1.2 copy-start.5
  79.6 12.8 %all-to-all-start.2 = ((bf16[8,224,128]{2,1,0:T(8,128)(2,1)}), bf16[8,224,128]{2,1,0:T(8,128)(2,1)S(1)}, u32[]{:S(2)}, u32[]{:S(2)}) async-start(bf16[8,224,128]{2,1,0:T(8,128)(2,1)} %mix_project.1), calls=%async_computation.2 | async-start | bytes 917504 | tf_op jit(solution)/shard_map/all_to_all | solution.py:364
  92.5 0.9 collective-permute-start.8
  93.5 18.2 %collective-permute-start.11 = (bf16[224,128]{1,0:T(8,128)(2,1)S(1)}, bf16[224,128]{1,0:T(8,128)(2,1)S(1)}, u32[]{:S(2)}, u32[]{:S(2)}) collective-permute-start(bf16[224,128]{1,0:T(8,128)(2,1)S(1)} %fusion.17), channel_id=1, source_target_pairs={{0,192},{64,0},{128,64},{192,128},{1,193},{65,1},{129,65},{193,129... | collective-permute-start | bytes 172040 | tf_op jit(solution)/shard_map/ppermute | solution.py:29
  105.3 6.9 %collective-permute-start.10 = (bf16[224,128]{1,0:T(8,128)(2,1)S(1)}, bf16[224,128]{1,0:T(8,128)(2,1)S(1)}, u32[]{:S(2)}, u32[]{:S(2)}) collective-permute-start(bf16[224,128]{1,0:T(8,128)(2,1)S(1)} %fusion.17), channel_id=1, source_target_pairs={{0,128},{64,192},{128,0},{192,64},{1,129},{65,193},{129,1},{193,65... | collective-permute-start | bytes 172040 | tf_op jit(solution)/shard_map/ppermute | solution.py:29
  109.4 5.7 %collective-permute-start.9 = (bf16[224,128]{1,0:T(8,128)(2,1)S(1)}, bf16[224,128]{1,0:T(8,128)(2,1)S(1)}, u32[]{:S(2)}, u32[]{:S(2)}) collective-permute-start(bf16[224,128]{1,0:T(8,128)(2,1)S(1)} %fusion.17), channel_id=1, source_target_pairs={{0,64},{64,128},{128,192},{192,0},{1,65},{65,129},{129,193},{193,1... | collective-permute-start | bytes 172040 | tf_op jit(solution)/shard_map/ppermute | solution.py:29
  115.1 19.4 %copy-start.2 = (bf16[896,576]{0,1:T(8,128)(2,1)S(1)}, bf16[896,576]{0,1:T(8,128)(2,1)}, u32[]{:S(2)}) copy-start(bf16[896,576]{0,1:T(8,128)(2,1)} %param.23) | copy-start | bytes 3096580
  115.1 19.4 %copy-start.3 = (bf16[896,576]{0,1:T(8,128)(2,1)S(1)}, bf16[896,576]{0,1:T(8,128)(2,1)}, u32[]{:S(2)}) copy-start(bf16[896,576]{0,1:T(8,128)(2,1)} %param.24) | copy-start | bytes 3096580
  115.2 8.5 %collective-permute-start.14 = (bf16[4,224,128]{2,1,0:T(8,128)(2,1)S(1)}, bf16[4,224,128]{2,1,0:T(8,128)(2,1)S(1)}, u32[]{:S(2)}, u32[]{:S(2)}) collective-permute-start(bf16[4,224,128]{2,1,0:T(8,128)(2,1)S(1)} %get-tuple-element.73), channel_id=1, source_target_pairs={{0,48},{16,0},{32,16},{48,32},{1,49},{17,1},{33,17},{49,33},{2,50}... | collective-permute-start | bytes 688136 | tf_op jit(solution)/shard_map/ppermute | solution.py:29
  117.9 6.5 %collective-permute-start.13 = (bf16[4,224,128]{2,1,0:T(8,128)(2,1)S(1)}, bf16[4,224,128]{2,1,0:T(8,128)(2,1)S(1)}, u32[]{:S(2)}, u32[]{:S(2)}) collective-permute-start(bf16[4,224,128]{2,1,0:T(8,128)(2,1)S(1)} %get-tuple-element.73), channel_id=1, source_target_pairs={{0,32},{16,48},{32,0},{48,16},{1,33},{17,49},{33,1},{49,17},{2,34}... | collective-permute-start | bytes 688136 | tf_op jit(solution)/shard_map/ppermute | solution.py:29
  118.1 11.6 %collective-permute-start.12 = (bf16[4,224,128]{2,1,0:T(8,128)(2,1)S(1)}, bf16[4,224,128]{2,1,0:T(8,128)(2,1)S(1)}, u32[]{:S(2)}, u32[]{:S(2)}) collective-permute-start(bf16[4,224,128]{2,1,0:T(8,128)(2,1)S(1)} %get-tuple-element.73), channel_id=1, source_target_pairs={{0,16},{16,32},{32,48},{48,0},{1,17},{17,33},{33,49},{49,1},{2,18}... | collective-permute-start | bytes 688136 | tf_op jit(solution)/shard_map/ppermute | solution.py:29
  129.8 4.7 %collective-permute-start.15 = (bf16[4,4,224,128]{3,2,1,0:T(8,128)(2,1)S(1)}, bf16[4,4,224,128]{3,2,1,0:T(8,128)(2,1)S(1)}, u32[]{:S(2)}, u32[]{:S(2)}) collective-permute-start(bf16[4,4,224,128]{3,2,1,0:T(8,128)(2,1)S(1)} %pad_maximum_fusion.own_ref), channel_id=1, source_target_pairs={{0,8},{8,0},{1,9},{9,1},{2,10},{10,2},{3,11},{11,3},{4,12},{12,4},... | collective-permute-start | bytes 2752520 | tf_op jit(solution)/shard_map/ppermute | solution.py:29
  136.3 10.8 %collective-permute-start.22 = (bf16[1168,128]{1,0:T(8,128)(2,1)S(1)}, bf16[1168,128]{1,0:T(8,128)(2,1)S(1)}, u32[]{:S(2)}, u32[]{:S(2)}) collective-permute-start(bf16[1168,128]{1,0:T(8,128)(2,1)S(1)} %get-tuple-element.54), channel_id=1, source_target_pairs={{0,5},{1,4},{2,7},{3,6},{4,1},{5,0},{6,3},{7,2},{8,13},{9,12},{10,... | collective-permute-start | bytes 897032 | tf_op jit(solution)/shard_map/ppermute | solution.py:360
  136.4 18.4 %collective-permute-start.21 = (bf16[1168,128]{1,0:T(8,128)(2,1)S(1)}, bf16[1168,128]{1,0:T(8,128)(2,1)S(1)}, u32[]{:S(2)}, u32[]{:S(2)}) collective-permute-start(bf16[1168,128]{1,0:T(8,128)(2,1)S(1)} %get-tuple-element.53), channel_id=1, source_target_pairs={{0,7},{1,6},{2,1},{3,0},{4,3},{5,2},{6,5},{7,4},{8,15},{9,14},{10,... | collective-permute-start | bytes 897032 | tf_op jit(solution)/shard_map/ppermute | solution.py:360
  138.8 21.1 %collective-permute-start.20 = (bf16[1168,128]{1,0:T(8,128)(2,1)S(1)}, bf16[1168,128]{1,0:T(8,128)(2,1)S(1)}, u32[]{:S(2)}, u32[]{:S(2)}) collective-permute-start(bf16[1168,128]{1,0:T(8,128)(2,1)S(1)} %get-tuple-element.52), channel_id=1, source_target_pairs={{0,3},{1,2},{2,5},{3,4},{4,7},{5,6},{6,1},{7,0},{8,11},{9,10},{10,... | collective-permute-start | bytes 897032 | tf_op jit(solution)/shard_map/ppermute | solution.py:360
  139.6 26.1 %collective-permute-start.19 = (bf16[1168,128]{1,0:T(8,128)(2,1)S(1)}, bf16[1168,128]{1,0:T(8,128)(2,1)S(1)}, u32[]{:S(2)}, u32[]{:S(2)}) collective-permute-start(bf16[1168,128]{1,0:T(8,128)(2,1)S(1)} %get-tuple-element.51), channel_id=1, source_target_pairs={{0,1},{1,0},{2,3},{3,2},{4,5},{5,4},{6,7},{7,6},{8,9},{9,8},{10,11... | collective-permute-start | bytes 897032 | tf_op jit(solution)/shard_map/ppermute | solution.py:360
  141.8 23.9 %collective-permute-start.18 = (bf16[1168,128]{1,0:T(8,128)(2,1)S(1)}, bf16[1168,128]{1,0:T(8,128)(2,1)S(1)}, u32[]{:S(2)}, u32[]{:S(2)}) collective-permute-start(bf16[1168,128]{1,0:T(8,128)(2,1)S(1)} %get-tuple-element.50), channel_id=1, source_target_pairs={{0,4},{1,5},{2,6},{3,7},{4,0},{5,1},{6,2},{7,3},{8,12},{9,13},{10,... | collective-permute-start | bytes 897032 | tf_op jit(solution)/shard_map/ppermute | solution.py:360
  147.1 21.2 %collective-permute-start.17 = (bf16[1168,128]{1,0:T(8,128)(2,1)S(1)}, bf16[1168,128]{1,0:T(8,128)(2,1)S(1)}, u32[]{:S(2)}, u32[]{:S(2)}) collective-permute-start(bf16[1168,128]{1,0:T(8,128)(2,1)S(1)} %get-tuple-element.49), channel_id=1, source_target_pairs={{0,6},{1,7},{2,0},{3,1},{4,2},{5,3},{6,4},{7,5},{8,14},{9,15},{10,... | collective-permute-start | bytes 897032 | tf_op jit(solution)/shard_map/ppermute | solution.py:360
  154.8 13.5 %collective-permute-start.16 = (bf16[1168,128]{1,0:T(8,128)(2,1)S(1)}, bf16[1168,128]{1,0:T(8,128)(2,1)S(1)}, u32[]{:S(2)}, u32[]{:S(2)}) collective-permute-start(bf16[1168,128]{1,0:T(8,128)(2,1)S(1)} %get-tuple-element.48), channel_id=1, source_target_pairs={{0,2},{1,3},{2,4},{3,5},{4,6},{5,7},{6,0},{7,1},{8,10},{9,11},{10,... | collective-permute-start | bytes 897032 | tf_op jit(solution)/shard_map/ppermute | solution.py:360
  168.3 20.6 %copy-start.4 = (bf16[576,896]{1,0:T(8,128)(2,1)S(1)}, bf16[576,896]{1,0:T(8,128)(2,1)}, u32[]{:S(2)}) copy-start(bf16[576,896]{1,0:T(8,128)(2,1)} %refs_8_.3) | copy-start | bytes 3096580
  168.7 5.2 %collective-permute-start.23 = (bf16[576,128]{1,0:T(8,128)(2,1)S(1)}, bf16[576,128]{1,0:T(8,128)(2,1)S(1)}, u32[]{:S(2)}, u32[]{:S(2)}) collective-permute-start(bf16[576,128]{1,0:T(8,128)(2,1)S(1)} %fusion.8.refs_4_), channel_id=1, source_target_pairs={{0,1},{1,0},{2,3},{3,2},{4,5},{5,4},{6,7},{7,6},{8,9},{9,8},{10,11... | collective-permute-start | bytes 442376 | tf_op jit(solution)/shard_map/ppermute | solution.py:360
  169.0 8.9 %collective-permute-start.24 = (bf16[576,128]{1,0:T(8,128)(2,1)S(1)}, bf16[576,128]{1,0:T(8,128)(2,1)S(1)}, u32[]{:S(2)}, u32[]{:S(2)}) collective-permute-start(bf16[576,128]{1,0:T(8,128)(2,1)S(1)} %fusion.8.refs_4_), channel_id=1, source_target_pairs={{0,3},{1,2},{2,5},{3,4},{4,7},{5,6},{6,1},{7,0},{8,11},{9,10},{10,... | collective-permute-start | bytes 442376 | tf_op jit(solution)/shard_map/ppermute | solution.py:360
  170.0 9.0 %collective-permute-start.25 = (bf16[576,128]{1,0:T(8,128)(2,1)S(1)}, bf16[576,128]{1,0:T(8,128)(2,1)S(1)}, u32[]{:S(2)}, u32[]{:S(2)}) collective-permute-start(bf16[576,128]{1,0:T(8,128)(2,1)S(1)} %fusion.8.refs_4_), channel_id=1, source_target_pairs={{0,5},{1,4},{2,7},{3,6},{4,1},{5,0},{6,3},{7,2},{8,13},{9,12},{10,... | collective-permute-start | bytes 442376 | tf_op jit(solution)/shard_map/ppermute | solution.py:360
  171.3 10.9 %collective-permute-start.26 = (bf16[576,128]{1,0:T(8,128)(2,1)S(1)}, bf16[576,128]{1,0:T(8,128)(2,1)S(1)}, u32[]{:S(2)}, u32[]{:S(2)}) collective-permute-start(bf16[576,128]{1,0:T(8,128)(2,1)S(1)} %fusion.8.refs_4_), channel_id=1, source_target_pairs={{0,7},{1,6},{2,1},{3,0},{4,3},{5,2},{6,5},{7,4},{8,15},{9,14},{10,... | collective-permute-start | bytes 442376 | tf_op jit(solution)/shard_map/ppermute | solution.py:360
  173.1 10.2 %collective-permute-start.27 = (bf16[576,128]{1,0:T(8,128)(2,1)S(1)}, bf16[576,128]{1,0:T(8,128)(2,1)S(1)}, u32[]{:S(2)}, u32[]{:S(2)}) collective-permute-start(bf16[576,128]{1,0:T(8,128)(2,1)S(1)} %fusion.8.refs_4_), channel_id=1, source_target_pairs={{0,2},{1,3},{2,4},{3,5},{4,6},{5,7},{6,0},{7,1},{8,10},{9,11},{10,... | collective-permute-start | bytes 442376 | tf_op jit(solution)/shard_map/ppermute | solution.py:360
  174.0 12.4 %collective-permute-start.28 = (bf16[576,128]{1,0:T(8,128)(2,1)S(1)}, bf16[576,128]{1,0:T(8,128)(2,1)S(1)}, u32[]{:S(2)}, u32[]{:S(2)}) collective-permute-start(bf16[576,128]{1,0:T(8,128)(2,1)S(1)} %fusion.8.refs_4_), channel_id=1, source_target_pairs={{0,4},{1,5},{2,6},{3,7},{4,0},{5,1},{6,2},{7,3},{8,12},{9,13},{10,... | collective-permute-start | bytes 442376 | tf_op jit(solution)/shard_map/ppermute | solution.py:360
  178.0 10.9 %collective-permute-start.29 = (bf16[576,128]{1,0:T(8,128)(2,1)S(1)}, bf16[576,128]{1,0:T(8,128)(2,1)S(1)}, u32[]{:S(2)}, u32[]{:S(2)}) collective-permute-start(bf16[576,128]{1,0:T(8,128)(2,1)S(1)} %fusion.8.refs_4_), channel_id=1, source_target_pairs={{0,6},{1,7},{2,0},{3,1},{4,2},{5,3},{6,4},{7,5},{8,14},{9,15},{10,... | collective-permute-start | bytes 442376 | tf_op jit(solution)/shard_map/ppermute | solution.py:360
  182.2 8.7 %copy-start.6 = (bf16[576,128]{1,0:T(8,128)(2,1)}, bf16[576,128]{1,0:T(8,128)(2,1)S(1)}, u32[]{:S(2)}) copy-start(bf16[576,128]{1,0:T(8,128)(2,1)S(1)} %collective-permute-done.26.refs_3_) | copy-start | bytes 442372
  183.2 7.7 %copy-start.8 = (bf16[576,128]{1,0:T(8,128)(2,1)}, bf16[576,128]{1,0:T(8,128)(2,1)S(1)}, u32[]{:S(2)}) copy-start(bf16[576,128]{1,0:T(8,128)(2,1)S(1)} %collective-permute-done.27.refs_5_) | copy-start | bytes 442372
  186.4 4.5 %copy-start.10 = (bf16[576,128]{1,0:T(8,128)(2,1)}, bf16[576,128]{1,0:T(8,128)(2,1)S(1)}, u32[]{:S(2)}) copy-start(bf16[576,128]{1,0:T(8,128)(2,1)S(1)} %collective-permute-done.28.refs_6_) | copy-start | bytes 442372
  188.9 2.0 copy-start.12
  190.9 3.8 %collective-permute-start.30 = (bf16[4,128,896]{2,1,0:T(8,128)(2,1)}, bf16[4,128,896]{2,1,0:T(8,128)(2,1)}, u32[]{:S(2)}, u32[]{:S(2)}) collective-permute-start(bf16[4,128,896]{2,1,0:T(8,128)(2,1)} %down.3), channel_id=1, source_target_pairs={{0,8},{8,0},{1,9},{9,1},{2,10},{10,2},{3,11},{11,3},{4,12},{12,4},... | collective-permute-start | bytes 2752520 | tf_op jit(solution)/shard_map/ppermute | solution.py:29
  192.5 0.9 copy-start.7
  192.5 1.0 copy-start.9
  192.5 1.0 copy-start.11
  192.5 1.1 copy-start.13
  196.2 6.9 %collective-permute-start.33 = (bf16[128,896]{1,0:T(8,128)(2,1)S(1)}, bf16[128,896]{1,0:T(8,128)(2,1)S(1)}, u32[]{:S(2)}, u32[]{:S(2)}) collective-permute-start(bf16[128,896]{1,0:T(8,128)(2,1)S(1)} %get-tuple-element.64), channel_id=1, source_target_pairs={{0,48},{16,0},{32,16},{48,32},{1,49},{17,1},{33,17},{49,33},{2,50}... | collective-permute-start | bytes 688136 | tf_op jit(solution)/shard_map/ppermute | solution.py:29
  196.8 8.0 %collective-permute-start.32 = (bf16[128,896]{1,0:T(8,128)(2,1)S(1)}, bf16[128,896]{1,0:T(8,128)(2,1)S(1)}, u32[]{:S(2)}, u32[]{:S(2)}) collective-permute-start(bf16[128,896]{1,0:T(8,128)(2,1)S(1)} %get-tuple-element.65), channel_id=1, source_target_pairs={{0,32},{16,48},{32,0},{48,16},{1,33},{17,49},{33,1},{49,17},{2,34}... | collective-permute-start | bytes 688136 | tf_op jit(solution)/shard_map/ppermute | solution.py:29
  197.0 13.7 %collective-permute-start.31 = (bf16[128,896]{1,0:T(8,128)(2,1)S(1)}, bf16[128,896]{1,0:T(8,128)(2,1)S(1)}, u32[]{:S(2)}, u32[]{:S(2)}) collective-permute-start(bf16[128,896]{1,0:T(8,128)(2,1)S(1)} %get-tuple-element.63), channel_id=1, source_target_pairs={{0,16},{16,32},{32,48},{48,0},{1,17},{17,33},{33,49},{49,1},{2,18}... | collective-permute-start | bytes 688136 | tf_op jit(solution)/shard_map/ppermute | solution.py:29
  211.8 23.0 %all-to-all-start.3 = ((bf16[32,8,896]{2,1,0:T(8,128)(2,1)}), bf16[32,8,896]{2,1,0:T(8,128)(2,1)S(1)}, u32[]{:S(2)}, u32[]{:S(2)}) async-start(bf16[32,8,896]{2,1,0:T(8,128)(2,1)} %fusion.1), calls=%async_computation.3 | async-start | bytes 917504 | tf_op jit(solution)/shard_map/all_to_all | solution.py:364
